TPU v7x, 32 devices: a whole 2x2x4 slice. The times are simulated.
32 devices in a mesh: mp: 2 (over x), lat: 2 (over y), lon: 8 (over z, core).
Axes of the slice: x: 2, y: 2, z: 4, core: 2. Of those that a mesh axis runs over, the one named last changes fastest.
Arguments:
- adjoint: float32 [2, 2, 72, 32, 1024], P('mp', None, None, 'lat', 'lon'), may hold values from -6 to 6
- courant: float32 [2, 2, 32, 1024], P('mp', None, 'lat', 'lon'), may hold values from 0.05 to 0.45
- diffusivity: float32 [2, 71, 32, 1024], P('mp', None, 'lat', 'lon'), may hold values from 0.005 to 0.24
- coupling: float32 [2, 32, 1024], P('mp', 'lat', 'lon'), may hold values from 0.05 to 0.45
- partner: int32 [2, 2048], P('mp', ('lat', 'lon')), may hold values from 0 to 2047, as said below
- mask: int32 [2, 32, 1024], P('mp', 'lat', 'lon'), may hold values from 0 to 1, as said below
Outputs:
- result_adjoint: float32 [2, 2, 72, 32, 1024], P('mp', None, None, 'lat', 'lon')
Inputs may be any that keep to these rules, and one draw needn't show every extreme that they name: partner[0, q] is the ocean tile coupled to atmosphere tile q and partner[1] is its inverse, tiles numbered as in the first step; the tiles of one device have partners on exactly 8 devices, 16 tiles on each. `mask`: 1 marks a cell over sea; coupled tiles carry the same flags cell by cell.
All inputs are finite; a program needn't handle non-finite values.
Results may differ from a plain program's by a relative error of at most 0.00002.
Values sent between devices are 32-bit elements; how exact they have to be, the bound alone decides.
No kernel may reach another device: no remote copies, remote signals or barrier semaphores. Data moves between devices by JAX's collectives and lax.ppermute only.
A program may use at most 64 MiB of HBM per device.

v0:
```python
import jax
import jax.numpy as jnp
from jax import lax
from jax.sharding import PartitionSpec as P

TILE = 16
STEPS = 4


def passed_along(block, axis, distance):
    devices = range(lax.axis_size(axis))
    route = [((i - distance) % len(devices), i) for i in devices]
    return lax.ppermute(block, axis, route)


def shifted(value, axis, steps):
    count = lax.axis_size(axis)
    first, last = (max(0, -steps), min(count, count - steps))
    return lax.ppermute(value, axis, [(source, source + steps) for source in range(first, last)])


def from_partner(array, axis, apart):
    return lax.ppermute(array, axis, [(i, i ^ 1 << apart) for i in range(lax.axis_size(axis))])


def advect_local(fields, zonal, meridional, weight):
    eastward = zonal * fields
    northward = meridional * fields
    east_edge = passed_along(eastward[..., 0:1], "lon", -1)
    north_edge = shifted(northward[..., 0:1, :], "lat", -1)
    east_next = jnp.concatenate([eastward[..., 1:], east_edge], axis=-1)
    north_next = jnp.concatenate([northward[..., 1:, :], north_edge], axis=-2)
    return weight * fields + east_next + north_next


def diffuse(fields, kappa):
    fluxes = kappa * (fields[:, 1:] - fields[:, :-1])
    edge = jnp.zeros_like(fields[:, :1])
    return fields + jnp.concatenate([fluxes, edge], 1) - jnp.concatenate([edge, fluxes], 1)


def local_tiles(surface):
    tracers, rows_here, cols_here = surface.shape
    shaped = surface.reshape(tracers, rows_here, cols_here // TILE, TILE)
    return shaped.transpose(1, 2, 0, 3).reshape(rows_here * (cols_here // TILE), tracers * TILE)


def from_local_tiles(tile_rows, tracers, rows_here, cols_here):
    shaped = tile_rows.reshape(rows_here, cols_here // TILE, tracers, TILE)
    return shaped.transpose(2, 0, 1, 3).reshape(tracers, rows_here, cols_here)


def send_slots(routing, tile_count, capacity):
    target = routing // tile_count
    same_target = target[:, None] == target[None, :]
    positions = jnp.arange(tile_count, dtype=jnp.int32)
    earlier = jnp.sum(same_target & (positions[None, :] < positions[:, None]), axis=1)
    return target * capacity + earlier


def recv_slots(routing, tile_count, capacity):
    target = routing // tile_count
    local_slot = routing % tile_count
    same_target = target[:, None] == target[None, :]
    earlier = jnp.sum(same_target & (local_slot[None, :] < local_slot[:, None]), axis=1)
    return target * capacity + earlier


def local(adjoint, courant, diffusivity, coupling, partner, mask):
    fields = adjoint[0]
    zonal = courant[0, 0]
    meridional = courant[0, 1]
    weight = 1.0 - zonal - meridional
    kappa = diffusivity[0][None]
    scale_field = coupling[0]
    routing = partner[0]
    tracers, levels, rows_here, cols_here = fields.shape
    tile_count = routing.shape[0]
    groups = lax.axis_size("lat") * lax.axis_size("lon")
    capacity = max(2, 2 * tile_count // groups)
    wet_tiles = local_tiles(
        jnp.broadcast_to(mask[0].astype(jnp.float32), (tracers, rows_here, cols_here))
    )
    arrive_slot = recv_slots(routing, tile_count, capacity)
    depart_slot = send_slots(routing, tile_count, capacity)
    for step_index in range(STEPS):
        fields = diffuse(advect_local(fields, zonal, meridional, weight), kappa)
        surface = fields[:, 0]
        own_tiles = local_tiles(surface)
        scaled = local_tiles(scale_field * surface)
        empty_slots = jnp.zeros((groups * capacity, scaled.shape[1]), jnp.float32)
        buffer = empty_slots.at[depart_slot].set(scaled)
        moved_slots = lax.all_to_all(
            buffer, ("lat", "lon"), split_axis=0, concat_axis=0, tiled=True
        )
        arrived = from_partner(moved_slots, "mp", 0)
        received = arrived[arrive_slot]
        new_tiles = own_tiles + wet_tiles * (received - scaled)
        fields = fields.at[:, 0].set(from_local_tiles(new_tiles, tracers, rows_here, cols_here))
    return fields[None]


def solution(mesh):
    placed = (
        P("mp", None, None, "lat", "lon"),
        P("mp", None, "lat", "lon"),
        P("mp", None, "lat", "lon"),
        P("mp", "lat", "lon"),
        P("mp", ("lat", "lon")),
        P("mp", "lat", "lon"),
    )
    return jax.shard_map(
        local,
        mesh=mesh,
        in_specs=placed,
        out_specs=P("mp", None, None, "lat", "lon"),
        check_vma=False,
    )
```

profile of v0, /device:TPU:0, one launch (start us, length us, event | category | flops | bytes accessed | tf_op | source)
XLA Modules:
  0.0 197.3 jit_solution(8891782636066742667)
XLA Ops:
  0.9 2.2 %copy.54 = f32[1,2,72,16,128]{2,3,4,1,0:T(8,128)S(1)} copy(f32[1,2,72,16,128]{4,3,2,1,0:T(8,128)} %param.14) | data formatting | bytes 2359296 | tf_op args[0]
  4.5 4.5 %collective-permute-start = (f32[2,72,16,1]{1,2,3,0:T(8,128)}, f32[2,72,16,1]{1,2,3,0:T(8,128)S(1)}, u32[]{:S(2)}, u32[]{:S(2)}) collective-permute-start(f32[2,72,16,1]{1,2,3,0:T(8,128)} %slice.229), channel_id=1, source_target_pairs={{1,0},{2,1},{3,2},{4,3},{5,4},{6,5},{7,6},{0,7},{9,8},{10,9},{11,1... | collective-permute-start | bytes 27656 | tf_op jit(solution)/shard_map/ppermute | solution.py:13
  17.0 2.9 %fusion.4 = f32[2,72,16,128]{1,2,3,0:T(8,128)S(1)} fusion(f32[2,72,16,1]{1,2,3,0:T(8,128)S(1)} %collective-permute-done, f32[2,72,16,127]{1,2,3,0:T(8,128)} %slice.228, f32[2,72,1,128]{1,2,3,0:T(1,128)S(1)} %collective-permute-done.1, f32[2,72,15,128]{1,2,3,0:T(8,128)} %slice.230, f32[1,2,72,16,128]{2,3,4,1,0:T(8,128)S(1)} %copy.54, f32[16,128]{0,1:T(8,128)S(1)} %copy.53), kind=kLoop, calls=%fused_computation.17 | loop fusion | flops 1474560 | bytes 4726784 | tf_op jit(solution)/shard_map/add | solution.py:33
  27.9 10.8 %all_to_all.48 = f32[16,1,512]{2,1,0:T(1,128)} all-to-all(f32[16,1,512]{2,1,0:T(1,128)} %reshape.425), channel_id=1, replica_groups=mesh['mp'=2,'lat'=2,'lon'=8] {'lat','lon'}, dimensions={0} | all-to-all | bytes 65536 | tf_op jit(solution)/shard_map/all_to_all | solution.py:93
  39.3 2.1 %reduce.8 = f32[16,512]{1,0:T(8,128)} reduce(f32[16,1,512]{2,1,0:T(1,128)} %all_to_all.48, f32[]{:T(128)} %broadcast.325), dimensions={1}, to_apply=%all_to_all.33.reduce_sub_computation | reduce | bytes 65540 | tf_op jit(solution)/shard_map/all_to_all | solution.py:93
  53.0 2.1 %copy.61 = f32[2,1,16,128]{1,2,3,0:T(8,128)} copy(f32[2,1,16,128]{3,2,0,1:T(8,128)S(1)} %reshape.347) | data formatting | bytes 32768 | tf_op jit(solution)/shard_map/reshape.100
  55.1 5.9 %scatter.49 = f32[2,72,16,128]{1,2,3,0:T(8,128)S(1)} dynamic-update-slice(f32[2,72,16,128]{1,2,3,0:T(8,128)S(1)} %pad_subtract_fusion.3, f32[2,1,16,128]{1,2,3,0:T(8,128)} %copy.61, s32[]{:T(128)} %constant.123.clone.1, s32[]{:T(128)} %constant.123.clone.1, s32[]{:T(128)} %constant.123.clone.1, s32[]{:T(128)} %constant.123.clone.1) | dynamic-update-slice | bytes 32772 | tf_op jit(solution)/shard_map/scatter | solution.py:99
  65.0 3.6 %collective-permute-done.4 = f32[2,72,1,128]{1,2,3,0:T(1,128)S(1)} collective-permute-done((f32[2,72,1,128]{1,2,3,0:T(1,128)S(1)}, f32[2,72,1,128]{1,2,3,0:T(1,128)S(1)}, u32[]{:S(2)}, u32[]{:S(2)}) %collective-permute-start.4) | collective-permute-done | bytes 73760 | tf_op jit(solution)/shard_map/ppermute | solution.py:19
  77.3 10.7 %all_to_all.49 = f32[16,1,512]{2,1,0:T(1,128)} all-to-all(f32[16,1,512]{2,1,0:T(1,128)} %reshape.427), channel_id=1, replica_groups=mesh['mp'=2,'lat'=2,'lon'=8] {'lat','lon'}, dimensions={0} | all-to-all | bytes 65536 | tf_op jit(solution)/shard_map/all_to_all | solution.py:93
  88.1 2.1 %reduce.9 = f32[16,512]{1,0:T(8,128)} reduce(f32[16,1,512]{2,1,0:T(1,128)} %all_to_all.49, f32[]{:T(128)} %broadcast.325), dimensions={1}, to_apply=%all_to_all.36.reduce_sub_computation | reduce | bytes 65540 | tf_op jit(solution)/shard_map/all_to_all | solution.py:93
  93.2 3.8 %collective-permute-done.5 = f32[256,32]{1,0:T(8,128)S(1)} collective-permute-done((f32[256,32]{1,0:T(8,128)}, f32[256,32]{1,0:T(8,128)S(1)}, u32[]{:S(2)}, u32[]{:S(2)}) %collective-permute-start.5) | collective-permute-done | bytes 32800 | tf_op jit(solution)/shard_map/ppermute | solution.py:23
  101.9 2.1 %copy.65 = f32[2,1,16,128]{1,2,3,0:T(8,128)} copy(f32[2,1,16,128]{3,2,0,1:T(8,128)S(1)} %reshape.349) | data formatting | bytes 32768 | tf_op jit(solution)/shard_map/reshape.111
  104.0 5.9 %scatter.51 = f32[2,72,16,128]{1,2,3,0:T(8,128)S(1)} dynamic-update-slice(f32[2,72,16,128]{1,2,3,0:T(8,128)S(1)} %pad_subtract_fusion.2, f32[2,1,16,128]{1,2,3,0:T(8,128)} %copy.65, s32[]{:T(128)} %constant.123.clone.1, s32[]{:T(128)} %constant.123.clone.1, s32[]{:T(128)} %constant.123.clone.1, s32[]{:T(128)} %constant.123.clone.1) | dynamic-update-slice | bytes 32772 | tf_op jit(solution)/shard_map/scatter | solution.py:99
  113.6 4.0 %collective-permute-done.7 = f32[2,72,1,128]{1,2,3,0:T(1,128)S(1)} collective-permute-done((f32[2,72,1,128]{1,2,3,0:T(1,128)S(1)}, f32[2,72,1,128]{1,2,3,0:T(1,128)S(1)}, u32[]{:S(2)}, u32[]{:S(2)}) %collective-permute-start.7) | collective-permute-done | bytes 73760 | tf_op jit(solution)/shard_map/ppermute | solution.py:19
  126.3 10.7 %all_to_all.50 = f32[16,1,512]{2,1,0:T(1,128)} all-to-all(f32[16,1,512]{2,1,0:T(1,128)} %reshape.429), channel_id=1, replica_groups=mesh['mp'=2,'lat'=2,'lon'=8] {'lat','lon'}, dimensions={0} | all-to-all | bytes 65536 | tf_op jit(solution)/shard_map/all_to_all | solution.py:93
  137.0 2.1 %reduce.10 = f32[16,512]{1,0:T(8,128)} reduce(f32[16,1,512]{2,1,0:T(1,128)} %all_to_all.50, f32[]{:T(128)} %broadcast.325), dimensions={1}, to_apply=%all_to_all.39.reduce_sub_computation | reduce | bytes 65540 | tf_op jit(solution)/shard_map/all_to_all | solution.py:93
  142.1 3.8 %collective-permute-done.8 = f32[256,32]{1,0:T(8,128)S(1)} collective-permute-done((f32[256,32]{1,0:T(8,128)}, f32[256,32]{1,0:T(8,128)S(1)}, u32[]{:S(2)}, u32[]{:S(2)}) %collective-permute-start.8) | collective-permute-done | bytes 32800 | tf_op jit(solution)/shard_map/ppermute | solution.py:23
  150.9 2.1 %copy.69 = f32[2,1,16,128]{1,2,3,0:T(8,128)} copy(f32[2,1,16,128]{3,2,0,1:T(8,128)S(1)} %reshape.351) | data formatting | bytes 32768 | tf_op jit(solution)/shard_map/reshape.122
  153.0 5.9 %scatter.53 = f32[2,72,16,128]{1,2,3,0:T(8,128)S(1)} dynamic-update-slice(f32[2,72,16,128]{1,2,3,0:T(8,128)S(1)} %pad_subtract_fusion.1, f32[2,1,16,128]{1,2,3,0:T(8,128)} %copy.69, s32[]{:T(128)} %constant.123.clone.1, s32[]{:T(128)} %constant.123.clone.1, s32[]{:T(128)} %constant.123.clone.1, s32[]{:T(128)} %constant.123.clone.1) | dynamic-update-slice | bytes 32772 | tf_op jit(solution)/shard_map/scatter | solution.py:99
  162.5 4.0 %collective-permute-done.10 = f32[2,72,1,128]{1,2,3,0:T(1,128)S(1)} collective-permute-done((f32[2,72,1,128]{1,2,3,0:T(1,128)S(1)}, f32[2,72,1,128]{1,2,3,0:T(1,128)S(1)}, u32[]{:S(2)}, u32[]{:S(2)}) %collective-permute-start.10) | collective-permute-done | bytes 73760 | tf_op jit(solution)/shard_map/ppermute | solution.py:19
  170.8 9.4 %all_to_all.51 = f32[16,1,512]{2,1,0:T(1,128)S(1)} all-to-all(f32[16,1,512]{2,1,0:T(1,128)S(1)} %reshape.431), channel_id=1, replica_groups=mesh['mp'=2,'lat'=2,'lon'=8] {'lat','lon'}, dimensions={0} | all-to-all | bytes 65536 | tf_op jit(solution)/shard_map/all_to_all | solution.py:93
  182.6 3.6 %collective-permute-done.11 = f32[256,32]{1,0:T(8,128)S(1)} collective-permute-done((f32[256,32]{1,0:T(8,128)S(1)}, f32[256,32]{1,0:T(8,128)S(1)}, u32[]{:S(2)}, u32[]{:S(2)}) %collective-permute-start.11) | collective-permute-done | bytes 32800 | tf_op jit(solution)/shard_map/ppermute | solution.py:23
  187.2 2.1 %copy.73 = f32[1,2,1,16,128]{2,3,4,1,0:T(8,128)} copy(f32[1,2,1,16,128]{4,3,1,2,0:T(8,128)S(1)} %broadcast_in_dim.5) | data formatting | bytes 32768 | tf_op jit(solution)/shard_map/broadcast_in_dim | solution.py:100
  189.3 5.9 %scatter.55 = f32[1,2,72,16,128]{2,3,4,1,0:T(8,128)S(1)} dynamic-update-slice(f32[1,2,72,16,128]{2,3,4,1,0:T(8,128)S(1)} %bitcast.140, f32[1,2,1,16,128]{2,3,4,1,0:T(8,128)} %copy.73, s32[]{:T(128)} %constant.123.clone.1, s32[]{:T(128)} %constant.123.clone.1, s32[]{:T(128)} %constant.123.clone.1, s32[]{:T(128)} %constant.123.clone.1, s32[]{:T(128)} %constant.123.clone.1) | dynamic-update-slice | bytes 32772 | tf_op jit(solution)/shard_map/scatter | solution.py:99
  (127 shorter events, 84.1 us)
Async XLA Ops:
  3.1 7.9 %copy-start.6 = (s32[1,128]{1,0:T(1,128)S(1)}, s32[1,128]{1,0:T(1,128)}, u32[]{:S(2)}) copy-start(s32[1,128]{1,0:T(1,128)} %param.18) | copy-start | bytes 1540
  4.5 12.5 %collective-permute-start = (f32[2,72,16,1]{1,2,3,0:T(8,128)}, f32[2,72,16,1]{1,2,3,0:T(8,128)S(1)}, u32[]{:S(2)}, u32[]{:S(2)}) collective-permute-start(f32[2,72,16,1]{1,2,3,0:T(8,128)} %slice.229), channel_id=1, source_target_pairs={{1,0},{2,1},{3,2},{4,3},{5,4},{6,5},{7,6},{0,7},{9,8},{10,9},{11,1... | collective-permute-start | bytes 27656 | tf_op jit(solution)/shard_map/ppermute | solution.py:13
  9.7 7.3 %collective-permute-start.1 = (f32[2,72,1,128]{1,2,3,0:T(1,128)}, f32[2,72,1,128]{1,2,3,0:T(1,128)S(1)}, u32[]{:S(2)}, u32[]{:S(2)}) collective-permute-start(f32[2,72,1,128]{1,2,3,0:T(1,128)} %slice.231), channel_id=1, source_target_pairs={{8,0},{9,1},{10,2},{11,3},{12,4},{13,5},{14,6},{15,7},{24,16},{25,... | collective-permute-start | bytes 221192 | tf_op jit(solution)/shard_map/ppermute | solution.py:19
  13.7 1.6 copy-start.5
  22.1 20.8 %copy-start.1 = (f32[2,16,8,16]{3,2,1,0:T(8,128)}, f32[2,16,8,16]{3,2,1,0:T(8,128)S(1)}, u32[]{:S(2)}) copy-start(f32[2,16,8,16]{3,2,1,0:T(8,128)S(1)} %reshape_squeeze.12) | copy-start | bytes 49156
  42.9 5.3 %collective-permute-start.2 = (f32[256,32]{1,0:T(8,128)}, f32[256,32]{1,0:T(8,128)S(1)}, u32[]{:S(2)}, u32[]{:S(2)}) collective-permute-start(f32[256,32]{1,0:T(8,128)} %bitcast.146), channel_id=1, source_target_pairs={{0,16},{16,0},{1,17},{17,1},{2,18},{18,2},{3,19},{19,3},{4,20},{20... | collective-permute-start | bytes 98312 | tf_op jit(solution)/shard_map/ppermute | solution.py:23
  45.0 16.0 %copy-start.4 = (s32[1024]{0:T(1024)}, s32[1024]{0:T(1024)S(1)}, u32[]{:S(2)}) copy-start(s32[1024]{0:T(1024)S(1)} %pad_clamp_fusion) | copy-start | bytes 12292
  61.8 6.9 %collective-permute-start.4 = (f32[2,72,1,128]{1,2,3,0:T(1,128)S(1)}, f32[2,72,1,128]{1,2,3,0:T(1,128)S(1)}, u32[]{:S(2)}, u32[]{:S(2)}) collective-permute-start(f32[2,72,1,128]{1,2,3,0:T(1,128)S(1)} %slice.238), channel_id=1, source_target_pairs={{8,0},{9,1},{10,2},{11,3},{12,4},{13,5},{14,6},{15,7},{24,16},{25,... | collective-permute-start | bytes 221192 | tf_op jit(solution)/shard_map/ppermute | solution.py:19
  63.1 1.9 collective-permute-start.3
  71.5 20.2 %copy-start.2 = (f32[2,16,8,16]{3,2,1,0:T(8,128)}, f32[2,16,8,16]{3,2,1,0:T(8,128)S(1)}, u32[]{:S(2)}) copy-start(f32[2,16,8,16]{3,2,1,0:T(8,128)S(1)} %reshape_squeeze.13) | copy-start | bytes 49156
  91.7 5.3 %collective-permute-start.5 = (f32[256,32]{1,0:T(8,128)}, f32[256,32]{1,0:T(8,128)S(1)}, u32[]{:S(2)}, u32[]{:S(2)}) collective-permute-start(f32[256,32]{1,0:T(8,128)} %bitcast.147), channel_id=1, source_target_pairs={{0,16},{16,0},{1,17},{17,1},{2,18},{18,2},{3,19},{19,3},{4,20},{20... | collective-permute-start | bytes 98312 | tf_op jit(solution)/shard_map/ppermute | solution.py:23
  110.8 6.9 %collective-permute-start.7 = (f32[2,72,1,128]{1,2,3,0:T(1,128)S(1)}, f32[2,72,1,128]{1,2,3,0:T(1,128)S(1)}, u32[]{:S(2)}, u32[]{:S(2)}) collective-permute-start(f32[2,72,1,128]{1,2,3,0:T(1,128)S(1)} %slice.245), channel_id=1, source_target_pairs={{8,0},{9,1},{10,2},{11,3},{12,4},{13,5},{14,6},{15,7},{24,16},{25,... | collective-permute-start | bytes 221192 | tf_op jit(solution)/shard_map/ppermute | solution.py:19
  112.1 1.5 collective-permute-start.6
  120.4 20.2 %copy-start.3 = (f32[2,16,8,16]{3,2,1,0:T(8,128)}, f32[2,16,8,16]{3,2,1,0:T(8,128)S(1)}, u32[]{:S(2)}) copy-start(f32[2,16,8,16]{3,2,1,0:T(8,128)S(1)} %reshape_squeeze.14) | copy-start | bytes 49156
  140.7 5.3 %collective-permute-start.8 = (f32[256,32]{1,0:T(8,128)}, f32[256,32]{1,0:T(8,128)S(1)}, u32[]{:S(2)}, u32[]{:S(2)}) collective-permute-start(f32[256,32]{1,0:T(8,128)} %bitcast.148), channel_id=1, source_target_pairs={{0,16},{16,0},{1,17},{17,1},{2,18},{18,2},{3,19},{19,3},{4,20},{20... | collective-permute-start | bytes 98312 | tf_op jit(solution)/shard_map/ppermute | solution.py:23
  159.7 6.9 %collective-permute-start.10 = (f32[2,72,1,128]{1,2,3,0:T(1,128)S(1)}, f32[2,72,1,128]{1,2,3,0:T(1,128)S(1)}, u32[]{:S(2)}, u32[]{:S(2)}) collective-permute-start(f32[2,72,1,128]{1,2,3,0:T(1,128)S(1)} %slice.252), channel_id=1, source_target_pairs={{8,0},{9,1},{10,2},{11,3},{12,4},{13,5},{14,6},{15,7},{24,16},{25,... | collective-permute-start | bytes 221192 | tf_op jit(solution)/shard_map/ppermute | solution.py:19
  161.0 1.5 collective-permute-start.9
  168.5 18.6 %copy-start = (f32[16,8,16]{2,1,0:T(8,128)S(1)}, f32[16,8,16]{2,1,0:T(8,128)}, u32[]{:S(2)}) copy-start(f32[16,8,16]{2,1,0:T(8,128)} %convert_element_type.14) | copy-start | bytes 24580
  181.0 5.2 %collective-permute-start.11 = (f32[256,32]{1,0:T(8,128)S(1)}, f32[256,32]{1,0:T(8,128)S(1)}, u32[]{:S(2)}, u32[]{:S(2)}) collective-permute-start(f32[256,32]{1,0:T(8,128)S(1)} %bitcast.149), channel_id=1, source_target_pairs={{0,16},{16,0},{1,17},{17,1},{2,18},{18,2},{3,19},{19,3},{4,20},{20... | collective-permute-start | bytes 98312 | tf_op jit(solution)/shard_map/ppermute | solution.py:23
where the time goes:
time: 199 us; the launch traced here: 197 us
  local copies, waits for them, and re-layouts  83 us (42%)
  blocking collectives  41.6 us (21%)
  waiting for transfers between devices  28 us (14%)
  other arithmetic  27.8 us (14%)
  starting transfers between devices  16.3 us (8%)
    all_to_all x4, blocking collectives, local(): lax.all_to_all(buffer, ('lat', 'lon'), split_axis=0, concat_axis=0, tiled...  41.6 us
    scatter x5, local copies, waits for them, and re-layouts, local(): fields.at[:, 0]  25.7 us
    ppermute x4, waiting for transfers between devices, from_partner(): lax.ppermute(array, axis, [(i, i ^ 1 << apart) for i in range(lax.axis_si...  13 us
    unnamed x23, local copies, waits for them, and re-layouts  11.8 us
    ppermute x4, waiting for transfers between devices, shifted(): lax.ppermute(value, axis, [(source, source + steps) for source in range(f...  11.7 us
    another operation x6, local copies, waits for them, and re-layouts  9.32 us
    gather x8, local copies, waits for them, and re-layouts, local(): received = arrived[arrive_slot]  7.7 us
    all_to_all x4, other arithmetic, local(): lax.all_to_all(buffer, ('lat', 'lon'), split_axis=0, concat_axis=0, tiled...  7.13 us
  transfers between devices with their start and end apart: 12, of which 10 were waited for; matrix products, arithmetic and copies ran while one was open for 5% of the time, Pallas kernels for 0%

commit v1 on v0

v1 whole, which is shorter than its diff:
```python
import functools

import jax
import jax.numpy as jnp
from jax import lax
from jax.experimental import pallas as pl
from jax.experimental.pallas import tpu as pltpu
from jax.sharding import PartitionSpec as P

TILE = 16
STEPS = 4
F32 = jnp.float32
BF16 = jnp.bfloat16


def lane_iota(shape):
    return lax.broadcasted_iota(jnp.int32, shape, len(shape) - 1)


def row_iota(shape):
    return lax.broadcasted_iota(jnp.int32, shape, len(shape) - 2)


def lane_roll(value, shift):
    return pltpu.roll(value, shift % value.shape[-1], 1)


def three_parts(value):
    high = value.astype(BF16)
    rest = value - high.astype(F32)
    middle = rest.astype(BF16)
    low = (rest - middle.astype(F32)).astype(BF16)
    return high, middle, low


def picked(one_hot, value):
    total = None
    for part in three_parts(value):
        term = jnp.dot(one_hot, part, preferred_element_type=F32)
        total = term if total is None else total + term
    return total


def next_row(value):
    return pltpu.roll(value, value.shape[0] - 1, 0)


def edges_kernel(fields_ref, courant_ref, north_ref, east_ref):
    tracers, levels, rows, cols = fields_ref.shape
    zonal = courant_ref[0]
    first_row = courant_ref[1][0:1, :]
    lane = lane_iota((rows, cols))
    for tracer in range(tracers):
        gathered = jnp.zeros((rows, cols), F32)
        for k in range(levels):
            field = fields_ref[tracer, k]
            north_ref[tracer, k : k + 1, :] = first_row * field[0:1, :]
            gathered = jnp.where(lane == k, lane_roll(zonal * field, k), gathered)
        east_ref[tracer] = gathered


def mixing_kernel(
    fields_ref, kappa_ref, courant_ref, north_in, east_in, out_ref, north_ref, east_ref
):
    tracers, levels, rows, cols = fields_ref.shape
    zonal, meridional = courant_ref[0], courant_ref[1]
    weight = (1.0 - zonal) - meridional
    first_row = meridional[0:1, :]
    lane = lane_iota((rows, cols))
    row = row_iota((rows, cols))
    for tracer in range(tracers):
        east_edges = east_in[tracer]
        gathered = jnp.zeros((rows, cols), F32)
        upper = None
        flux_above = None

        def advected(k):
            field = fields_ref[tracer, k]
            eastward = zonal * field
            northward = meridional * field
            east = jnp.where(
                lane == cols - 1, lane_roll(east_edges, cols - 1 - k), lane_roll(eastward, cols - 1)
            )
            edge = jnp.broadcast_to(north_in[tracer, k : k + 1, :], (rows, cols))
            north = jnp.where(row == rows - 1, edge, next_row(northward))
            return (weight * field + east) + north

        here = advected(0)
        for k in range(levels):
            result = here
            if k + 1 < levels:
                below = advected(k + 1)
                flux = kappa_ref[k] * (below - here)
                result = result + flux
            if k > 0:
                result = result - flux_above
            out_ref[tracer, k] = result
            if k > 0:
                north_ref[tracer, k : k + 1, :] = first_row * result[0:1, :]
                gathered = jnp.where(lane == k, lane_roll(zonal * result, k), gathered)
            else:
                north_ref[tracer, k : k + 1, :] = jnp.zeros((1, cols), F32)
            if k + 1 < levels:
                here, flux_above = below, flux
        east_ref[tracer] = gathered


def send_surface(surface, below, refs, send_ref):
    courant_ref, kappa_ref, coupling_ref, west_ref, south_ref, pack_ref = refs
    tracers = len(surface)
    zonal, meridional = courant_ref[0], courant_ref[1]
    weight = (1.0 - zonal) - meridional
    rows, cols = zonal.shape
    groups = cols // TILE
    lane = lane_iota((rows, cols))
    row = row_iota((rows, cols))
    kappa = kappa_ref[0]
    coupling = coupling_ref[...]
    group = lane // TILE
    tiles, edge_north, edge_east = [], [], []
    place = lane == (row % groups) * TILE + (TILE - 1) - row // groups
    west_a = lane_roll(west_ref[0], 1)
    west_b = lane_roll(west_ref[1], 1)
    for tracer in range(tracers):
        parts = []
        for field in (surface[tracer], below[tracer]):
            eastward, northward = zonal * field, meridional * field
            east = jnp.where(lane == cols - 1, 0.0, lane_roll(eastward, cols - 1))
            north = jnp.where(row == rows - 1, 0.0, next_row(northward))
            parts.append((eastward, northward, (weight * field + east) + north))
        (east0, north0, here), (east1, north1, under) = parts
        mixed = here + kappa * (under - here)
        scaled = coupling * mixed
        edge_north.append(
            south_ref[0, rows - 1 : rows, :] * north0[0:1] + south_ref[1, rows - 1 : rows, :] * north1[0:1]
        )
        column = west_a * east0 + west_b * east1
        column = jnp.broadcast_to(column[:, 0:1], (rows, cols))
        edge_east.append(jnp.sum(jnp.where(place, column, 0.0), axis=0, keepdims=True))
        blocks = []
        for c in range(groups):
            block = jnp.where(group == c, scaled, 0.0)
            shift = TILE
            while shift < cols:
                block = block + lane_roll(block, shift)
                shift *= 2
            blocks.append(block)
        tiles.append(jnp.concatenate(blocks, axis=0))
    slots = picked(pack_ref[...], jnp.concatenate(tiles, axis=0))
    height = slots.shape[0] // groups
    slot_group = lane_iota((height, cols)) // TILE
    packed = jnp.zeros((height, cols), F32)
    for g in range(groups):
        packed = jnp.where(slot_group == g, slots[g * height : (g + 1) * height], packed)
    devices = send_ref.shape[0] // 2
    per_device = height // devices
    edges = jnp.concatenate(edge_north + edge_east, axis=0)
    for half in range(2):
        for device in range(devices):
            send_ref[half * devices + device, 0:per_device, :] = packed[
                device * per_device : (device + 1) * per_device
            ]
            send_ref[half * devices + device, per_device : per_device + 2 * tracers, :] = edges


def receive_surface(model_ref, recv_ref, pick_ref, place_ref, surface, coupling_ref, mask_ref):
    devices = recv_ref.shape[0] // 2
    rows, cols = coupling_ref.shape
    groups = cols // TILE
    tracers = len(surface)
    other = (1 - model_ref[0]) * devices
    slab = recv_ref[pl.ds(other, devices)].reshape(devices * recv_ref.shape[1], cols)
    table = jnp.concatenate([slab, lane_roll(slab, 1)], axis=0)
    found = picked(pick_ref[...], table)
    count = rows * groups
    group = lane_iota((rows, cols)) // TILE
    wet = mask_ref[...].astype(F32)
    coupling = coupling_ref[...]
    updated = []
    for tracer in range(tracers):
        total = None
        for kind in range(3):
            start = (kind * tracers + tracer) * count
            term = jnp.where(place_ref[kind] > 0, found[start : start + count], 0.0)
            total = term if total is None else total + term
        shift = TILE
        while shift < cols:
            total = total + lane_roll(total, shift)
            shift *= 2
        received = jnp.zeros((rows, cols), F32)
        for c in range(groups):
            received = jnp.where(group == c, total[c * rows : (c + 1) * rows], received)
        own = surface[tracer]
        updated.append(own + wet * (received - coupling * own))
    return updated


def first_send_kernel(fields_ref, *refs):
    *inputs, send_ref = refs
    tracers = fields_ref.shape[0]
    surface = [fields_ref[tracer, 0] for tracer in range(tracers)]
    below = [fields_ref[tracer, 1] for tracer in range(tracers)]
    send_surface(surface, below, inputs, send_ref)


def exchange_kernel(
    model_ref, fields_ref, recv_ref, pick_ref, place_ref, mask_ref, north_in, east_in, *refs
):
    *inputs, fields_out, send_ref, north_ref, east_ref = refs
    courant_ref, _, coupling_ref = inputs[:3]
    tracers = fields_ref.shape[0]
    surface = [fields_ref[tracer, 0] for tracer in range(tracers)]
    surface = receive_surface(model_ref, recv_ref, pick_ref, place_ref, surface, coupling_ref, mask_ref)
    below = [fields_ref[tracer, 1] for tracer in range(tracers)]
    send_surface(surface, below, inputs, send_ref)
    zonal, meridional = courant_ref[0], courant_ref[1]
    lane = lane_iota(zonal.shape)
    north_ref[...] = north_in[...]
    for tracer in range(tracers):
        fields_out[tracer, 0] = surface[tracer]
        fields_out[tracer, 1] = below[tracer]
        north_ref[tracer, 0:1, :] = meridional[0:1, :] * surface[tracer][0:1, :]
        east_ref[tracer] = jnp.where(lane == 0, zonal * surface[tracer], east_in[tracer])


def last_kernel(model_ref, fields_ref, recv_ref, pick_ref, place_ref, mask_ref, coupling_ref, fields_out):
    tracers = fields_ref.shape[0]
    surface = [fields_ref[tracer, 0] for tracer in range(tracers)]
    surface = receive_surface(model_ref, recv_ref, pick_ref, place_ref, surface, coupling_ref, mask_ref)
    for tracer in range(tracers):
        fields_out[tracer, 0] = surface[tracer]


VMEM_LIMIT = 32 * 1024 * 1024


def whole(array):
    zeros = (0,) * array.ndim
    return pl.BlockSpec(array.shape, lambda i: zeros)


def top(array, levels):
    tracers, _, rows, cols = array.shape
    return pl.BlockSpec((tracers, levels, rows, cols), lambda i: (0, 0, 0, 0))


SCALAR = pl.BlockSpec(memory_space=pltpu.SMEM)


def call(kernel, operands, specs, out_shape, out_specs, name, aliases=None, flops=0, moved=0):
    return pl.pallas_call(
        kernel,
        grid=(1,),
        in_specs=specs,
        out_shape=out_shape,
        out_specs=out_specs,
        input_output_aliases=aliases or {},
        name=name,
        cost_estimate=pl.CostEstimate(flops=flops, bytes_accessed=moved, transcendentals=0),
        compiler_params=pltpu.CompilerParams(vmem_limit_bytes=VMEM_LIMIT),
    )(*operands)


def like(array):
    return jax.ShapeDtypeStruct(array.shape, array.dtype)


def routing_tables(partner, rows, cols, capacity, main_rows, tracers):
    groups = cols // TILE
    count = rows * groups
    n_lat, n_lon = lax.axis_size("lat"), lax.axis_size("lon")
    devices = n_lat * n_lon
    per_device = main_rows * tracers
    partner = partner.reshape(rows, groups).T.reshape(count)
    own = (jnp.arange(count) % rows) * groups + jnp.arange(count) // rows
    target, slot = partner // count, partner % count
    same = target[:, None] == target[None, :]
    sent = jnp.sum(same & (own[None, :] < own[:, None]), axis=1)
    came = jnp.sum(same & (slot[None, :] < slot[:, None]), axis=1)
    height = devices * per_device
    packs = []
    for tracer in range(tracers):
        index = (sent % groups) * height + target * per_device + tracer * main_rows + sent // groups
        packs.append(jnp.arange(groups * height)[:, None] == index[None, :])
    pack = jnp.concatenate(packs, axis=1).astype(BF16)
    deep = per_device + 2 * tracers
    row, group = slot // groups, slot % groups
    lat, lon = target // n_lon, target % n_lon
    north_ok = (row == rows - 1) & (lat < n_lat - 1)
    east_ok = group == groups - 1
    east_device = lat * n_lon + (lon + 1) % n_lon
    picks = []
    for tracer in range(tracers):
        picks.append(target * deep + tracer * main_rows + came // groups)
    for tracer in range(tracers):
        picks.append(jnp.where(north_ok, (target + n_lon) * deep + per_device + tracer, -1))
    for tracer in range(tracers):
        index = east_device * deep + per_device + tracers + tracer + (row // groups) * (devices * deep)
        picks.append(jnp.where(east_ok, index, -1))
    picks = jnp.concatenate(picks)
    pick = (picks[:, None] == jnp.arange(2 * devices * deep)[None, :]).astype(BF16)
    lane = jnp.arange(cols)[None, :]
    place = jnp.stack(
        [
            lane // TILE == (came % groups)[:, None],
            lane // TILE == group[:, None],
            lane == (row % groups)[:, None] * TILE + TILE - 1,
        ]
    ).astype(F32)
    return pack, pick, place


def local(adjoint, courant, diffusivity, coupling, partner, mask):
    fields = adjoint[0]
    courant, kappa, coupling, partner, mask = courant[0], diffusivity[0], coupling[0], partner[0], mask[0]
    tracers, levels, rows, cols = fields.shape
    groups = cols // TILE
    count = rows * groups
    n_lat, n_lon = lax.axis_size("lat"), lax.axis_size("lon")
    devices = n_lat * n_lon
    capacity = max(2, 2 * count // devices)
    main_rows = -(-capacity // groups)
    deep = main_rows * tracers + 2 * tracers
    model = lax.axis_index("mp").astype(jnp.int32).reshape(1)
    last_row = lax.axis_index("lat") == n_lat - 1

    top_kappa = kappa[0]
    share = jnp.stack([coupling * (1.0 - top_kappa), coupling * top_kappa])
    from_west = lax.ppermute(share, "lon", [(i, (i + 1) % n_lon) for i in range(n_lon)])
    from_south = lax.ppermute(share, "lat", [(i, (i + 1) % n_lat) for i in range(n_lat)])

    def halo(north, east):
        north = lax.ppermute(north, "lat", [((i + 1) % n_lat, i) for i in range(n_lat)])
        east = lax.ppermute(east, "lon", [((i + 1) % n_lon, i) for i in range(n_lon)])
        return jnp.where(last_row, 0.0, north), east

    north_shape = jax.ShapeDtypeStruct((tracers, levels, cols), F32)
    east_shape = jax.ShapeDtypeStruct((tracers, rows, cols), F32)
    send_shape = jax.ShapeDtypeStruct((2 * devices, deep, cols), F32)
    field_bytes = 4 * tracers * levels * rows * cols

    north, east = call(
        edges_kernel,
        (fields, courant),
        [whole(fields), whole(courant)],
        (north_shape, east_shape),
        (whole(north_shape), whole(east_shape)),
        "edges",
        flops=field_bytes,
        moved=field_bytes,
    )
    pack, pick, place = routing_tables(partner, rows, cols, capacity, main_rows, tracers)
    kappa_top = kappa[0:1]
    sending = (courant, kappa_top, coupling, from_west, from_south, pack)
    sending_specs = [whole(a) for a in sending]
    send = call(
        first_send_kernel,
        (fields, *sending),
        [top(fields, 2), *sending_specs],
        send_shape,
        whole(send_shape),
        "first_send",
    )
    for step in range(STEPS):
        recv = lax.all_to_all(send, ("mp", "lat", "lon"), split_axis=0, concat_axis=0, tiled=True)
        north_in, east_in = halo(north, east)
        fields, north, east = call(
            mixing_kernel,
            (fields, kappa, courant, north_in, east_in),
            [whole(a) for a in (fields, kappa, courant, north_in, east_in)],
            (like(fields), north_shape, east_shape),
            (whole(fields), whole(north_shape), whole(east_shape)),
            "mixing",
            flops=10 * field_bytes,
            moved=3 * field_bytes,
        )
        if step + 1 < STEPS:
            arriving = (model, fields, recv, pick, place, mask, north, east)
            specs = [SCALAR, top(fields, 2), *(whole(a) for a in arriving[2:])]
            fields, send, north, east = call(
                exchange_kernel,
                (*arriving, *sending),
                [*specs, *sending_specs],
                (like(fields), send_shape, north_shape, east_shape),
                (top(fields, 2), whole(send_shape), whole(north_shape), whole(east_shape)),
                "exchange",
                aliases={1: 0},
            )
        else:
            arriving = (model, fields, recv, pick, place, mask, coupling)
            specs = [SCALAR, top(fields, 1), *(whole(a) for a in arriving[2:])]
            fields = call(
                last_kernel,
                arriving,
                specs,
                like(fields),
                top(fields, 1),
                "last",
                aliases={1: 0},
            )
    return fields[None]


def solution(mesh):
    placed = (
        P("mp", None, None, "lat", "lon"),
        P("mp", None, "lat", "lon"),
        P("mp", None, "lat", "lon"),
        P("mp", "lat", "lon"),
        P("mp", ("lat", "lon")),
        P("mp", "lat", "lon"),
    )
    return jax.shard_map(
        local,
        mesh=mesh,
        in_specs=placed,
        out_specs=P("mp", None, None, "lat", "lon"),
        check_vma=False,
    )
```

time: 199 us -> 108 us (0.54)
  local copies, waits for them, and re-layouts: 83 us -> 10.3 us
  Pallas kernels: 0 us -> 50.1 us
  blocking collectives: 41.6 us -> 0 us
  other arithmetic: 27.8 us -> 2.34 us
  waiting for transfers between devices: 28 us -> 4.32 us
  starting transfers between devices: 16.3 us -> 39.8 us
    pallas_call x0 -> x10, Pallas kernels: none -> 50.1 us  [call(): pl.pallas_call(kernel, grid=(1,), in_specs=specs, out_shape=out_shape, ou...]
    all_to_all x4 -> x0, blocking collectives: 41.6 us -> none  [local(): lax.all_to_all(buffer, ('lat', 'lon'), split_axis=0, concat_axis=0, tiled...]
    scatter x9 -> x0, local copies, waits for them, and re-layouts: 32 us -> none  [the longest x5 25.7 us: local(): fields.at[:, 0]]
    ppermute x12 -> x10, waiting for transfers between devices: 28 us -> 4.31 us  [the longest x4 4.29 us: halo(): lax.ppermute(east, 'lon', [((i + 1) % n_lon, i) for i in range(n_lon)])]
    all_to_all x0 -> x4, starting transfers between devices: none -> 18.2 us  [local(): lax.all_to_all(send, ('mp', 'lat', 'lon'), split_axis=0, concat_axis=0, t...]
    another operation x10 -> x1, local copies, waits for them, and re-layouts: 9.7 us -> 0.08 us  [routing_tables(): partner = partner.reshape(rows, groups).T.reshape(count)]
    slice x20 -> x1, local copies, waits for them, and re-layouts: 8.73 us -> 0.7 us  [local(): kappa_top = kappa[0:1]]
    gather x8 -> x0, local copies, waits for them, and re-layouts: 7.7 us -> none  [local(): received = arrived[arrive_slot]]
  transfers between devices with their start and end apart: 12 -> 14, of which waited for: 10 -> 3; matrix products, arithmetic and copies ran while one was open for 5% -> 3% of each run, Pallas kernels for 0% -> 38%
where the time goes in v1:
time: 108 us; the launch traced here: 107 us
  Pallas kernels  50.1 us (46%)
  starting transfers between devices  39.8 us (37%)
  local copies, waits for them, and re-layouts  10.3 us (10%)
  waiting for transfers between devices  4.32 us (4%)
  other arithmetic  2.34 us (2%)
    pallas_call x10, Pallas kernels, call(): pl.pallas_call(kernel, grid=(1,), in_specs=specs, out_shape=out_shape, ou...  50.1 us
    all_to_all x4, starting transfers between devices, local(): lax.all_to_all(send, ('mp', 'lat', 'lon'), split_axis=0, concat_axis=0, t...  18.2 us
    ppermute x4, starting transfers between devices, halo(): lax.ppermute(east, 'lon', [((i + 1) % n_lon, i) for i in range(n_lon)])  13.9 us
    unnamed x29, local copies, waits for them, and re-layouts  9.37 us
    ppermute x4, starting transfers between devices, halo(): lax.ppermute(north, 'lat', [((i + 1) % n_lat, i) for i in range(n_lat)])  4.83 us
    ppermute x4, waiting for transfers between devices, halo(): lax.ppermute(east, 'lon', [((i + 1) % n_lon, i) for i in range(n_lon)])  4.29 us
    ppermute x1, starting transfers between devices, local(): lax.ppermute(share, 'lat', [(i, (i + 1) % n_lat) for i in range(n_lat)])  2.97 us
  transfers between devices with their start and end apart: 14, of which 3 were waited for; matrix products, arithmetic and copies ran while one was open for 3% of the time, Pallas kernels for 38%

profile of v1, /device:TPU:0, one launch (start us, length us, event | category | flops | bytes accessed | tf_op | source)
XLA Modules:
  0.0 107.2 jit_solution(4492653461132951627)
XLA Ops:
  0.8 3.0 %collective-permute-start.3 = (f32[2,16,128]{2,1,0:T(8,128)S(1)}, f32[2,16,128]{2,1,0:T(8,128)S(1)}, u32[]{:S(2)}, u32[]{:S(2)}) collective-permute-start(f32[2,16,128]{2,1,0:T(8,128)S(1)} %pad_maximum_fusion), channel_id=1, source_target_pairs={{0,8},{8,0},{1,9},{9,1},{2,10},{10,2},{3,11},{11,3},{4,12},{12,4},... | collective-permute-start | bytes 49160 | tf_op jit(solution)/shard_map/ppermute | solution.py:330
  6.1 3.6 %collective-permute-start.1 = (f32[2,16,128]{2,1,0:T(8,128)S(1)}, f32[2,16,128]{2,1,0:T(8,128)S(1)}, u32[]{:S(2)}, u32[]{:S(2)}) collective-permute-start(f32[2,16,128]{2,1,0:T(8,128)S(1)} %get-tuple-element.30), channel_id=1, source_target_pairs={{1,0},{2,1},{3,2},{4,3},{5,4},{6,5},{7,6},{0,7},{9,8},{10,9},{11,1... | collective-permute-start | bytes 49160 | tf_op jit(solution)/shard_map/ppermute | solution.py:334
  12.9 1.3 %first_send.1 = f32[32,8,128]{2,1,0:T(8,128)} custom-call(f32[2,72,16,128]{3,2,1,0:T(8,128)S(1)} %bitcast.15, f32[2,16,128]{2,1,0:T(8,128)S(1)} %bitcast.22, f32[1,16,128]{2,1,0:T(8,128)S(1)} %slice_bitcast_fusion.refs_1_, f32[16,128]{1,0:T(8,128)S(1)} %bitcast.30, f32[2,16,128]{2,1,0:T(8,128)S(1)} %collective-permute-done.2.refs_3_, ...), custom_call_target="tpu_custom_call" | custom-call | tf_op jit(solution)/shard_map/first_send/pallas_call | solution.py:251
  14.2 4.5 %all-to-all-start = ((f32[32,8,128]{2,1,0:T(8,128)}), f32[32,8,128]{2,1,0:T(8,128)S(1)}, u32[]{:S(2)}, u32[]{:S(2)}) async-start(f32[32,8,128]{2,1,0:T(8,128)} %first_send.1), calls=%async_computation | async-start | bytes 262144 | tf_op jit(solution)/shard_map/all_to_all | solution.py:365
  18.8 9.6 %mixing.4 = (f32[2,72,16,128]{3,2,1,0:T(8,128)S(1)}, f32[2,72,128]{2,1,0:T(8,128)S(1)}, f32[2,16,128]{2,1,0:T(8,128)S(1)}) custom-call(f32[2,72,16,128]{3,2,1,0:T(8,128)S(1)} %bitcast.16, f32[71,16,128]{2,1,0:T(8,128)S(1)} %bitcast.17, f32[2,16,128]{2,1,0:T(8,128)S(1)} %bitcast.23, f32[2,72,128]{2,1,0:T(8,128)S(1)} %broadcast_select_fusion.3.north_in, ...), custom_call_target="tpu_custom_call" | custom-call | flops 11796480 | bytes 3538944 | tf_op jit(solution)/shard_map/mixing/pallas_call | solution.py:251
  30.6 2.4 %exchange.3 = (f32[2,72,16,128]{3,2,1,0:T(8,128)S(1)}, f32[32,8,128]{2,1,0:T(8,128)}, f32[2,72,128]{2,1,0:T(8,128)S(1)}, f32[2,16,128]{2,1,0:T(8,128)S(1)}) custom-call(s32[1]{0:T(128)} %bitcast.model_ref, f32[2,72,16,128]{3,2,1,0:T(8,128)S(1)} %copy-done.6, f32[32,8,128]{2,1,0:T(8,128)S(1)} %all-to-all-done.recv_ref, ...), custom_call_target="tpu_custom_call", output_to_operand_aliasing={{0}: (1, {})} | custom-call | tf_op jit(solution)/shard_map/exchange/pallas_call | solution.py:251
  34.1 1.8 %collective-permute-start.4 = (f32[2,72,128]{2,1,0:T(8,128)S(1)}, f32[2,72,128]{2,1,0:T(8,128)S(1)}, u32[]{:S(2)}, u32[]{:S(2)}) collective-permute-start(f32[2,72,128]{2,1,0:T(8,128)S(1)} %get-tuple-element.35), channel_id=1, source_target_pairs={{8,0},{0,8},{9,1},{1,9},{10,2},{2,10},{11,3},{3,11},{12,4},{4,12},... | collective-permute-start | bytes 221192 | tf_op jit(solution)/shard_map/ppermute | solution.py:333
  35.8 4.6 %all-to-all-start.1 = ((f32[32,8,128]{2,1,0:T(8,128)}), f32[32,8,128]{2,1,0:T(8,128)S(1)}, u32[]{:S(2)}, u32[]{:S(2)}) async-start(f32[32,8,128]{2,1,0:T(8,128)} %get-tuple-element.38), calls=%async_computation.1 | async-start | bytes 262144 | tf_op jit(solution)/shard_map/all_to_all | solution.py:365
  40.5 3.4 %collective-permute-start.5 = (f32[2,16,128]{2,1,0:T(8,128)S(1)}, f32[2,16,128]{2,1,0:T(8,128)S(1)}, u32[]{:S(2)}, u32[]{:S(2)}) collective-permute-start(f32[2,16,128]{2,1,0:T(8,128)S(1)} %get-tuple-element.36), channel_id=1, source_target_pairs={{1,0},{2,1},{3,2},{4,3},{5,4},{6,5},{7,6},{0,7},{9,8},{10,9},{11,1... | collective-permute-start | bytes 49160 | tf_op jit(solution)/shard_map/ppermute | solution.py:334
  43.9 1.4 %collective-permute-done.5.east_in = f32[2,16,128]{2,1,0:T(8,128)S(1)} collective-permute-done((f32[2,16,128]{2,1,0:T(8,128)S(1)}, f32[2,16,128]{2,1,0:T(8,128)S(1)}, u32[]{:S(2)}, u32[]{:S(2)}) %collective-permute-start.5) | collective-permute-done | bytes 16416 | tf_op jit(solution)/shard_map/ppermute | solution.py:334
  46.6 9.6 %mixing.5 = (f32[2,72,16,128]{3,2,1,0:T(8,128)S(1)}, f32[2,72,128]{2,1,0:T(8,128)S(1)}, f32[2,16,128]{2,1,0:T(8,128)S(1)}) custom-call(f32[2,72,16,128]{3,2,1,0:T(8,128)S(1)} %copy-done.8, f32[71,16,128]{2,1,0:T(8,128)S(1)} %bitcast.18, f32[2,16,128]{2,1,0:T(8,128)S(1)} %bitcast.25, f32[2,72,128]{2,1,0:T(8,128)S(1)} %broadcast_select_fusion.2.north_in, ...), custom_call_target="tpu_custom_call" | custom-call | flops 11796480 | bytes 3538944 | tf_op jit(solution)/shard_map/mixing/pallas_call | solution.py:251
  56.2 2.4 %exchange.4 = (f32[2,72,16,128]{3,2,1,0:T(8,128)S(1)}, f32[32,8,128]{2,1,0:T(8,128)}, f32[2,72,128]{2,1,0:T(8,128)S(1)}, f32[2,16,128]{2,1,0:T(8,128)S(1)}) custom-call(s32[1]{0:T(128)} %bitcast.model_ref, f32[2,72,16,128]{3,2,1,0:T(8,128)S(1)} %get-tuple-element.37.fields_ref, ...), custom_call_target="tpu_custom_call", output_to_operand_aliasing={{0}: (1, {})} | custom-call | tf_op jit(solution)/shard_map/exchange/pallas_call | solution.py:251
  59.6 1.5 %collective-permute-start.6 = (f32[2,72,128]{2,1,0:T(8,128)S(1)}, f32[2,72,128]{2,1,0:T(8,128)S(1)}, u32[]{:S(2)}, u32[]{:S(2)}) collective-permute-start(f32[2,72,128]{2,1,0:T(8,128)S(1)} %get-tuple-element.42), channel_id=1, source_target_pairs={{8,0},{0,8},{9,1},{1,9},{10,2},{2,10},{11,3},{3,11},{12,4},{4,12},... | collective-permute-start | bytes 221192 | tf_op jit(solution)/shard_map/ppermute | solution.py:333
  61.1 4.5 %all-to-all-start.2 = ((f32[32,8,128]{2,1,0:T(8,128)}), f32[32,8,128]{2,1,0:T(8,128)S(1)}, u32[]{:S(2)}, u32[]{:S(2)}) async-start(f32[32,8,128]{2,1,0:T(8,128)} %get-tuple-element.45), calls=%async_computation.2 | async-start | bytes 262144 | tf_op jit(solution)/shard_map/all_to_all | solution.py:365
  65.6 3.4 %collective-permute-start.7 = (f32[2,16,128]{2,1,0:T(8,128)S(1)}, f32[2,16,128]{2,1,0:T(8,128)S(1)}, u32[]{:S(2)}, u32[]{:S(2)}) collective-permute-start(f32[2,16,128]{2,1,0:T(8,128)S(1)} %get-tuple-element.43), channel_id=1, source_target_pairs={{1,0},{2,1},{3,2},{4,3},{5,4},{6,5},{7,6},{0,7},{9,8},{10,9},{11,1... | collective-permute-start | bytes 49160 | tf_op jit(solution)/shard_map/ppermute | solution.py:334
  69.1 1.4 %collective-permute-done.7.east_in = f32[2,16,128]{2,1,0:T(8,128)S(1)} collective-permute-done((f32[2,16,128]{2,1,0:T(8,128)S(1)}, f32[2,16,128]{2,1,0:T(8,128)S(1)}, u32[]{:S(2)}, u32[]{:S(2)}) %collective-permute-start.7) | collective-permute-done | bytes 16416 | tf_op jit(solution)/shard_map/ppermute | solution.py:334
  71.8 9.6 %mixing.6 = (f32[2,72,16,128]{3,2,1,0:T(8,128)S(1)}, f32[2,72,128]{2,1,0:T(8,128)S(1)}, f32[2,16,128]{2,1,0:T(8,128)S(1)}) custom-call(f32[2,72,16,128]{3,2,1,0:T(8,128)S(1)} %copy-done.4, f32[71,16,128]{2,1,0:T(8,128)S(1)} %bitcast.19, f32[2,16,128]{2,1,0:T(8,128)S(1)} %bitcast.27, f32[2,72,128]{2,1,0:T(8,128)S(1)} %broadcast_select_fusion.1.north_in, ...), custom_call_target="tpu_custom_call" | custom-call | flops 11796480 | bytes 3538944 | tf_op jit(solution)/shard_map/mixing/pallas_call | solution.py:251
  81.3 2.4 %exchange.5 = (f32[2,72,16,128]{3,2,1,0:T(8,128)S(1)}, f32[32,8,128]{2,1,0:T(8,128)}, f32[2,72,128]{2,1,0:T(8,128)S(1)}, f32[2,16,128]{2,1,0:T(8,128)S(1)}) custom-call(s32[1]{0:T(128)} %bitcast.model_ref, f32[2,72,16,128]{3,2,1,0:T(8,128)S(1)} %get-tuple-element.44.fields_ref, ...), custom_call_target="tpu_custom_call", output_to_operand_aliasing={{0}: (1, {})} | custom-call | tf_op jit(solution)/shard_map/exchange/pallas_call | solution.py:251
  83.7 1.5 %collective-permute-start.8 = (f32[2,72,128]{2,1,0:T(8,128)S(1)}, f32[2,72,128]{2,1,0:T(8,128)S(1)}, u32[]{:S(2)}, u32[]{:S(2)}) collective-permute-start(f32[2,72,128]{2,1,0:T(8,128)S(1)} %get-tuple-element.49), channel_id=1, source_target_pairs={{8,0},{0,8},{9,1},{1,9},{10,2},{2,10},{11,3},{3,11},{12,4},{4,12},... | collective-permute-start | bytes 221192 | tf_op jit(solution)/shard_map/ppermute | solution.py:333
  85.2 4.5 %all-to-all-start.3 = ((f32[32,8,128]{2,1,0:T(8,128)}), f32[32,8,128]{2,1,0:T(8,128)S(1)}, u32[]{:S(2)}, u32[]{:S(2)}) async-start(f32[32,8,128]{2,1,0:T(8,128)} %get-tuple-element.52), calls=%async_computation.3 | async-start | bytes 262144 | tf_op jit(solution)/shard_map/all_to_all | solution.py:365
  89.8 3.4 %collective-permute-start.9 = (f32[2,16,128]{2,1,0:T(8,128)S(1)}, f32[2,16,128]{2,1,0:T(8,128)S(1)}, u32[]{:S(2)}, u32[]{:S(2)}) collective-permute-start(f32[2,16,128]{2,1,0:T(8,128)S(1)} %get-tuple-element.50), channel_id=1, source_target_pairs={{1,0},{2,1},{3,2},{4,3},{5,4},{6,5},{7,6},{0,7},{9,8},{10,9},{11,1... | collective-permute-start | bytes 49160 | tf_op jit(solution)/shard_map/ppermute | solution.py:334
  93.2 1.4 %collective-permute-done.9.east_in = f32[2,16,128]{2,1,0:T(8,128)S(1)} collective-permute-done((f32[2,16,128]{2,1,0:T(8,128)S(1)}, f32[2,16,128]{2,1,0:T(8,128)S(1)}, u32[]{:S(2)}, u32[]{:S(2)}) %collective-permute-start.9) | collective-permute-done | bytes 16416 | tf_op jit(solution)/shard_map/ppermute | solution.py:334
  94.6 10.5 %mixing.7 = (f32[2,72,16,128]{3,2,1,0:T(8,128)}, f32[2,72,128]{2,1,0:T(8,128)}, f32[2,16,128]{2,1,0:T(8,128)}) custom-call(f32[2,72,16,128]{3,2,1,0:T(8,128)S(1)} %get-tuple-element.48.fields_ref, f32[71,16,128]{2,1,0:T(8,128)S(1)} %bitcast.20, f32[2,16,128]{2,1,0:T(8,128)S(1)} %bitcast.29, f32[2,72,128]{2,1,0:T(8,128)S(1)} %broadcast_select_fusion.north_in, ...), custom_call_target="tpu_custom_call" | custom-call | flops 11796480 | bytes 3538944 | tf_op jit(solution)/shard_map/mixing/pallas_call | solution.py:251
  105.2 2.1 %last.1 = f32[2,72,16,128]{3,2,1,0:T(8,128)} custom-call(s32[1]{0:T(128)} %bitcast.model_ref, f32[2,72,16,128]{3,2,1,0:T(8,128)} %get-tuple-element.51.fields_ref, f32[32,8,128]{2,1,0:T(8,128)S(1)} %all-to-all-done.3.recv_ref, bf16[768,256]{1,0:T(8,128)(2,1)S(1)} %fusion.pick_ref, ...), custom_call_target="tpu_custom_call", output_to_operand_aliasing={{}: (1, {})} | custom-call | tf_op jit(solution)/shard_map/last/pallas_call | solution.py:251
  (73 shorter events, 13.1 us)
Async XLA Ops:
  0.0 12.9 %copy-start.11 = (f32[1,16,128]{2,1,0:T(8,128)S(1)}, f32[1,16,128]{2,1,0:T(8,128)}, u32[]{:S(2)}) copy-start(f32[1,16,128]{2,1,0:T(8,128)} %param.9) | copy-start | bytes 24580
  0.0 12.9 %copy-start.10 = (f32[1,2,16,128]{3,2,1,0:T(8,128)S(1)}, f32[1,2,16,128]{3,2,1,0:T(8,128)}, u32[]{:S(2)}) copy-start(f32[1,2,16,128]{3,2,1,0:T(8,128)} %param.7) | copy-start | bytes 49156
  0.0 11.0 %copy-start.13 = (s32[1,128]{1,0:T(1,128)S(1)}, s32[1,128]{1,0:T(1,128)}, u32[]{:S(2)}) copy-start(s32[1,128]{1,0:T(1,128)} %param.10) | copy-start | bytes 1540
  0.8 12.1 %collective-permute-start.3 = (f32[2,16,128]{2,1,0:T(8,128)S(1)}, f32[2,16,128]{2,1,0:T(8,128)S(1)}, u32[]{:S(2)}, u32[]{:S(2)}) collective-permute-start(f32[2,16,128]{2,1,0:T(8,128)S(1)} %pad_maximum_fusion), channel_id=1, source_target_pairs={{0,8},{8,0},{1,9},{9,1},{2,10},{10,2},{3,11},{11,3},{4,12},{12,4},... | collective-permute-start | bytes 49160 | tf_op jit(solution)/shard_map/ppermute | solution.py:330
  3.7 9.1 %collective-permute-start.2 = (f32[2,16,128]{2,1,0:T(8,128)S(1)}, f32[2,16,128]{2,1,0:T(8,128)S(1)}, u32[]{:S(2)}, u32[]{:S(2)}) collective-permute-start(f32[2,16,128]{2,1,0:T(8,128)S(1)} %pad_maximum_fusion), channel_id=1, source_target_pairs={{0,1},{1,2},{2,3},{3,4},{4,5},{5,6},{6,7},{7,0},{8,9},{9,10},{10,1... | collective-permute-start | bytes 49160 | tf_op jit(solution)/shard_map/ppermute | solution.py:329
  3.8 1.3 %copy-start = (f32[1,2,72,16,128]{4,3,2,1,0:T(8,128)S(1)}, f32[1,2,72,16,128]{4,3,2,1,0:T(8,128)}, u32[]{:S(2)}) copy-start(f32[1,2,72,16,128]{4,3,2,1,0:T(8,128)} %param.6) | copy-start | bytes 3538948
  5.7 7.1 %copy-start.1 = (f32[1,2,72,16,128]{4,3,2,1,0:T(8,128)S(1)}, f32[1,2,72,16,128]{4,3,2,1,0:T(8,128)}, u32[]{:S(2)}) copy-start(f32[1,2,72,16,128]{4,3,2,1,0:T(8,128)} %param.6) | copy-start | bytes 3538948
  6.1 12.7 %collective-permute-start.1 = (f32[2,16,128]{2,1,0:T(8,128)S(1)}, f32[2,16,128]{2,1,0:T(8,128)S(1)}, u32[]{:S(2)}, u32[]{:S(2)}) collective-permute-start(f32[2,16,128]{2,1,0:T(8,128)S(1)} %get-tuple-element.30), channel_id=1, source_target_pairs={{1,0},{2,1},{3,2},{4,3},{5,4},{6,5},{7,6},{0,7},{9,8},{10,9},{11,1... | collective-permute-start | bytes 49160 | tf_op jit(solution)/shard_map/ppermute | solution.py:334
  9.7 9.0 %collective-permute-start = (f32[2,72,128]{2,1,0:T(8,128)S(1)}, f32[2,72,128]{2,1,0:T(8,128)S(1)}, u32[]{:S(2)}, u32[]{:S(2)}) collective-permute-start(f32[2,72,128]{2,1,0:T(8,128)S(1)} %get-tuple-element.29), channel_id=1, source_target_pairs={{8,0},{0,8},{9,1},{1,9},{10,2},{2,10},{11,3},{3,11},{12,4},{4,12},... | collective-permute-start | bytes 221192 | tf_op jit(solution)/shard_map/ppermute | solution.py:333
  12.8 6.0 %copy-start.2 = (f32[1,71,16,128]{3,2,1,0:T(8,128)S(1)}, f32[1,71,16,128]{3,2,1,0:T(8,128)}, u32[]{:S(2)}) copy-start(f32[1,71,16,128]{3,2,1,0:T(8,128)} %param.8) | copy-start | bytes 1744900
  14.2 15.2 %all-to-all-start = ((f32[32,8,128]{2,1,0:T(8,128)}), f32[32,8,128]{2,1,0:T(8,128)S(1)}, u32[]{:S(2)}, u32[]{:S(2)}) async-start(f32[32,8,128]{2,1,0:T(8,128)} %first_send.1), calls=%async_computation | async-start | bytes 262144 | tf_op jit(solution)/shard_map/all_to_all | solution.py:365
  18.7 10.7 %copy-start.12 = (s32[1,16,128]{2,1,0:T(8,128)S(1)}, s32[1,16,128]{2,1,0:T(8,128)}, u32[]{:S(2)}) copy-start(s32[1,16,128]{2,1,0:T(8,128)} %param.11) | copy-start | bytes 24580
  29.4 1.3 %copy-start.6 = (f32[2,72,16,128]{3,2,1,0:T(8,128)S(1)}, f32[2,72,16,128]{3,2,1,0:T(8,128)}, u32[]{:S(2)}) copy-start(f32[2,72,16,128]{3,2,1,0:T(8,128)} %copy-done.5) | copy-start | bytes 3538948
  34.1 9.8 %collective-permute-start.4 = (f32[2,72,128]{2,1,0:T(8,128)S(1)}, f32[2,72,128]{2,1,0:T(8,128)S(1)}, u32[]{:S(2)}, u32[]{:S(2)}) collective-permute-start(f32[2,72,128]{2,1,0:T(8,128)S(1)} %get-tuple-element.35), channel_id=1, source_target_pairs={{8,0},{0,8},{9,1},{1,9},{10,2},{2,10},{11,3},{3,11},{12,4},{4,12},... | collective-permute-start | bytes 221192 | tf_op jit(solution)/shard_map/ppermute | solution.py:333
  35.8 20.3 %all-to-all-start.1 = ((f32[32,8,128]{2,1,0:T(8,128)}), f32[32,8,128]{2,1,0:T(8,128)S(1)}, u32[]{:S(2)}, u32[]{:S(2)}) async-start(f32[32,8,128]{2,1,0:T(8,128)} %get-tuple-element.38), calls=%async_computation.1 | async-start | bytes 262144 | tf_op jit(solution)/shard_map/all_to_all | solution.py:365
  40.5 4.9 %collective-permute-start.5 = (f32[2,16,128]{2,1,0:T(8,128)S(1)}, f32[2,16,128]{2,1,0:T(8,128)S(1)}, u32[]{:S(2)}, u32[]{:S(2)}) collective-permute-start(f32[2,16,128]{2,1,0:T(8,128)S(1)} %get-tuple-element.36), channel_id=1, source_target_pairs={{1,0},{2,1},{3,2},{4,3},{5,4},{6,5},{7,6},{0,7},{9,8},{10,9},{11,1... | collective-permute-start | bytes 49160 | tf_op jit(solution)/shard_map/ppermute | solution.py:334
  45.3 1.3 %copy-start.8 = (f32[2,72,16,128]{3,2,1,0:T(8,128)S(1)}, f32[2,72,16,128]{3,2,1,0:T(8,128)}, u32[]{:S(2)}) copy-start(f32[2,72,16,128]{3,2,1,0:T(8,128)} %copy-done.7) | copy-start | bytes 3538948
  59.6 9.5 %collective-permute-start.6 = (f32[2,72,128]{2,1,0:T(8,128)S(1)}, f32[2,72,128]{2,1,0:T(8,128)S(1)}, u32[]{:S(2)}, u32[]{:S(2)}) collective-permute-start(f32[2,72,128]{2,1,0:T(8,128)S(1)} %get-tuple-element.42), channel_id=1, source_target_pairs={{8,0},{0,8},{9,1},{1,9},{10,2},{2,10},{11,3},{3,11},{12,4},{4,12},... | collective-permute-start | bytes 221192 | tf_op jit(solution)/shard_map/ppermute | solution.py:333
  61.1 20.2 %all-to-all-start.2 = ((f32[32,8,128]{2,1,0:T(8,128)}), f32[32,8,128]{2,1,0:T(8,128)S(1)}, u32[]{:S(2)}, u32[]{:S(2)}) async-start(f32[32,8,128]{2,1,0:T(8,128)} %get-tuple-element.45), calls=%async_computation.2 | async-start | bytes 262144 | tf_op jit(solution)/shard_map/all_to_all | solution.py:365
  65.6 4.9 %collective-permute-start.7 = (f32[2,16,128]{2,1,0:T(8,128)S(1)}, f32[2,16,128]{2,1,0:T(8,128)S(1)}, u32[]{:S(2)}, u32[]{:S(2)}) collective-permute-start(f32[2,16,128]{2,1,0:T(8,128)S(1)} %get-tuple-element.43), channel_id=1, source_target_pairs={{1,0},{2,1},{3,2},{4,3},{5,4},{6,5},{7,6},{0,7},{9,8},{10,9},{11,1... | collective-permute-start | bytes 49160 | tf_op jit(solution)/shard_map/ppermute | solution.py:334
  70.5 1.3 %copy-start.4 = (f32[2,72,16,128]{3,2,1,0:T(8,128)S(1)}, f32[2,72,16,128]{3,2,1,0:T(8,128)}, u32[]{:S(2)}) copy-start(f32[2,72,16,128]{3,2,1,0:T(8,128)} %copy-done.3) | copy-start | bytes 3538948
  83.7 9.5 %collective-permute-start.8 = (f32[2,72,128]{2,1,0:T(8,128)S(1)}, f32[2,72,128]{2,1,0:T(8,128)S(1)}, u32[]{:S(2)}, u32[]{:S(2)}) collective-permute-start(f32[2,72,128]{2,1,0:T(8,128)S(1)} %get-tuple-element.49), channel_id=1, source_target_pairs={{8,0},{0,8},{9,1},{1,9},{10,2},{2,10},{11,3},{3,11},{12,4},{4,12},... | collective-permute-start | bytes 221192 | tf_op jit(solution)/shard_map/ppermute | solution.py:333
  85.2 19.9 %all-to-all-start.3 = ((f32[32,8,128]{2,1,0:T(8,128)}), f32[32,8,128]{2,1,0:T(8,128)S(1)}, u32[]{:S(2)}, u32[]{:S(2)}) async-start(f32[32,8,128]{2,1,0:T(8,128)} %get-tuple-element.52), calls=%async_computation.3 | async-start | bytes 262144 | tf_op jit(solution)/shard_map/all_to_all | solution.py:365
  89.8 4.9 %collective-permute-start.9 = (f32[2,16,128]{2,1,0:T(8,128)S(1)}, f32[2,16,128]{2,1,0:T(8,128)S(1)}, u32[]{:S(2)}, u32[]{:S(2)}) collective-permute-start(f32[2,16,128]{2,1,0:T(8,128)S(1)} %get-tuple-element.50), channel_id=1, source_target_pairs={{1,0},{2,1},{3,2},{4,3},{5,4},{6,5},{7,6},{0,7},{9,8},{10,9},{11,1... | collective-permute-start | bytes 49160 | tf_op jit(solution)/shard_map/ppermute | solution.py:334
  (4 other events, 3.8 us)

commit v2 on v1

--- a/solution.py
+++ b/solution.py
@@ -60,7 +60,7 @@
 
 
 def mixing_kernel(
-    fields_ref, kappa_ref, courant_ref, north_in, east_in, out_ref, north_ref, east_ref
+    fields_ref, surface_ref, kappa_ref, courant_ref, north_in, east_in, out_ref, top_ref, north_ref, east_ref
 ):
     tracers, levels, rows, cols = fields_ref.shape
     zonal, meridional = courant_ref[0], courant_ref[1]
@@ -70,12 +70,10 @@
     row = row_iota((rows, cols))
     for tracer in range(tracers):
         east_edges = east_in[tracer]
-        gathered = jnp.zeros((rows, cols), F32)
-        upper = None
         flux_above = None
 
         def advected(k):
-            field = fields_ref[tracer, k]
+            field = surface_ref[tracer] if k == 0 else fields_ref[tracer, k]
             eastward = zonal * field
             northward = meridional * field
             east = jnp.where(
@@ -95,13 +93,14 @@
             if k > 0:
                 result = result - flux_above
             out_ref[tracer, k] = result
-            if k > 0:
-                north_ref[tracer, k : k + 1, :] = first_row * result[0:1, :]
-                gathered = jnp.where(lane == k, lane_roll(zonal * result, k), gathered)
-            else:
-                north_ref[tracer, k : k + 1, :] = jnp.zeros((1, cols), F32)
+            if k < 2:
+                top_ref[tracer, k] = result
+            north_ref[tracer, k : k + 1, :] = first_row * result[0:1, :]
             if k + 1 < levels:
                 here, flux_above = below, flux
+        gathered = jnp.zeros((rows, cols), F32)
+        for k in range(levels):
+            gathered = jnp.where(lane == k, lane_roll(zonal * out_ref[tracer, k], k), gathered)
         east_ref[tracer] = gathered
 
 
@@ -206,7 +205,7 @@
 def exchange_kernel(
     model_ref, fields_ref, recv_ref, pick_ref, place_ref, mask_ref, north_in, east_in, *refs
 ):
-    *inputs, fields_out, send_ref, north_ref, east_ref = refs
+    *inputs, surface_out, send_ref, north_ref, east_ref = refs
     courant_ref, _, coupling_ref = inputs[:3]
     tracers = fields_ref.shape[0]
     surface = [fields_ref[tracer, 0] for tracer in range(tracers)]
@@ -217,8 +216,7 @@
     lane = lane_iota(zonal.shape)
     north_ref[...] = north_in[...]
     for tracer in range(tracers):
-        fields_out[tracer, 0] = surface[tracer]
-        fields_out[tracer, 1] = below[tracer]
+        surface_out[tracer] = surface[tracer]
         north_ref[tracer, 0:1, :] = meridional[0:1, :] * surface[tracer][0:1, :]
         east_ref[tracer] = jnp.where(lane == 0, zonal * surface[tracer], east_in[tracer])
 
@@ -361,30 +359,33 @@
         whole(send_shape),
         "first_send",
     )
+    surface = fields[:, 0]
     for step in range(STEPS):
         recv = lax.all_to_all(send, ("mp", "lat", "lon"), split_axis=0, concat_axis=0, tiled=True)
         north_in, east_in = halo(north, east)
-        fields, north, east = call(
+        mixing = (fields, surface, kappa, courant, north_in, east_in)
+        top_shape = jax.ShapeDtypeStruct((tracers, 2, rows, cols), F32)
+        shapes = (like(fields), top_shape, north_shape, east_shape)
+        fields, two_levels, north, east = call(
             mixing_kernel,
-            (fields, kappa, courant, north_in, east_in),
-            [whole(a) for a in (fields, kappa, courant, north_in, east_in)],
-            (like(fields), north_shape, east_shape),
-            (whole(fields), whole(north_shape), whole(east_shape)),
+            mixing,
+            [whole(a) for a in mixing],
+            shapes,
+            tuple(whole(a) for a in shapes),
             "mixing",
             flops=10 * field_bytes,
             moved=3 * field_bytes,
         )
         if step + 1 < STEPS:
-            arriving = (model, fields, recv, pick, place, mask, north, east)
-            specs = [SCALAR, top(fields, 2), *(whole(a) for a in arriving[2:])]
-            fields, send, north, east = call(
+            arriving = (model, two_levels, recv, pick, place, mask, north, east)
+            specs = [SCALAR, *(whole(a) for a in arriving[1:])]
+            surface, send, north, east = call(
                 exchange_kernel,
                 (*arriving, *sending),
                 [*specs, *sending_specs],
-                (like(fields), send_shape, north_shape, east_shape),
-                (top(fields, 2), whole(send_shape), whole(north_shape), whole(east_shape)),
+                (like(surface), send_shape, north_shape, east_shape),
+                (whole(surface), whole(send_shape), whole(north_shape), whole(east_shape)),
                 "exchange",
-                aliases={1: 0},
             )
         else:
             arriving = (model, fields, recv, pick, place, mask, coupling)

time: 108 us -> 74.4 us (0.69)
  Pallas kernels: 50.1 us -> 15.9 us
  waiting for transfers between devices: 4.32 us -> 14.1 us
  starting transfers between devices: 39.8 us -> 34.5 us
  local copies, waits for them, and re-layouts: 10.3 us -> 6.75 us
    pallas_call x10, Pallas kernels: 50.1 us -> 15.9 us  [call(): pl.pallas_call(kernel, grid=(1,), in_specs=specs, out_shape=out_shape, ou...]
    all_to_all x4, waiting for transfers between devices: 0.01 us -> 9.78 us  [local(): lax.all_to_all(send, ('mp', 'lat', 'lon'), split_axis=0, concat_axis=0, t...]
    unnamed x29 -> x25, local copies, waits for them, and re-layouts: 9.37 us -> 5.82 us
    all_to_all x4, starting transfers between devices: 18.2 us -> 15.2 us  [local(): lax.all_to_all(send, ('mp', 'lat', 'lon'), split_axis=0, concat_axis=0, t...]
    ppermute x4, starting transfers between devices: 4.83 us -> 2.46 us  [halo(): lax.ppermute(north, 'lat', [((i + 1) % n_lat, i) for i in range(n_lat)])]
  transfers between devices with their start and end apart: 14 -> 14, of which waited for: 3 -> 7; matrix products, arithmetic and copies ran while one was open for 3% -> 4% of each run, Pallas kernels for 38% -> 9%
where the time goes in v2:
time: 74.4 us; the launch traced here: 73.8 us
  starting transfers between devices  34.5 us (46%)
  Pallas kernels  15.9 us (21%)
  waiting for transfers between devices  14.1 us (19%)
  local copies, waits for them, and re-layouts  6.75 us (9%)
  other arithmetic  2.3 us (3%)
    pallas_call x10, Pallas kernels, call(): pl.pallas_call(kernel, grid=(1,), in_specs=specs, out_shape=out_shape, ou...  15.9 us
    all_to_all x4, starting transfers between devices, local(): lax.all_to_all(send, ('mp', 'lat', 'lon'), split_axis=0, concat_axis=0, t...  15.2 us
    ppermute x4, starting transfers between devices, halo(): lax.ppermute(east, 'lon', [((i + 1) % n_lon, i) for i in range(n_lon)])  13.9 us
    all_to_all x4, waiting for transfers between devices, local(): lax.all_to_all(send, ('mp', 'lat', 'lon'), split_axis=0, concat_axis=0, t...  9.78 us
    unnamed x25, local copies, waits for them, and re-layouts  5.82 us
    ppermute x4, waiting for transfers between devices, halo(): lax.ppermute(east, 'lon', [((i + 1) % n_lon, i) for i in range(n_lon)])  4.29 us
    ppermute x1, starting transfers between devices, local(): lax.ppermute(share, 'lat', [(i, (i + 1) % n_lat) for i in range(n_lat)])  3.03 us
    ppermute x4, starting transfers between devices, halo(): lax.ppermute(north, 'lat', [((i + 1) % n_lat, i) for i in range(n_lat)])  2.46 us
  transfers between devices with their start and end apart: 14, of which 7 were waited for; matrix products, arithmetic and copies ran while one was open for 4% of the time, Pallas kernels for 9%

profile of v2, /device:TPU:0, one launch (start us, length us, event | category | flops | bytes accessed | tf_op | source)
XLA Modules:
  0.0 73.8 jit_solution(9730428783889149403)
XLA Ops:
  0.7 3.0 %collective-permute-start.3 = (f32[2,16,128]{2,1,0:T(8,128)S(1)}, f32[2,16,128]{2,1,0:T(8,128)S(1)}, u32[]{:S(2)}, u32[]{:S(2)}) collective-permute-start(f32[2,16,128]{2,1,0:T(8,128)S(1)} %pad_maximum_fusion), channel_id=1, source_target_pairs={{0,8},{8,0},{1,9},{9,1},{2,10},{10,2},{3,11},{11,3},{4,12},{12,4},... | collective-permute-start | bytes 49160 | tf_op jit(solution)/shard_map/ppermute | solution.py:328
  3.8 1.3 %copy-done = f32[1,2,72,16,128]{4,3,2,1,0:T(8,128)S(1)} copy-done((f32[1,2,72,16,128]{4,3,2,1,0:T(8,128)S(1)}, f32[1,2,72,16,128]{4,3,2,1,0:T(8,128)}, u32[]{:S(2)}) %copy-start) | copy-done | bytes 1179672
  6.1 3.6 %collective-permute-start.1 = (f32[2,16,128]{2,1,0:T(8,128)S(1)}, f32[2,16,128]{2,1,0:T(8,128)S(1)}, u32[]{:S(2)}, u32[]{:S(2)}) collective-permute-start(f32[2,16,128]{2,1,0:T(8,128)S(1)} %get-tuple-element.33), channel_id=1, source_target_pairs={{1,0},{2,1},{3,2},{4,3},{5,4},{6,5},{7,6},{0,7},{9,8},{10,9},{11,1... | collective-permute-start | bytes 49160 | tf_op jit(solution)/shard_map/ppermute | solution.py:332
  12.9 1.3 %first_send.1 = f32[32,8,128]{2,1,0:T(8,128)} custom-call(f32[2,72,16,128]{3,2,1,0:T(8,128)S(1)} %bitcast.18, f32[2,16,128]{2,1,0:T(8,128)S(1)} %bitcast.25, f32[1,16,128]{2,1,0:T(8,128)S(1)} %slice_bitcast_fusion.1.refs_1_, f32[16,128]{1,0:T(8,128)S(1)} %bitcast.33, f32[2,16,128]{2,1,0:T(8,128)S(1)} %collective-permute-done.2.refs_3_, ...), custom_call_target="tpu_custom_call" | custom-call | tf_op jit(solution)/shard_map/first_send/pallas_call | solution.py:249
  14.2 4.5 %all-to-all-start = ((f32[32,8,128]{2,1,0:T(8,128)}), f32[32,8,128]{2,1,0:T(8,128)S(1)}, u32[]{:S(2)}, u32[]{:S(2)}) async-start(f32[32,8,128]{2,1,0:T(8,128)} %first_send.1), calls=%async_computation | async-start | bytes 262144 | tf_op jit(solution)/shard_map/all_to_all | solution.py:364
  20.8 6.1 %all-to-all-done.recv_ref = f32[32,8,128]{2,1,0:T(8,128)S(1)} async-done(((f32[32,8,128]{2,1,0:T(8,128)}), f32[32,8,128]{2,1,0:T(8,128)S(1)}, u32[]{:S(2)}, u32[]{:S(2)}) %all-to-all-start) | async-done | bytes 131104 | tf_op jit(solution)/shard_map/all_to_all | solution.py:364
  26.9 2.4 %exchange.3 = (f32[2,16,128]{2,1,0:T(8,128)S(1)}, f32[32,8,128]{2,1,0:T(8,128)}, f32[2,72,128]{2,1,0:T(8,128)S(1)}, f32[2,16,128]{2,1,0:T(8,128)S(1)}) custom-call(s32[1]{0:T(128)} %bitcast.model_ref, f32[2,2,16,128]{3,2,1,0:T(8,128)S(1)} %get-tuple-element.35.fields_ref, f32[32,8,128]{2,1,0:T(8,128)S(1)} %all-to-all-done.recv_ref, ...), custom_call_target="tpu_custom_call" | custom-call | tf_op jit(solution)/shard_map/exchange/pallas_call | solution.py:249
  30.1 2.6 %all-to-all-start.1 = ((f32[32,8,128]{2,1,0:T(8,128)}), f32[32,8,128]{2,1,0:T(8,128)S(1)}, u32[]{:S(2)}, u32[]{:S(2)}) async-start(f32[32,8,128]{2,1,0:T(8,128)} %get-tuple-element.43), calls=%async_computation.1 | async-start | bytes 262144 | tf_op jit(solution)/shard_map/all_to_all | solution.py:364
  32.7 3.4 %collective-permute-start.5 = (f32[2,16,128]{2,1,0:T(8,128)S(1)}, f32[2,16,128]{2,1,0:T(8,128)S(1)}, u32[]{:S(2)}, u32[]{:S(2)}) collective-permute-start(f32[2,16,128]{2,1,0:T(8,128)S(1)} %get-tuple-element.40), channel_id=1, source_target_pairs={{1,0},{2,1},{3,2},{4,3},{5,4},{6,5},{7,6},{0,7},{9,8},{10,9},{11,1... | collective-permute-start | bytes 49160 | tf_op jit(solution)/shard_map/ppermute | solution.py:332
  36.1 1.4 %collective-permute-done.5.east_in = f32[2,16,128]{2,1,0:T(8,128)S(1)} collective-permute-done((f32[2,16,128]{2,1,0:T(8,128)S(1)}, f32[2,16,128]{2,1,0:T(8,128)S(1)}, u32[]{:S(2)}, u32[]{:S(2)}) %collective-permute-start.5) | collective-permute-done | bytes 16416 | tf_op jit(solution)/shard_map/ppermute | solution.py:332
  39.6 1.3 %all-to-all-done.1.recv_ref = f32[32,8,128]{2,1,0:T(8,128)S(1)} async-done(((f32[32,8,128]{2,1,0:T(8,128)}), f32[32,8,128]{2,1,0:T(8,128)S(1)}, u32[]{:S(2)}, u32[]{:S(2)}) %all-to-all-start.1) | async-done | bytes 131104 | tf_op jit(solution)/shard_map/all_to_all | solution.py:364
  40.9 2.4 %exchange.4 = (f32[2,16,128]{2,1,0:T(8,128)S(1)}, f32[32,8,128]{2,1,0:T(8,128)}, f32[2,72,128]{2,1,0:T(8,128)S(1)}, f32[2,16,128]{2,1,0:T(8,128)S(1)}) custom-call(s32[1]{0:T(128)} %bitcast.model_ref, f32[2,2,16,128]{3,2,1,0:T(8,128)S(1)} %get-tuple-element.42.fields_ref, f32[32,8,128]{2,1,0:T(8,128)S(1)} %all-to-all-done.1.recv_ref, ...), custom_call_target="tpu_custom_call" | custom-call | tf_op jit(solution)/shard_map/exchange/pallas_call | solution.py:249
  44.1 3.9 %all-to-all-start.2 = ((f32[32,8,128]{2,1,0:T(8,128)}), f32[32,8,128]{2,1,0:T(8,128)S(1)}, u32[]{:S(2)}, u32[]{:S(2)}) async-start(f32[32,8,128]{2,1,0:T(8,128)} %get-tuple-element.51), calls=%async_computation.2 | async-start | bytes 262144 | tf_op jit(solution)/shard_map/all_to_all | solution.py:364
  48.0 3.4 %collective-permute-start.7 = (f32[2,16,128]{2,1,0:T(8,128)S(1)}, f32[2,16,128]{2,1,0:T(8,128)S(1)}, u32[]{:S(2)}, u32[]{:S(2)}) collective-permute-start(f32[2,16,128]{2,1,0:T(8,128)S(1)} %get-tuple-element.48), channel_id=1, source_target_pairs={{1,0},{2,1},{3,2},{4,3},{5,4},{6,5},{7,6},{0,7},{9,8},{10,9},{11,1... | collective-permute-start | bytes 49160 | tf_op jit(solution)/shard_map/ppermute | solution.py:332
  51.4 1.4 %collective-permute-done.7.east_in = f32[2,16,128]{2,1,0:T(8,128)S(1)} collective-permute-done((f32[2,16,128]{2,1,0:T(8,128)S(1)}, f32[2,16,128]{2,1,0:T(8,128)S(1)}, u32[]{:S(2)}, u32[]{:S(2)}) %collective-permute-start.7) | collective-permute-done | bytes 16416 | tf_op jit(solution)/shard_map/ppermute | solution.py:332
  52.9 1.3 %copy-done.6 = f32[2,72,16,128]{3,2,1,0:T(8,128)S(1)} copy-done((f32[2,72,16,128]{3,2,1,0:T(8,128)S(1)}, f32[2,72,16,128]{3,2,1,0:T(8,128)}, u32[]{:S(2)}) %copy-start.6) | copy-done | bytes 1179672
  55.1 1.0 %all-to-all-done.2.recv_ref = f32[32,8,128]{2,1,0:T(8,128)S(1)} async-done(((f32[32,8,128]{2,1,0:T(8,128)}), f32[32,8,128]{2,1,0:T(8,128)S(1)}, u32[]{:S(2)}, u32[]{:S(2)}) %all-to-all-start.2) | async-done | bytes 131104 | tf_op jit(solution)/shard_map/all_to_all | solution.py:364
  56.2 2.4 %exchange.5 = (f32[2,16,128]{2,1,0:T(8,128)S(1)}, f32[32,8,128]{2,1,0:T(8,128)}, f32[2,72,128]{2,1,0:T(8,128)S(1)}, f32[2,16,128]{2,1,0:T(8,128)S(1)}) custom-call(s32[1]{0:T(128)} %bitcast.model_ref, f32[2,2,16,128]{3,2,1,0:T(8,128)S(1)} %get-tuple-element.50.fields_ref, f32[32,8,128]{2,1,0:T(8,128)S(1)} %all-to-all-done.2.recv_ref, ...), custom_call_target="tpu_custom_call" | custom-call | tf_op jit(solution)/shard_map/exchange/pallas_call | solution.py:249
  59.4 4.2 %all-to-all-start.3 = ((f32[32,8,128]{2,1,0:T(8,128)}), f32[32,8,128]{2,1,0:T(8,128)S(1)}, u32[]{:S(2)}, u32[]{:S(2)}) async-start(f32[32,8,128]{2,1,0:T(8,128)} %get-tuple-element.58), calls=%async_computation.3 | async-start | bytes 262144 | tf_op jit(solution)/shard_map/all_to_all | solution.py:364
  63.6 3.4 %collective-permute-start.9 = (f32[2,16,128]{2,1,0:T(8,128)S(1)}, f32[2,16,128]{2,1,0:T(8,128)S(1)}, u32[]{:S(2)}, u32[]{:S(2)}) collective-permute-start(f32[2,16,128]{2,1,0:T(8,128)S(1)} %get-tuple-element.56), channel_id=1, source_target_pairs={{1,0},{2,1},{3,2},{4,3},{5,4},{6,5},{7,6},{0,7},{9,8},{10,9},{11,1... | collective-permute-start | bytes 49160 | tf_op jit(solution)/shard_map/ppermute | solution.py:332
  67.0 1.4 %collective-permute-done.9.east_in = f32[2,16,128]{2,1,0:T(8,128)S(1)} collective-permute-done((f32[2,16,128]{2,1,0:T(8,128)S(1)}, f32[2,16,128]{2,1,0:T(8,128)S(1)}, u32[]{:S(2)}, u32[]{:S(2)}) %collective-permute-start.9) | collective-permute-done | bytes 16416 | tf_op jit(solution)/shard_map/ppermute | solution.py:332
  68.4 2.0 %mixing.7 = (f32[2,72,16,128]{3,2,1,0:T(8,128)}, f32[2,2,16,128]{3,2,1,0:T(8,128)}, f32[2,72,128]{2,1,0:T(8,128)}, f32[2,16,128]{2,1,0:T(8,128)}) custom-call(f32[2,72,16,128]{3,2,1,0:T(8,128)S(1)} %get-tuple-element.49.fields_ref, f32[2,16,128]{2,1,0:T(8,128)S(1)} %get-tuple-element.54.surface_ref, f32[71,16,128]{2,1,0:T(8,128)S(1)} %bitcast.23, ...), custom_call_target="tpu_custom_call" | custom-call | flops 11796480 | bytes 3538944 | tf_op jit(solution)/shard_map/mixing/pallas_call | solution.py:249
  70.4 1.4 %all-to-all-done.3.recv_ref = f32[32,8,128]{2,1,0:T(8,128)S(1)} async-done(((f32[32,8,128]{2,1,0:T(8,128)}), f32[32,8,128]{2,1,0:T(8,128)S(1)}, u32[]{:S(2)}, u32[]{:S(2)}) %all-to-all-start.3) | async-done | bytes 131104 | tf_op jit(solution)/shard_map/all_to_all | solution.py:364
  71.8 2.1 %last.1 = f32[2,72,16,128]{3,2,1,0:T(8,128)} custom-call(s32[1]{0:T(128)} %bitcast.model_ref, f32[2,72,16,128]{3,2,1,0:T(8,128)} %get-tuple-element.57.fields_ref, f32[32,8,128]{2,1,0:T(8,128)S(1)} %all-to-all-done.3.recv_ref, bf16[768,256]{1,0:T(8,128)(2,1)S(1)} %fusion.pick_ref, ...), custom_call_target="tpu_custom_call", output_to_operand_aliasing={{}: (1, {})} | custom-call | tf_op jit(solution)/shard_map/last/pallas_call | solution.py:249
  (70 shorter events, 12.3 us)
Async XLA Ops:
  0.0 11.0 %copy-start.11 = (s32[1,128]{1,0:T(1,128)S(1)}, s32[1,128]{1,0:T(1,128)}, u32[]{:S(2)}) copy-start(s32[1,128]{1,0:T(1,128)} %param.10) | copy-start | bytes 1540
  0.7 12.2 %copy-start.4 = (f32[1,2,16,128]{3,2,1,0:T(8,128)S(1)}, f32[1,2,16,128]{3,2,1,0:T(8,128)}, u32[]{:S(2)}) copy-start(f32[1,2,16,128]{3,2,1,0:T(8,128)} %param.7) | copy-start | bytes 49156
  0.7 12.2 %copy-start.9 = (f32[1,16,128]{2,1,0:T(8,128)S(1)}, f32[1,16,128]{2,1,0:T(8,128)}, u32[]{:S(2)}) copy-start(f32[1,16,128]{2,1,0:T(8,128)} %param.9) | copy-start | bytes 24580
  0.7 12.1 %collective-permute-start.3 = (f32[2,16,128]{2,1,0:T(8,128)S(1)}, f32[2,16,128]{2,1,0:T(8,128)S(1)}, u32[]{:S(2)}, u32[]{:S(2)}) collective-permute-start(f32[2,16,128]{2,1,0:T(8,128)S(1)} %pad_maximum_fusion), channel_id=1, source_target_pairs={{0,8},{8,0},{1,9},{9,1},{2,10},{10,2},{3,11},{11,3},{4,12},{12,4},... | collective-permute-start | bytes 49160 | tf_op jit(solution)/shard_map/ppermute | solution.py:328
  3.8 9.1 %collective-permute-start.2 = (f32[2,16,128]{2,1,0:T(8,128)S(1)}, f32[2,16,128]{2,1,0:T(8,128)S(1)}, u32[]{:S(2)}, u32[]{:S(2)}) collective-permute-start(f32[2,16,128]{2,1,0:T(8,128)S(1)} %pad_maximum_fusion), channel_id=1, source_target_pairs={{0,1},{1,2},{2,3},{3,4},{4,5},{5,6},{6,7},{7,0},{8,9},{9,10},{10,1... | collective-permute-start | bytes 49160 | tf_op jit(solution)/shard_map/ppermute | solution.py:327
  3.8 1.3 %copy-start = (f32[1,2,72,16,128]{4,3,2,1,0:T(8,128)S(1)}, f32[1,2,72,16,128]{4,3,2,1,0:T(8,128)}, u32[]{:S(2)}) copy-start(f32[1,2,72,16,128]{4,3,2,1,0:T(8,128)} %param.6) | copy-start | bytes 3538948
  5.8 4.7 %copy-start.1 = (f32[1,2,72,16,128]{4,3,2,1,0:T(8,128)S(1)}, f32[1,2,72,16,128]{4,3,2,1,0:T(8,128)}, u32[]{:S(2)}) copy-start(f32[1,2,72,16,128]{4,3,2,1,0:T(8,128)} %param.6) | copy-start | bytes 3538948
  6.1 12.7 %collective-permute-start.1 = (f32[2,16,128]{2,1,0:T(8,128)S(1)}, f32[2,16,128]{2,1,0:T(8,128)S(1)}, u32[]{:S(2)}, u32[]{:S(2)}) collective-permute-start(f32[2,16,128]{2,1,0:T(8,128)S(1)} %get-tuple-element.33), channel_id=1, source_target_pairs={{1,0},{2,1},{3,2},{4,3},{5,4},{6,5},{7,6},{0,7},{9,8},{10,9},{11,1... | collective-permute-start | bytes 49160 | tf_op jit(solution)/shard_map/ppermute | solution.py:332
  9.7 9.0 %collective-permute-start = (f32[2,72,128]{2,1,0:T(8,128)S(1)}, f32[2,72,128]{2,1,0:T(8,128)S(1)}, u32[]{:S(2)}, u32[]{:S(2)}) collective-permute-start(f32[2,72,128]{2,1,0:T(8,128)S(1)} %get-tuple-element.32), channel_id=1, source_target_pairs={{8,0},{0,8},{9,1},{1,9},{10,2},{2,10},{11,3},{3,11},{12,4},{4,12},... | collective-permute-start | bytes 221192 | tf_op jit(solution)/shard_map/ppermute | solution.py:331
  12.9 6.0 %copy-start.2 = (f32[1,71,16,128]{3,2,1,0:T(8,128)S(1)}, f32[1,71,16,128]{3,2,1,0:T(8,128)}, u32[]{:S(2)}) copy-start(f32[1,71,16,128]{3,2,1,0:T(8,128)} %param.8) | copy-start | bytes 1744900
  14.2 12.7 %all-to-all-start = ((f32[32,8,128]{2,1,0:T(8,128)}), f32[32,8,128]{2,1,0:T(8,128)S(1)}, u32[]{:S(2)}, u32[]{:S(2)}) async-start(f32[32,8,128]{2,1,0:T(8,128)} %first_send.1), calls=%async_computation | async-start | bytes 262144 | tf_op jit(solution)/shard_map/all_to_all | solution.py:364
  18.7 8.2 %copy-start.10 = (s32[1,16,128]{2,1,0:T(8,128)S(1)}, s32[1,16,128]{2,1,0:T(8,128)}, u32[]{:S(2)}) copy-start(s32[1,16,128]{2,1,0:T(8,128)} %param.11) | copy-start | bytes 24580
  19.8 1.0 %copy-start.7 = (f32[2,72,16,128]{3,2,1,0:T(8,128)}, f32[2,72,16,128]{3,2,1,0:T(8,128)S(1)}, u32[]{:S(2)}) copy-start(f32[2,72,16,128]{3,2,1,0:T(8,128)S(1)} %get-tuple-element.34.fields_ref) | copy-start | bytes 3538948
  26.9 10.6 %copy-start.8 = (f32[2,72,16,128]{3,2,1,0:T(8,128)S(1)}, f32[2,72,16,128]{3,2,1,0:T(8,128)}, u32[]{:S(2)}) copy-start(f32[2,72,16,128]{3,2,1,0:T(8,128)} %copy-done.7) | copy-start | bytes 3538948
  29.3 6.8 %collective-permute-start.4 = (f32[2,72,128]{2,1,0:T(8,128)S(1)}, f32[2,72,128]{2,1,0:T(8,128)S(1)}, u32[]{:S(2)}, u32[]{:S(2)}) collective-permute-start(f32[2,72,128]{2,1,0:T(8,128)S(1)} %get-tuple-element.39), channel_id=1, source_target_pairs={{8,0},{0,8},{9,1},{1,9},{10,2},{2,10},{11,3},{3,11},{12,4},{4,12},... | collective-permute-start | bytes 221192 | tf_op jit(solution)/shard_map/ppermute | solution.py:331
  30.1 10.7 %all-to-all-start.1 = ((f32[32,8,128]{2,1,0:T(8,128)}), f32[32,8,128]{2,1,0:T(8,128)S(1)}, u32[]{:S(2)}, u32[]{:S(2)}) async-start(f32[32,8,128]{2,1,0:T(8,128)} %get-tuple-element.43), calls=%async_computation.1 | async-start | bytes 262144 | tf_op jit(solution)/shard_map/all_to_all | solution.py:364
  32.7 4.9 %collective-permute-start.5 = (f32[2,16,128]{2,1,0:T(8,128)S(1)}, f32[2,16,128]{2,1,0:T(8,128)S(1)}, u32[]{:S(2)}, u32[]{:S(2)}) collective-permute-start(f32[2,16,128]{2,1,0:T(8,128)S(1)} %get-tuple-element.40), channel_id=1, source_target_pairs={{1,0},{2,1},{3,2},{4,3},{5,4},{6,5},{7,6},{0,7},{9,8},{10,9},{11,1... | collective-permute-start | bytes 49160 | tf_op jit(solution)/shard_map/ppermute | solution.py:332
  43.3 8.2 %collective-permute-start.6 = (f32[2,72,128]{2,1,0:T(8,128)S(1)}, f32[2,72,128]{2,1,0:T(8,128)S(1)}, u32[]{:S(2)}, u32[]{:S(2)}) collective-permute-start(f32[2,72,128]{2,1,0:T(8,128)S(1)} %get-tuple-element.47), channel_id=1, source_target_pairs={{8,0},{0,8},{9,1},{1,9},{10,2},{2,10},{11,3},{3,11},{12,4},{4,12},... | collective-permute-start | bytes 221192 | tf_op jit(solution)/shard_map/ppermute | solution.py:331
  44.1 12.1 %all-to-all-start.2 = ((f32[32,8,128]{2,1,0:T(8,128)}), f32[32,8,128]{2,1,0:T(8,128)S(1)}, u32[]{:S(2)}, u32[]{:S(2)}) async-start(f32[32,8,128]{2,1,0:T(8,128)} %get-tuple-element.51), calls=%async_computation.2 | async-start | bytes 262144 | tf_op jit(solution)/shard_map/all_to_all | solution.py:364
  48.0 4.9 %collective-permute-start.7 = (f32[2,16,128]{2,1,0:T(8,128)S(1)}, f32[2,16,128]{2,1,0:T(8,128)S(1)}, u32[]{:S(2)}, u32[]{:S(2)}) collective-permute-start(f32[2,16,128]{2,1,0:T(8,128)S(1)} %get-tuple-element.48), channel_id=1, source_target_pairs={{1,0},{2,1},{3,2},{4,3},{5,4},{6,5},{7,6},{0,7},{9,8},{10,9},{11,1... | collective-permute-start | bytes 49160 | tf_op jit(solution)/shard_map/ppermute | solution.py:332
  52.9 1.3 %copy-start.6 = (f32[2,72,16,128]{3,2,1,0:T(8,128)S(1)}, f32[2,72,16,128]{3,2,1,0:T(8,128)}, u32[]{:S(2)}) copy-start(f32[2,72,16,128]{3,2,1,0:T(8,128)} %copy-done.5) | copy-start | bytes 3538948
  58.6 8.4 %collective-permute-start.8 = (f32[2,72,128]{2,1,0:T(8,128)S(1)}, f32[2,72,128]{2,1,0:T(8,128)S(1)}, u32[]{:S(2)}, u32[]{:S(2)}) collective-permute-start(f32[2,72,128]{2,1,0:T(8,128)S(1)} %get-tuple-element.55), channel_id=1, source_target_pairs={{8,0},{0,8},{9,1},{1,9},{10,2},{2,10},{11,3},{3,11},{12,4},{4,12},... | collective-permute-start | bytes 221192 | tf_op jit(solution)/shard_map/ppermute | solution.py:331
  59.4 12.4 %all-to-all-start.3 = ((f32[32,8,128]{2,1,0:T(8,128)}), f32[32,8,128]{2,1,0:T(8,128)S(1)}, u32[]{:S(2)}, u32[]{:S(2)}) async-start(f32[32,8,128]{2,1,0:T(8,128)} %get-tuple-element.58), calls=%async_computation.3 | async-start | bytes 262144 | tf_op jit(solution)/shard_map/all_to_all | solution.py:364
  63.6 4.9 %collective-permute-start.9 = (f32[2,16,128]{2,1,0:T(8,128)S(1)}, f32[2,16,128]{2,1,0:T(8,128)S(1)}, u32[]{:S(2)}, u32[]{:S(2)}) collective-permute-start(f32[2,16,128]{2,1,0:T(8,128)S(1)} %get-tuple-element.56), channel_id=1, source_target_pairs={{1,0},{2,1},{3,2},{4,3},{5,4},{6,5},{7,6},{0,7},{9,8},{10,9},{11,1... | collective-permute-start | bytes 49160 | tf_op jit(solution)/shard_map/ppermute | solution.py:332
  (2 other events, 1.7 us)

commit v3 on v1

v3 whole, which is shorter than its diff:
```python
import functools

import jax
import jax.numpy as jnp
from jax import lax
from jax.experimental import pallas as pl
from jax.experimental.pallas import tpu as pltpu
from jax.sharding import PartitionSpec as P

TILE = 16
STEPS = 4
F32 = jnp.float32
BF16 = jnp.bfloat16
PACKED = 32


def lane_iota(shape):
    return lax.broadcasted_iota(jnp.int32, shape, len(shape) - 1)


def row_iota(shape):
    return lax.broadcasted_iota(jnp.int32, shape, len(shape) - 2)


def lane_roll(value, shift):
    shift = shift % value.shape[-1]
    return value if shift == 0 else pltpu.roll(value, shift, 1)


def next_row(value):
    return pltpu.roll(value, value.shape[0] - 1, 0)


def three_parts(value):
    high = value.astype(BF16)
    rest = value - high.astype(F32)
    middle = rest.astype(BF16)
    low = (rest - middle.astype(F32)).astype(BF16)
    return high, middle, low


def picked(one_hot, value):
    total = None
    for part in three_parts(value):
        term = jnp.dot(one_hot, part, preferred_element_type=F32)
        total = term if total is None else total + term
    return total


def halo_kernel(after_ref, fields_ref, kappa_ref, courant_ref, rows_ref, columns_ref, corner_ref):
    tracers, levels, rows, cols = fields_ref.shape
    lane = lane_iota((rows, cols))
    upper = row_iota((2 * STEPS, cols)) < STEPS
    pairs = levels // 2

    def first_rows(read, count, start):
        for pair in range(pairs):
            one = read(2 * pair)
            two = read(2 * pair + 1) if 2 * pair + 1 < count else jnp.zeros_like(one)
            rows_ref[start + pair] = jnp.where(upper, one, pltpu.roll(two, STEPS, 0))

    def first_columns(read, count, start):
        for tile in range(-(-levels // PACKED)):
            gathered = jnp.zeros((rows, cols), F32)
            for k in range(tile * PACKED, min((tile + 1) * PACKED, count)):
                place = k % PACKED
                gathered = jnp.where(lane // STEPS == place, lane_roll(read(k), place * STEPS), gathered)
            spot = slice((start + tile) * cols, (start + tile + 1) * cols)
            columns_ref[:, spot] = gathered
            corner_ref[:, spot] = gathered[0 : 2 * STEPS]

    tiles = -(-levels // PACKED)
    for tracer in range(tracers):
        first_rows(lambda k: fields_ref[tracer, k, 0 : 2 * STEPS, :], levels, tracer * pairs)
        first_columns(lambda k: fields_ref[tracer, k], levels, tracer * tiles)
    first_rows(lambda k: kappa_ref[k, 0 : 2 * STEPS, :], levels - 1, tracers * pairs)
    first_columns(lambda k: kappa_ref[k], levels - 1, tracers * tiles)
    rows_ref[(tracers + 1) * pairs] = jnp.where(
        upper,
        courant_ref[0, 0 : 2 * STEPS, :],
        pltpu.roll(courant_ref[1, 0 : 2 * STEPS, :], STEPS, 0),
    )
    for which in range(2):
        repeated = jnp.where(lane < STEPS, courant_ref[which], 0.0)
        shift = STEPS
        while shift < cols:
            repeated = repeated + lane_roll(repeated, shift)
            shift *= 2
        spot = slice(((tracers + 1) * tiles + which) * cols, ((tracers + 1) * tiles + which + 1) * cols)
        columns_ref[:, spot] = repeated
        corner_ref[:, spot] = repeated[0 : 2 * STEPS]


def wide_steps(spot_ref, refs, tracer, levels, tracers, all_levels, first_field, store, each_step):
    kappa_ref, courant_ref, rows_ref, columns_ref, corner_ref, state = refs
    rows, cols = courant_ref.shape[1:]
    pairs = all_levels // 2
    tiles = -(-all_levels // PACKED)
    used = -(-levels // PACKED)
    tall = rows + 2 * STEPS
    has_north = spot_ref[3] > 0
    lane = lane_iota((tall, cols))

    def with_rows(block, start, k):
        extra = rows_ref[start + k // 2]
        if k % 2:
            extra = pltpu.roll(extra, STEPS, 0)
        return jnp.concatenate([block, jnp.where(has_north, extra, 0.0)], axis=0)

    def strip(index):
        spot = slice(index * cols, (index + 1) * cols)
        corner = jnp.where(has_north, corner_ref[:, spot], 0.0)
        return jnp.concatenate([columns_ref[:, spot], corner], axis=0)

    last = rows_ref[(tracers + 1) * pairs]
    last = jnp.where(has_north, last, 0.0)
    zonal = jnp.concatenate([courant_ref[0], last], axis=0)
    meridional = jnp.concatenate([courant_ref[1], pltpu.roll(last, STEPS, 0)], axis=0)
    weight = (1.0 - zonal) - meridional
    side_zonal = strip((tracers + 1) * tiles)
    side_meridional = strip((tracers + 1) * tiles + 1)
    side_weight = (1.0 - side_zonal) - side_meridional
    side = [strip(tracer * tiles + i) for i in range(used)]
    side_kappa = [strip(tracers * tiles + i) for i in range(used)]
    end = (levels - (used - 1) * PACKED) * STEPS
    if levels < all_levels:
        side_kappa[-1] = jnp.where(lane < end, side_kappa[-1], 0.0)

    def lanes_on(tiles_in, shift):
        out = []
        for i, tile in enumerate(tiles_in):
            turned = lane_roll(tile, -shift)
            other = tiles_in[(i + 1 if shift > 0 else i - 1) % len(tiles_in)]
            if len(tiles_in) > 1:
                inside = lane < cols - shift if shift > 0 else lane >= -shift
                turned = jnp.where(inside, turned, lane_roll(other, -shift))
            out.append(turned)
        return out

    for step in range(STEPS):
        height = rows if step == STEPS - 1 else tall
        z, m, w = zonal[:height], meridional[:height], weight[:height]
        at_end = lane[:height] == cols - 1
        side_east = [side_zonal * tile for tile in side]

        def field_of(k):
            if step == 0:
                return with_rows(first_field(k), tracer * pairs, k)
            return state[k]

        def advected(k):
            field = field_of(k)
            edge = lane_roll(side_east[k // PACKED], cols - 1 - (k % PACKED) * STEPS)
            east = jnp.where(at_end, edge[:height], lane_roll((z * field[:height]), cols - 1))
            north = next_row(meridional * field)[:height]
            return (w * field[:height] + east) + north

        here = advected(0)
        above = None
        for k in range(levels):
            result = here
            if k + 1 < levels:
                below = advected(k + 1)
                kappa = kappa_ref[k]
                if height > rows:
                    kappa = with_rows(kappa, tracers * pairs, k)
                flux = kappa * (below - here)
                result = result + flux
            if k > 0:
                result = result - above
            if step == STEPS - 1:
                store(k, result)
            else:
                state[k] = result
            if k + 1 < levels:
                here, above = below, flux
        if step < STEPS - 1:
            east = lanes_on(side_east, 1)
            advected_side = [
                (side_weight * tile + turned) + next_row(side_meridional * tile)
                for tile, turned in zip(side, east)
            ]
            under = lanes_on(advected_side, STEPS)
            fluxes = [kap * (low - adv) for kap, low, adv in zip(side_kappa, under, advected_side)]
            over = lanes_on(fluxes, -STEPS)
            side = [(adv + flux) - up for adv, flux, up in zip(advected_side, fluxes, over)]
            if each_step is not None:
                each_step(step + 1, zonal, meridional, side_zonal, side)


def early_kernel(
    after_ref, spot_ref, fields_ref, kappa_ref, courant_ref, rows_ref, columns_ref, corner_ref,
    values_ref, north_ref, east_ref, state, *, all_levels,
):
    tracers, levels, rows, cols = fields_ref.shape
    refs = (kappa_ref, courant_ref, rows_ref, columns_ref, corner_ref, state)
    for tracer in range(tracers):

        def each_step(step, zonal, meridional, side_zonal, side):
            for j in range(2):
                k = step + j
                field = state[k]
                values_ref[step - 1, tracer, j] = field[:rows]
                line = ((step - 1) * tracers + tracer) * 2 + j
                north_ref[line : line + 1, :] = meridional[rows : rows + 1] * field[rows : rows + 1]
                east_ref[step - 1, tracer, j] = lane_roll(side_zonal * side[0], cols - 1 - k * STEPS)[:rows]

        wide_steps(
            spot_ref, refs, tracer, levels, tracers, all_levels,
            lambda k: fields_ref[tracer, k], lambda k, value: None, each_step,
        )


def deep_kernel(*refs, tracer, tracers):
    _, spot_ref, fields_ref, *rest = refs
    *halo, out_ref, state = rest[-7:] if len(rest) == 7 else rest[1:]
    levels = fields_ref.shape[1]

    def store(k, value):
        if k >= STEPS:
            out_ref[0, k] = value

    for k in range(STEPS):
        out_ref[0, k] = jnp.zeros(out_ref.shape[2:], F32)
    wide_steps(
        spot_ref, (*halo, state), tracer, levels, tracers, levels, lambda k: fields_ref[0, k], store, None
    )


def send_surface(late, below, refs, send_ref, model):
    courant_ref, kappa_ref, coupling_ref, west_ref, south_ref, pack_ref = refs
    tracers = len(late)
    zonal, meridional = courant_ref[0], courant_ref[1]
    weight = (1.0 - zonal) - meridional
    rows, cols = zonal.shape
    groups = cols // TILE
    lane = lane_iota((rows, cols))
    row = row_iota((rows, cols))
    kappa = kappa_ref[0]
    coupling = coupling_ref[...]
    group = lane // TILE
    tiles, edge_north, edge_east = [], [], []
    place = lane == (row % groups) * TILE + (TILE - 1) - row // groups
    west_a = lane_roll(west_ref[0], 1)
    west_b = lane_roll(west_ref[1], 1)
    own_north, own_east = [], jnp.zeros((rows, cols), F32)
    for tracer in range(tracers):
        parts = []
        for field in (late[tracer][0], below[tracer]):
            eastward, northward = zonal * field, meridional * field
            east = jnp.where(lane == cols - 1, 0.0, lane_roll(eastward, cols - 1))
            north = jnp.where(row == rows - 1, 0.0, next_row(northward))
            parts.append((eastward, northward, (weight * field + east) + north))
        (east0, north0, here), (east1, north1, under) = parts
        mixed = here + kappa * (under - here)
        scaled = coupling * mixed
        edge_north.append(
            south_ref[0, rows - 1 : rows, :] * north0[0:1] + south_ref[1, rows - 1 : rows, :] * north1[0:1]
        )
        column = west_a * east0 + west_b * east1
        column = jnp.broadcast_to(column[:, 0:1], (rows, cols))
        edge_east.append(jnp.sum(jnp.where(place, column, 0.0), axis=0, keepdims=True))
        for k, field in enumerate(late[tracer]):
            own_north.append(meridional[0:1] * field[0:1])
            column = jnp.broadcast_to((zonal * field)[:, 0:1], (rows, cols))
            spot = (tracer * len(late[tracer]) + k) * rows + row
            own_east = jnp.where(lane == spot, column, own_east)
        blocks = []
        for c in range(groups):
            block = jnp.where(group == c, scaled, 0.0)
            shift = TILE
            while shift < cols:
                block = block + lane_roll(block, shift)
                shift *= 2
            blocks.append(block)
        tiles.append(jnp.concatenate(blocks, axis=0))
    slots = picked(pack_ref[...], jnp.concatenate(tiles, axis=0))
    height = slots.shape[0] // groups
    slot_group = lane_iota((height, cols)) // TILE
    packed = jnp.zeros((height, cols), F32)
    for g in range(groups):
        packed = jnp.where(slot_group == g, slots[g * height : (g + 1) * height], packed)
    devices = send_ref.shape[0] // 2
    per_device = height // devices
    edges = jnp.concatenate(edge_north + edge_east, axis=0)
    deep = send_ref.shape[1]
    own = own_north + [jnp.zeros((1, cols), F32)] * (deep - 1 - len(own_north))
    own = jnp.concatenate(own + [jnp.sum(own_east, axis=0, keepdims=True)], axis=0)
    used = per_device + 2 * tracers
    for device in range(devices):
        there = (1 - model) * devices + device
        send_ref[there, 0:per_device, :] = packed[device * per_device : (device + 1) * per_device]
        send_ref[there, per_device:used, :] = edges
        if used < deep:
            send_ref[there, used:deep, :] = jnp.zeros((deep - used, cols), F32)
        send_ref[model * devices + device] = own


def receive_surface(model, recv_ref, pick_ref, place_ref, surface, coupling_ref, mask_ref):
    devices = recv_ref.shape[0] // 2
    rows, cols = coupling_ref.shape
    groups = cols // TILE
    tracers = len(surface)
    other = (1 - model) * devices
    slab = recv_ref[pl.ds(other, devices)].reshape(devices * recv_ref.shape[1], cols)
    table = jnp.concatenate([slab, lane_roll(slab, 1)], axis=0)
    found = picked(pick_ref[...], table)
    count = rows * groups
    group = lane_iota((rows, cols)) // TILE
    wet = mask_ref[...].astype(F32)
    coupling = coupling_ref[...]
    updated = []
    for tracer in range(tracers):
        total = None
        for kind in range(3):
            start = (kind * tracers + tracer) * count
            term = jnp.where(place_ref[kind] > 0, found[start : start + count], 0.0)
            total = term if total is None else total + term
        shift = TILE
        while shift < cols:
            total = total + lane_roll(total, shift)
            shift *= 2
        received = jnp.zeros((rows, cols), F32)
        for c in range(groups):
            received = jnp.where(group == c, total[c * rows : (c + 1) * rows], received)
        own = surface[tracer]
        updated.append(own + wet * (received - coupling * own))
    return updated


def upper_levels(spot_ref, recv_ref, late, early, refs):
    courant_ref, kappa_ref = refs
    zonal, meridional = courant_ref[0], courant_ref[1]
    weight = (1.0 - zonal) - meridional
    rows, cols = zonal.shape
    lane = lane_iota((rows, cols))
    row = row_iota((rows, cols))
    devices = recv_ref.shape[0] // 2
    mine = spot_ref[0] * devices
    from_east = recv_ref[mine + spot_ref[1]]
    from_north = jnp.where(spot_ref[3] > 0, recv_ref[mine + spot_ref[2]], 0.0)
    east_line = jnp.broadcast_to(from_east[from_east.shape[0] - 1 :], (rows, cols))
    stepped = []
    for tracer in range(len(late)):
        count = len(late[tracer])
        moved = []
        for k in range(count + len(early[tracer])):
            if k < count:
                field = late[tracer][k]
                index = tracer * count + k
                north_edge = from_north[index : index + 1]
                column = jnp.where(lane == index * rows + row, east_line, 0.0)
                east_edge = jnp.sum(column, axis=1, keepdims=True)
            else:
                field, north_edge, east_edge = early[tracer][k - count]
            east = jnp.where(lane == cols - 1, east_edge, lane_roll(zonal * field, cols - 1))
            north = jnp.where(row == rows - 1, north_edge, next_row(meridional * field))
            moved.append((weight * field + east) + north)
        out, above = [], None
        for k in range(len(moved) - 1):
            flux = kappa_ref[k] * (moved[k + 1] - moved[k])
            result = moved[k] + flux
            if k > 0:
                result = result - above
            out.append(result)
            above = flux
        stepped.append(out)
    return stepped


def early_levels(step, early_refs, tracer, tracers):
    if early_refs is None:
        return []
    values_ref, north_ref, east_ref = early_refs
    found = []
    for j in range(2):
        line = ((step - 1) * tracers + tracer) * 2 + j
        found.append((values_ref[step - 1, tracer, j], north_ref[line : line + 1, :], east_ref[step - 1, tracer, j]))
    return found


def first_send_kernel(spot_ref, fields_ref, *refs):
    *inputs, send_ref = refs
    tracers, levels = fields_ref.shape[:2]
    late = [[fields_ref[tracer, k] for k in range(levels)] for tracer in range(tracers)]
    send_surface(late, [values[1] for values in late], inputs, send_ref, spot_ref[0])


def exchange_kernel(spot_ref, late_ref, recv_ref, pick_ref, place_ref, mask_ref, *refs, step, last):
    early_refs, refs = (refs[:3], refs[3:]) if step > 0 else (None, refs)
    if last:
        *inputs, out_ref = refs
    else:
        *inputs, late_out, send_ref = refs
    courant_ref, kappa_ref, coupling_ref = inputs[:3]
    tracers = late_ref.shape[0]
    late = [[late_ref[tracer, k] for k in range(late_ref.shape[1])] for tracer in range(tracers)]
    early = [early_levels(step, early_refs, tracer, tracers) for tracer in range(tracers)]
    stepped = upper_levels(spot_ref, recv_ref, late, early, (courant_ref, kappa_ref))
    surface = [values[0] for values in stepped]
    surface = receive_surface(spot_ref[0], recv_ref, pick_ref, place_ref, surface, coupling_ref, mask_ref)
    for tracer in range(tracers):
        stepped[tracer][0] = surface[tracer]
    if last:
        for tracer in range(tracers):
            for k in range(STEPS):
                out_ref[tracer, k] = stepped[tracer][k]
        return
    kept = late_out.shape[1]
    for tracer in range(tracers):
        for k in range(kept):
            late_out[tracer, k] = stepped[tracer][k]
    send_surface(
        [values[:kept] for values in stepped], [values[1] for values in stepped], inputs, send_ref, spot_ref[0]
    )


VMEM_LIMIT = 32 * 1024 * 1024


def whole(array):
    zeros = (0,) * array.ndim
    return pl.BlockSpec(array.shape, lambda i: zeros)


def top(array, levels):
    tracers, _, rows, cols = array.shape
    return pl.BlockSpec((tracers, levels, rows, cols), lambda i: (0, 0, 0, 0))


SCALAR = pl.BlockSpec(memory_space=pltpu.SMEM)
UNREAD = pl.BlockSpec(memory_space=pl.ANY)


def call(kernel, operands, specs, out_shape, out_specs, name, aliases=None, scratch=(), flops=0, moved=0):
    return pl.pallas_call(
        kernel,
        grid=(1,),
        in_specs=specs,
        out_shape=out_shape,
        out_specs=out_specs,
        scratch_shapes=list(scratch),
        input_output_aliases=aliases or {},
        name=name,
        cost_estimate=pl.CostEstimate(flops=flops, bytes_accessed=moved, transcendentals=0),
        compiler_params=pltpu.CompilerParams(vmem_limit_bytes=VMEM_LIMIT),
    )(*operands)


def shaped(*shape):
    return jax.ShapeDtypeStruct(shape, F32)


def tile_order(partner, rows, groups):
    count = rows * groups
    a = lax.broadcasted_iota(jnp.int32, (count, count), 0)
    b = lax.broadcasted_iota(jnp.int32, (count, count), 1)
    turn = (a == (b % rows) * groups + b // rows).astype(BF16)
    both = jnp.concatenate([partner // count, partner % count], axis=0)
    both = jnp.concatenate([both, jnp.zeros((6, count), jnp.int32)], axis=0).astype(F32).astype(BF16)
    lines = jnp.dot(both, turn, preferred_element_type=F32)
    columns = lax.dot_general(turn, both, (((0,), (1,)), ((), ())), preferred_element_type=F32)
    lines, columns = lines.astype(jnp.int32), columns.astype(jnp.int32)
    return lines[0:1], lines[1:2], columns[:, 0:1], columns[:, 1:2]


def pack_kernel(partner_ref, pack_ref, *, rows, groups, main_rows, tracers):
    count = rows * groups
    line_target, _, column_target, _ = tile_order(partner_ref[...], rows, groups)
    a = lax.broadcasted_iota(jnp.int32, (count, count), 0)
    b = lax.broadcasted_iota(jnp.int32, (count, count), 1)
    place_a = (a % rows) * groups + a // rows
    place_b = (b % rows) * groups + b // rows
    ahead = (column_target == line_target) & (place_a < place_b)
    sent = jnp.sum(ahead.astype(F32), axis=0, keepdims=True).astype(jnp.int32)
    height = pack_ref.shape[0] // groups
    per_device = main_rows * tracers
    slot = lax.broadcasted_iota(jnp.int32, (pack_ref.shape[0], count), 0)
    for tracer in range(tracers):
        index = (sent % groups) * height + line_target * per_device + tracer * main_rows + sent // groups
        pack_ref[:, tracer * count : (tracer + 1) * count] = (slot == index).astype(F32).astype(BF16)


def pick_kernel(
    after_ref, partner_ref, pick_ref, place_ref, *, rows, groups, main_rows, tracers, n_lat, n_lon, deep
):
    count = rows * groups
    per_device = main_rows * tracers
    devices = n_lat * n_lon
    line_target, line_slot, target, slot = tile_order(partner_ref[...], rows, groups)
    ahead = (target == line_target) & (line_slot < slot)
    came = jnp.sum(ahead.astype(F32), axis=1, keepdims=True).astype(jnp.int32)
    row, group = slot // groups, slot % groups
    lat, lon = target // n_lon, target % n_lon
    north_ok = (row == rows - 1) & (lat < n_lat - 1)
    east_ok = group == groups - 1
    east_device = lat * n_lon + (lon + 1) % n_lon
    index = lax.broadcasted_iota(jnp.int32, (count, pick_ref.shape[1]), 1)
    for tracer in range(tracers):
        picks = (
            target * deep + tracer * main_rows + came // groups,
            jnp.where(north_ok, (target + n_lon) * deep + per_device + tracer, -1),
            jnp.where(
                east_ok,
                east_device * deep + per_device + tracers + tracer + (row // groups) * (devices * deep),
                -1,
            ),
        )
        for kind, pick in enumerate(picks):
            start = (kind * tracers + tracer) * count
            pick_ref[start : start + count, :] = (pick == index).astype(F32).astype(BF16)
    lane = lax.broadcasted_iota(jnp.int32, (count, groups * TILE), 1)
    place_ref[0] = (lane // TILE == came % groups).astype(F32)
    place_ref[1] = (lane // TILE == group).astype(F32)
    place_ref[2] = (lane == (row % groups) * TILE + TILE - 1).astype(F32)


def local(adjoint, courant, diffusivity, coupling, partner, mask):
    fields = adjoint[0]
    courant, kappa, coupling, mask = courant[0], diffusivity[0], coupling[0], mask[0]
    tracers, levels, rows, cols = fields.shape
    groups = cols // TILE
    count = rows * groups
    n_lat, n_lon = lax.axis_size("lat"), lax.axis_size("lon")
    devices = n_lat * n_lon
    capacity = max(2, 2 * count // devices)
    main_rows = -(-capacity // groups)
    deep = max(8, main_rows * tracers + 2 * tracers)
    lat, lon = lax.axis_index("lat"), lax.axis_index("lon")
    spot = jnp.stack(
        [
            lax.axis_index("mp"),
            lat * n_lon + (lon + 1) % n_lon,
            ((lat + 1) % n_lat) * n_lon + lon,
            (lat < n_lat - 1).astype(jnp.int32),
        ]
    ).astype(jnp.int32)

    share = jnp.stack([coupling * (1.0 - kappa[0]), coupling * kappa[0]])
    from_west = lax.ppermute(share, "lon", [(i, (i + 1) % n_lon) for i in range(n_lon)])
    from_south = lax.ppermute(share, "lat", [(i, (i + 1) % n_lat) for i in range(n_lat)])

    sizes = dict(rows=rows, groups=groups, main_rows=main_rows, tracers=tracers)
    per_device = main_rows * tracers
    pack_shape = jax.ShapeDtypeStruct((groups * devices * per_device, tracers * count), BF16)
    pack = call(
        functools.partial(pack_kernel, **sizes),
        (partner,),
        [whole(partner)],
        pack_shape,
        whole(pack_shape),
        "pack_table",
    )
    upper = kappa[:STEPS]
    sending = (courant, upper, coupling, from_west, from_south, pack)
    sending_specs = [whole(a) for a in sending]
    send_shape = shaped(2 * devices, deep, cols)
    send = call(
        first_send_kernel,
        (spot, fields, *sending),
        [SCALAR, top(fields, 3), *sending_specs],
        send_shape,
        whole(send_shape),
        "first_send",
    )
    recv = lax.all_to_all(send, ("mp", "lat", "lon"), split_axis=0, concat_axis=0, tiled=True)

    pick_shape = jax.ShapeDtypeStruct((3 * tracers * count, 2 * devices * deep), BF16)
    place_shape = shaped(3, count, cols)
    pick, place = call(
        functools.partial(pick_kernel, n_lat=n_lat, n_lon=n_lon, deep=deep, **sizes),
        (send, partner),
        [UNREAD, whole(partner)],
        (pick_shape, place_shape),
        (whole(pick_shape), whole(place_shape)),
        "pick_table",
    )
    tiles = -(-levels // PACKED)
    width = ((tracers + 1) * tiles + 2) * cols
    halo_shapes = (
        shaped((tracers + 1) * (levels // 2) + 1, 2 * STEPS, cols),
        shaped(rows, width),
        shaped(2 * STEPS, width),
    )
    north, east, corner = call(
        halo_kernel,
        (send, fields, kappa, courant),
        [UNREAD, *(whole(a) for a in (fields, kappa, courant))],
        halo_shapes,
        tuple(whole(a) for a in halo_shapes),
        "halo",
        moved=4 * fields.size,
    )
    north = lax.ppermute(north, "lat", [((i + 1) % n_lat, i) for i in range(n_lat)])
    east = lax.ppermute(east, "lon", [((i + 1) % n_lon, i) for i in range(n_lon)])
    corner = lax.ppermute(
        corner,
        ("lat", "lon"),
        [
            (((i + 1) % n_lat) * n_lon + (j + 1) % n_lon, i * n_lon + j)
            for i in range(n_lat)
            for j in range(n_lon)
        ],
    )
    halo = (courant, north, east, corner)
    halo_specs = [whole(a) for a in halo]
    field_bytes = 4 * fields.size
    tall = rows + 2 * STEPS

    late, early, out = fields, (), None
    for step in range(STEPS):
        if step > 0:
            recv = lax.all_to_all(send, ("mp", "lat", "lon"), split_axis=0, concat_axis=0, tiled=True)
        if step == 1:
            shown = 2 * STEPS
            early_shapes = (
                shaped(STEPS - 1, tracers, 2, rows, cols),
                shaped(-(-(STEPS - 1) * tracers * 2 // 8) * 8, cols),
                shaped(STEPS - 1, tracers, 2, rows, cols),
            )
            early = call(
                functools.partial(early_kernel, all_levels=levels),
                (send, spot, fields, kappa, *halo),
                [
                    UNREAD,
                    SCALAR,
                    top(fields, shown),
                    pl.BlockSpec((shown, rows, cols), lambda i: (0, 0, 0)),
                    *halo_specs,
                ],
                early_shapes,
                tuple(whole(a) for a in early_shapes),
                "early_levels",
                scratch=[pltpu.VMEM((shown, tall, cols), F32)],
                flops=field_bytes,
                moved=field_bytes,
            )
        if step > 1:
            for tracer in range(step - 2, tracers if step == STEPS - 1 else step - 1):
                before = () if out is None else (out,)
                block = pl.BlockSpec((1, levels, rows, cols), lambda i, tracer=tracer: (tracer, 0, 0, 0))
                out = call(
                    functools.partial(deep_kernel, tracer=tracer, tracers=tracers),
                    (send, spot, fields, *before, kappa, *halo),
                    [UNREAD, SCALAR, block, *(UNREAD for _ in before), whole(kappa), *halo_specs],
                    shaped(*fields.shape),
                    block,
                    "deep_levels",
                    aliases={3: 0} if before else None,
                    scratch=[pltpu.VMEM((levels, tall, cols), F32)],
                    flops=10 * field_bytes,
                    moved=field_bytes,
                )
        last = step == STEPS - 1
        kept = step + 1
        arriving = (spot, late, recv, pick, place, mask, *early)
        late_spec = top(late, 3) if step == 0 else whole(late)
        specs = [SCALAR, late_spec, *(whole(a) for a in arriving[2:])]
        kernel = functools.partial(exchange_kernel, step=step, last=last)
        if last:
            operands = (*arriving, *sending[:3], out)
            fields = call(
                lambda *refs: kernel(*refs[:-2], refs[-1]),
                operands,
                [*specs, *sending_specs[:3], UNREAD],
                shaped(*fields.shape),
                top(fields, STEPS),
                "last_exchange",
                aliases={len(operands) - 1: 0},
            )
        else:
            late_shape = shaped(tracers, kept, rows, cols)
            late, send = call(
                kernel,
                (*arriving, *sending),
                [*specs, *sending_specs],
                (late_shape, send_shape),
                (whole(late_shape), whole(send_shape)),
                "exchange",
            )
    return fields[None]


def solution(mesh):
    placed = (
        P("mp", None, None, "lat", "lon"),
        P("mp", None, "lat", "lon"),
        P("mp", None, "lat", "lon"),
        P("mp", "lat", "lon"),
        P("mp", ("lat", "lon")),
        P("mp", "lat", "lon"),
    )
    return jax.shard_map(
        local,
        mesh=mesh,
        in_specs=placed,
        out_specs=P("mp", None, None, "lat", "lon"),
        check_vma=False,
    )
```

time: 108 us -> 76.1 us (0.70)
  Pallas kernels: 50.1 us -> 23.1 us
  starting transfers between devices: 39.8 us -> 19.9 us
  blocking collectives: 0 us -> 12.5 us
  waiting for transfers between devices: 4.32 us -> 8.37 us
  other arithmetic: 2.34 us -> 0.8 us
    pallas_call x10 -> x11, Pallas kernels: 50.1 us -> 23.1 us  [call(): pl.pallas_call(kernel, grid=(1,), in_specs=specs, out_shape=out_shape, ou...]
    all_to_all x0 -> x1, blocking collectives: none -> 12.5 us  [local(): lax.all_to_all(send, ('mp', 'lat', 'lon'), split_axis=0, concat_axis=0, t...]
    ppermute x8 -> x3, starting transfers between devices: 18.7 us -> 6.49 us  [the longest x1 3.43 us: local(): lax.ppermute(east, 'lon', [((i + 1) % n_lon, i) for i in range(n_lon)])]
    all_to_all x4 -> x3, starting transfers between devices: 18.2 us -> 10.3 us  [local(): lax.all_to_all(send, ('mp', 'lat', 'lon'), split_axis=0, concat_axis=0, t...]
    all_to_all x4 -> x3, waiting for transfers between devices: 0.01 us -> 4.3 us  [local(): lax.all_to_all(send, ('mp', 'lat', 'lon'), split_axis=0, concat_axis=0, t...]
    ppermute x8 -> x3, waiting for transfers between devices: 4.3 us -> 3.1 us  [the longest x1 3.09 us: local(): lax.ppermute(corner, ('lat', 'lon'), [((i + 1) % n_lat * n_lon + (j + 1)...]
    unnamed x29 -> x54, local copies, waits for them, and re-layouts: 9.37 us -> 9.49 us
  transfers between devices with their start and end apart: 14 -> 8, of which waited for: 3 -> 3; matrix products, arithmetic and copies ran while one was open for 3% -> 1% of each run, Pallas kernels for 38% -> 19%
where the time goes in v3:
time: 76.1 us; the launch traced here: 75.2 us
  Pallas kernels  23.1 us (30%)
  starting transfers between devices  19.9 us (26%)
  blocking collectives  12.5 us (16%)
  local copies, waits for them, and re-layouts  10.3 us (14%)
  waiting for transfers between devices  8.37 us (11%)
  other arithmetic  0.8 us (1%)
    pallas_call x11, Pallas kernels, call(): pl.pallas_call(kernel, grid=(1,), in_specs=specs, out_shape=out_shape, ou...  23.1 us
    all_to_all x1, blocking collectives, local(): lax.all_to_all(send, ('mp', 'lat', 'lon'), split_axis=0, concat_axis=0, t...  12.5 us
    all_to_all x3, starting transfers between devices, local(): lax.all_to_all(send, ('mp', 'lat', 'lon'), split_axis=0, concat_axis=0, t...  10.3 us
    unnamed x54, local copies, waits for them, and re-layouts  9.49 us
    all_to_all x3, waiting for transfers between devices, local(): lax.all_to_all(send, ('mp', 'lat', 'lon'), split_axis=0, concat_axis=0, t...  4.3 us
    ppermute x1, starting transfers between devices, local(): lax.ppermute(east, 'lon', [((i + 1) % n_lon, i) for i in range(n_lon)])  3.43 us
    ppermute x1, waiting for transfers between devices, local(): lax.ppermute(corner, ('lat', 'lon'), [((i + 1) % n_lat * n_lon + (j + 1)...  3.09 us
    ppermute x1, starting transfers between devices, local(): lax.ppermute(share, 'lat', [(i, (i + 1) % n_lat) for i in range(n_lat)])  2.59 us
  transfers between devices with their start and end apart: 8, of which 3 were waited for; matrix products, arithmetic and copies ran while one was open for 1% of the time, Pallas kernels for 19%

profile of v3, /device:TPU:0, one launch (start us, length us, event | category | flops | bytes accessed | tf_op | source)
XLA Modules:
  0.0 75.2 jit_solution(4118057584974344369)
XLA Ops:
  0.0 0.7 fusion
  1.2 2.6 %collective-permute-start.1 = (f32[2,16,128]{2,1,0:T(8,128)S(1)}, f32[2,16,128]{2,1,0:T(8,128)S(1)}, u32[]{:S(2)}, u32[]{:S(2)}) collective-permute-start(f32[2,16,128]{2,1,0:T(8,128)S(1)} %pad_maximum_fusion), channel_id=1, source_target_pairs={{0,8},{8,0},{1,9},{9,1},{2,10},{10,2},{3,11},{11,3},{4,12},{12,4},... | collective-permute-start | bytes 49160 | tf_op jit(solution)/shard_map/ppermute | solution.py:541
  3.8 0.8 %slice_bitcast_fusion.refs_1_.refs_4_.refs_10_ = f32[4,16,128]{2,1,0:T(8,128)S(1)} fusion(f32[1,71,16,128]{3,2,1,0:T(8,128)} %param.8), kind=kLoop, calls=%fused_computation | loop fusion | bytes 65536 | tf_op jit(solution)/shard_map/slice | solution.py:554
  5.7 1.0 %collective-permute-done.refs_3_.refs_6_ = f32[2,16,128]{2,1,0:T(8,128)S(1)} collective-permute-done((f32[2,16,128]{2,1,0:T(8,128)S(1)}, f32[2,16,128]{2,1,0:T(8,128)S(1)}, u32[]{:S(2)}, u32[]{:S(2)}) %collective-permute-start) | collective-permute-done | bytes 16416 | tf_op jit(solution)/shard_map/ppermute | solution.py:540
  6.7 1.3 %copy-done = f32[1,2,72,16,128]{4,3,2,1,0:T(8,128)S(1)} copy-done((f32[1,2,72,16,128]{4,3,2,1,0:T(8,128)S(1)}, f32[1,2,72,16,128]{4,3,2,1,0:T(8,128)}, u32[]{:S(2)}) %copy-start) | copy-done | bytes 1179672
  9.4 1.9 %first_send.1.after_ref = f32[32,8,128]{2,1,0:T(8,128)} custom-call(s32[4]{0:T(128)S(1)} %pad_add_fusion.spot_ref.refs_1_.refs_0_, f32[2,72,16,128]{3,2,1,0:T(8,128)S(1)} %bitcast.17, f32[2,16,128]{2,1,0:T(8,128)S(1)} %bitcast.27, f32[4,16,128]{2,1,0:T(8,128)S(1)} %slice_bitcast_fusion.refs_1_.refs_4_.refs_10_, f32[16,128]{1,0:T(8,128)S(1)} %bitcast.36, ...), custom_call_target="tpu_custom_call" | custom-call | tf_op jit(solution)/shard_map/first_send/pallas_call | solution.py:436
  11.3 5.2 %all-to-all-start = ((f32[32,8,128]{2,1,0:T(8,128)}), f32[32,8,128]{2,1,0:T(8,128)S(1)}, u32[]{:S(2)}, u32[]{:S(2)}) async-start(f32[32,8,128]{2,1,0:T(8,128)} %first_send.1.after_ref), calls=%async_computation | async-start | bytes 262144 | tf_op jit(solution)/shard_map/all_to_all | solution.py:566
  16.5 1.4 %halo.1 = (f32[109,8,128]{2,1,0:T(8,128)}, f32[16,1408]{1,0:T(8,128)S(1)}, f32[8,1408]{1,0:T(8,128)S(1)}) custom-call(f32[32,8,128]{2,1,0:T(8,128)} %first_send.1.after_ref, f32[2,72,16,128]{3,2,1,0:T(8,128)S(1)} %bitcast.18, f32[71,16,128]{2,1,0:T(8,128)S(1)} %bitcast.23, f32[2,16,128]{2,1,0:T(8,128)S(1)} %bitcast.28), custom_call_target="tpu_custom_call" | custom-call | bytes 1179648 | tf_op jit(solution)/shard_map/halo/pallas_call | solution.py:436
  17.9 1.8 %collective-permute-start.2 = (f32[109,8,128]{2,1,0:T(8,128)}, f32[109,8,128]{2,1,0:T(8,128)S(1)}, u32[]{:S(2)}, u32[]{:S(2)}) collective-permute-start(f32[109,8,128]{2,1,0:T(8,128)} %get-tuple-element.23), channel_id=1, source_target_pairs={{8,0},{0,8},{9,1},{1,9},{10,2},{2,10},{11,3},{3,11},{12,4},{4,12},... | collective-permute-start | bytes 1339400 | tf_op jit(solution)/shard_map/ppermute | solution.py:594
  20.3 4.3 %all-to-all-done.recv_ref = f32[32,8,128]{2,1,0:T(8,128)S(1)} async-done(((f32[32,8,128]{2,1,0:T(8,128)}), f32[32,8,128]{2,1,0:T(8,128)S(1)}, u32[]{:S(2)}, u32[]{:S(2)}) %all-to-all-start) | async-done | bytes 131104 | tf_op jit(solution)/shard_map/all_to_all | solution.py:566
  24.7 3.0 %exchange.3 = (f32[2,1,16,128]{3,2,1,0:T(8,128)S(1)}, f32[32,8,128]{2,1,0:T(8,128)}) custom-call(s32[4]{0:T(128)S(1)} %pad_add_fusion.spot_ref.refs_1_.refs_0_, f32[2,72,16,128]{3,2,1,0:T(8,128)S(1)} %bitcast.19, f32[32,8,128]{2,1,0:T(8,128)S(1)} %all-to-all-done.recv_ref, bf16[768,256]{1,0:T(8,128)(2,1)S(1)} %get-tuple-element.19.pick_ref.refs_3_, ...), custom_call_target="tpu_custom_call" | custom-call | tf_op jit(solution)/shard_map/exchange/pallas_call | solution.py:436
  27.6 2.6 %all-to-all-start.1 = ((f32[32,8,128]{2,1,0:T(8,128)}), f32[32,8,128]{2,1,0:T(8,128)S(1)}, u32[]{:S(2)}, u32[]{:S(2)}) async-start(f32[32,8,128]{2,1,0:T(8,128)} %get-tuple-element.22.after_ref), calls=%async_computation.1 | async-start | bytes 262144 | tf_op jit(solution)/shard_map/all_to_all | solution.py:613
  30.2 3.4 %collective-permute-start.3 = (f32[16,1408]{1,0:T(8,128)}, f32[16,1408]{1,0:T(8,128)S(1)}, u32[]{:S(2)}, u32[]{:S(2)}) collective-permute-start(f32[16,1408]{1,0:T(8,128)} %copy-done.25), channel_id=1, source_target_pairs={{1,0},{2,1},{3,2},{4,3},{5,4},{6,5},{7,6},{0,7},{9,8},{10,9},{11,1... | collective-permute-start | bytes 270344 | tf_op jit(solution)/shard_map/ppermute | solution.py:595
  33.6 1.3 %collective-permute-start.4 = (f32[8,1408]{1,0:T(8,128)}, f32[8,1408]{1,0:T(8,128)S(1)}, u32[]{:S(2)}, u32[]{:S(2)}) collective-permute-start(f32[8,1408]{1,0:T(8,128)} %copy-done.26), channel_id=1, source_target_pairs={{9,0},{10,1},{11,2},{12,3},{13,4},{14,5},{15,6},{8,7},{1,8},{2,9},... | collective-permute-start | bytes 135176 | tf_op jit(solution)/shard_map/ppermute | solution.py:596
  34.9 3.1 %collective-permute-done.4.corner_ref.refs_7_.refs_8_ = f32[8,1408]{1,0:T(8,128)S(1)} collective-permute-done((f32[8,1408]{1,0:T(8,128)}, f32[8,1408]{1,0:T(8,128)S(1)}, u32[]{:S(2)}, u32[]{:S(2)}) %collective-permute-start.4) | collective-permute-done | bytes 45088 | tf_op jit(solution)/shard_map/ppermute | solution.py:596
  38.0 1.3 %early_levels.1 = (f32[3,2,2,16,128]{4,3,2,1,0:T(8,128)S(1)}, f32[16,128]{1,0:T(8,128)S(1)}, f32[3,2,2,16,128]{4,3,2,1,0:T(8,128)S(1)}) custom-call(f32[32,8,128]{2,1,0:T(8,128)} %get-tuple-element.22.after_ref, s32[4]{0:T(128)S(1)} %pad_add_fusion.spot_ref.refs_1_.refs_0_, f32[2,72,16,128]{3,2,1,0:T(8,128)S(1)} %bitcast.20, f32[71,16,128]{2,1,0:T(8,128)S(1)} %bitcast.24, ...), custom_call_target="tpu_custom_call" | custom-call | flops 1179648 | bytes 1179648 | tf_op jit(solution)/shard_map/early_levels/pallas_call | solution.py:436
  43.4 2.3 %exchange.4 = (f32[2,2,16,128]{3,2,1,0:T(8,128)S(1)}, f32[32,8,128]{2,1,0:T(8,128)S(1)}) custom-call(s32[4]{0:T(128)S(1)} %pad_add_fusion.spot_ref.refs_1_.refs_0_, f32[2,1,16,128]{3,2,1,0:T(8,128)S(1)} %copy-done.22, f32[32,8,128]{2,1,0:T(8,128)S(1)} %all-to-all-done.1.recv_ref, bf16[768,256]{1,0:T(8,128)(2,1)S(1)} %get-tuple-element.19.pick_ref.refs_3_, ...), custom_call_target="tpu_custom_call" | custom-call | tf_op jit(solution)/shard_map/exchange/pallas_call | solution.py:436
  45.7 12.5 %all_to_all.20.recv_ref = f32[32,8,128]{2,1,0:T(8,128)S(1)} all-to-all(f32[32,8,128]{2,1,0:T(8,128)S(1)} %get-tuple-element.30.refs_0_), channel_id=1, replica_groups=mesh['mp'=2,'lat'=2,'lon'=8] {'mp','lat','lon'}, dimensions={0} | all-to-all | bytes 262144 | tf_op jit(solution)/shard_map/all_to_all | solution.py:613
  58.9 3.0 %exchange.5 = (f32[2,3,16,128]{3,2,1,0:T(8,128)S(1)}, f32[32,8,128]{2,1,0:T(8,128)}) custom-call(s32[4]{0:T(128)S(1)} %pad_add_fusion.spot_ref.refs_1_.refs_0_, f32[2,2,16,128]{3,2,1,0:T(8,128)S(1)} %get-tuple-element.29.late_ref, f32[32,8,128]{2,1,0:T(8,128)S(1)} %all_to_all.20.recv_ref, bf16[768,256]{1,0:T(8,128)(2,1)S(1)} %get-tuple-element.19.pick_ref.refs_3_, ...), custom_call_target="tpu_custom_call" | custom-call | tf_op jit(solution)/shard_map/exchange/pallas_call | solution.py:436
  62.5 2.6 %all-to-all-start.3 = ((f32[32,8,128]{2,1,0:T(8,128)}), f32[32,8,128]{2,1,0:T(8,128)S(1)}, u32[]{:S(2)}, u32[]{:S(2)}) async-start(f32[32,8,128]{2,1,0:T(8,128)} %get-tuple-element.32.refs_0_), calls=%async_computation.3 | async-start | bytes 262144 | tf_op jit(solution)/shard_map/all_to_all | solution.py:613
  65.1 0.8 %copy-done.8 = f32[8,1408]{1,0:T(8,128)S(1)} copy-done((f32[8,1408]{1,0:T(8,128)S(1)}, f32[8,1408]{1,0:T(8,128)}, u32[]{:S(2)}) %copy-start.8) | copy-done | bytes 45080
  65.8 3.7 %deep_levels.2.refs_3_ = f32[2,72,16,128]{3,2,1,0:T(8,128)} custom-call(f32[32,8,128]{2,1,0:T(8,128)S(1)} %copy-done.6, s32[4]{0:T(128)S(1)} %pad_add_fusion.spot_ref.refs_1_.refs_0_, f32[2,72,16,128]{3,2,1,0:T(8,128)S(1)} %bitcast.21, f32[71,16,128]{2,1,0:T(8,128)S(1)} %bitcast.25, f32[2,16,128]{2,1,0:T(8,128)S(1)} %bitcast.33, ...), custom_call_target="tpu_custom_call" | custom-call | flops 11796480 | bytes 1179648 | tf_op jit(solution)/shard_map/deep_levels/pallas_call | solution.py:436
  69.5 3.7 %deep_levels.3.refs_12_ = f32[2,72,16,128]{3,2,1,0:T(8,128)} custom-call(f32[32,8,128]{2,1,0:T(8,128)} %get-tuple-element.32.refs_0_, s32[4]{0:T(128)S(1)} %pad_add_fusion.spot_ref.refs_1_.refs_0_, f32[2,72,16,128]{3,2,1,0:T(8,128)S(1)} %bitcast.22, f32[2,72,16,128]{3,2,1,0:T(8,128)} %deep_levels.2.refs_3_, ...), custom_call_target="tpu_custom_call", output_to_operand_aliasing={{}: (3, {})} | custom-call | flops 11796480 | bytes 1179648 | tf_op jit(solution)/shard_map/deep_levels/pallas_call | solution.py:436
  73.3 1.9 %last_exchange.1 = f32[2,72,16,128]{3,2,1,0:T(8,128)} custom-call(s32[4]{0:T(128)S(1)} %pad_add_fusion.spot_ref.refs_1_.refs_0_, f32[2,3,16,128]{3,2,1,0:T(8,128)S(1)} %copy-done.20, f32[32,8,128]{2,1,0:T(8,128)S(1)} %all-to-all-done.3.refs_2_, bf16[768,256]{1,0:T(8,128)(2,1)S(1)} %get-tuple-element.19.pick_ref.refs_3_, ...), custom_call_target="tpu_custom_call", output_to_operand_aliasing={{}: (12, {})} | custom-call | tf_op jit(solution)/shard_map/last_exchange/pallas_call | solution.py:436
  (62 shorter events, 9.1 us)
Async XLA Ops:
  0.7 15.7 %copy-start.4 = (f32[1,2,16,128]{3,2,1,0:T(8,128)S(1)}, f32[1,2,16,128]{3,2,1,0:T(8,128)}, u32[]{:S(2)}) copy-start(f32[1,2,16,128]{3,2,1,0:T(8,128)} %param.7) | copy-start | bytes 49156
  0.7 6.0 %collective-permute-start = (f32[2,16,128]{2,1,0:T(8,128)S(1)}, f32[2,16,128]{2,1,0:T(8,128)S(1)}, u32[]{:S(2)}, u32[]{:S(2)}) collective-permute-start(f32[2,16,128]{2,1,0:T(8,128)S(1)} %pad_maximum_fusion), channel_id=1, source_target_pairs={{0,1},{1,2},{2,3},{3,4},{4,5},{5,6},{6,7},{7,0},{8,9},{9,10},{10,1... | collective-permute-start | bytes 49160 | tf_op jit(solution)/shard_map/ppermute | solution.py:540
  1.2 5.5 %collective-permute-start.1 = (f32[2,16,128]{2,1,0:T(8,128)S(1)}, f32[2,16,128]{2,1,0:T(8,128)S(1)}, u32[]{:S(2)}, u32[]{:S(2)}) collective-permute-start(f32[2,16,128]{2,1,0:T(8,128)S(1)} %pad_maximum_fusion), channel_id=1, source_target_pairs={{0,8},{8,0},{1,9},{9,1},{2,10},{10,2},{3,11},{11,3},{4,12},{12,4},... | collective-permute-start | bytes 49160 | tf_op jit(solution)/shard_map/ppermute | solution.py:541
  6.7 17.9 %copy-start.11 = (f32[2,16,128]{2,1,0:T(8,128)}, f32[2,16,128]{2,1,0:T(8,128)S(1)}, u32[]{:S(2)}) copy-start(f32[2,16,128]{2,1,0:T(8,128)S(1)} %collective-permute-done.1.refs_4_.refs_7_) | copy-start | bytes 49156
  6.7 1.3 %copy-start = (f32[1,2,72,16,128]{4,3,2,1,0:T(8,128)S(1)}, f32[1,2,72,16,128]{4,3,2,1,0:T(8,128)}, u32[]{:S(2)}) copy-start(f32[1,2,72,16,128]{4,3,2,1,0:T(8,128)} %param.6) | copy-start | bytes 3538948
  9.4 7.1 %copy-start.1 = (f32[1,2,72,16,128]{4,3,2,1,0:T(8,128)S(1)}, f32[1,2,72,16,128]{4,3,2,1,0:T(8,128)}, u32[]{:S(2)}) copy-start(f32[1,2,72,16,128]{4,3,2,1,0:T(8,128)} %param.6) | copy-start | bytes 3538948
  9.4 7.1 %copy-start.2 = (f32[1,71,16,128]{3,2,1,0:T(8,128)S(1)}, f32[1,71,16,128]{3,2,1,0:T(8,128)}, u32[]{:S(2)}) copy-start(f32[1,71,16,128]{3,2,1,0:T(8,128)} %param.8) | copy-start | bytes 1744900
  11.3 8.4 %copy-start.24 = (s32[1,128]{1,0:T(1,128)S(1)}, s32[1,128]{1,0:T(1,128)}, u32[]{:S(2)}) copy-start(s32[1,128]{1,0:T(1,128)} %partner_ref.3) | copy-start | bytes 1540
  11.3 13.4 %copy-start.10 = (f32[1,16,128]{2,1,0:T(8,128)S(1)}, f32[1,16,128]{2,1,0:T(8,128)}, u32[]{:S(2)}) copy-start(f32[1,16,128]{2,1,0:T(8,128)} %param.9) | copy-start | bytes 24580
  11.3 13.4 %copy-start.13 = (s32[1,16,128]{2,1,0:T(8,128)S(1)}, s32[1,16,128]{2,1,0:T(8,128)}, u32[]{:S(2)}) copy-start(s32[1,16,128]{2,1,0:T(8,128)} %param.11) | copy-start | bytes 24580
  11.3 13.4 %all-to-all-start = ((f32[32,8,128]{2,1,0:T(8,128)}), f32[32,8,128]{2,1,0:T(8,128)S(1)}, u32[]{:S(2)}, u32[]{:S(2)}) async-start(f32[32,8,128]{2,1,0:T(8,128)} %first_send.1.after_ref), calls=%async_computation | async-start | bytes 262144 | tf_op jit(solution)/shard_map/all_to_all | solution.py:566
  17.9 1.8 %copy-start.25 = (f32[16,1408]{1,0:T(8,128)}, f32[16,1408]{1,0:T(8,128)S(1)}, u32[]{:S(2)}) copy-start(f32[16,1408]{1,0:T(8,128)S(1)} %get-tuple-element.24) | copy-start | bytes 270340
  17.9 6.8 %copy-start.26 = (f32[8,1408]{1,0:T(8,128)}, f32[8,1408]{1,0:T(8,128)S(1)}, u32[]{:S(2)}) copy-start(f32[8,1408]{1,0:T(8,128)S(1)} %get-tuple-element.25) | copy-start | bytes 135172
  17.9 20.1 %collective-permute-start.2 = (f32[109,8,128]{2,1,0:T(8,128)}, f32[109,8,128]{2,1,0:T(8,128)S(1)}, u32[]{:S(2)}, u32[]{:S(2)}) collective-permute-start(f32[109,8,128]{2,1,0:T(8,128)} %get-tuple-element.23), channel_id=1, source_target_pairs={{8,0},{0,8},{9,1},{1,9},{10,2},{2,10},{11,3},{3,11},{12,4},{4,12},... | collective-permute-start | bytes 1339400 | tf_op jit(solution)/shard_map/ppermute | solution.py:594
  27.6 10.4 %copy-start.21 = (f32[2,1,16,128]{3,2,1,0:T(8,128)}, f32[2,1,16,128]{3,2,1,0:T(8,128)S(1)}, u32[]{:S(2)}) copy-start(f32[2,1,16,128]{3,2,1,0:T(8,128)S(1)} %get-tuple-element.21.late_ref) | copy-start | bytes 49156
  27.6 12.9 %all-to-all-start.1 = ((f32[32,8,128]{2,1,0:T(8,128)}), f32[32,8,128]{2,1,0:T(8,128)S(1)}, u32[]{:S(2)}, u32[]{:S(2)}) async-start(f32[32,8,128]{2,1,0:T(8,128)} %get-tuple-element.22.after_ref), calls=%async_computation.1 | async-start | bytes 262144 | tf_op jit(solution)/shard_map/all_to_all | solution.py:613
  30.2 7.8 %collective-permute-start.3 = (f32[16,1408]{1,0:T(8,128)}, f32[16,1408]{1,0:T(8,128)S(1)}, u32[]{:S(2)}, u32[]{:S(2)}) collective-permute-start(f32[16,1408]{1,0:T(8,128)} %copy-done.25), channel_id=1, source_target_pairs={{1,0},{2,1},{3,2},{4,3},{5,4},{6,5},{7,6},{0,7},{9,8},{10,9},{11,1... | collective-permute-start | bytes 270344 | tf_op jit(solution)/shard_map/ppermute | solution.py:595
  33.6 4.4 %collective-permute-start.4 = (f32[8,1408]{1,0:T(8,128)}, f32[8,1408]{1,0:T(8,128)S(1)}, u32[]{:S(2)}, u32[]{:S(2)}) collective-permute-start(f32[8,1408]{1,0:T(8,128)} %copy-done.26), channel_id=1, source_target_pairs={{9,0},{10,1},{11,2},{12,3},{13,4},{14,5},{15,6},{8,7},{1,8},{2,9},... | collective-permute-start | bytes 135176 | tf_op jit(solution)/shard_map/ppermute | solution.py:596
  58.9 6.2 %copy-start.6 = (f32[32,8,128]{2,1,0:T(8,128)S(1)}, f32[32,8,128]{2,1,0:T(8,128)}, u32[]{:S(2)}) copy-start(f32[32,8,128]{2,1,0:T(8,128)} %copy-done.5) | copy-start | bytes 393220
  62.5 10.8 %all-to-all-start.3 = ((f32[32,8,128]{2,1,0:T(8,128)}), f32[32,8,128]{2,1,0:T(8,128)S(1)}, u32[]{:S(2)}, u32[]{:S(2)}) async-start(f32[32,8,128]{2,1,0:T(8,128)} %get-tuple-element.32.refs_0_), calls=%async_computation.3 | async-start | bytes 262144 | tf_op jit(solution)/shard_map/all_to_all | solution.py:613
  65.0 0.8 %copy-start.8 = (f32[8,1408]{1,0:T(8,128)S(1)}, f32[8,1408]{1,0:T(8,128)}, u32[]{:S(2)}) copy-start(f32[8,1408]{1,0:T(8,128)} %copy-done.7) | copy-start | bytes 135172
  69.5 3.7 %copy-start.15 = (s32[1,16,128]{2,1,0:T(8,128)S(1)}, s32[1,16,128]{2,1,0:T(8,128)}, u32[]{:S(2)}) copy-start(s32[1,16,128]{2,1,0:T(8,128)} %param.11) | copy-start | bytes 24580
  69.5 3.7 %copy-start.18 = (f32[16,128]{1,0:T(8,128)S(1)}, f32[16,128]{1,0:T(8,128)}, u32[]{:S(2)}) copy-start(f32[16,128]{1,0:T(8,128)} %copy-done.16) | copy-start | bytes 24580
  69.5 3.7 %copy-start.20 = (f32[2,3,16,128]{3,2,1,0:T(8,128)S(1)}, f32[2,3,16,128]{3,2,1,0:T(8,128)}, u32[]{:S(2)}) copy-start(f32[2,3,16,128]{3,2,1,0:T(8,128)} %copy-done.19) | copy-start | bytes 147460
  (11 other events, 7.4 us)

commit v4 on v3

--- a/solution.py
+++ b/solution.py
@@ -12,6 +12,13 @@
 F32 = jnp.float32
 BF16 = jnp.bfloat16
 PACKED = 32
+SLAB = 4
+ZONAL, MERIDIONAL, KAPPA = 0, 1, 2
+COUPLING = KAPPA + STEPS
+WEST = COUPLING + 1
+SOUTH = WEST + 2
+WET = SOUTH + 2
+PLACE = WET + 1
 
 
 def lane_iota(shape):
@@ -190,7 +197,7 @@
 
 def early_kernel(
     after_ref, spot_ref, fields_ref, kappa_ref, courant_ref, rows_ref, columns_ref, corner_ref,
-    values_ref, north_ref, east_ref, state, *, all_levels,
+    early_ref, state, *, all_levels,
 ):
     tracers, levels, rows, cols = fields_ref.shape
     refs = (kappa_ref, courant_ref, rows_ref, columns_ref, corner_ref, state)
@@ -200,10 +207,12 @@
             for j in range(2):
                 k = step + j
                 field = state[k]
-                values_ref[step - 1, tracer, j] = field[:rows]
                 line = ((step - 1) * tracers + tracer) * 2 + j
-                north_ref[line : line + 1, :] = meridional[rows : rows + 1] * field[rows : rows + 1]
-                east_ref[step - 1, tracer, j] = lane_roll(side_zonal * side[0], cols - 1 - k * STEPS)[:rows]
+                early_ref[2 * line] = field[:rows]
+                early_ref[2 * line + 1] = lane_roll(side_zonal * side[0], cols - 1 - k * STEPS)[:rows]
+                early_ref[early_ref.shape[0] - 1, line : line + 1, :] = (
+                    meridional[rows : rows + 1] * field[rows : rows + 1]
+                )
 
         wide_steps(
             spot_ref, refs, tracer, levels, tracers, all_levels,
@@ -227,22 +236,22 @@
     )
 
 
-def send_surface(late, below, refs, send_ref, model):
-    courant_ref, kappa_ref, coupling_ref, west_ref, south_ref, pack_ref = refs
+def send_surface(late, below, static_ref, table_ref, send_ref, model, deep_rows):
     tracers = len(late)
-    zonal, meridional = courant_ref[0], courant_ref[1]
+    zonal, meridional = static_ref[ZONAL], static_ref[MERIDIONAL]
     weight = (1.0 - zonal) - meridional
     rows, cols = zonal.shape
     groups = cols // TILE
     lane = lane_iota((rows, cols))
     row = row_iota((rows, cols))
-    kappa = kappa_ref[0]
-    coupling = coupling_ref[...]
+    kappa = static_ref[KAPPA]
+    coupling = static_ref[COUPLING]
     group = lane // TILE
     tiles, edge_north, edge_east = [], [], []
     place = lane == (row % groups) * TILE + (TILE - 1) - row // groups
-    west_a = lane_roll(west_ref[0], 1)
-    west_b = lane_roll(west_ref[1], 1)
+    west_a = lane_roll(static_ref[WEST], 1)
+    west_b = lane_roll(static_ref[WEST + 1], 1)
+    south_a, south_b = static_ref[SOUTH], static_ref[SOUTH + 1]
     own_north, own_east = [], jnp.zeros((rows, cols), F32)
     for tracer in range(tracers):
         parts = []
@@ -254,9 +263,7 @@
         (east0, north0, here), (east1, north1, under) = parts
         mixed = here + kappa * (under - here)
         scaled = coupling * mixed
-        edge_north.append(
-            south_ref[0, rows - 1 : rows, :] * north0[0:1] + south_ref[1, rows - 1 : rows, :] * north1[0:1]
-        )
+        edge_north.append(south_a[rows - 1 : rows] * north0[0:1] + south_b[rows - 1 : rows] * north1[0:1])
         column = west_a * east0 + west_b * east1
         column = jnp.broadcast_to(column[:, 0:1], (rows, cols))
         edge_east.append(jnp.sum(jnp.where(place, column, 0.0), axis=0, keepdims=True))
@@ -274,63 +281,73 @@
                 shift *= 2
             blocks.append(block)
         tiles.append(jnp.concatenate(blocks, axis=0))
-    slots = picked(pack_ref[...], jnp.concatenate(tiles, axis=0))
-    height = slots.shape[0] // groups
-    slot_group = lane_iota((height, cols)) // TILE
-    packed = jnp.zeros((height, cols), F32)
+    devices = send_ref.shape[0] // 2
+    height = devices * SLAB
+    slots = picked(table_ref[deep_rows : deep_rows + groups * height, 0 : rows * groups], jnp.concatenate(tiles, axis=1))
+    slot_group = (lane_iota((height, tracers * cols)) % cols) // TILE
+    packed = jnp.zeros((height, tracers * cols), F32)
     for g in range(groups):
         packed = jnp.where(slot_group == g, slots[g * height : (g + 1) * height], packed)
-    devices = send_ref.shape[0] // 2
-    per_device = height // devices
-    edges = jnp.concatenate(edge_north + edge_east, axis=0)
-    deep = send_ref.shape[1]
-    own = own_north + [jnp.zeros((1, cols), F32)] * (deep - 1 - len(own_north))
+    first, second = packed[:, :cols], packed[:, cols:]
+    upper = row_iota((2 * SLAB, cols)) < SLAB
+    empty = jnp.zeros((SLAB - 2, cols), F32)
+    edges = jnp.concatenate(
+        [empty, edge_north[0], edge_east[0], empty, edge_north[1], edge_east[1]], axis=0
+    )
+    own = own_north + [jnp.zeros((1, cols), F32)] * (2 * SLAB - 1 - len(own_north))
     own = jnp.concatenate(own + [jnp.sum(own_east, axis=0, keepdims=True)], axis=0)
-    used = per_device + 2 * tracers
-    for device in range(devices):
-        there = (1 - model) * devices + device
-        send_ref[there, 0:per_device, :] = packed[device * per_device : (device + 1) * per_device]
-        send_ref[there, per_device:used, :] = edges
-        if used < deep:
-            send_ref[there, used:deep, :] = jnp.zeros((deep - used, cols), F32)
-        send_ref[model * devices + device] = own
-
-
-def receive_surface(model, recv_ref, pick_ref, place_ref, surface, coupling_ref, mask_ref):
+    for pair in range(devices // 2):
+        one, two = (half[pair * 2 * SLAB : (pair + 1) * 2 * SLAB] for half in (first, second))
+        there = (1 - model) * devices + 2 * pair
+        send_ref[there] = jnp.where(upper, one, pltpu.roll(two, SLAB, 0)) + edges
+        send_ref[there + 1] = jnp.where(upper, pltpu.roll(one, SLAB, 0), two) + edges
+        send_ref[model * devices + 2 * pair] = own
+        send_ref[model * devices + 2 * pair + 1] = own
+
+
+def receive_surface(model, recv_ref, table_ref, static_ref, surface):
     devices = recv_ref.shape[0] // 2
-    rows, cols = coupling_ref.shape
+    rows, cols = surface[0].shape
     groups = cols // TILE
     tracers = len(surface)
+    count = rows * groups
     other = (1 - model) * devices
-    slab = recv_ref[pl.ds(other, devices)].reshape(devices * recv_ref.shape[1], cols)
-    table = jnp.concatenate([slab, lane_roll(slab, 1)], axis=0)
-    found = picked(pick_ref[...], table)
-    count = rows * groups
+    upper = row_iota((2 * SLAB, cols)) < SLAB
+    first, second = [], []
+    for pair in range(devices // 2):
+        one, two = recv_ref[other + 2 * pair], recv_ref[other + 2 * pair + 1]
+        first.append(jnp.where(upper, one, pltpu.roll(two, SLAB, 0)))
+        second.append(jnp.where(upper, pltpu.roll(one, SLAB, 0), two))
+    halves = [jnp.concatenate(half, axis=0) for half in (first, second)]
+    slab = jnp.concatenate(halves, axis=1)
+    shifted = jnp.concatenate([lane_roll(half, 1) for half in halves], axis=1)
+    found = picked(table_ref[0 : 3 * count], jnp.concatenate([slab, shifted], axis=0))
     group = lane_iota((rows, cols)) // TILE
-    wet = mask_ref[...].astype(F32)
-    coupling = coupling_ref[...]
+    wet, coupling = static_ref[WET], static_ref[COUPLING]
     updated = []
     for tracer in range(tracers):
-        total = None
-        for kind in range(3):
-            start = (kind * tracers + tracer) * count
-            term = jnp.where(place_ref[kind] > 0, found[start : start + count], 0.0)
-            total = term if total is None else total + term
-        shift = TILE
-        while shift < cols:
-            total = total + lane_roll(total, shift)
-            shift *= 2
         received = jnp.zeros((rows, cols), F32)
         for c in range(groups):
-            received = jnp.where(group == c, total[c * rows : (c + 1) * rows], received)
+            total = None
+            for kind in range(3):
+                start = kind * count + c * rows
+                place = static_ref[PLACE + kind * groups + c]
+                term = jnp.where(
+                    place > 0, found[start : start + rows, tracer * cols : (tracer + 1) * cols], 0.0
+                )
+                total = term if total is None else total + term
+            shift = TILE
+            while shift < cols:
+                total = total + lane_roll(total, shift)
+                shift *= 2
+            received = jnp.where(group == c, total, received)
         own = surface[tracer]
         updated.append(own + wet * (received - coupling * own))
     return updated
 
 
-def upper_levels(spot_ref, recv_ref, late, early, refs):
-    courant_ref, kappa_ref = refs
-    zonal, meridional = courant_ref[0], courant_ref[1]
+def upper_levels(spot_ref, recv_ref, late, early, static_ref):
+    zonal, meridional = static_ref[ZONAL], static_ref[MERIDIONAL]
     weight = (1.0 - zonal) - meridional
     rows, cols = zonal.shape
     lane = lane_iota((rows, cols))
@@ -358,7 +375,7 @@
             moved.append((weight * field + east) + north)
         out, above = [], None
         for k in range(len(moved) - 1):
-            flux = kappa_ref[k] * (moved[k + 1] - moved[k])
+            flux = static_ref[KAPPA + k] * (moved[k + 1] - moved[k])
             result = moved[k] + flux
             if k > 0:
                 result = result - above
@@ -368,54 +385,54 @@
     return stepped
 
 
-def early_levels(step, early_refs, tracer, tracers):
-    if early_refs is None:
+def early_levels(step, early_ref, tracer, tracers):
+    if step == 0:
         return []
-    values_ref, north_ref, east_ref = early_refs
     found = []
     for j in range(2):
         line = ((step - 1) * tracers + tracer) * 2 + j
-        found.append((values_ref[step - 1, tracer, j], north_ref[line : line + 1, :], east_ref[step - 1, tracer, j]))
+        norths = early_ref[early_ref.shape[0] - 1]
+        found.append((early_ref[2 * line], norths[line : line + 1], early_ref[2 * line + 1]))
     return found
 
 
-def first_send_kernel(spot_ref, fields_ref, *refs):
-    *inputs, send_ref = refs
+def first_send_kernel(spot_ref, fields_ref, static_ref, table_ref, send_ref, *, deep_rows):
     tracers, levels = fields_ref.shape[:2]
     late = [[fields_ref[tracer, k] for k in range(levels)] for tracer in range(tracers)]
-    send_surface(late, [values[1] for values in late], inputs, send_ref, spot_ref[0])
-
-
-def exchange_kernel(spot_ref, late_ref, recv_ref, pick_ref, place_ref, mask_ref, *refs, step, last):
-    early_refs, refs = (refs[:3], refs[3:]) if step > 0 else (None, refs)
-    if last:
-        *inputs, out_ref = refs
-    else:
-        *inputs, late_out, send_ref = refs
-    courant_ref, kappa_ref, coupling_ref = inputs[:3]
+    send_surface(late, [values[1] for values in late], static_ref, table_ref, send_ref, spot_ref[0], deep_rows)
+
+
+def exchange_kernel(spot_ref, late_ref, recv_ref, static_ref, table_ref, *refs, step, deep_rows, unread):
+    early_ref, refs = (refs[0], refs[1:]) if step > 0 else (None, refs)
+    refs = refs[unread:]
     tracers = late_ref.shape[0]
     late = [[late_ref[tracer, k] for k in range(late_ref.shape[1])] for tracer in range(tracers)]
-    early = [early_levels(step, early_refs, tracer, tracers) for tracer in range(tracers)]
-    stepped = upper_levels(spot_ref, recv_ref, late, early, (courant_ref, kappa_ref))
+    early = [early_levels(step, early_ref, tracer, tracers) for tracer in range(tracers)]
+    stepped = upper_levels(spot_ref, recv_ref, late, early, static_ref)
     surface = [values[0] for values in stepped]
-    surface = receive_surface(spot_ref[0], recv_ref, pick_ref, place_ref, surface, coupling_ref, mask_ref)
+    surface = receive_surface(spot_ref[0], recv_ref, table_ref, static_ref, surface)
     for tracer in range(tracers):
         stepped[tracer][0] = surface[tracer]
-    if last:
+    if step == STEPS - 1:
+        (out_ref,) = refs
         for tracer in range(tracers):
             for k in range(STEPS):
                 out_ref[tracer, k] = stepped[tracer][k]
         return
+    late_out, send_ref = refs
     kept = late_out.shape[1]
     for tracer in range(tracers):
         for k in range(kept):
             late_out[tracer, k] = stepped[tracer][k]
     send_surface(
-        [values[:kept] for values in stepped], [values[1] for values in stepped], inputs, send_ref, spot_ref[0]
-    )
-
-
-VMEM_LIMIT = 32 * 1024 * 1024
+        [values[:kept] for values in stepped],
+        [values[1] for values in stepped],
+        static_ref,
+        table_ref,
+        send_ref,
+        spot_ref[0],
+        deep_rows,
+    )
 
 
 def whole(array):
@@ -429,21 +446,22 @@
 
 
 SCALAR = pl.BlockSpec(memory_space=pltpu.SMEM)
+NEAR = pl.BlockSpec(memory_space=pltpu.VMEM)
 UNREAD = pl.BlockSpec(memory_space=pl.ANY)
 
 
-def call(kernel, operands, specs, out_shape, out_specs, name, aliases=None, scratch=(), flops=0, moved=0):
+def call(kernel, operands, specs, out_shape, out_specs, name, grid=(), aliases=None, scratch=(), us=1):
     return pl.pallas_call(
         kernel,
-        grid=(1,),
+        grid=grid,
         in_specs=specs,
         out_shape=out_shape,
         out_specs=out_specs,
         scratch_shapes=list(scratch),
         input_output_aliases=aliases or {},
         name=name,
-        cost_estimate=pl.CostEstimate(flops=flops, bytes_accessed=moved, transcendentals=0),
-        compiler_params=pltpu.CompilerParams(vmem_limit_bytes=VMEM_LIMIT),
+        cost_estimate=pl.CostEstimate(flops=0, bytes_accessed=us * 3_000_000, transcendentals=0),
+        compiler_params=pltpu.CompilerParams(vmem_limit_bytes=16 * 1024 * 1024),
     )(*operands)
 
 
@@ -464,55 +482,62 @@
     return lines[0:1], lines[1:2], columns[:, 0:1], columns[:, 1:2]
 
 
-def pack_kernel(partner_ref, pack_ref, *, rows, groups, main_rows, tracers):
+def tables_kernel(partner_ref, table_ref, place_ref, *, rows, groups, n_lat, n_lon):
     count = rows * groups
-    line_target, _, column_target, _ = tile_order(partner_ref[...], rows, groups)
+    devices = n_lat * n_lon
+    line_target, line_slot, target, slot = tile_order(partner_ref[...], rows, groups)
     a = lax.broadcasted_iota(jnp.int32, (count, count), 0)
     b = lax.broadcasted_iota(jnp.int32, (count, count), 1)
-    place_a = (a % rows) * groups + a // rows
-    place_b = (b % rows) * groups + b // rows
-    ahead = (column_target == line_target) & (place_a < place_b)
+    same = target == line_target
+    came = jnp.sum((same & (line_slot < slot)).astype(F32), axis=1, keepdims=True).astype(jnp.int32)
+    ahead = same & ((a % rows) * groups + a // rows < (b % rows) * groups + b // rows)
     sent = jnp.sum(ahead.astype(F32), axis=0, keepdims=True).astype(jnp.int32)
-    height = pack_ref.shape[0] // groups
-    per_device = main_rows * tracers
-    slot = lax.broadcasted_iota(jnp.int32, (pack_ref.shape[0], count), 0)
-    for tracer in range(tracers):
-        index = (sent % groups) * height + line_target * per_device + tracer * main_rows + sent // groups
-        pack_ref[:, tracer * count : (tracer + 1) * count] = (slot == index).astype(F32).astype(BF16)
-
-
-def pick_kernel(
-    after_ref, partner_ref, pick_ref, place_ref, *, rows, groups, main_rows, tracers, n_lat, n_lon, deep
-):
-    count = rows * groups
-    per_device = main_rows * tracers
-    devices = n_lat * n_lon
-    line_target, line_slot, target, slot = tile_order(partner_ref[...], rows, groups)
-    ahead = (target == line_target) & (line_slot < slot)
-    came = jnp.sum(ahead.astype(F32), axis=1, keepdims=True).astype(jnp.int32)
+
     row, group = slot // groups, slot % groups
     lat, lon = target // n_lon, target % n_lon
     north_ok = (row == rows - 1) & (lat < n_lat - 1)
     east_ok = group == groups - 1
     east_device = lat * n_lon + (lon + 1) % n_lon
-    index = lax.broadcasted_iota(jnp.int32, (count, pick_ref.shape[1]), 1)
-    for tracer in range(tracers):
-        picks = (
-            target * deep + tracer * main_rows + came // groups,
-            jnp.where(north_ok, (target + n_lon) * deep + per_device + tracer, -1),
-            jnp.where(
-                east_ok,
-                east_device * deep + per_device + tracers + tracer + (row // groups) * (devices * deep),
-                -1,
-            ),
-        )
-        for kind, pick in enumerate(picks):
-            start = (kind * tracers + tracer) * count
-            pick_ref[start : start + count, :] = (pick == index).astype(F32).astype(BF16)
+    east_row = (east_device + (row // groups) * devices) * SLAB + SLAB - 1
+    picks = (
+        target * SLAB + came // groups,
+        jnp.where(north_ok, (target + n_lon) * SLAB + SLAB - 2, -1),
+        jnp.where(east_ok, east_row, -1),
+    )
+    index = lax.broadcasted_iota(jnp.int32, (count, table_ref.shape[1]), 1)
+    for kind, pick in enumerate(picks):
+        table_ref[kind * count : (kind + 1) * count, :] = (pick == index).astype(F32).astype(BF16)
+    height = devices * SLAB
+    packing = (sent % groups) * height + line_target * SLAB + sent // groups
+    slots = lax.broadcasted_iota(jnp.int32, (groups * height, count), 0)
+    table_ref[3 * count :, 0:count] = (slots == packing).astype(F32).astype(BF16)
+    if table_ref.shape[1] > count:
+        table_ref[3 * count :, count:] = jnp.zeros((groups * height, table_ref.shape[1] - count), BF16)
+
     lane = lax.broadcasted_iota(jnp.int32, (count, groups * TILE), 1)
-    place_ref[0] = (lane // TILE == came % groups).astype(F32)
-    place_ref[1] = (lane // TILE == group).astype(F32)
-    place_ref[2] = (lane == (row % groups) * TILE + TILE - 1).astype(F32)
+    places = (
+        lane // TILE == came % groups,
+        lane // TILE == group,
+        lane == (row % groups) * TILE + TILE - 1,
+    )
+    for kind, place in enumerate(places):
+        place = place.astype(F32)
+        for c in range(groups):
+            place_ref[kind * groups + c] = place[c * rows : (c + 1) * rows]
+
+
+def static_kernel(courant_ref, kappa_ref, coupling_ref, mask_ref, west_ref, south_ref, place_ref, static_ref):
+    static_ref[ZONAL] = courant_ref[0]
+    static_ref[MERIDIONAL] = courant_ref[1]
+    for k in range(STEPS):
+        static_ref[KAPPA + k] = kappa_ref[k]
+    static_ref[COUPLING] = coupling_ref[...]
+    for k in range(2):
+        static_ref[WEST + k] = west_ref[k]
+        static_ref[SOUTH + k] = south_ref[k]
+    static_ref[WET] = mask_ref[...].astype(F32)
+    for k in range(place_ref.shape[0]):
+        static_ref[PLACE + k] = place_ref[k]
 
 
 def local(adjoint, courant, diffusivity, coupling, partner, mask):
@@ -523,9 +548,6 @@
     count = rows * groups
     n_lat, n_lon = lax.axis_size("lat"), lax.axis_size("lon")
     devices = n_lat * n_lon
-    capacity = max(2, 2 * count // devices)
-    main_rows = -(-capacity // groups)
-    deep = max(8, main_rows * tracers + 2 * tracers)
     lat, lon = lax.axis_index("lat"), lax.axis_index("lon")
     spot = jnp.stack(
         [
@@ -540,41 +562,39 @@
     from_west = lax.ppermute(share, "lon", [(i, (i + 1) % n_lon) for i in range(n_lon)])
     from_south = lax.ppermute(share, "lat", [(i, (i + 1) % n_lat) for i in range(n_lat)])
 
-    sizes = dict(rows=rows, groups=groups, main_rows=main_rows, tracers=tracers)
-    per_device = main_rows * tracers
-    pack_shape = jax.ShapeDtypeStruct((groups * devices * per_device, tracers * count), BF16)
-    pack = call(
-        functools.partial(pack_kernel, **sizes),
+    def exchanged(send):
+        return lax.all_to_all(send, ("mp", "lat", "lon"), split_axis=0, concat_axis=0, tiled=True)
+
+    deep_rows = 3 * count
+    table_shape = jax.ShapeDtypeStruct(
+        (deep_rows + groups * devices * SLAB, max(count, 2 * devices * SLAB)), BF16
+    )
+    place_shape = shaped(3 * groups, rows, cols)
+    table, place = call(
+        functools.partial(tables_kernel, rows=rows, groups=groups, n_lat=n_lat, n_lon=n_lon),
         (partner,),
-        [whole(partner)],
-        pack_shape,
-        whole(pack_shape),
-        "pack_table",
-    )
-    upper = kappa[:STEPS]
-    sending = (courant, upper, coupling, from_west, from_south, pack)
-    sending_specs = [whole(a) for a in sending]
-    send_shape = shaped(2 * devices, deep, cols)
+        [NEAR],
+        (table_shape, place_shape),
+        (NEAR, NEAR),
+        "tables",
+    )
+    gathered = (courant, kappa, coupling, mask, from_west, from_south, place)
+    static_shape = shaped(PLACE + 3 * groups, rows, cols)
+    static_specs = [whole(a) for a in gathered]
+    static_specs[1] = pl.BlockSpec((STEPS, rows, cols), lambda i: (0, 0, 0))
+    static = call(static_kernel, gathered, static_specs, static_shape, whole(static_shape), "static", grid=(1,))
+    send_shape = shaped(2 * devices, 2 * SLAB, cols)
+    late = fields[:, :3]
     send = call(
-        first_send_kernel,
-        (spot, fields, *sending),
-        [SCALAR, top(fields, 3), *sending_specs],
+        functools.partial(first_send_kernel, deep_rows=deep_rows),
+        (spot, late, static, table),
+        [SCALAR, NEAR, NEAR, NEAR],
         send_shape,
-        whole(send_shape),
+        NEAR,
         "first_send",
     )
-    recv = lax.all_to_all(send, ("mp", "lat", "lon"), split_axis=0, concat_axis=0, tiled=True)
-
-    pick_shape = jax.ShapeDtypeStruct((3 * tracers * count, 2 * devices * deep), BF16)
-    place_shape = shaped(3, count, cols)
-    pick, place = call(
-        functools.partial(pick_kernel, n_lat=n_lat, n_lon=n_lon, deep=deep, **sizes),
-        (send, partner),
-        [UNREAD, whole(partner)],
-        (pick_shape, place_shape),
-        (whole(pick_shape), whole(place_shape)),
-        "pick_table",
-    )
+    recv = exchanged(send)
+
     tiles = -(-levels // PACKED)
     width = ((tracers + 1) * tiles + 2) * cols
     halo_shapes = (
@@ -589,7 +609,8 @@
         halo_shapes,
         tuple(whole(a) for a in halo_shapes),
         "halo",
-        moved=4 * fields.size,
+        grid=(1,),
+        us=2,
     )
     north = lax.ppermute(north, "lat", [((i + 1) % n_lat, i) for i in range(n_lat)])
     east = lax.ppermute(east, "lon", [((i + 1) % n_lon, i) for i in range(n_lon)])
@@ -604,36 +625,36 @@
     )
     halo = (courant, north, east, corner)
     halo_specs = [whole(a) for a in halo]
-    field_bytes = 4 * fields.size
     tall = rows + 2 * STEPS
 
-    late, early, out = fields, (), None
+    early, out = (), None
     for step in range(STEPS):
         if step > 0:
-            recv = lax.all_to_all(send, ("mp", "lat", "lon"), split_axis=0, concat_axis=0, tiled=True)
+            recv = exchanged(send)
+        after = ()
+        if step == 0:
+            after = (east, corner)
         if step == 1:
             shown = 2 * STEPS
-            early_shapes = (
-                shaped(STEPS - 1, tracers, 2, rows, cols),
-                shaped(-(-(STEPS - 1) * tracers * 2 // 8) * 8, cols),
-                shaped(STEPS - 1, tracers, 2, rows, cols),
-            )
-            early = call(
-                functools.partial(early_kernel, all_levels=levels),
-                (send, spot, fields, kappa, *halo),
-                [
-                    UNREAD,
-                    SCALAR,
-                    top(fields, shown),
-                    pl.BlockSpec((shown, rows, cols), lambda i: (0, 0, 0)),
-                    *halo_specs,
-                ],
-                early_shapes,
-                tuple(whole(a) for a in early_shapes),
-                "early_levels",
-                scratch=[pltpu.VMEM((shown, tall, cols), F32)],
-                flops=field_bytes,
-                moved=field_bytes,
+            early_shape = shaped((STEPS - 1) * tracers * 4 + 1, rows, cols)
+            early = (
+                call(
+                    functools.partial(early_kernel, all_levels=levels),
+                    (send, spot, fields, kappa, *halo),
+                    [
+                        UNREAD,
+                        SCALAR,
+                        top(fields, shown),
+                        pl.BlockSpec((shown, rows, cols), lambda i: (0, 0, 0)),
+                        *halo_specs,
+                    ],
+                    early_shape,
+                    whole(early_shape),
+                    "early_levels",
+                    grid=(1,),
+                    scratch=[pltpu.VMEM((shown, tall, cols), F32)],
+                    us=2,
+                ),
             )
         if step > 1:
             for tracer in range(step - 2, tracers if step == STEPS - 1 else step - 1):
@@ -646,39 +667,35 @@
                     shaped(*fields.shape),
                     block,
                     "deep_levels",
+                    grid=(1,),
                     aliases={3: 0} if before else None,
                     scratch=[pltpu.VMEM((levels, tall, cols), F32)],
-                    flops=10 * field_bytes,
-                    moved=field_bytes,
+                    us=4,
                 )
-        last = step == STEPS - 1
-        kept = step + 1
-        arriving = (spot, late, recv, pick, place, mask, *early)
-        late_spec = top(late, 3) if step == 0 else whole(late)
-        specs = [SCALAR, late_spec, *(whole(a) for a in arriving[2:])]
-        kernel = functools.partial(exchange_kernel, step=step, last=last)
-        if last:
-            operands = (*arriving, *sending[:3], out)
-            fields = call(
-                lambda *refs: kernel(*refs[:-2], refs[-1]),
+            after = (out,)
+        operands = (spot, late, recv, static, table, *early, *after)
+        specs = [SCALAR, *(NEAR for _ in operands[1 : len(operands) - len(after)]), *(UNREAD for _ in after)]
+        kernel = functools.partial(exchange_kernel, step=step, deep_rows=deep_rows, unread=len(after))
+        if step == STEPS - 1:
+            specs[1 : len(operands) - len(after)] = [whole(a) for a in operands[1 : len(operands) - len(after)]]
+            return call(
+                kernel,
                 operands,
-                [*specs, *sending_specs[:3], UNREAD],
+                specs,
                 shaped(*fields.shape),
                 top(fields, STEPS),
                 "last_exchange",
+                grid=(1,),
                 aliases={len(operands) - 1: 0},
-            )
-        else:
-            late_shape = shaped(tracers, kept, rows, cols)
-            late, send = call(
-                kernel,
-                (*arriving, *sending),
-                [*specs, *sending_specs],
-                (late_shape, send_shape),
-                (whole(late_shape), whole(send_shape)),
-                "exchange",
-            )
-    return fields[None]
+            )[None]
+        late, send = call(
+            kernel,
+            operands,
+            specs,
+            (shaped(tracers, step + 1, rows, cols), send_shape),
+            (NEAR, NEAR),
+            "exchange",
+        )
 
 
 def solution(mesh):

time: 76.1 us -> 78.9 us (1.037)
  waiting for transfers between devices: 8.37 us -> 27.9 us
  blocking collectives: 12.5 us -> 0 us
  local copies, waits for them, and re-layouts: 10.3 us -> 5.91 us
  starting transfers between devices: 19.9 us -> 20.9 us
    all_to_all x1 -> x0, blocking collectives: 12.5 us -> none  [local(): lax.all_to_all(send, ('mp', 'lat', 'lon'), split_axis=0, concat_axis=0, t...]
    all_to_all x3 -> x4, waiting for transfers between devices: 4.3 us -> 15.8 us  [exchanged(): lax.all_to_all(send, ('mp', 'lat', 'lon'), split_axis=0, concat_axis=0, t...]
    ppermute x1, waiting for transfers between devices: 3.09 us -> 9.33 us  [local(): lax.ppermute(corner, ('lat', 'lon'), [((i + 1) % n_lat * n_lon + (j + 1)...]
    unnamed x54 -> x18, local copies, waits for them, and re-layouts: 9.49 us -> 5.11 us
    all_to_all x3 -> x4, starting transfers between devices: 10.3 us -> 12.7 us  [exchanged(): lax.all_to_all(send, ('mp', 'lat', 'lon'), split_axis=0, concat_axis=0, t...]
    ppermute x1, waiting for transfers between devices: 0.97 us -> 2.73 us  [local(): lax.ppermute(share, 'lon', [(i, (i + 1) % n_lon) for i in range(n_lon)])]
  transfers between devices with their start and end apart: 8 -> 9, of which waited for: 3 -> 5; matrix products, arithmetic and copies ran while one was open for 1% -> 1% of each run, Pallas kernels for 19% -> 17%
where the time goes in v4:
time: 78.9 us; the launch traced here: 78.2 us
  waiting for transfers between devices  27.9 us (35%)
  Pallas kernels  22.6 us (29%)
  starting transfers between devices  20.9 us (26%)
  local copies, waits for them, and re-layouts  5.91 us (7%)
  other arithmetic  0.81 us (1%)
    pallas_call x11, Pallas kernels, call(): pl.pallas_call(kernel, grid=grid, in_specs=specs, out_shape=out_shape, ou...  22.6 us
    all_to_all x4, waiting for transfers between devices, exchanged(): lax.all_to_all(send, ('mp', 'lat', 'lon'), split_axis=0, concat_axis=0, t...  15.8 us
    all_to_all x4, starting transfers between devices, exchanged(): lax.all_to_all(send, ('mp', 'lat', 'lon'), split_axis=0, concat_axis=0, t...  12.7 us
    ppermute x1, waiting for transfers between devices, local(): lax.ppermute(corner, ('lat', 'lon'), [((i + 1) % n_lat * n_lon + (j + 1)...  9.33 us
    unnamed x18, local copies, waits for them, and re-layouts  5.11 us
    ppermute x1, starting transfers between devices, local(): lax.ppermute(share, 'lat', [(i, (i + 1) % n_lat) for i in range(n_lat)])  3.03 us
    ppermute x1, starting transfers between devices, local(): lax.ppermute(east, 'lon', [((i + 1) % n_lon, i) for i in range(n_lon)])  2.82 us
    ppermute x1, waiting for transfers between devices, local(): lax.ppermute(share, 'lon', [(i, (i + 1) % n_lon) for i in range(n_lon)])  2.73 us
  transfers between devices with their start and end apart: 9, of which 5 were waited for; matrix products, arithmetic and copies ran while one was open for 1% of the time, Pallas kernels for 17%

profile of v4, /device:TPU:0, one launch (start us, length us, event | category | flops | bytes accessed | tf_op | source)
XLA Modules:
  0.0 78.2 jit_solution(8024503993128796648)
XLA Ops:
  0.7 3.0 %collective-permute-start.1 = (f32[2,16,128]{2,1,0:T(8,128)S(1)}, f32[2,16,128]{2,1,0:T(8,128)S(1)}, u32[]{:S(2)}, u32[]{:S(2)}) collective-permute-start(f32[2,16,128]{2,1,0:T(8,128)S(1)} %pad_maximum_fusion), channel_id=1, source_target_pairs={{0,8},{8,0},{1,9},{9,1},{2,10},{10,2},{3,11},{11,3},{4,12},{12,4},... | collective-permute-start | bytes 49160 | tf_op jit(solution)/shard_map/ppermute | solution.py:563
  3.9 0.8 %slice.10.fields_ref.late_ref = f32[2,3,16,128]{3,2,1,0:T(8,128)S(1)} slice(f32[2,72,16,128]{3,2,1,0:T(8,128)} %bitcast.15), slice={[0:2], [0:3], [0:16], [0:128]} | slice | bytes 98304 | tf_op jit(solution)/shard_map/slice | solution.py:587
  6.0 2.7 %collective-permute-done.west_ref = f32[2,16,128]{2,1,0:T(8,128)S(1)} collective-permute-done((f32[2,16,128]{2,1,0:T(8,128)S(1)}, f32[2,16,128]{2,1,0:T(8,128)S(1)}, u32[]{:S(2)}, u32[]{:S(2)}) %collective-permute-start) | collective-permute-done | bytes 16416 | tf_op jit(solution)/shard_map/ppermute | solution.py:562
  8.7 1.1 %copy-done.2 = f32[1,71,16,128]{3,2,1,0:T(8,128)S(1)} copy-done((f32[1,71,16,128]{3,2,1,0:T(8,128)S(1)}, f32[1,71,16,128]{3,2,1,0:T(8,128)}, u32[]{:S(2)}) %copy-start.2) | copy-done | bytes 581656
  11.9 1.9 %first_send.1.after_ref = f32[32,8,128]{2,1,0:T(8,128)} custom-call(s32[4]{0:T(128)S(1)} %pad_add_fusion.spot_ref.refs_1_, f32[2,3,16,128]{3,2,1,0:T(8,128)S(1)} %slice.10.fields_ref.late_ref, f32[36,16,128]{2,1,0:T(8,128)S(1)} %static.1.static_ref, bf16[896,128]{1,0:T(8,128)(2,1)S(1)} %get-tuple-element.17.table_ref), custom_call_target="tpu_custom_call" | custom-call | bytes 3000000 | tf_op jit(solution)/shard_map/first_send/pallas_call | solution.py:454
  13.8 3.1 %all-to-all-start = ((f32[32,8,128]{2,1,0:T(8,128)}), f32[32,8,128]{2,1,0:T(8,128)S(1)}, u32[]{:S(2)}, u32[]{:S(2)}) async-start(f32[32,8,128]{2,1,0:T(8,128)} %first_send.1.after_ref), calls=%async_computation | async-start | bytes 262144 | tf_op jit(solution)/shard_map/all_to_all | solution.py:566
  16.9 1.4 %halo.1 = (f32[109,8,128]{2,1,0:T(8,128)}, f32[16,1408]{1,0:T(8,128)S(1)}, f32[8,1408]{1,0:T(8,128)S(1)}) custom-call(f32[32,8,128]{2,1,0:T(8,128)} %first_send.1.after_ref, f32[2,72,16,128]{3,2,1,0:T(8,128)S(1)} %bitcast.16, f32[71,16,128]{2,1,0:T(8,128)S(1)} %bitcast.21, f32[2,16,128]{2,1,0:T(8,128)S(1)} %bitcast.26), custom_call_target="tpu_custom_call" | custom-call | bytes 6000000 | tf_op jit(solution)/shard_map/halo/pallas_call | solution.py:454
  18.3 1.8 %collective-permute-start.4 = (f32[109,8,128]{2,1,0:T(8,128)}, f32[109,8,128]{2,1,0:T(8,128)S(1)}, u32[]{:S(2)}, u32[]{:S(2)}) collective-permute-start(f32[109,8,128]{2,1,0:T(8,128)} %get-tuple-element.22), channel_id=1, source_target_pairs={{8,0},{0,8},{9,1},{1,9},{10,2},{2,10},{11,3},{3,11},{12,4},{4,12},... | collective-permute-start | bytes 1339400 | tf_op jit(solution)/shard_map/ppermute | solution.py:615
  20.1 2.8 %collective-permute-start.2 = (f32[16,1408]{1,0:T(8,128)S(1)}, f32[16,1408]{1,0:T(8,128)S(1)}, u32[]{:S(2)}, u32[]{:S(2)}) collective-permute-start(f32[16,1408]{1,0:T(8,128)S(1)} %get-tuple-element.18), channel_id=1, source_target_pairs={{1,0},{2,1},{3,2},{4,3},{5,4},{6,5},{7,6},{0,7},{9,8},{10,9},{11,1... | collective-permute-start | bytes 270344 | tf_op jit(solution)/shard_map/ppermute | solution.py:616
  23.5 9.3 %collective-permute-done.3.refs_1_.corner_ref.refs_7_.refs_8_ = f32[8,1408]{1,0:T(8,128)S(1)} collective-permute-done((f32[8,1408]{1,0:T(8,128)S(1)}, f32[8,1408]{1,0:T(8,128)S(1)}, u32[]{:S(2)}, u32[]{:S(2)}) %collective-permute-start.3) | collective-permute-done | bytes 45088 | tf_op jit(solution)/shard_map/ppermute | solution.py:617
  32.9 2.7 %exchange.3 = (f32[2,1,16,128]{3,2,1,0:T(8,128)S(1)}, f32[32,8,128]{2,1,0:T(8,128)}) custom-call(s32[4]{0:T(128)S(1)} %pad_add_fusion.spot_ref.refs_1_, f32[2,3,16,128]{3,2,1,0:T(8,128)S(1)} %slice.10.fields_ref.late_ref, f32[32,8,128]{2,1,0:T(8,128)S(1)} %all-to-all-done.recv_ref, f32[36,16,128]{2,1,0:T(8,128)S(1)} %static.1.static_ref, ...), custom_call_target="tpu_custom_call" | custom-call | bytes 3000000 | tf_op jit(solution)/shard_map/exchange/pallas_call | solution.py:454
  35.6 4.5 %all-to-all-start.1 = ((f32[32,8,128]{2,1,0:T(8,128)}), f32[32,8,128]{2,1,0:T(8,128)S(1)}, u32[]{:S(2)}, u32[]{:S(2)}) async-start(f32[32,8,128]{2,1,0:T(8,128)} %get-tuple-element.21.after_ref), calls=%async_computation.1 | async-start | bytes 262144 | tf_op jit(solution)/shard_map/all_to_all | solution.py:566
  40.1 1.3 %early_levels.1.refs_0_ = f32[25,16,128]{2,1,0:T(8,128)S(1)} custom-call(f32[32,8,128]{2,1,0:T(8,128)} %get-tuple-element.21.after_ref, s32[4]{0:T(128)S(1)} %pad_add_fusion.spot_ref.refs_1_, f32[2,72,16,128]{3,2,1,0:T(8,128)S(1)} %bitcast.17, f32[71,16,128]{2,1,0:T(8,128)S(1)} %bitcast.22, f32[2,16,128]{2,1,0:T(8,128)S(1)} %bitcast.27, ...), custom_call_target="tpu_custom_call" | custom-call | bytes 6000000 | tf_op jit(solution)/shard_map/early_levels/pallas_call | solution.py:454
  41.4 6.9 %all-to-all-done.1.recv_ref = f32[32,8,128]{2,1,0:T(8,128)S(1)} async-done(((f32[32,8,128]{2,1,0:T(8,128)}), f32[32,8,128]{2,1,0:T(8,128)S(1)}, u32[]{:S(2)}, u32[]{:S(2)}) %all-to-all-start.1) | async-done | bytes 131104 | tf_op jit(solution)/shard_map/all_to_all | solution.py:566
  48.2 2.7 %exchange.4 = (f32[2,2,16,128]{3,2,1,0:T(8,128)S(1)}, f32[32,8,128]{2,1,0:T(8,128)}) custom-call(s32[4]{0:T(128)S(1)} %pad_add_fusion.spot_ref.refs_1_, f32[2,1,16,128]{3,2,1,0:T(8,128)S(1)} %get-tuple-element.20.late_ref, f32[32,8,128]{2,1,0:T(8,128)S(1)} %all-to-all-done.1.recv_ref, f32[36,16,128]{2,1,0:T(8,128)S(1)} %static.1.static_ref, ...), custom_call_target="tpu_custom_call" | custom-call | bytes 3000000 | tf_op jit(solution)/shard_map/exchange/pallas_call | solution.py:454
  51.0 2.6 %all-to-all-start.2 = ((f32[32,8,128]{2,1,0:T(8,128)}), f32[32,8,128]{2,1,0:T(8,128)S(1)}, u32[]{:S(2)}, u32[]{:S(2)}) async-start(f32[32,8,128]{2,1,0:T(8,128)} %get-tuple-element.24.refs_0_), calls=%async_computation.2 | async-start | bytes 262144 | tf_op jit(solution)/shard_map/all_to_all | solution.py:566
  53.5 3.7 %deep_levels.2.refs_1_.refs_3_ = f32[2,72,16,128]{3,2,1,0:T(8,128)} custom-call(f32[32,8,128]{2,1,0:T(8,128)} %get-tuple-element.24.refs_0_, s32[4]{0:T(128)S(1)} %pad_add_fusion.spot_ref.refs_1_, f32[2,72,16,128]{3,2,1,0:T(8,128)S(1)} %bitcast.18, f32[71,16,128]{2,1,0:T(8,128)S(1)} %bitcast.23, f32[2,16,128]{2,1,0:T(8,128)S(1)} %bitcast.28, ...), custom_call_target="tpu_custom_call" | custom-call | bytes 12000000 | tf_op jit(solution)/shard_map/deep_levels/pallas_call | solution.py:454
  57.2 4.5 %all-to-all-done.2.recv_ref = f32[32,8,128]{2,1,0:T(8,128)S(1)} async-done(((f32[32,8,128]{2,1,0:T(8,128)}), f32[32,8,128]{2,1,0:T(8,128)S(1)}, u32[]{:S(2)}, u32[]{:S(2)}) %all-to-all-start.2) | async-done | bytes 131104 | tf_op jit(solution)/shard_map/all_to_all | solution.py:566
  61.7 1.3 %copy-done.1 = f32[2,72,16,128]{3,2,1,0:T(8,128)S(1)} copy-done((f32[2,72,16,128]{3,2,1,0:T(8,128)S(1)}, f32[2,72,16,128]{3,2,1,0:T(8,128)}, u32[]{:S(2)}) %copy-start.1) | copy-done | bytes 1179672
  63.0 2.7 %exchange.5 = (f32[2,3,16,128]{3,2,1,0:T(8,128)S(1)}, f32[32,8,128]{2,1,0:T(8,128)}) custom-call(s32[4]{0:T(128)S(1)} %pad_add_fusion.spot_ref.refs_1_, f32[2,2,16,128]{3,2,1,0:T(8,128)S(1)} %get-tuple-element.23.late_ref, f32[32,8,128]{2,1,0:T(8,128)S(1)} %all-to-all-done.2.recv_ref, f32[36,16,128]{2,1,0:T(8,128)S(1)} %static.1.static_ref, ...), custom_call_target="tpu_custom_call" | custom-call | bytes 3000000 | tf_op jit(solution)/shard_map/exchange/pallas_call | solution.py:454
  65.7 2.6 %all-to-all-start.3 = ((f32[32,8,128]{2,1,0:T(8,128)}), f32[32,8,128]{2,1,0:T(8,128)S(1)}, u32[]{:S(2)}, u32[]{:S(2)}) async-start(f32[32,8,128]{2,1,0:T(8,128)} %get-tuple-element.26.refs_0_), calls=%async_computation.3 | async-start | bytes 262144 | tf_op jit(solution)/shard_map/all_to_all | solution.py:566
  68.3 3.7 %deep_levels.3.refs_1_ = f32[2,72,16,128]{3,2,1,0:T(8,128)} custom-call(f32[32,8,128]{2,1,0:T(8,128)} %get-tuple-element.26.refs_0_, s32[4]{0:T(128)S(1)} %pad_add_fusion.spot_ref.refs_1_, f32[2,72,16,128]{3,2,1,0:T(8,128)S(1)} %bitcast.19, f32[2,72,16,128]{3,2,1,0:T(8,128)} %deep_levels.2.refs_1_.refs_3_, ...), custom_call_target="tpu_custom_call", output_to_operand_aliasing={{}: (3, {})} | custom-call | bytes 12000000 | tf_op jit(solution)/shard_map/deep_levels/pallas_call | solution.py:454
  72.0 4.5 %all-to-all-done.3.recv_ref = f32[32,8,128]{2,1,0:T(8,128)S(1)} async-done(((f32[32,8,128]{2,1,0:T(8,128)}), f32[32,8,128]{2,1,0:T(8,128)S(1)}, u32[]{:S(2)}, u32[]{:S(2)}) %all-to-all-start.3) | async-done | bytes 131104 | tf_op jit(solution)/shard_map/all_to_all | solution.py:566
  76.4 1.8 %last_exchange.1 = f32[2,72,16,128]{3,2,1,0:T(8,128)} custom-call(s32[4]{0:T(128)S(1)} %pad_add_fusion.spot_ref.refs_1_, f32[2,3,16,128]{3,2,1,0:T(8,128)S(1)} %get-tuple-element.25.late_ref, f32[32,8,128]{2,1,0:T(8,128)S(1)} %all-to-all-done.3.recv_ref, f32[36,16,128]{2,1,0:T(8,128)S(1)} %static.1.static_ref, ...), custom_call_target="tpu_custom_call", output_to_operand_aliasing={{}: (6, {})} | custom-call | bytes 3000000 | tf_op jit(solution)/shard_map/last_exchange/pallas_call | solution.py:454
  (27 shorter events, 4.9 us)
Async XLA Ops:
  0.0 16.9 %copy-start.5 = (f32[1,2,16,128]{3,2,1,0:T(8,128)S(1)}, f32[1,2,16,128]{3,2,1,0:T(8,128)}, u32[]{:S(2)}) copy-start(f32[1,2,16,128]{3,2,1,0:T(8,128)} %param.7) | copy-start | bytes 49156
  0.7 16.2 %copy-start = (f32[1,2,72,16,128]{4,3,2,1,0:T(8,128)S(1)}, f32[1,2,72,16,128]{4,3,2,1,0:T(8,128)}, u32[]{:S(2)}) copy-start(f32[1,2,72,16,128]{4,3,2,1,0:T(8,128)} %param.6) | copy-start | bytes 3538948
  0.7 5.3 %collective-permute-start.1 = (f32[2,16,128]{2,1,0:T(8,128)S(1)}, f32[2,16,128]{2,1,0:T(8,128)S(1)}, u32[]{:S(2)}, u32[]{:S(2)}) collective-permute-start(f32[2,16,128]{2,1,0:T(8,128)S(1)} %pad_maximum_fusion), channel_id=1, source_target_pairs={{0,8},{8,0},{1,9},{9,1},{2,10},{10,2},{3,11},{11,3},{4,12},{12,4},... | collective-permute-start | bytes 49160 | tf_op jit(solution)/shard_map/ppermute | solution.py:563
  3.8 5.0 %collective-permute-start = (f32[2,16,128]{2,1,0:T(8,128)S(1)}, f32[2,16,128]{2,1,0:T(8,128)S(1)}, u32[]{:S(2)}, u32[]{:S(2)}) collective-permute-start(f32[2,16,128]{2,1,0:T(8,128)S(1)} %pad_maximum_fusion), channel_id=1, source_target_pairs={{0,1},{1,2},{2,3},{3,4},{4,5},{5,6},{6,7},{7,0},{8,9},{9,10},{10,1... | collective-permute-start | bytes 49160 | tf_op jit(solution)/shard_map/ppermute | solution.py:562
  4.7 0.7 copy-start.8
  8.7 1.1 %copy-start.2 = (f32[1,71,16,128]{3,2,1,0:T(8,128)S(1)}, f32[1,71,16,128]{3,2,1,0:T(8,128)}, u32[]{:S(2)}) copy-start(f32[1,71,16,128]{3,2,1,0:T(8,128)} %param.8) | copy-start | bytes 1744900
  9.8 0.7 copy-start.4
  10.5 0.7 copy-start.6
  11.2 0.7 copy-start.7
  11.9 5.0 %copy-start.3 = (f32[1,71,16,128]{3,2,1,0:T(8,128)S(1)}, f32[1,71,16,128]{3,2,1,0:T(8,128)}, u32[]{:S(2)}) copy-start(f32[1,71,16,128]{3,2,1,0:T(8,128)} %param.8) | copy-start | bytes 1744900
  13.8 19.1 %all-to-all-start = ((f32[32,8,128]{2,1,0:T(8,128)}), f32[32,8,128]{2,1,0:T(8,128)S(1)}, u32[]{:S(2)}, u32[]{:S(2)}) async-start(f32[32,8,128]{2,1,0:T(8,128)} %first_send.1.after_ref), calls=%async_computation | async-start | bytes 262144 | tf_op jit(solution)/shard_map/all_to_all | solution.py:566
  18.3 21.8 %collective-permute-start.4 = (f32[109,8,128]{2,1,0:T(8,128)}, f32[109,8,128]{2,1,0:T(8,128)S(1)}, u32[]{:S(2)}, u32[]{:S(2)}) collective-permute-start(f32[109,8,128]{2,1,0:T(8,128)} %get-tuple-element.22), channel_id=1, source_target_pairs={{8,0},{0,8},{9,1},{1,9},{10,2},{2,10},{11,3},{3,11},{12,4},{4,12},... | collective-permute-start | bytes 1339400 | tf_op jit(solution)/shard_map/ppermute | solution.py:615
  20.1 12.8 %collective-permute-start.2 = (f32[16,1408]{1,0:T(8,128)S(1)}, f32[16,1408]{1,0:T(8,128)S(1)}, u32[]{:S(2)}, u32[]{:S(2)}) collective-permute-start(f32[16,1408]{1,0:T(8,128)S(1)} %get-tuple-element.18), channel_id=1, source_target_pairs={{1,0},{2,1},{3,2},{4,3},{5,4},{6,5},{7,6},{0,7},{9,8},{10,9},{11,1... | collective-permute-start | bytes 270344 | tf_op jit(solution)/shard_map/ppermute | solution.py:616
  22.9 9.9 %collective-permute-start.3 = (f32[8,1408]{1,0:T(8,128)S(1)}, f32[8,1408]{1,0:T(8,128)S(1)}, u32[]{:S(2)}, u32[]{:S(2)}) collective-permute-start(f32[8,1408]{1,0:T(8,128)S(1)} %get-tuple-element.19), channel_id=1, source_target_pairs={{9,0},{10,1},{11,2},{12,3},{13,4},{14,5},{15,6},{8,7},{1,8},{2,9},... | collective-permute-start | bytes 135176 | tf_op jit(solution)/shard_map/ppermute | solution.py:617
  35.6 12.7 %all-to-all-start.1 = ((f32[32,8,128]{2,1,0:T(8,128)}), f32[32,8,128]{2,1,0:T(8,128)S(1)}, u32[]{:S(2)}, u32[]{:S(2)}) async-start(f32[32,8,128]{2,1,0:T(8,128)} %get-tuple-element.21.after_ref), calls=%async_computation.1 | async-start | bytes 262144 | tf_op jit(solution)/shard_map/all_to_all | solution.py:566
  51.0 10.7 %all-to-all-start.2 = ((f32[32,8,128]{2,1,0:T(8,128)}), f32[32,8,128]{2,1,0:T(8,128)S(1)}, u32[]{:S(2)}, u32[]{:S(2)}) async-start(f32[32,8,128]{2,1,0:T(8,128)} %get-tuple-element.24.refs_0_), calls=%async_computation.2 | async-start | bytes 262144 | tf_op jit(solution)/shard_map/all_to_all | solution.py:566
  61.7 1.3 %copy-start.1 = (f32[2,72,16,128]{3,2,1,0:T(8,128)S(1)}, f32[2,72,16,128]{3,2,1,0:T(8,128)}, u32[]{:S(2)}) copy-start(f32[2,72,16,128]{3,2,1,0:T(8,128)} %deep_levels.2.refs_1_.refs_3_) | copy-start | bytes 3538948
  65.7 10.7 %all-to-all-start.3 = ((f32[32,8,128]{2,1,0:T(8,128)}), f32[32,8,128]{2,1,0:T(8,128)S(1)}, u32[]{:S(2)}, u32[]{:S(2)}) async-start(f32[32,8,128]{2,1,0:T(8,128)} %get-tuple-element.26.refs_0_), calls=%async_computation.3 | async-start | bytes 262144 | tf_op jit(solution)/shard_map/all_to_all | solution.py:566

commit v5 on v4

--- a/solution.py
+++ b/solution.py
@@ -633,7 +633,7 @@
             recv = exchanged(send)
         after = ()
         if step == 0:
-            after = (east, corner)
+            after = (east,)
         if step == 1:
             shown = 2 * STEPS
             early_shape = shaped((STEPS - 1) * tracers * 4 + 1, rows, cols)

time: 78.9 us -> 73.9 us (0.937)
  waiting for transfers between devices: 27.9 us -> 16.4 us
  starting transfers between devices: 20.9 us -> 27.4 us
    ppermute x1, waiting for transfers between devices: 9.33 us -> 1.71 us  [local(): lax.ppermute(corner, ('lat', 'lon'), [((i + 1) % n_lat * n_lon + (j + 1)...]
    all_to_all x4, waiting for transfers between devices: 15.8 us -> 9.8 us  [exchanged(): lax.all_to_all(send, ('mp', 'lat', 'lon'), split_axis=0, concat_axis=0, t...]
    ppermute x1, starting transfers between devices: 0.61 us -> 4.36 us  [local(): lax.ppermute(corner, ('lat', 'lon'), [((i + 1) % n_lat * n_lon + (j + 1)...]
    all_to_all x4, starting transfers between devices: 12.7 us -> 15.5 us  [exchanged(): lax.all_to_all(send, ('mp', 'lat', 'lon'), split_axis=0, concat_axis=0, t...]
    ppermute x1, waiting for transfers between devices: 0.01 us -> 2.14 us  [local(): lax.ppermute(east, 'lon', [((i + 1) % n_lon, i) for i in range(n_lon)])]
  transfers between devices with their start and end apart: 9 -> 9, of which waited for: 5 -> 7; matrix products, arithmetic and copies ran while one was open for 1% -> 1% of each run, Pallas kernels for 17% -> 18%
where the time goes in v5:
time: 73.9 us; the launch traced here: 73.2 us
  starting transfers between devices  27.4 us (37%)
  Pallas kernels  22.6 us (31%)
  waiting for transfers between devices  16.4 us (22%)
  local copies, waits for them, and re-layouts  5.91 us (8%)
  other arithmetic  0.81 us (1%)
    pallas_call x11, Pallas kernels, call(): pl.pallas_call(kernel, grid=grid, in_specs=specs, out_shape=out_shape, ou...  22.6 us
    all_to_all x4, starting transfers between devices, exchanged(): lax.all_to_all(send, ('mp', 'lat', 'lon'), split_axis=0, concat_axis=0, t...  15.5 us
    all_to_all x4, waiting for transfers between devices, exchanged(): lax.all_to_all(send, ('mp', 'lat', 'lon'), split_axis=0, concat_axis=0, t...  9.8 us
    unnamed x18, local copies, waits for them, and re-layouts  5.11 us
    ppermute x1, starting transfers between devices, local(): lax.ppermute(corner, ('lat', 'lon'), [((i + 1) % n_lat * n_lon + (j + 1)...  4.36 us
    ppermute x1, starting transfers between devices, local(): lax.ppermute(share, 'lat', [(i, (i + 1) % n_lat) for i in range(n_lat)])  3.03 us
    ppermute x1, starting transfers between devices, local(): lax.ppermute(east, 'lon', [((i + 1) % n_lon, i) for i in range(n_lon)])  2.82 us
    ppermute x1, waiting for transfers between devices, local(): lax.ppermute(share, 'lon', [(i, (i + 1) % n_lon) for i in range(n_lon)])  2.73 us
  transfers between devices with their start and end apart: 9, of which 7 were waited for; matrix products, arithmetic and copies ran while one was open for 1% of the time, Pallas kernels for 18%

profile of v5, /device:TPU:0, one launch (start us, length us, event | category | flops | bytes accessed | tf_op | source)
XLA Modules:
  0.0 73.2 jit_solution(4539633445943066479)
XLA Ops:
  0.7 3.0 %collective-permute-start.1 = (f32[2,16,128]{2,1,0:T(8,128)S(1)}, f32[2,16,128]{2,1,0:T(8,128)S(1)}, u32[]{:S(2)}, u32[]{:S(2)}) collective-permute-start(f32[2,16,128]{2,1,0:T(8,128)S(1)} %pad_maximum_fusion), channel_id=1, source_target_pairs={{0,8},{8,0},{1,9},{9,1},{2,10},{10,2},{3,11},{11,3},{4,12},{12,4},... | collective-permute-start | bytes 49160 | tf_op jit(solution)/shard_map/ppermute | solution.py:563
  6.0 2.7 %collective-permute-done.west_ref = f32[2,16,128]{2,1,0:T(8,128)S(1)} collective-permute-done((f32[2,16,128]{2,1,0:T(8,128)S(1)}, f32[2,16,128]{2,1,0:T(8,128)S(1)}, u32[]{:S(2)}, u32[]{:S(2)}) %collective-permute-start) | collective-permute-done | bytes 16416 | tf_op jit(solution)/shard_map/ppermute | solution.py:562
  8.7 1.1 %copy-done.2 = f32[1,71,16,128]{3,2,1,0:T(8,128)S(1)} copy-done((f32[1,71,16,128]{3,2,1,0:T(8,128)S(1)}, f32[1,71,16,128]{3,2,1,0:T(8,128)}, u32[]{:S(2)}) %copy-start.2) | copy-done | bytes 581656
  11.9 1.9 %first_send.1.after_ref = f32[32,8,128]{2,1,0:T(8,128)} custom-call(s32[4]{0:T(128)S(1)} %pad_add_fusion.spot_ref.refs_1_, f32[2,3,16,128]{3,2,1,0:T(8,128)S(1)} %slice.10.fields_ref.late_ref, f32[36,16,128]{2,1,0:T(8,128)S(1)} %static.1.static_ref, bf16[896,128]{1,0:T(8,128)(2,1)S(1)} %get-tuple-element.17.table_ref), custom_call_target="tpu_custom_call" | custom-call | bytes 3000000 | tf_op jit(solution)/shard_map/first_send/pallas_call | solution.py:454
  13.8 3.1 %all-to-all-start = ((f32[32,8,128]{2,1,0:T(8,128)}), f32[32,8,128]{2,1,0:T(8,128)S(1)}, u32[]{:S(2)}, u32[]{:S(2)}) async-start(f32[32,8,128]{2,1,0:T(8,128)} %first_send.1.after_ref), calls=%async_computation | async-start | bytes 262144 | tf_op jit(solution)/shard_map/all_to_all | solution.py:566
  16.9 1.4 %halo.1 = (f32[109,8,128]{2,1,0:T(8,128)}, f32[16,1408]{1,0:T(8,128)S(1)}, f32[8,1408]{1,0:T(8,128)S(1)}) custom-call(f32[32,8,128]{2,1,0:T(8,128)} %first_send.1.after_ref, f32[2,72,16,128]{3,2,1,0:T(8,128)S(1)} %bitcast.16, f32[71,16,128]{2,1,0:T(8,128)S(1)} %bitcast.21, f32[2,16,128]{2,1,0:T(8,128)S(1)} %bitcast.26), custom_call_target="tpu_custom_call" | custom-call | bytes 6000000 | tf_op jit(solution)/shard_map/halo/pallas_call | solution.py:454
  18.3 1.8 %collective-permute-start.3 = (f32[109,8,128]{2,1,0:T(8,128)}, f32[109,8,128]{2,1,0:T(8,128)S(1)}, u32[]{:S(2)}, u32[]{:S(2)}) collective-permute-start(f32[109,8,128]{2,1,0:T(8,128)} %get-tuple-element.21), channel_id=1, source_target_pairs={{8,0},{0,8},{9,1},{1,9},{10,2},{2,10},{11,3},{3,11},{12,4},{4,12},... | collective-permute-start | bytes 1339400 | tf_op jit(solution)/shard_map/ppermute | solution.py:615
  20.1 2.8 %collective-permute-start.2 = (f32[16,1408]{1,0:T(8,128)S(1)}, f32[16,1408]{1,0:T(8,128)S(1)}, u32[]{:S(2)}, u32[]{:S(2)}) collective-permute-start(f32[16,1408]{1,0:T(8,128)S(1)} %get-tuple-element.18), channel_id=1, source_target_pairs={{1,0},{2,1},{3,2},{4,3},{5,4},{6,5},{7,6},{0,7},{9,8},{10,9},{11,1... | collective-permute-start | bytes 270344 | tf_op jit(solution)/shard_map/ppermute | solution.py:616
  22.9 2.1 %collective-permute-done.2.refs_0_.columns_ref.refs_6_.refs_7_ = f32[16,1408]{1,0:T(8,128)S(1)} collective-permute-done((f32[16,1408]{1,0:T(8,128)S(1)}, f32[16,1408]{1,0:T(8,128)S(1)}, u32[]{:S(2)}, u32[]{:S(2)}) %collective-permute-start.2) | collective-permute-done | bytes 90144 | tf_op jit(solution)/shard_map/ppermute | solution.py:616
  25.1 2.7 %exchange.3 = (f32[2,1,16,128]{3,2,1,0:T(8,128)S(1)}, f32[32,8,128]{2,1,0:T(8,128)}) custom-call(s32[4]{0:T(128)S(1)} %pad_add_fusion.spot_ref.refs_1_, f32[2,3,16,128]{3,2,1,0:T(8,128)S(1)} %slice.10.fields_ref.late_ref, f32[32,8,128]{2,1,0:T(8,128)S(1)} %all-to-all-done.recv_ref, f32[36,16,128]{2,1,0:T(8,128)S(1)} %static.1.static_ref, ...), custom_call_target="tpu_custom_call" | custom-call | bytes 3000000 | tf_op jit(solution)/shard_map/exchange/pallas_call | solution.py:454
  27.8 4.8 %all-to-all-start.1 = ((f32[32,8,128]{2,1,0:T(8,128)}), f32[32,8,128]{2,1,0:T(8,128)S(1)}, u32[]{:S(2)}, u32[]{:S(2)}) async-start(f32[32,8,128]{2,1,0:T(8,128)} %get-tuple-element.20.after_ref), calls=%async_computation.1 | async-start | bytes 262144 | tf_op jit(solution)/shard_map/all_to_all | solution.py:566
  32.7 4.4 %collective-permute-start.4 = (f32[8,1408]{1,0:T(8,128)S(1)}, f32[8,1408]{1,0:T(8,128)S(1)}, u32[]{:S(2)}, u32[]{:S(2)}) collective-permute-start(f32[8,1408]{1,0:T(8,128)S(1)} %get-tuple-element.22), channel_id=1, source_target_pairs={{9,0},{10,1},{11,2},{12,3},{13,4},{14,5},{15,6},{8,7},{1,8},{2,9},... | collective-permute-start | bytes 135176 | tf_op jit(solution)/shard_map/ppermute | solution.py:617
  37.0 1.7 %collective-permute-done.4.corner_ref.refs_7_.refs_8_ = f32[8,1408]{1,0:T(8,128)S(1)} collective-permute-done((f32[8,1408]{1,0:T(8,128)S(1)}, f32[8,1408]{1,0:T(8,128)S(1)}, u32[]{:S(2)}, u32[]{:S(2)}) %collective-permute-start.4) | collective-permute-done | bytes 45088 | tf_op jit(solution)/shard_map/ppermute | solution.py:617
  38.8 1.3 %early_levels.1.refs_0_ = f32[25,16,128]{2,1,0:T(8,128)S(1)} custom-call(f32[32,8,128]{2,1,0:T(8,128)} %get-tuple-element.20.after_ref, s32[4]{0:T(128)S(1)} %pad_add_fusion.spot_ref.refs_1_, f32[2,72,16,128]{3,2,1,0:T(8,128)S(1)} %bitcast.17, f32[71,16,128]{2,1,0:T(8,128)S(1)} %bitcast.22, f32[2,16,128]{2,1,0:T(8,128)S(1)} %bitcast.27, ...), custom_call_target="tpu_custom_call" | custom-call | bytes 6000000 | tf_op jit(solution)/shard_map/early_levels/pallas_call | solution.py:454
  40.9 2.7 %exchange.4 = (f32[2,2,16,128]{3,2,1,0:T(8,128)S(1)}, f32[32,8,128]{2,1,0:T(8,128)}) custom-call(s32[4]{0:T(128)S(1)} %pad_add_fusion.spot_ref.refs_1_, f32[2,1,16,128]{3,2,1,0:T(8,128)S(1)} %get-tuple-element.19.late_ref, f32[32,8,128]{2,1,0:T(8,128)S(1)} %all-to-all-done.1.recv_ref, f32[36,16,128]{2,1,0:T(8,128)S(1)} %static.1.static_ref, ...), custom_call_target="tpu_custom_call" | custom-call | bytes 3000000 | tf_op jit(solution)/shard_map/exchange/pallas_call | solution.py:454
  43.6 4.9 %all-to-all-start.2 = ((f32[32,8,128]{2,1,0:T(8,128)}), f32[32,8,128]{2,1,0:T(8,128)S(1)}, u32[]{:S(2)}, u32[]{:S(2)}) async-start(f32[32,8,128]{2,1,0:T(8,128)} %get-tuple-element.24.refs_0_), calls=%async_computation.2 | async-start | bytes 262144 | tf_op jit(solution)/shard_map/all_to_all | solution.py:566
  48.5 3.7 %deep_levels.2.refs_1_.refs_3_ = f32[2,72,16,128]{3,2,1,0:T(8,128)} custom-call(f32[32,8,128]{2,1,0:T(8,128)} %get-tuple-element.24.refs_0_, s32[4]{0:T(128)S(1)} %pad_add_fusion.spot_ref.refs_1_, f32[2,72,16,128]{3,2,1,0:T(8,128)S(1)} %bitcast.18, f32[71,16,128]{2,1,0:T(8,128)S(1)} %bitcast.23, f32[2,16,128]{2,1,0:T(8,128)S(1)} %bitcast.28, ...), custom_call_target="tpu_custom_call" | custom-call | bytes 12000000 | tf_op jit(solution)/shard_map/deep_levels/pallas_call | solution.py:454
  52.2 4.5 %all-to-all-done.2.recv_ref = f32[32,8,128]{2,1,0:T(8,128)S(1)} async-done(((f32[32,8,128]{2,1,0:T(8,128)}), f32[32,8,128]{2,1,0:T(8,128)S(1)}, u32[]{:S(2)}, u32[]{:S(2)}) %all-to-all-start.2) | async-done | bytes 131104 | tf_op jit(solution)/shard_map/all_to_all | solution.py:566
  56.7 1.3 %copy-done.1 = f32[2,72,16,128]{3,2,1,0:T(8,128)S(1)} copy-done((f32[2,72,16,128]{3,2,1,0:T(8,128)S(1)}, f32[2,72,16,128]{3,2,1,0:T(8,128)}, u32[]{:S(2)}) %copy-start.1) | copy-done | bytes 1179672
  58.0 2.7 %exchange.5 = (f32[2,3,16,128]{3,2,1,0:T(8,128)S(1)}, f32[32,8,128]{2,1,0:T(8,128)}) custom-call(s32[4]{0:T(128)S(1)} %pad_add_fusion.spot_ref.refs_1_, f32[2,2,16,128]{3,2,1,0:T(8,128)S(1)} %get-tuple-element.23.late_ref, f32[32,8,128]{2,1,0:T(8,128)S(1)} %all-to-all-done.2.recv_ref, f32[36,16,128]{2,1,0:T(8,128)S(1)} %static.1.static_ref, ...), custom_call_target="tpu_custom_call" | custom-call | bytes 3000000 | tf_op jit(solution)/shard_map/exchange/pallas_call | solution.py:454
  60.7 2.6 %all-to-all-start.3 = ((f32[32,8,128]{2,1,0:T(8,128)}), f32[32,8,128]{2,1,0:T(8,128)S(1)}, u32[]{:S(2)}, u32[]{:S(2)}) async-start(f32[32,8,128]{2,1,0:T(8,128)} %get-tuple-element.26.refs_0_), calls=%async_computation.3 | async-start | bytes 262144 | tf_op jit(solution)/shard_map/all_to_all | solution.py:566
  63.3 3.7 %deep_levels.3.refs_1_ = f32[2,72,16,128]{3,2,1,0:T(8,128)} custom-call(f32[32,8,128]{2,1,0:T(8,128)} %get-tuple-element.26.refs_0_, s32[4]{0:T(128)S(1)} %pad_add_fusion.spot_ref.refs_1_, f32[2,72,16,128]{3,2,1,0:T(8,128)S(1)} %bitcast.19, f32[2,72,16,128]{3,2,1,0:T(8,128)} %deep_levels.2.refs_1_.refs_3_, ...), custom_call_target="tpu_custom_call", output_to_operand_aliasing={{}: (3, {})} | custom-call | bytes 12000000 | tf_op jit(solution)/shard_map/deep_levels/pallas_call | solution.py:454
  67.0 4.5 %all-to-all-done.3.recv_ref = f32[32,8,128]{2,1,0:T(8,128)S(1)} async-done(((f32[32,8,128]{2,1,0:T(8,128)}), f32[32,8,128]{2,1,0:T(8,128)S(1)}, u32[]{:S(2)}, u32[]{:S(2)}) %all-to-all-start.3) | async-done | bytes 131104 | tf_op jit(solution)/shard_map/all_to_all | solution.py:566
  71.4 1.8 %last_exchange.1 = f32[2,72,16,128]{3,2,1,0:T(8,128)} custom-call(s32[4]{0:T(128)S(1)} %pad_add_fusion.spot_ref.refs_1_, f32[2,3,16,128]{3,2,1,0:T(8,128)S(1)} %get-tuple-element.25.late_ref, f32[32,8,128]{2,1,0:T(8,128)S(1)} %all-to-all-done.3.recv_ref, f32[36,16,128]{2,1,0:T(8,128)S(1)} %static.1.static_ref, ...), custom_call_target="tpu_custom_call", output_to_operand_aliasing={{}: (6, {})} | custom-call | bytes 3000000 | tf_op jit(solution)/shard_map/last_exchange/pallas_call | solution.py:454
  (27 shorter events, 6.0 us)
Async XLA Ops:
  0.0 16.9 %copy-start.5 = (f32[1,2,16,128]{3,2,1,0:T(8,128)S(1)}, f32[1,2,16,128]{3,2,1,0:T(8,128)}, u32[]{:S(2)}) copy-start(f32[1,2,16,128]{3,2,1,0:T(8,128)} %param.7) | copy-start | bytes 49156
  0.7 16.2 %copy-start = (f32[1,2,72,16,128]{4,3,2,1,0:T(8,128)S(1)}, f32[1,2,72,16,128]{4,3,2,1,0:T(8,128)}, u32[]{:S(2)}) copy-start(f32[1,2,72,16,128]{4,3,2,1,0:T(8,128)} %param.6) | copy-start | bytes 3538948
  0.7 5.3 %collective-permute-start.1 = (f32[2,16,128]{2,1,0:T(8,128)S(1)}, f32[2,16,128]{2,1,0:T(8,128)S(1)}, u32[]{:S(2)}, u32[]{:S(2)}) collective-permute-start(f32[2,16,128]{2,1,0:T(8,128)S(1)} %pad_maximum_fusion), channel_id=1, source_target_pairs={{0,8},{8,0},{1,9},{9,1},{2,10},{10,2},{3,11},{11,3},{4,12},{12,4},... | collective-permute-start | bytes 49160 | tf_op jit(solution)/shard_map/ppermute | solution.py:563
  3.8 5.0 %collective-permute-start = (f32[2,16,128]{2,1,0:T(8,128)S(1)}, f32[2,16,128]{2,1,0:T(8,128)S(1)}, u32[]{:S(2)}, u32[]{:S(2)}) collective-permute-start(f32[2,16,128]{2,1,0:T(8,128)S(1)} %pad_maximum_fusion), channel_id=1, source_target_pairs={{0,1},{1,2},{2,3},{3,4},{4,5},{5,6},{6,7},{7,0},{8,9},{9,10},{10,1... | collective-permute-start | bytes 49160 | tf_op jit(solution)/shard_map/ppermute | solution.py:562
  4.7 0.7 copy-start.8
  8.7 1.1 %copy-start.2 = (f32[1,71,16,128]{3,2,1,0:T(8,128)S(1)}, f32[1,71,16,128]{3,2,1,0:T(8,128)}, u32[]{:S(2)}) copy-start(f32[1,71,16,128]{3,2,1,0:T(8,128)} %param.8) | copy-start | bytes 1744900
  9.8 0.7 copy-start.4
  10.5 0.7 copy-start.6
  11.2 0.7 copy-start.7
  11.9 5.0 %copy-start.3 = (f32[1,71,16,128]{3,2,1,0:T(8,128)S(1)}, f32[1,71,16,128]{3,2,1,0:T(8,128)}, u32[]{:S(2)}) copy-start(f32[1,71,16,128]{3,2,1,0:T(8,128)} %param.8) | copy-start | bytes 1744900
  13.8 11.3 %all-to-all-start = ((f32[32,8,128]{2,1,0:T(8,128)}), f32[32,8,128]{2,1,0:T(8,128)S(1)}, u32[]{:S(2)}, u32[]{:S(2)}) async-start(f32[32,8,128]{2,1,0:T(8,128)} %first_send.1.after_ref), calls=%async_computation | async-start | bytes 262144 | tf_op jit(solution)/shard_map/all_to_all | solution.py:566
  18.3 20.4 %collective-permute-start.3 = (f32[109,8,128]{2,1,0:T(8,128)}, f32[109,8,128]{2,1,0:T(8,128)S(1)}, u32[]{:S(2)}, u32[]{:S(2)}) collective-permute-start(f32[109,8,128]{2,1,0:T(8,128)} %get-tuple-element.21), channel_id=1, source_target_pairs={{8,0},{0,8},{9,1},{1,9},{10,2},{2,10},{11,3},{3,11},{12,4},{4,12},... | collective-permute-start | bytes 1339400 | tf_op jit(solution)/shard_map/ppermute | solution.py:615
  20.1 5.0 %collective-permute-start.2 = (f32[16,1408]{1,0:T(8,128)S(1)}, f32[16,1408]{1,0:T(8,128)S(1)}, u32[]{:S(2)}, u32[]{:S(2)}) collective-permute-start(f32[16,1408]{1,0:T(8,128)S(1)} %get-tuple-element.18), channel_id=1, source_target_pairs={{1,0},{2,1},{3,2},{4,3},{5,4},{6,5},{7,6},{0,7},{9,8},{10,9},{11,1... | collective-permute-start | bytes 270344 | tf_op jit(solution)/shard_map/ppermute | solution.py:616
  27.8 13.0 %all-to-all-start.1 = ((f32[32,8,128]{2,1,0:T(8,128)}), f32[32,8,128]{2,1,0:T(8,128)S(1)}, u32[]{:S(2)}, u32[]{:S(2)}) async-start(f32[32,8,128]{2,1,0:T(8,128)} %get-tuple-element.20.after_ref), calls=%async_computation.1 | async-start | bytes 262144 | tf_op jit(solution)/shard_map/all_to_all | solution.py:566
  32.7 6.1 %collective-permute-start.4 = (f32[8,1408]{1,0:T(8,128)S(1)}, f32[8,1408]{1,0:T(8,128)S(1)}, u32[]{:S(2)}, u32[]{:S(2)}) collective-permute-start(f32[8,1408]{1,0:T(8,128)S(1)} %get-tuple-element.22), channel_id=1, source_target_pairs={{9,0},{10,1},{11,2},{12,3},{13,4},{14,5},{15,6},{8,7},{1,8},{2,9},... | collective-permute-start | bytes 135176 | tf_op jit(solution)/shard_map/ppermute | solution.py:617
  43.6 13.1 %all-to-all-start.2 = ((f32[32,8,128]{2,1,0:T(8,128)}), f32[32,8,128]{2,1,0:T(8,128)S(1)}, u32[]{:S(2)}, u32[]{:S(2)}) async-start(f32[32,8,128]{2,1,0:T(8,128)} %get-tuple-element.24.refs_0_), calls=%async_computation.2 | async-start | bytes 262144 | tf_op jit(solution)/shard_map/all_to_all | solution.py:566
  56.7 1.3 %copy-start.1 = (f32[2,72,16,128]{3,2,1,0:T(8,128)S(1)}, f32[2,72,16,128]{3,2,1,0:T(8,128)}, u32[]{:S(2)}) copy-start(f32[2,72,16,128]{3,2,1,0:T(8,128)} %deep_levels.2.refs_1_.refs_3_) | copy-start | bytes 3538948
  60.7 10.7 %all-to-all-start.3 = ((f32[32,8,128]{2,1,0:T(8,128)}), f32[32,8,128]{2,1,0:T(8,128)S(1)}, u32[]{:S(2)}, u32[]{:S(2)}) async-start(f32[32,8,128]{2,1,0:T(8,128)} %get-tuple-element.26.refs_0_), calls=%async_computation.3 | async-start | bytes 262144 | tf_op jit(solution)/shard_map/all_to_all | solution.py:566

commit v6 on v5

--- a/solution.py
+++ b/solution.py
@@ -11,14 +11,22 @@
 STEPS = 4
 F32 = jnp.float32
 BF16 = jnp.bfloat16
+UPPER = 8
 PACKED = 32
 SLAB = 4
 ZONAL, MERIDIONAL, KAPPA = 0, 1, 2
 COUPLING = KAPPA + STEPS
-WEST = COUPLING + 1
-SOUTH = WEST + 2
-WET = SOUTH + 2
-PLACE = WET + 1
+WET = COUPLING + 1
+
+
+class Place:
+    def __init__(self):
+        n_lat, n_lon = lax.axis_size("lat"), lax.axis_size("lon")
+        lat, lon = lax.axis_index("lat"), lax.axis_index("lon")
+        self.model = lax.axis_index("mp")
+        self.east = lat * n_lon + lax.rem(lon + 1, n_lon)
+        self.north = lax.rem(lat + 1, n_lat) * n_lon + lon
+        self.has_north = lat < n_lat - 1
 
 
 def lane_iota(shape):
@@ -54,17 +62,21 @@
     return total
 
 
-def halo_kernel(after_ref, fields_ref, kappa_ref, courant_ref, rows_ref, columns_ref, corner_ref):
+def halo_kernel(fields_ref, kappa_ref, courant_ref, upper_ref, deep_ref, columns_ref, corner_ref):
     tracers, levels, rows, cols = fields_ref.shape
     lane = lane_iota((rows, cols))
     upper = row_iota((2 * STEPS, cols)) < STEPS
-    pairs = levels // 2
-
-    def first_rows(read, count, start):
-        for pair in range(pairs):
+    upper_pairs, deep_pairs = UPPER // 2, (levels - UPPER) // 2
+
+    def first_rows(read, count, which):
+        for pair in range(levels // 2):
             one = read(2 * pair)
             two = read(2 * pair + 1) if 2 * pair + 1 < count else jnp.zeros_like(one)
-            rows_ref[start + pair] = jnp.where(upper, one, pltpu.roll(two, STEPS, 0))
+            both = jnp.where(upper, one, pltpu.roll(two, STEPS, 0))
+            if pair < upper_pairs:
+                upper_ref[which * upper_pairs + pair] = both
+            else:
+                deep_ref[which * deep_pairs + pair - upper_pairs] = both
 
     def first_columns(read, count, start):
         for tile in range(-(-levels // PACKED)):
@@ -78,11 +90,11 @@
 
     tiles = -(-levels // PACKED)
     for tracer in range(tracers):
-        first_rows(lambda k: fields_ref[tracer, k, 0 : 2 * STEPS, :], levels, tracer * pairs)
+        first_rows(lambda k: fields_ref[tracer, k, 0 : 2 * STEPS, :], levels, tracer)
         first_columns(lambda k: fields_ref[tracer, k], levels, tracer * tiles)
-    first_rows(lambda k: kappa_ref[k, 0 : 2 * STEPS, :], levels - 1, tracers * pairs)
+    first_rows(lambda k: kappa_ref[k, 0 : 2 * STEPS, :], levels - 1, tracers)
     first_columns(lambda k: kappa_ref[k], levels - 1, tracers * tiles)
-    rows_ref[(tracers + 1) * pairs] = jnp.where(
+    upper_ref[(tracers + 1) * upper_pairs] = jnp.where(
         upper,
         courant_ref[0, 0 : 2 * STEPS, :],
         pltpu.roll(courant_ref[1, 0 : 2 * STEPS, :], STEPS, 0),
@@ -98,18 +110,21 @@
         corner_ref[:, spot] = repeated[0 : 2 * STEPS]
 
 
-def wide_steps(spot_ref, refs, tracer, levels, tracers, all_levels, first_field, store, each_step):
-    kappa_ref, courant_ref, rows_ref, columns_ref, corner_ref, state = refs
+def wide_steps(refs, tracer, levels, tracers, all_levels, first_field, store, each_step):
+    kappa_ref, courant_ref, rows_refs, columns_ref, corner_ref, state = refs
     rows, cols = courant_ref.shape[1:]
-    pairs = all_levels // 2
+    upper_pairs, deep_pairs = UPPER // 2, (all_levels - UPPER) // 2
     tiles = -(-all_levels // PACKED)
     used = -(-levels // PACKED)
     tall = rows + 2 * STEPS
-    has_north = spot_ref[3] > 0
+    has_north = Place().has_north
     lane = lane_iota((tall, cols))
 
-    def with_rows(block, start, k):
-        extra = rows_ref[start + k // 2]
+    def with_rows(block, which, k):
+        if k < UPPER:
+            extra = rows_refs[0][which * upper_pairs + k // 2]
+        else:
+            extra = rows_refs[1][which * deep_pairs + (k - UPPER) // 2]
         if k % 2:
             extra = pltpu.roll(extra, STEPS, 0)
         return jnp.concatenate([block, jnp.where(has_north, extra, 0.0)], axis=0)
@@ -119,7 +134,7 @@
         corner = jnp.where(has_north, corner_ref[:, spot], 0.0)
         return jnp.concatenate([columns_ref[:, spot], corner], axis=0)
 
-    last = rows_ref[(tracers + 1) * pairs]
+    last = rows_refs[0][(tracers + 1) * upper_pairs]
     last = jnp.where(has_north, last, 0.0)
     zonal = jnp.concatenate([courant_ref[0], last], axis=0)
     meridional = jnp.concatenate([courant_ref[1], pltpu.roll(last, STEPS, 0)], axis=0)
@@ -152,7 +167,7 @@
 
         def field_of(k):
             if step == 0:
-                return with_rows(first_field(k), tracer * pairs, k)
+                return with_rows(first_field(k), tracer, k)
             return state[k]
 
         def advected(k):
@@ -170,7 +185,7 @@
                 below = advected(k + 1)
                 kappa = kappa_ref[k]
                 if height > rows:
-                    kappa = with_rows(kappa, tracers * pairs, k)
+                    kappa = with_rows(kappa, tracers, k)
                 flux = kappa * (below - here)
                 result = result + flux
             if k > 0:
@@ -196,11 +211,10 @@
 
 
 def early_kernel(
-    after_ref, spot_ref, fields_ref, kappa_ref, courant_ref, rows_ref, columns_ref, corner_ref,
-    early_ref, state, *, all_levels,
+    fields_ref, kappa_ref, courant_ref, rows_ref, columns_ref, corner_ref, early_ref, state, *, all_levels
 ):
     tracers, levels, rows, cols = fields_ref.shape
-    refs = (kappa_ref, courant_ref, rows_ref, columns_ref, corner_ref, state)
+    refs = (kappa_ref, courant_ref, (rows_ref,), columns_ref, corner_ref, state)
     for tracer in range(tracers):
 
         def each_step(step, zonal, meridional, side_zonal, side):
@@ -215,14 +229,13 @@
                 )
 
         wide_steps(
-            spot_ref, refs, tracer, levels, tracers, all_levels,
+            refs, tracer, levels, tracers, all_levels,
             lambda k: fields_ref[tracer, k], lambda k, value: None, each_step,
         )
 
 
-def deep_kernel(*refs, tracer, tracers):
-    _, spot_ref, fields_ref, *rest = refs
-    *halo, out_ref, state = rest[-7:] if len(rest) == 7 else rest[1:]
+def deep_kernel(after_ref, fields_ref, *refs, tracer, tracers):
+    kappa_ref, courant_ref, *rows_refs, columns_ref, corner_ref, out_ref, token_ref, state = refs[-9:]
     levels = fields_ref.shape[1]
 
     def store(k, value):
@@ -232,11 +245,15 @@
     for k in range(STEPS):
         out_ref[0, k] = jnp.zeros(out_ref.shape[2:], F32)
     wide_steps(
-        spot_ref, (*halo, state), tracer, levels, tracers, levels, lambda k: fields_ref[0, k], store, None
-    )
-
-
-def send_surface(late, below, static_ref, table_ref, send_ref, model, deep_rows):
+        (kappa_ref, courant_ref, rows_refs, columns_ref, corner_ref, state),
+        tracer, levels, tracers, levels, lambda k: fields_ref[0, k], store, None,
+    )
+    token_ref[...] = jnp.zeros(token_ref.shape, F32)
+
+
+def send_surface(late, below, static_refs, table_ref, send_ref, deep_rows):
+    static_ref, west_ref, south_ref, _ = static_refs
+    model = Place().model
     tracers = len(late)
     zonal, meridional = static_ref[ZONAL], static_ref[MERIDIONAL]
     weight = (1.0 - zonal) - meridional
@@ -249,9 +266,9 @@
     group = lane // TILE
     tiles, edge_north, edge_east = [], [], []
     place = lane == (row % groups) * TILE + (TILE - 1) - row // groups
-    west_a = lane_roll(static_ref[WEST], 1)
-    west_b = lane_roll(static_ref[WEST + 1], 1)
-    south_a, south_b = static_ref[SOUTH], static_ref[SOUTH + 1]
+    west_a = lane_roll(west_ref[0], 1)
+    west_b = lane_roll(west_ref[1], 1)
+    south_a, south_b = south_ref[0], south_ref[1]
     own_north, own_east = [], jnp.zeros((rows, cols), F32)
     for tracer in range(tracers):
         parts = []
@@ -305,13 +322,14 @@
         send_ref[model * devices + 2 * pair + 1] = own
 
 
-def receive_surface(model, recv_ref, table_ref, static_ref, surface):
+def receive_surface(recv_ref, table_ref, static_refs, surface):
     devices = recv_ref.shape[0] // 2
     rows, cols = surface[0].shape
     groups = cols // TILE
     tracers = len(surface)
     count = rows * groups
-    other = (1 - model) * devices
+    static_ref, _, _, place_ref = static_refs
+    other = (1 - Place().model) * devices
     upper = row_iota((2 * SLAB, cols)) < SLAB
     first, second = [], []
     for pair in range(devices // 2):
@@ -331,7 +349,7 @@
             total = None
             for kind in range(3):
                 start = kind * count + c * rows
-                place = static_ref[PLACE + kind * groups + c]
+                place = place_ref[kind * groups + c]
                 term = jnp.where(
                     place > 0, found[start : start + rows, tracer * cols : (tracer + 1) * cols], 0.0
                 )
@@ -346,16 +364,17 @@
     return updated
 
 
-def upper_levels(spot_ref, recv_ref, late, early, static_ref):
+def upper_levels(recv_ref, late, early, static_ref):
     zonal, meridional = static_ref[ZONAL], static_ref[MERIDIONAL]
     weight = (1.0 - zonal) - meridional
     rows, cols = zonal.shape
     lane = lane_iota((rows, cols))
     row = row_iota((rows, cols))
     devices = recv_ref.shape[0] // 2
-    mine = spot_ref[0] * devices
-    from_east = recv_ref[mine + spot_ref[1]]
-    from_north = jnp.where(spot_ref[3] > 0, recv_ref[mine + spot_ref[2]], 0.0)
+    here = Place()
+    mine = here.model * devices
+    from_east = recv_ref[mine + here.east]
+    from_north = jnp.where(here.has_north, recv_ref[mine + here.north], 0.0)
     east_line = jnp.broadcast_to(from_east[from_east.shape[0] - 1 :], (rows, cols))
     stepped = []
     for tracer in range(len(late)):
@@ -396,21 +415,24 @@
     return found
 
 
-def first_send_kernel(spot_ref, fields_ref, static_ref, table_ref, send_ref, *, deep_rows):
-    tracers, levels = fields_ref.shape[:2]
-    late = [[fields_ref[tracer, k] for k in range(levels)] for tracer in range(tracers)]
-    send_surface(late, [values[1] for values in late], static_ref, table_ref, send_ref, spot_ref[0], deep_rows)
-
-
-def exchange_kernel(spot_ref, late_ref, recv_ref, static_ref, table_ref, *refs, step, deep_rows, unread):
+def first_send_kernel(late_ref, *refs, deep_rows, carried):
+    *static_refs, table_ref = refs[:5]
+    send_ref = refs[5 + carried]
+    tracers, levels = late_ref.shape[:2]
+    late = [[late_ref[tracer, k] for k in range(levels)] for tracer in range(tracers)]
+    send_surface(late, [values[1] for values in late], static_refs, table_ref, send_ref, deep_rows)
+
+
+def exchange_kernel(late_ref, recv_ref, *refs, step, deep_rows, unread, carried=0):
+    static_refs, table_ref, refs = refs[:4], refs[4], refs[5:]
     early_ref, refs = (refs[0], refs[1:]) if step > 0 else (None, refs)
-    refs = refs[unread:]
+    refs = refs[unread:] if step == STEPS - 1 else refs[unread + carried : unread + carried + 2]
     tracers = late_ref.shape[0]
     late = [[late_ref[tracer, k] for k in range(late_ref.shape[1])] for tracer in range(tracers)]
     early = [early_levels(step, early_ref, tracer, tracers) for tracer in range(tracers)]
-    stepped = upper_levels(spot_ref, recv_ref, late, early, static_ref)
+    stepped = upper_levels(recv_ref, late, early, static_refs[0])
     surface = [values[0] for values in stepped]
-    surface = receive_surface(spot_ref[0], recv_ref, table_ref, static_ref, surface)
+    surface = receive_surface(recv_ref, table_ref, static_refs, surface)
     for tracer in range(tracers):
         stepped[tracer][0] = surface[tracer]
     if step == STEPS - 1:
@@ -427,10 +449,9 @@
     send_surface(
         [values[:kept] for values in stepped],
         [values[1] for values in stepped],
-        static_ref,
+        static_refs,
         table_ref,
         send_ref,
-        spot_ref[0],
         deep_rows,
     )
 
@@ -445,7 +466,6 @@
     return pl.BlockSpec((tracers, levels, rows, cols), lambda i: (0, 0, 0, 0))
 
 
-SCALAR = pl.BlockSpec(memory_space=pltpu.SMEM)
 NEAR = pl.BlockSpec(memory_space=pltpu.VMEM)
 UNREAD = pl.BlockSpec(memory_space=pl.ANY)
 
@@ -526,20 +546,6 @@
             place_ref[kind * groups + c] = place[c * rows : (c + 1) * rows]
 
 
-def static_kernel(courant_ref, kappa_ref, coupling_ref, mask_ref, west_ref, south_ref, place_ref, static_ref):
-    static_ref[ZONAL] = courant_ref[0]
-    static_ref[MERIDIONAL] = courant_ref[1]
-    for k in range(STEPS):
-        static_ref[KAPPA + k] = kappa_ref[k]
-    static_ref[COUPLING] = coupling_ref[...]
-    for k in range(2):
-        static_ref[WEST + k] = west_ref[k]
-        static_ref[SOUTH + k] = south_ref[k]
-    static_ref[WET] = mask_ref[...].astype(F32)
-    for k in range(place_ref.shape[0]):
-        static_ref[PLACE + k] = place_ref[k]
-
-
 def local(adjoint, courant, diffusivity, coupling, partner, mask):
     fields = adjoint[0]
     courant, kappa, coupling, mask = courant[0], diffusivity[0], coupling[0], mask[0]
@@ -548,15 +554,6 @@
     count = rows * groups
     n_lat, n_lon = lax.axis_size("lat"), lax.axis_size("lon")
     devices = n_lat * n_lon
-    lat, lon = lax.axis_index("lat"), lax.axis_index("lon")
-    spot = jnp.stack(
-        [
-            lax.axis_index("mp"),
-            lat * n_lon + (lon + 1) % n_lon,
-            ((lat + 1) % n_lat) * n_lon + lon,
-            (lat < n_lat - 1).astype(jnp.int32),
-        ]
-    ).astype(jnp.int32)
 
     share = jnp.stack([coupling * (1.0 - kappa[0]), coupling * kappa[0]])
     from_west = lax.ppermute(share, "lon", [(i, (i + 1) % n_lon) for i in range(n_lon)])
@@ -569,50 +566,51 @@
     table_shape = jax.ShapeDtypeStruct(
         (deep_rows + groups * devices * SLAB, max(count, 2 * devices * SLAB)), BF16
     )
-    place_shape = shaped(3 * groups, rows, cols)
     table, place = call(
         functools.partial(tables_kernel, rows=rows, groups=groups, n_lat=n_lat, n_lon=n_lon),
         (partner,),
         [NEAR],
-        (table_shape, place_shape),
+        (table_shape, shaped(3 * groups, rows, cols)),
         (NEAR, NEAR),
         "tables",
     )
-    gathered = (courant, kappa, coupling, mask, from_west, from_south, place)
-    static_shape = shaped(PLACE + 3 * groups, rows, cols)
-    static_specs = [whole(a) for a in gathered]
-    static_specs[1] = pl.BlockSpec((STEPS, rows, cols), lambda i: (0, 0, 0))
-    static = call(static_kernel, gathered, static_specs, static_shape, whole(static_shape), "static", grid=(1,))
-    send_shape = shaped(2 * devices, 2 * SLAB, cols)
-    late = fields[:, :3]
-    send = call(
-        functools.partial(first_send_kernel, deep_rows=deep_rows),
-        (spot, late, static, table),
-        [SCALAR, NEAR, NEAR, NEAR],
-        send_shape,
-        NEAR,
-        "first_send",
-    )
-    recv = exchanged(send)
+    planes = jnp.concatenate([courant, kappa[:STEPS], coupling[None], mask[None].astype(F32)], axis=0)
+    statics = (planes, from_west, from_south, place, table)
 
     tiles = -(-levels // PACKED)
     width = ((tracers + 1) * tiles + 2) * cols
     halo_shapes = (
-        shaped((tracers + 1) * (levels // 2) + 1, 2 * STEPS, cols),
+        shaped((tracers + 1) * (UPPER // 2) + 1, 2 * STEPS, cols),
+        shaped((tracers + 1) * ((levels - UPPER) // 2), 2 * STEPS, cols),
         shaped(rows, width),
         shaped(2 * STEPS, width),
     )
-    north, east, corner = call(
+    packed = call(
         halo_kernel,
-        (send, fields, kappa, courant),
-        [UNREAD, *(whole(a) for a in (fields, kappa, courant))],
+        (fields, kappa, courant),
+        [whole(a) for a in (fields, kappa, courant)],
         halo_shapes,
         tuple(whole(a) for a in halo_shapes),
         "halo",
         grid=(1,),
         us=2,
     )
-    north = lax.ppermute(north, "lat", [((i + 1) % n_lat, i) for i in range(n_lat)])
+    send_shape = shaped(2 * devices, 2 * SLAB, cols)
+    late = fields[:, :3]
+    carried = (packed[0], packed[2], packed[3])
+    send, *carried = call(
+        functools.partial(first_send_kernel, deep_rows=deep_rows, carried=len(carried)),
+        (late, *statics, *carried),
+        [*(NEAR for _ in range(6)), *(UNREAD for _ in carried)],
+        (send_shape, *(shaped(*a.shape) for a in carried)),
+        (NEAR, *(UNREAD for _ in carried)),
+        "first_send",
+        aliases={6 + i: 1 + i for i in range(len(carried))},
+    )
+    recv = exchanged(send)
+    upper, east, corner = carried
+    from_north = [((i + 1) % n_lat, i) for i in range(n_lat)]
+    upper = lax.ppermute(upper, "lat", from_north)
     east = lax.ppermute(east, "lon", [((i + 1) % n_lon, i) for i in range(n_lon)])
     corner = lax.ppermute(
         corner,
@@ -623,79 +621,80 @@
             for j in range(n_lon)
         ],
     )
-    halo = (courant, north, east, corner)
-    halo_specs = [whole(a) for a in halo]
     tall = rows + 2 * STEPS
 
-    early, out = (), None
+    early, out, after = (), None, (upper, east, corner)
     for step in range(STEPS):
         if step > 0:
             recv = exchanged(send)
-        after = ()
-        if step == 0:
-            after = (east,)
         if step == 1:
-            shown = 2 * STEPS
+            deep = lax.ppermute(deep, "lat", from_north)
             early_shape = shaped((STEPS - 1) * tracers * 4 + 1, rows, cols)
             early = (
                 call(
                     functools.partial(early_kernel, all_levels=levels),
-                    (send, spot, fields, kappa, *halo),
+                    (fields, kappa, courant, upper, east, corner),
                     [
-                        UNREAD,
-                        SCALAR,
-                        top(fields, shown),
-                        pl.BlockSpec((shown, rows, cols), lambda i: (0, 0, 0)),
-                        *halo_specs,
+                        top(fields, UPPER),
+                        pl.BlockSpec((UPPER, rows, cols), lambda i: (0, 0, 0)),
+                        *(whole(a) for a in (courant, upper, east, corner)),
                     ],
                     early_shape,
                     whole(early_shape),
                     "early_levels",
                     grid=(1,),
-                    scratch=[pltpu.VMEM((shown, tall, cols), F32)],
+                    scratch=[pltpu.VMEM((UPPER, tall, cols), F32)],
                     us=2,
                 ),
             )
         if step > 1:
+            halo = (kappa, courant, upper, deep, east, corner)
             for tracer in range(step - 2, tracers if step == STEPS - 1 else step - 1):
                 before = () if out is None else (out,)
                 block = pl.BlockSpec((1, levels, rows, cols), lambda i, tracer=tracer: (tracer, 0, 0, 0))
-                out = call(
+                token = shaped(8, cols)
+                out, token = call(
                     functools.partial(deep_kernel, tracer=tracer, tracers=tracers),
-                    (send, spot, fields, *before, kappa, *halo),
-                    [UNREAD, SCALAR, block, *(UNREAD for _ in before), whole(kappa), *halo_specs],
-                    shaped(*fields.shape),
-                    block,
+                    (send, fields, *before, *halo),
+                    [UNREAD, block, *(UNREAD for _ in before), *(whole(a) for a in halo)],
+                    (shaped(*fields.shape), token),
+                    (block, whole(token)),
                     "deep_levels",
                     grid=(1,),
-                    aliases={3: 0} if before else None,
+                    aliases={2: 0} if before else None,
                     scratch=[pltpu.VMEM((levels, tall, cols), F32)],
                     us=4,
                 )
+            after = (token,)
+        if step == STEPS - 1:
             after = (out,)
-        operands = (spot, late, recv, static, table, *early, *after)
-        specs = [SCALAR, *(NEAR for _ in operands[1 : len(operands) - len(after)]), *(UNREAD for _ in after)]
+        operands = (late, recv, *statics, *early, *after)
+        near = len(operands) - len(after)
         kernel = functools.partial(exchange_kernel, step=step, deep_rows=deep_rows, unread=len(after))
         if step == STEPS - 1:
-            specs[1 : len(operands) - len(after)] = [whole(a) for a in operands[1 : len(operands) - len(after)]]
             return call(
                 kernel,
                 operands,
-                specs,
+                [*(whole(a) for a in operands[:near]), UNREAD],
                 shaped(*fields.shape),
                 top(fields, STEPS),
                 "last_exchange",
                 grid=(1,),
-                aliases={len(operands) - 1: 0},
+                aliases={near: 0},
             )[None]
-        late, send = call(
-            kernel,
-            operands,
-            specs,
-            (shaped(tracers, step + 1, rows, cols), send_shape),
-            (NEAR, NEAR),
+        carry = (packed[1],) if step == 0 else ()
+        late, send, *carry = call(
+            functools.partial(kernel, carried=len(carry)),
+            (*operands, *carry),
+            [*(NEAR for _ in range(near)), *(UNREAD for _ in (*after, *carry))],
+            (shaped(tracers, step + 1, rows, cols), send_shape, *(shaped(*a.shape) for a in carry)),
+            (NEAR, NEAR, *(UNREAD for _ in carry)),
             "exchange",
+            aliases={len(operands): 2} if carry else None,
         )
+        if carry:
+            (deep,) = carry
+        after = ()
 
 
 def solution(mesh):

time: 73.9 us -> 69.7 us (0.943)
  Pallas kernels: 22.6 us -> 17.5 us
  starting transfers between devices: 27.4 us -> 24 us
  waiting for transfers between devices: 16.4 us -> 19.1 us
  other arithmetic: 0.81 us -> 2.16 us
    all_to_all x4, waiting for transfers between devices: 9.8 us -> 15.6 us  [exchanged(): lax.all_to_all(send, ('mp', 'lat', 'lon'), split_axis=0, concat_axis=0, t...]
    pallas_call x11 -> x10, Pallas kernels: 22.6 us -> 17.5 us  [call(): pl.pallas_call(kernel, grid=grid, in_specs=specs, out_shape=out_shape, ou...]
    ppermute x1, starting transfers between devices: 4.36 us -> 0.05 us  [local(): lax.ppermute(corner, ('lat', 'lon'), [((i + 1) % n_lat * n_lon + (j + 1)...]
    ppermute x1, waiting for transfers between devices: 2.73 us -> 0.01 us  [local(): lax.ppermute(share, 'lon', [(i, (i + 1) % n_lon) for i in range(n_lon)])]
    ppermute x1, waiting for transfers between devices: 2.14 us -> 0.01 us  [local(): lax.ppermute(east, 'lon', [((i + 1) % n_lon, i) for i in range(n_lon)])]
    ppermute x1, waiting for transfers between devices: 1.71 us -> 3.53 us  [local(): lax.ppermute(corner, ('lat', 'lon'), [((i + 1) % n_lat * n_lon + (j + 1)...]
    ppermute x1 -> x2, starting transfers between devices: 1.77 us -> 3.33 us  [the longest x1 1.83 us: local(): deep = lax.ppermute(deep, 'lat', from_north)]
    all_to_all x4, starting transfers between devices: 15.5 us -> 14.2 us  [exchanged(): lax.all_to_all(send, ('mp', 'lat', 'lon'), split_axis=0, concat_axis=0, t...]
  transfers between devices with their start and end apart: 9 -> 10, of which waited for: 7 -> 4; matrix products, arithmetic and copies ran while one was open for 1% -> 4% of each run, Pallas kernels for 18% -> 15%
where the time goes in v6:
time: 69.7 us; the launch traced here: 69 us
  starting transfers between devices  24 us (34%)
  waiting for transfers between devices  19.1 us (27%)
  Pallas kernels  17.5 us (25%)
  local copies, waits for them, and re-layouts  6.02 us (9%)
  other arithmetic  2.16 us (3%)
    pallas_call x10, Pallas kernels, call(): pl.pallas_call(kernel, grid=grid, in_specs=specs, out_shape=out_shape, ou...  17.5 us
    all_to_all x4, waiting for transfers between devices, exchanged(): lax.all_to_all(send, ('mp', 'lat', 'lon'), split_axis=0, concat_axis=0, t...  15.6 us
    all_to_all x4, starting transfers between devices, exchanged(): lax.all_to_all(send, ('mp', 'lat', 'lon'), split_axis=0, concat_axis=0, t...  14.2 us
    unnamed x16, local copies, waits for them, and re-layouts  4.46 us
    ppermute x1, waiting for transfers between devices, local(): lax.ppermute(corner, ('lat', 'lon'), [((i + 1) % n_lat * n_lon + (j + 1)...  3.53 us
    ppermute x1, starting transfers between devices, local(): lax.ppermute(east, 'lon', [((i + 1) % n_lon, i) for i in range(n_lon)])  3.43 us
    ppermute x1, starting transfers between devices, local(): lax.ppermute(share, 'lat', [(i, (i + 1) % n_lat) for i in range(n_lat)])  2.97 us
    ppermute x1, starting transfers between devices, local(): deep = lax.ppermute(deep, 'lat', from_north)  1.83 us
  transfers between devices with their start and end apart: 10, of which 4 were waited for; matrix products, arithmetic and copies ran while one was open for 4% of the time, Pallas kernels for 15%

profile of v6, /device:TPU:0, one launch (start us, length us, event | category | flops | bytes accessed | tf_op | source)
XLA Modules:
  0.0 69.0 jit_solution(12325570026847995931)
XLA Ops:
  0.7 3.0 %collective-permute-start.1 = (f32[2,16,128]{2,1,0:T(8,128)S(1)}, f32[2,16,128]{2,1,0:T(8,128)S(1)}, u32[]{:S(2)}, u32[]{:S(2)}) collective-permute-start(f32[2,16,128]{2,1,0:T(8,128)S(1)} %pad_maximum_fusion.1), channel_id=1, source_target_pairs={{0,8},{8,0},{1,9},{9,1},{2,10},{10,2},{3,11},{11,3},{4,12},{12,4},... | collective-permute-start | bytes 49160 | tf_op jit(solution)/shard_map/ppermute | solution.py:560
  3.7 0.8 %slice_bitcast_fusion = f32[4,16,128]{2,1,0:T(8,128)S(1)} fusion(f32[1,71,16,128]{3,2,1,0:T(8,128)} %param.8), kind=kLoop, calls=%fused_computation.1 | loop fusion | bytes 65536 | tf_op jit(solution)/shard_map/slice | solution.py:577
  5.9 0.8 %slice.18.late_ref = f32[2,3,16,128]{3,2,1,0:T(8,128)S(1)} slice(f32[2,72,16,128]{3,2,1,0:T(8,128)} %bitcast.11), slice={[0:2], [0:3], [0:16], [0:128]} | slice | bytes 98304 | tf_op jit(solution)/shard_map/slice | solution.py:599
  8.0 1.3 %copy-done = f32[1,2,72,16,128]{4,3,2,1,0:T(8,128)S(1)} copy-done((f32[1,2,72,16,128]{4,3,2,1,0:T(8,128)S(1)}, f32[1,2,72,16,128]{4,3,2,1,0:T(8,128)}, u32[]{:S(2)}) %copy-start) | copy-done | bytes 1179672
  9.3 1.1 %copy-done.2 = f32[1,71,16,128]{3,2,1,0:T(8,128)S(1)} copy-done((f32[1,71,16,128]{3,2,1,0:T(8,128)S(1)}, f32[1,71,16,128]{3,2,1,0:T(8,128)}, u32[]{:S(2)}) %copy-start.2) | copy-done | bytes 581656
  11.8 1.3 %first_send.1 = (f32[32,8,128]{2,1,0:T(8,128)}, f32[13,8,128]{2,1,0:T(8,128)S(1)}, f32[16,1408]{1,0:T(8,128)S(1)}, f32[8,1408]{1,0:T(8,128)S(1)}) custom-call(f32[2,3,16,128]{3,2,1,0:T(8,128)S(1)} %slice.18.late_ref, f32[8,16,128]{2,1,0:T(8,128)S(1)} %pad_maximum_fusion.refs_0_, ...), custom_call_target="tpu_custom_call", output_to_operand_aliasing={{1}: (6, {}), {2}: (7, {}), {3}: (8, {})} | custom-call | bytes 3000000 | tf_op jit(solution)/shard_map/first_send/pallas_call | solution.py:474
  13.1 5.2 %all-to-all-start = ((f32[32,8,128]{2,1,0:T(8,128)}), f32[32,8,128]{2,1,0:T(8,128)S(1)}, u32[]{:S(2)}, u32[]{:S(2)}) async-start(f32[32,8,128]{2,1,0:T(8,128)} %get-tuple-element.30), calls=%async_computation | async-start | bytes 262144 | tf_op jit(solution)/shard_map/all_to_all | solution.py:563
  18.3 3.4 %collective-permute-start.3 = (f32[16,1408]{1,0:T(8,128)S(1)}, f32[16,1408]{1,0:T(8,128)S(1)}, u32[]{:S(2)}, u32[]{:S(2)}) collective-permute-start(f32[16,1408]{1,0:T(8,128)S(1)} %get-tuple-element.32), channel_id=1, source_target_pairs={{1,0},{2,1},{3,2},{4,3},{5,4},{6,5},{7,6},{0,7},{9,8},{10,9},{11,1... | collective-permute-start | bytes 270344 | tf_op jit(solution)/shard_map/ppermute | solution.py:614
  21.7 1.5 %collective-permute-start.2 = (f32[13,8,128]{2,1,0:T(8,128)S(1)}, f32[13,8,128]{2,1,0:T(8,128)S(1)}, u32[]{:S(2)}, u32[]{:S(2)}) collective-permute-start(f32[13,8,128]{2,1,0:T(8,128)S(1)} %get-tuple-element.31), channel_id=1, source_target_pairs={{8,0},{0,8},{9,1},{1,9},{10,2},{2,10},{11,3},{3,11},{12,4},{4,12},... | collective-permute-start | bytes 159752 | tf_op jit(solution)/shard_map/ppermute | solution.py:613
  23.3 3.5 %collective-permute-done.4.refs_7_.corner_ref.refs_5_.refs_6_ = f32[8,1408]{1,0:T(8,128)S(1)} collective-permute-done((f32[8,1408]{1,0:T(8,128)S(1)}, f32[8,1408]{1,0:T(8,128)S(1)}, u32[]{:S(2)}, u32[]{:S(2)}) %collective-permute-start.4) | collective-permute-done | bytes 45088 | tf_op jit(solution)/shard_map/ppermute | solution.py:615
  26.8 2.2 %exchange.3 = (f32[2,1,16,128]{3,2,1,0:T(8,128)S(1)}, f32[32,8,128]{2,1,0:T(8,128)}, f32[96,8,128]{2,1,0:T(8,128)S(1)}) custom-call(f32[2,3,16,128]{3,2,1,0:T(8,128)S(1)} %slice.18.late_ref, f32[32,8,128]{2,1,0:T(8,128)S(1)} %all-to-all-done.recv_ref, f32[8,16,128]{2,1,0:T(8,128)S(1)} %pad_maximum_fusion.refs_0_, ...), custom_call_target="tpu_custom_call", output_to_operand_aliasing={{2}: (10, {})} | custom-call | bytes 3000000 | tf_op jit(solution)/shard_map/exchange/pallas_call | solution.py:474
  29.8 3.9 %all-to-all-start.1 = ((f32[32,8,128]{2,1,0:T(8,128)}), f32[32,8,128]{2,1,0:T(8,128)S(1)}, u32[]{:S(2)}, u32[]{:S(2)}) async-start(f32[32,8,128]{2,1,0:T(8,128)} %get-tuple-element.36), calls=%async_computation.1 | async-start | bytes 262144 | tf_op jit(solution)/shard_map/all_to_all | solution.py:563
  33.7 1.8 %collective-permute-start.5 = (f32[96,8,128]{2,1,0:T(8,128)}, f32[96,8,128]{2,1,0:T(8,128)S(1)}, u32[]{:S(2)}, u32[]{:S(2)}) collective-permute-start(f32[96,8,128]{2,1,0:T(8,128)} %copy-done.6), channel_id=1, source_target_pairs={{8,0},{0,8},{9,1},{1,9},{10,2},{2,10},{11,3},{3,11},{12,4},{4,12},... | collective-permute-start | bytes 1179656 | tf_op jit(solution)/shard_map/ppermute | solution.py:631
  35.6 0.8 %early_levels.1.refs_5_ = f32[25,16,128]{2,1,0:T(8,128)S(1)} custom-call(f32[2,72,16,128]{3,2,1,0:T(8,128)S(1)} %bitcast.13, f32[71,16,128]{2,1,0:T(8,128)S(1)} %bitcast.17, f32[2,16,128]{2,1,0:T(8,128)S(1)} %bitcast.22, f32[13,8,128]{2,1,0:T(8,128)S(1)} %collective-permute-done.2.refs_5_.rows_ref.refs_2_.refs_3_, ...), custom_call_target="tpu_custom_call" | custom-call | bytes 6000000 | tf_op jit(solution)/shard_map/early_levels/pallas_call | solution.py:474
  36.3 5.6 %all-to-all-done.1.recv_ref = f32[32,8,128]{2,1,0:T(8,128)S(1)} async-done(((f32[32,8,128]{2,1,0:T(8,128)}), f32[32,8,128]{2,1,0:T(8,128)S(1)}, u32[]{:S(2)}, u32[]{:S(2)}) %all-to-all-start.1) | async-done | bytes 131104 | tf_op jit(solution)/shard_map/all_to_all | solution.py:563
  41.9 2.2 %exchange.4 = (f32[2,2,16,128]{3,2,1,0:T(8,128)S(1)}, f32[32,8,128]{2,1,0:T(8,128)}) custom-call(f32[2,1,16,128]{3,2,1,0:T(8,128)S(1)} %get-tuple-element.35.late_ref, f32[32,8,128]{2,1,0:T(8,128)S(1)} %all-to-all-done.1.recv_ref, f32[8,16,128]{2,1,0:T(8,128)S(1)} %pad_maximum_fusion.refs_0_, f32[2,16,128]{2,1,0:T(8,128)S(1)} %collective-permute-done.refs_1_, ...), custom_call_target="tpu_custom_call" | custom-call | bytes 3000000 | tf_op jit(solution)/shard_map/exchange/pallas_call | solution.py:474
  44.1 2.6 %all-to-all-start.2 = ((f32[32,8,128]{2,1,0:T(8,128)}), f32[32,8,128]{2,1,0:T(8,128)S(1)}, u32[]{:S(2)}, u32[]{:S(2)}) async-start(f32[32,8,128]{2,1,0:T(8,128)} %get-tuple-element.38.after_ref), calls=%async_computation.2 | async-start | bytes 262144 | tf_op jit(solution)/shard_map/all_to_all | solution.py:563
  46.7 3.2 %deep_levels.2 = (f32[2,72,16,128]{3,2,1,0:T(8,128)}, f32[8,128]{1,0:T(8,128)S(1)}) custom-call(f32[32,8,128]{2,1,0:T(8,128)} %get-tuple-element.38.after_ref, f32[2,72,16,128]{3,2,1,0:T(8,128)S(1)} %bitcast.14, f32[71,16,128]{2,1,0:T(8,128)S(1)} %bitcast.18, f32[2,16,128]{2,1,0:T(8,128)S(1)} %bitcast.23, ...), custom_call_target="tpu_custom_call" | custom-call | bytes 12000000 | tf_op jit(solution)/shard_map/deep_levels/pallas_call | solution.py:474
  49.8 5.0 %all-to-all-done.2.recv_ref = f32[32,8,128]{2,1,0:T(8,128)S(1)} async-done(((f32[32,8,128]{2,1,0:T(8,128)}), f32[32,8,128]{2,1,0:T(8,128)S(1)}, u32[]{:S(2)}, u32[]{:S(2)}) %all-to-all-start.2) | async-done | bytes 131104 | tf_op jit(solution)/shard_map/all_to_all | solution.py:563
  54.8 2.2 %exchange.5 = (f32[2,3,16,128]{3,2,1,0:T(8,128)S(1)}, f32[32,8,128]{2,1,0:T(8,128)}) custom-call(f32[2,2,16,128]{3,2,1,0:T(8,128)S(1)} %get-tuple-element.37.late_ref, f32[32,8,128]{2,1,0:T(8,128)S(1)} %all-to-all-done.2.recv_ref, f32[8,16,128]{2,1,0:T(8,128)S(1)} %pad_maximum_fusion.refs_0_, f32[2,16,128]{2,1,0:T(8,128)S(1)} %collective-permute-done.refs_1_, ...), custom_call_target="tpu_custom_call" | custom-call | bytes 3000000 | tf_op jit(solution)/shard_map/exchange/pallas_call | solution.py:474
  57.0 2.6 %all-to-all-start.3 = ((f32[32,8,128]{2,1,0:T(8,128)}), f32[32,8,128]{2,1,0:T(8,128)S(1)}, u32[]{:S(2)}, u32[]{:S(2)}) async-start(f32[32,8,128]{2,1,0:T(8,128)} %get-tuple-element.42.after_ref), calls=%async_computation.3 | async-start | bytes 262144 | tf_op jit(solution)/shard_map/all_to_all | solution.py:563
  59.6 3.2 %deep_levels.3 = (f32[2,72,16,128]{3,2,1,0:T(8,128)}, f32[8,128]{1,0:T(8,128)}) custom-call(f32[32,8,128]{2,1,0:T(8,128)} %get-tuple-element.42.after_ref, f32[2,72,16,128]{3,2,1,0:T(8,128)S(1)} %bitcast.15, f32[2,72,16,128]{3,2,1,0:T(8,128)} %get-tuple-element.43.refs_0_, f32[71,16,128]{2,1,0:T(8,128)S(1)} %bitcast.19, ...), custom_call_target="tpu_custom_call", output_to_operand_aliasing={{0}: (2, {})} | custom-call | bytes 12000000 | tf_op jit(solution)/shard_map/deep_levels/pallas_call | solution.py:474
  62.7 5.0 %all-to-all-done.3.recv_ref = f32[32,8,128]{2,1,0:T(8,128)S(1)} async-done(((f32[32,8,128]{2,1,0:T(8,128)}), f32[32,8,128]{2,1,0:T(8,128)S(1)}, u32[]{:S(2)}, u32[]{:S(2)}) %all-to-all-start.3) | async-done | bytes 131104 | tf_op jit(solution)/shard_map/all_to_all | solution.py:563
  67.7 1.2 %last_exchange.1 = f32[2,72,16,128]{3,2,1,0:T(8,128)} custom-call(f32[2,3,16,128]{3,2,1,0:T(8,128)S(1)} %get-tuple-element.41.late_ref, f32[32,8,128]{2,1,0:T(8,128)S(1)} %all-to-all-done.3.recv_ref, f32[8,16,128]{2,1,0:T(8,128)S(1)} %pad_maximum_fusion.refs_0_, f32[2,16,128]{2,1,0:T(8,128)S(1)} %collective-permute-done.refs_1_, ...), custom_call_target="tpu_custom_call", output_to_operand_aliasing={{}: (8, {})} | custom-call | bytes 3000000 | tf_op jit(solution)/shard_map/last_exchange/pallas_call | solution.py:474
  (28 shorter events, 5.7 us)
Async XLA Ops:
  0.7 11.0 %collective-permute-start.1 = (f32[2,16,128]{2,1,0:T(8,128)S(1)}, f32[2,16,128]{2,1,0:T(8,128)S(1)}, u32[]{:S(2)}, u32[]{:S(2)}) collective-permute-start(f32[2,16,128]{2,1,0:T(8,128)S(1)} %pad_maximum_fusion.1), channel_id=1, source_target_pairs={{0,8},{8,0},{1,9},{9,1},{2,10},{10,2},{3,11},{11,3},{4,12},{12,4},... | collective-permute-start | bytes 49160 | tf_op jit(solution)/shard_map/ppermute | solution.py:560
  3.7 8.1 %collective-permute-start = (f32[2,16,128]{2,1,0:T(8,128)S(1)}, f32[2,16,128]{2,1,0:T(8,128)S(1)}, u32[]{:S(2)}, u32[]{:S(2)}) collective-permute-start(f32[2,16,128]{2,1,0:T(8,128)S(1)} %pad_maximum_fusion.1), channel_id=1, source_target_pairs={{0,1},{1,2},{2,3},{3,4},{4,5},{5,6},{6,7},{7,0},{8,9},{9,10},{10,1... | collective-permute-start | bytes 49160 | tf_op jit(solution)/shard_map/ppermute | solution.py:559
  6.7 0.7 copy-start.7
  8.0 1.3 %copy-start = (f32[1,2,72,16,128]{4,3,2,1,0:T(8,128)S(1)}, f32[1,2,72,16,128]{4,3,2,1,0:T(8,128)}, u32[]{:S(2)}) copy-start(f32[1,2,72,16,128]{4,3,2,1,0:T(8,128)} %param.6) | copy-start | bytes 3538948
  9.3 1.1 %copy-start.2 = (f32[1,71,16,128]{3,2,1,0:T(8,128)S(1)}, f32[1,71,16,128]{3,2,1,0:T(8,128)}, u32[]{:S(2)}) copy-start(f32[1,71,16,128]{3,2,1,0:T(8,128)} %param.8) | copy-start | bytes 1744900
  10.4 0.7 %copy-start.4 = (f32[1,2,16,128]{3,2,1,0:T(8,128)S(1)}, f32[1,2,16,128]{3,2,1,0:T(8,128)}, u32[]{:S(2)}) copy-start(f32[1,2,16,128]{3,2,1,0:T(8,128)} %param.7) | copy-start | bytes 49156
  11.8 23.8 %copy-start.1 = (f32[1,2,72,16,128]{4,3,2,1,0:T(8,128)S(1)}, f32[1,2,72,16,128]{4,3,2,1,0:T(8,128)}, u32[]{:S(2)}) copy-start(f32[1,2,72,16,128]{4,3,2,1,0:T(8,128)} %param.6) | copy-start | bytes 3538948
  11.8 23.8 %copy-start.3 = (f32[1,71,16,128]{3,2,1,0:T(8,128)S(1)}, f32[1,71,16,128]{3,2,1,0:T(8,128)}, u32[]{:S(2)}) copy-start(f32[1,71,16,128]{3,2,1,0:T(8,128)} %param.8) | copy-start | bytes 1744900
  11.8 23.8 %copy-start.5 = (f32[1,2,16,128]{3,2,1,0:T(8,128)S(1)}, f32[1,2,16,128]{3,2,1,0:T(8,128)}, u32[]{:S(2)}) copy-start(f32[1,2,16,128]{3,2,1,0:T(8,128)} %param.7) | copy-start | bytes 49156
  13.1 13.7 %all-to-all-start = ((f32[32,8,128]{2,1,0:T(8,128)}), f32[32,8,128]{2,1,0:T(8,128)S(1)}, u32[]{:S(2)}, u32[]{:S(2)}) async-start(f32[32,8,128]{2,1,0:T(8,128)} %get-tuple-element.30), calls=%async_computation | async-start | bytes 262144 | tf_op jit(solution)/shard_map/all_to_all | solution.py:563
  18.3 8.5 %collective-permute-start.3 = (f32[16,1408]{1,0:T(8,128)S(1)}, f32[16,1408]{1,0:T(8,128)S(1)}, u32[]{:S(2)}, u32[]{:S(2)}) collective-permute-start(f32[16,1408]{1,0:T(8,128)S(1)} %get-tuple-element.32), channel_id=1, source_target_pairs={{1,0},{2,1},{3,2},{4,3},{5,4},{6,5},{7,6},{0,7},{9,8},{10,9},{11,1... | collective-permute-start | bytes 270344 | tf_op jit(solution)/shard_map/ppermute | solution.py:614
  21.7 5.1 %collective-permute-start.2 = (f32[13,8,128]{2,1,0:T(8,128)S(1)}, f32[13,8,128]{2,1,0:T(8,128)S(1)}, u32[]{:S(2)}, u32[]{:S(2)}) collective-permute-start(f32[13,8,128]{2,1,0:T(8,128)S(1)} %get-tuple-element.31), channel_id=1, source_target_pairs={{8,0},{0,8},{9,1},{1,9},{10,2},{2,10},{11,3},{3,11},{12,4},{4,12},... | collective-permute-start | bytes 159752 | tf_op jit(solution)/shard_map/ppermute | solution.py:613
  23.2 3.6 %collective-permute-start.4 = (f32[8,1408]{1,0:T(8,128)S(1)}, f32[8,1408]{1,0:T(8,128)S(1)}, u32[]{:S(2)}, u32[]{:S(2)}) collective-permute-start(f32[8,1408]{1,0:T(8,128)S(1)} %get-tuple-element.33), channel_id=1, source_target_pairs={{9,0},{10,1},{11,2},{12,3},{13,4},{14,5},{15,6},{8,7},{1,8},{2,9},... | collective-permute-start | bytes 135176 | tf_op jit(solution)/shard_map/ppermute | solution.py:615
  29.0 0.7 %copy-start.6 = (f32[96,8,128]{2,1,0:T(8,128)}, f32[96,8,128]{2,1,0:T(8,128)S(1)}, u32[]{:S(2)}) copy-start(f32[96,8,128]{2,1,0:T(8,128)S(1)} %get-tuple-element.39) | copy-start | bytes 1179652
  29.8 12.1 %all-to-all-start.1 = ((f32[32,8,128]{2,1,0:T(8,128)}), f32[32,8,128]{2,1,0:T(8,128)S(1)}, u32[]{:S(2)}, u32[]{:S(2)}) async-start(f32[32,8,128]{2,1,0:T(8,128)} %get-tuple-element.36), calls=%async_computation.1 | async-start | bytes 262144 | tf_op jit(solution)/shard_map/all_to_all | solution.py:563
  33.7 12.9 %collective-permute-start.5 = (f32[96,8,128]{2,1,0:T(8,128)}, f32[96,8,128]{2,1,0:T(8,128)S(1)}, u32[]{:S(2)}, u32[]{:S(2)}) collective-permute-start(f32[96,8,128]{2,1,0:T(8,128)} %copy-done.6), channel_id=1, source_target_pairs={{8,0},{0,8},{9,1},{1,9},{10,2},{2,10},{11,3},{3,11},{12,4},{4,12},... | collective-permute-start | bytes 1179656 | tf_op jit(solution)/shard_map/ppermute | solution.py:631
  44.1 10.7 %all-to-all-start.2 = ((f32[32,8,128]{2,1,0:T(8,128)}), f32[32,8,128]{2,1,0:T(8,128)S(1)}, u32[]{:S(2)}, u32[]{:S(2)}) async-start(f32[32,8,128]{2,1,0:T(8,128)} %get-tuple-element.38.after_ref), calls=%async_computation.2 | async-start | bytes 262144 | tf_op jit(solution)/shard_map/all_to_all | solution.py:563
  57.0 10.7 %all-to-all-start.3 = ((f32[32,8,128]{2,1,0:T(8,128)}), f32[32,8,128]{2,1,0:T(8,128)S(1)}, u32[]{:S(2)}, u32[]{:S(2)}) async-start(f32[32,8,128]{2,1,0:T(8,128)} %get-tuple-element.42.after_ref), calls=%async_computation.3 | async-start | bytes 262144 | tf_op jit(solution)/shard_map/all_to_all | solution.py:563

commit v7 on v6

--- a/solution.py
+++ b/solution.py
@@ -17,6 +17,9 @@
 ZONAL, MERIDIONAL, KAPPA = 0, 1, 2
 COUPLING = KAPPA + STEPS
 WET = COUPLING + 1
+WEST = WET + 1
+SOUTH = WEST + 2
+LATE = SOUTH + 2
 
 
 class Place:
@@ -25,6 +28,7 @@
         lat, lon = lax.axis_index("lat"), lax.axis_index("lon")
         self.model = lax.axis_index("mp")
         self.east = lat * n_lon + lax.rem(lon + 1, n_lon)
+        self.west = lat * n_lon + lax.rem(lon + n_lon - 1, n_lon)
         self.north = lax.rem(lat + 1, n_lat) * n_lon + lon
         self.has_north = lat < n_lat - 1
 
@@ -62,21 +66,17 @@
     return total
 
 
-def halo_kernel(fields_ref, kappa_ref, courant_ref, upper_ref, deep_ref, columns_ref, corner_ref):
+def pack_halo(fields_ref, kappa_ref, courant_ref, rows_ref, columns_ref):
     tracers, levels, rows, cols = fields_ref.shape
     lane = lane_iota((rows, cols))
     upper = row_iota((2 * STEPS, cols)) < STEPS
-    upper_pairs, deep_pairs = UPPER // 2, (levels - UPPER) // 2
+    pairs = levels // 2
 
     def first_rows(read, count, which):
-        for pair in range(levels // 2):
+        for pair in range(pairs):
             one = read(2 * pair)
             two = read(2 * pair + 1) if 2 * pair + 1 < count else jnp.zeros_like(one)
-            both = jnp.where(upper, one, pltpu.roll(two, STEPS, 0))
-            if pair < upper_pairs:
-                upper_ref[which * upper_pairs + pair] = both
-            else:
-                deep_ref[which * deep_pairs + pair - upper_pairs] = both
+            rows_ref[which * pairs + pair] = jnp.where(upper, one, pltpu.roll(two, STEPS, 0))
 
     def first_columns(read, count, start):
         for tile in range(-(-levels // PACKED)):
@@ -86,7 +86,6 @@
                 gathered = jnp.where(lane // STEPS == place, lane_roll(read(k), place * STEPS), gathered)
             spot = slice((start + tile) * cols, (start + tile + 1) * cols)
             columns_ref[:, spot] = gathered
-            corner_ref[:, spot] = gathered[0 : 2 * STEPS]
 
     tiles = -(-levels // PACKED)
     for tracer in range(tracers):
@@ -94,7 +93,7 @@
         first_columns(lambda k: fields_ref[tracer, k], levels, tracer * tiles)
     first_rows(lambda k: kappa_ref[k, 0 : 2 * STEPS, :], levels - 1, tracers)
     first_columns(lambda k: kappa_ref[k], levels - 1, tracers * tiles)
-    upper_ref[(tracers + 1) * upper_pairs] = jnp.where(
+    rows_ref[(tracers + 1) * pairs] = jnp.where(
         upper,
         courant_ref[0, 0 : 2 * STEPS, :],
         pltpu.roll(courant_ref[1, 0 : 2 * STEPS, :], STEPS, 0),
@@ -107,13 +106,12 @@
             shift *= 2
         spot = slice(((tracers + 1) * tiles + which) * cols, ((tracers + 1) * tiles + which + 1) * cols)
         columns_ref[:, spot] = repeated
-        corner_ref[:, spot] = repeated[0 : 2 * STEPS]
 
 
 def wide_steps(refs, tracer, levels, tracers, all_levels, first_field, store, each_step):
-    kappa_ref, courant_ref, rows_refs, columns_ref, corner_ref, state = refs
+    kappa_ref, courant_ref, rows_ref, columns_ref, state = refs
     rows, cols = courant_ref.shape[1:]
-    upper_pairs, deep_pairs = UPPER // 2, (all_levels - UPPER) // 2
+    pairs = all_levels // 2
     tiles = -(-all_levels // PACKED)
     used = -(-levels // PACKED)
     tall = rows + 2 * STEPS
@@ -121,20 +119,17 @@
     lane = lane_iota((tall, cols))
 
     def with_rows(block, which, k):
-        if k < UPPER:
-            extra = rows_refs[0][which * upper_pairs + k // 2]
-        else:
-            extra = rows_refs[1][which * deep_pairs + (k - UPPER) // 2]
+        extra = rows_ref[which * pairs + k // 2]
         if k % 2:
             extra = pltpu.roll(extra, STEPS, 0)
         return jnp.concatenate([block, jnp.where(has_north, extra, 0.0)], axis=0)
 
     def strip(index):
         spot = slice(index * cols, (index + 1) * cols)
-        corner = jnp.where(has_north, corner_ref[:, spot], 0.0)
+        corner = jnp.where(has_north, rows_ref[(tracers + 1) * pairs + 1 + index], 0.0)
         return jnp.concatenate([columns_ref[:, spot], corner], axis=0)
 
-    last = rows_refs[0][(tracers + 1) * upper_pairs]
+    last = rows_ref[(tracers + 1) * pairs]
     last = jnp.where(has_north, last, 0.0)
     zonal = jnp.concatenate([courant_ref[0], last], axis=0)
     meridional = jnp.concatenate([courant_ref[1], pltpu.roll(last, STEPS, 0)], axis=0)
@@ -211,17 +206,17 @@
 
 
 def early_kernel(
-    fields_ref, kappa_ref, courant_ref, rows_ref, columns_ref, corner_ref, early_ref, state, *, all_levels
+    fields_ref, kappa_ref, courant_ref, rows_ref, columns_ref, early_ref, state, *, all_levels
 ):
     tracers, levels, rows, cols = fields_ref.shape
-    refs = (kappa_ref, courant_ref, (rows_ref,), columns_ref, corner_ref, state)
+    refs = (kappa_ref, courant_ref, rows_ref, columns_ref, state)
     for tracer in range(tracers):
 
         def each_step(step, zonal, meridional, side_zonal, side):
-            for j in range(2):
+            for j in range(2 if step >= 2 else 0):
                 k = step + j
                 field = state[k]
-                line = ((step - 1) * tracers + tracer) * 2 + j
+                line = ((step - 2) * tracers + tracer) * 2 + j
                 early_ref[2 * line] = field[:rows]
                 early_ref[2 * line + 1] = lane_roll(side_zonal * side[0], cols - 1 - k * STEPS)[:rows]
                 early_ref[early_ref.shape[0] - 1, line : line + 1, :] = (
@@ -235,7 +230,7 @@
 
 
 def deep_kernel(after_ref, fields_ref, *refs, tracer, tracers):
-    kappa_ref, courant_ref, *rows_refs, columns_ref, corner_ref, out_ref, token_ref, state = refs[-9:]
+    kappa_ref, courant_ref, rows_ref, columns_ref, out_ref, token_ref, state = refs[-7:]
     levels = fields_ref.shape[1]
 
     def store(k, value):
@@ -245,15 +240,15 @@
     for k in range(STEPS):
         out_ref[0, k] = jnp.zeros(out_ref.shape[2:], F32)
     wide_steps(
-        (kappa_ref, courant_ref, rows_refs, columns_ref, corner_ref, state),
+        (kappa_ref, courant_ref, rows_ref, columns_ref, state),
         tracer, levels, tracers, levels, lambda k: fields_ref[0, k], store, None,
     )
     token_ref[...] = jnp.zeros(token_ref.shape, F32)
 
 
-def send_surface(late, below, static_refs, table_ref, send_ref, deep_rows):
-    static_ref, west_ref, south_ref, _ = static_refs
-    model = Place().model
+def send_surface(late, below, static_ref, table_ref, send_ref, deep_rows):
+    here = Place()
+    model = here.model
     tracers = len(late)
     zonal, meridional = static_ref[ZONAL], static_ref[MERIDIONAL]
     weight = (1.0 - zonal) - meridional
@@ -266,9 +261,9 @@
     group = lane // TILE
     tiles, edge_north, edge_east = [], [], []
     place = lane == (row % groups) * TILE + (TILE - 1) - row // groups
-    west_a = lane_roll(west_ref[0], 1)
-    west_b = lane_roll(west_ref[1], 1)
-    south_a, south_b = south_ref[0], south_ref[1]
+    west_a = lane_roll(static_ref[WEST], 1)
+    west_b = lane_roll(static_ref[WEST + 1], 1)
+    south_a, south_b = static_ref[SOUTH], static_ref[SOUTH + 1]
     own_north, own_east = [], jnp.zeros((rows, cols), F32)
     for tracer in range(tracers):
         parts = []
@@ -277,8 +272,8 @@
             east = jnp.where(lane == cols - 1, 0.0, lane_roll(eastward, cols - 1))
             north = jnp.where(row == rows - 1, 0.0, next_row(northward))
             parts.append((eastward, northward, (weight * field + east) + north))
-        (east0, north0, here), (east1, north1, under) = parts
-        mixed = here + kappa * (under - here)
+        (east0, north0, over), (east1, north1, under) = parts
+        mixed = over + kappa * (under - over)
         scaled = coupling * mixed
         edge_north.append(south_a[rows - 1 : rows] * north0[0:1] + south_b[rows - 1 : rows] * north1[0:1])
         column = west_a * east0 + west_b * east1
@@ -311,24 +306,25 @@
     edges = jnp.concatenate(
         [empty, edge_north[0], edge_east[0], empty, edge_north[1], edge_east[1]], axis=0
     )
-    own = own_north + [jnp.zeros((1, cols), F32)] * (2 * SLAB - 1 - len(own_north))
-    own = jnp.concatenate(own + [jnp.sum(own_east, axis=0, keepdims=True)], axis=0)
+    empty = [jnp.zeros((1, cols), F32)] * (2 * SLAB - 1)
+    own_north = jnp.concatenate((own_north + empty)[: 2 * SLAB], axis=0)
+    own_east = jnp.concatenate(empty + [jnp.sum(own_east, axis=0, keepdims=True)], axis=0)
     for pair in range(devices // 2):
         one, two = (half[pair * 2 * SLAB : (pair + 1) * 2 * SLAB] for half in (first, second))
         there = (1 - model) * devices + 2 * pair
         send_ref[there] = jnp.where(upper, one, pltpu.roll(two, SLAB, 0)) + edges
         send_ref[there + 1] = jnp.where(upper, pltpu.roll(one, SLAB, 0), two) + edges
-        send_ref[model * devices + 2 * pair] = own
-        send_ref[model * devices + 2 * pair + 1] = own
-
-
-def receive_surface(recv_ref, table_ref, static_refs, surface):
+        send_ref[model * devices + 2 * pair] = own_north
+        send_ref[model * devices + 2 * pair + 1] = own_north
+    send_ref[model * devices + here.west] = own_east
+
+
+def receive_surface(recv_ref, table_ref, static_ref, surface):
     devices = recv_ref.shape[0] // 2
     rows, cols = surface[0].shape
     groups = cols // TILE
     tracers = len(surface)
     count = rows * groups
-    static_ref, _, _, place_ref = static_refs
     other = (1 - Place().model) * devices
     upper = row_iota((2 * SLAB, cols)) < SLAB
     first, second = [], []
@@ -349,7 +345,7 @@
             total = None
             for kind in range(3):
                 start = kind * count + c * rows
-                place = place_ref[kind * groups + c]
+                place = static_ref[LATE + tracers * STEPS + kind * groups + c]
                 term = jnp.where(
                     place > 0, found[start : start + rows, tracer * cols : (tracer + 1) * cols], 0.0
                 )
@@ -405,34 +401,46 @@
 
 
 def early_levels(step, early_ref, tracer, tracers):
-    if step == 0:
+    if step < 2:
         return []
     found = []
     for j in range(2):
-        line = ((step - 1) * tracers + tracer) * 2 + j
+        line = ((step - 2) * tracers + tracer) * 2 + j
         norths = early_ref[early_ref.shape[0] - 1]
         found.append((early_ref[2 * line], norths[line : line + 1], early_ref[2 * line + 1]))
     return found
 
 
-def first_send_kernel(late_ref, *refs, deep_rows, carried):
-    *static_refs, table_ref = refs[:5]
-    send_ref = refs[5 + carried]
-    tracers, levels = late_ref.shape[:2]
-    late = [[late_ref[tracer, k] for k in range(levels)] for tracer in range(tracers)]
-    send_surface(late, [values[1] for values in late], static_refs, table_ref, send_ref, deep_rows)
-
-
-def exchange_kernel(late_ref, recv_ref, *refs, step, deep_rows, unread, carried=0):
-    static_refs, table_ref, refs = refs[:4], refs[4], refs[5:]
-    early_ref, refs = (refs[0], refs[1:]) if step > 0 else (None, refs)
-    refs = refs[unread:] if step == STEPS - 1 else refs[unread + carried : unread + carried + 2]
-    tracers = late_ref.shape[0]
-    late = [[late_ref[tracer, k] for k in range(late_ref.shape[1])] for tracer in range(tracers)]
+def first_send_kernel(west_ref, south_ref, table_ref, static_in, send_ref, static_ref, *, tracers, deep_rows):
+    for k in range(2):
+        static_ref[WEST + k] = west_ref[k]
+        static_ref[SOUTH + k] = south_ref[k]
+    late = [[static_in[LATE + tracer * STEPS + k] for k in range(STEPS)] for tracer in range(tracers)]
+    send_surface(late, [values[1] for values in late], static_ref, table_ref, send_ref, deep_rows)
+
+
+def exchange_kernel(static_in, recv_ref, table_ref, *refs, step, tracers, count, deep_rows, unread=0):
+    early_ref, refs = (refs[0], refs[1:]) if step >= 2 else (None, refs)
+    if step == 0:
+        east_ref, _, *refs, rows_ref, sems = refs
+        cols = rows_ref.shape[2]
+        tiles = east_ref.shape[1] // cols
+        corner = [
+            pltpu.make_async_copy(
+                east_ref.at[0 : 2 * STEPS, tile * cols : (tile + 1) * cols],
+                rows_ref.at[rows_ref.shape[0] - tiles + tile],
+                sems.at[tile],
+            )
+            for tile in range(tiles)
+        ]
+        for copy in corner:
+            copy.start()
+    refs = refs[unread:]
+    late = [[static_in[LATE + tracer * STEPS + k] for k in range(count)] for tracer in range(tracers)]
     early = [early_levels(step, early_ref, tracer, tracers) for tracer in range(tracers)]
-    stepped = upper_levels(recv_ref, late, early, static_refs[0])
+    stepped = upper_levels(recv_ref, late, early, static_in)
     surface = [values[0] for values in stepped]
-    surface = receive_surface(recv_ref, table_ref, static_refs, surface)
+    surface = receive_surface(recv_ref, table_ref, static_in, surface)
     for tracer in range(tracers):
         stepped[tracer][0] = surface[tracer]
     if step == STEPS - 1:
@@ -441,19 +449,14 @@
             for k in range(STEPS):
                 out_ref[tracer, k] = stepped[tracer][k]
         return
-    late_out, send_ref = refs
-    kept = late_out.shape[1]
+    static_ref, send_ref = refs
     for tracer in range(tracers):
-        for k in range(kept):
-            late_out[tracer, k] = stepped[tracer][k]
-    send_surface(
-        [values[:kept] for values in stepped],
-        [values[1] for values in stepped],
-        static_refs,
-        table_ref,
-        send_ref,
-        deep_rows,
-    )
+        for k, value in enumerate(stepped[tracer]):
+            static_ref[LATE + tracer * STEPS + k] = value
+    send_surface(stepped, [values[1] for values in stepped], static_in, table_ref, send_ref, deep_rows)
+    if step == 0:
+        for copy in corner:
+            copy.wait()
 
 
 def whole(array):
@@ -467,10 +470,11 @@
 
 
 NEAR = pl.BlockSpec(memory_space=pltpu.VMEM)
+FAR = pl.BlockSpec(memory_space=pltpu.HBM)
 UNREAD = pl.BlockSpec(memory_space=pl.ANY)
 
 
-def call(kernel, operands, specs, out_shape, out_specs, name, grid=(), aliases=None, scratch=(), us=1):
+def call(kernel, operands, specs, out_shape, out_specs, name, grid=(), aliases=None, scratch=(), us=1, mib=16):
     return pl.pallas_call(
         kernel,
         grid=grid,
@@ -481,7 +485,7 @@
         input_output_aliases=aliases or {},
         name=name,
         cost_estimate=pl.CostEstimate(flops=0, bytes_accessed=us * 3_000_000, transcendentals=0),
-        compiler_params=pltpu.CompilerParams(vmem_limit_bytes=16 * 1024 * 1024),
+        compiler_params=pltpu.CompilerParams(vmem_limit_bytes=mib * 1024 * 1024),
     )(*operands)
 
 
@@ -502,10 +506,10 @@
     return lines[0:1], lines[1:2], columns[:, 0:1], columns[:, 1:2]
 
 
-def tables_kernel(partner_ref, table_ref, place_ref, *, rows, groups, n_lat, n_lon):
+def write_tables(partner, table_ref, planes_ref, start, rows, groups, n_lat, n_lon):
     count = rows * groups
     devices = n_lat * n_lon
-    line_target, line_slot, target, slot = tile_order(partner_ref[...], rows, groups)
+    line_target, line_slot, target, slot = tile_order(partner, rows, groups)
     a = lax.broadcasted_iota(jnp.int32, (count, count), 0)
     b = lax.broadcasted_iota(jnp.int32, (count, count), 1)
     same = target == line_target
@@ -543,7 +547,36 @@
     for kind, place in enumerate(places):
         place = place.astype(F32)
         for c in range(groups):
-            place_ref[kind * groups + c] = place[c * rows : (c + 1) * rows]
+            planes_ref[start + kind * groups + c] = place[c * rows : (c + 1) * rows]
+
+
+def prepare_kernel(*refs, n_lat, n_lon):
+    sources, refs = refs[:6], refs[6:]
+    (table_ref, planes_ref, rows_ref, columns_ref), refs = refs[:4], refs[4:]
+    buffers, sems = refs[:6], refs[6]
+    copies = [
+        pltpu.make_async_copy(source, buffer, sems.at[i])
+        for i, (source, buffer) in enumerate(zip(sources, buffers))
+    ]
+    for copy in copies:
+        copy.start()
+    fields, kappa, courant, coupling, mask, partner = buffers
+    tracers, _, rows, cols = fields.shape
+    copies[5].wait()
+    write_tables(partner[...], table_ref, planes_ref, LATE + tracers * STEPS, rows, cols // TILE, n_lat, n_lon)
+    for copy in copies[1:5]:
+        copy.wait()
+    planes_ref[ZONAL] = courant[0]
+    planes_ref[MERIDIONAL] = courant[1]
+    for k in range(STEPS):
+        planes_ref[KAPPA + k] = kappa[k]
+    planes_ref[COUPLING] = coupling[...]
+    planes_ref[WET] = mask[...].astype(F32)
+    copies[0].wait()
+    for tracer in range(tracers):
+        for k in range(STEPS):
+            planes_ref[LATE + tracer * STEPS + k] = fields[tracer, k]
+    pack_halo(fields, kappa, courant, rows_ref, columns_ref)
 
 
 def local(adjoint, courant, diffusivity, coupling, partner, mask):
@@ -563,138 +596,120 @@
         return lax.all_to_all(send, ("mp", "lat", "lon"), split_axis=0, concat_axis=0, tiled=True)
 
     deep_rows = 3 * count
+    width = ((tracers + 1) * -(-levels // PACKED) + 2) * cols
+    sources = (fields, kappa, courant, coupling, mask, partner)
     table_shape = jax.ShapeDtypeStruct(
         (deep_rows + groups * devices * SLAB, max(count, 2 * devices * SLAB)), BF16
     )
-    table, place = call(
-        functools.partial(tables_kernel, rows=rows, groups=groups, n_lat=n_lat, n_lon=n_lon),
-        (partner,),
-        [NEAR],
-        (table_shape, shaped(3 * groups, rows, cols)),
+    planes_shape = shaped(LATE + tracers * STEPS + 3 * groups, rows, cols)
+    north_shape = shaped((tracers + 1) * (levels // 2) + 1 + width // cols, 2 * STEPS, cols)
+    table, planes, north, east = call(
+        functools.partial(prepare_kernel, n_lat=n_lat, n_lon=n_lon),
+        sources,
+        [FAR for _ in sources],
+        (table_shape, planes_shape, north_shape, shaped(rows, width)),
+        (NEAR, NEAR, NEAR, NEAR),
+        "prepare",
+        scratch=[*(pltpu.VMEM(a.shape, a.dtype) for a in sources), pltpu.SemaphoreType.DMA((len(sources),))],
+        us=2,
+        mib=53,
+    )
+    send_shape = shaped(2 * devices, 2 * SLAB, cols)
+    send, planes = call(
+        functools.partial(first_send_kernel, tracers=tracers, deep_rows=deep_rows),
+        (from_west, from_south, table, planes),
+        [NEAR, NEAR, NEAR, NEAR],
+        (send_shape, planes_shape),
         (NEAR, NEAR),
-        "tables",
-    )
-    planes = jnp.concatenate([courant, kappa[:STEPS], coupling[None], mask[None].astype(F32)], axis=0)
-    statics = (planes, from_west, from_south, place, table)
-
-    tiles = -(-levels // PACKED)
-    width = ((tracers + 1) * tiles + 2) * cols
-    halo_shapes = (
-        shaped((tracers + 1) * (UPPER // 2) + 1, 2 * STEPS, cols),
-        shaped((tracers + 1) * ((levels - UPPER) // 2), 2 * STEPS, cols),
-        shaped(rows, width),
-        shaped(2 * STEPS, width),
-    )
-    packed = call(
-        halo_kernel,
-        (fields, kappa, courant),
-        [whole(a) for a in (fields, kappa, courant)],
-        halo_shapes,
-        tuple(whole(a) for a in halo_shapes),
-        "halo",
-        grid=(1,),
-        us=2,
-    )
-    send_shape = shaped(2 * devices, 2 * SLAB, cols)
-    late = fields[:, :3]
-    carried = (packed[0], packed[2], packed[3])
-    send, *carried = call(
-        functools.partial(first_send_kernel, deep_rows=deep_rows, carried=len(carried)),
-        (late, *statics, *carried),
-        [*(NEAR for _ in range(6)), *(UNREAD for _ in carried)],
-        (send_shape, *(shaped(*a.shape) for a in carried)),
-        (NEAR, *(UNREAD for _ in carried)),
         "first_send",
-        aliases={6 + i: 1 + i for i in range(len(carried))},
+        aliases={3: 1},
     )
     recv = exchanged(send)
-    upper, east, corner = carried
-    from_north = [((i + 1) % n_lat, i) for i in range(n_lat)]
-    upper = lax.ppermute(upper, "lat", from_north)
     east = lax.ppermute(east, "lon", [((i + 1) % n_lon, i) for i in range(n_lon)])
-    corner = lax.ppermute(
-        corner,
-        ("lat", "lon"),
-        [
-            (((i + 1) % n_lat) * n_lon + (j + 1) % n_lon, i * n_lon + j)
-            for i in range(n_lat)
-            for j in range(n_lon)
-        ],
-    )
     tall = rows + 2 * STEPS
 
-    early, out, after = (), None, (upper, east, corner)
+    def deep_levels(tracer, before, halo):
+        block = pl.BlockSpec((1, levels, rows, cols), lambda i: (tracer, 0, 0, 0))
+        token = shaped(8, cols)
+        return call(
+            functools.partial(deep_kernel, tracer=tracer, tracers=tracers),
+            (send, fields, *before, *halo),
+            [UNREAD, block, *(UNREAD for _ in before), *(whole(a) for a in halo)],
+            (shaped(*fields.shape), token),
+            (block, whole(token)),
+            "deep_levels",
+            grid=(1,),
+            aliases={2: 0} if before else None,
+            scratch=[pltpu.VMEM((levels, tall, cols), F32)],
+            us=4,
+        )
+
+    reached = (STEPS, STEPS - 1, 2, 3)
     for step in range(STEPS):
         if step > 0:
             recv = exchanged(send)
+        kernel = functools.partial(
+            exchange_kernel, step=step, tracers=tracers, count=reached[step], deep_rows=deep_rows
+        )
+        operands = (planes, recv, table)
+        if step == 0:
+            planes, send, north = call(
+                kernel,
+                (*operands, east, north),
+                [*[NEAR] * 4, UNREAD],
+                (planes_shape, send_shape, north_shape),
+                (NEAR, NEAR, UNREAD),
+                "exchange",
+                aliases={0: 0, 4: 2},
+                scratch=[pltpu.SemaphoreType.DMA((width // cols,))],
+            )
+            north = lax.ppermute(north, "lat", [((i + 1) % n_lat, i) for i in range(n_lat)])
+            halo = (kappa, courant, north, east)
         if step == 1:
-            deep = lax.ppermute(deep, "lat", from_north)
-            early_shape = shaped((STEPS - 1) * tracers * 4 + 1, rows, cols)
-            early = (
-                call(
-                    functools.partial(early_kernel, all_levels=levels),
-                    (fields, kappa, courant, upper, east, corner),
-                    [
-                        top(fields, UPPER),
-                        pl.BlockSpec((UPPER, rows, cols), lambda i: (0, 0, 0)),
-                        *(whole(a) for a in (courant, upper, east, corner)),
-                    ],
-                    early_shape,
-                    whole(early_shape),
-                    "early_levels",
-                    grid=(1,),
-                    scratch=[pltpu.VMEM((UPPER, tall, cols), F32)],
-                    us=2,
-                ),
+            planes, send = call(
+                kernel, operands, [NEAR] * 3, (planes_shape, send_shape), (NEAR, NEAR), "exchange", aliases={0: 0}
             )
-        if step > 1:
-            halo = (kappa, courant, upper, deep, east, corner)
-            for tracer in range(step - 2, tracers if step == STEPS - 1 else step - 1):
-                before = () if out is None else (out,)
-                block = pl.BlockSpec((1, levels, rows, cols), lambda i, tracer=tracer: (tracer, 0, 0, 0))
-                token = shaped(8, cols)
-                out, token = call(
-                    functools.partial(deep_kernel, tracer=tracer, tracers=tracers),
-                    (send, fields, *before, *halo),
-                    [UNREAD, block, *(UNREAD for _ in before), *(whole(a) for a in halo)],
-                    (shaped(*fields.shape), token),
-                    (block, whole(token)),
-                    "deep_levels",
-                    grid=(1,),
-                    aliases={2: 0} if before else None,
-                    scratch=[pltpu.VMEM((levels, tall, cols), F32)],
-                    us=4,
-                )
-            after = (token,)
-        if step == STEPS - 1:
-            after = (out,)
-        operands = (late, recv, *statics, *early, *after)
-        near = len(operands) - len(after)
-        kernel = functools.partial(exchange_kernel, step=step, deep_rows=deep_rows, unread=len(after))
-        if step == STEPS - 1:
+        if step == 2:
+            early_shape = shaped((STEPS - 2) * tracers * 4 + 1, rows, cols)
+            early = call(
+                functools.partial(early_kernel, all_levels=levels),
+                (fields, *halo),
+                [
+                    top(fields, UPPER),
+                    pl.BlockSpec((UPPER, rows, cols), lambda i: (0, 0, 0)),
+                    *(whole(a) for a in halo[1:]),
+                ],
+                early_shape,
+                whole(early_shape),
+                "early_levels",
+                grid=(1,),
+                scratch=[pltpu.VMEM((UPPER, tall, cols), F32)],
+                us=2,
+            )
+            out, token = deep_levels(0, (), halo)
+            planes, send = call(
+                functools.partial(kernel, unread=1),
+                (*operands, early, token),
+                [*[NEAR] * 4, UNREAD],
+                (planes_shape, send_shape),
+                (NEAR, NEAR),
+                "exchange",
+                aliases={0: 0},
+            )
+        if step == 3:
+            for tracer in range(1, tracers):
+                out, token = deep_levels(tracer, (out,), halo)
+            operands = (*operands, early)
             return call(
-                kernel,
-                operands,
-                [*(whole(a) for a in operands[:near]), UNREAD],
+                functools.partial(kernel, unread=1),
+                (*operands, out),
+                [*(whole(a) for a in operands), UNREAD],
                 shaped(*fields.shape),
                 top(fields, STEPS),
                 "last_exchange",
                 grid=(1,),
-                aliases={near: 0},
+                aliases={len(operands): 0},
             )[None]
-        carry = (packed[1],) if step == 0 else ()
-        late, send, *carry = call(
-            functools.partial(kernel, carried=len(carry)),
-            (*operands, *carry),
-            [*(NEAR for _ in range(near)), *(UNREAD for _ in (*after, *carry))],
-            (shaped(tracers, step + 1, rows, cols), send_shape, *(shaped(*a.shape) for a in carry)),
-            (NEAR, NEAR, *(UNREAD for _ in carry)),
-            "exchange",
-            aliases={len(operands): 2} if carry else None,
-        )
-        if carry:
-            (deep,) = carry
-        after = ()
 
 
 def solution(mesh):

time: 69.7 us -> 65.8 us (0.944)
  local copies, waits for them, and re-layouts: 6.02 us -> 2.78 us
  starting transfers between devices: 24 us -> 21.8 us
  Pallas kernels: 17.5 us -> 19.4 us
  other arithmetic: 2.16 us -> 0.72 us
  waiting for transfers between devices: 19.1 us -> 20.3 us
    ppermute x1, waiting for transfers between devices: 0.01 us -> 2.14 us  [local(): lax.ppermute(east, 'lon', [((i + 1) % n_lon, i) for i in range(n_lon)])]
    pallas_call x10 -> x9, Pallas kernels: 17.5 us -> 19.4 us  [call(): pl.pallas_call(kernel, grid=grid, in_specs=specs, out_shape=out_shape, ou...]
    unnamed x16 -> x14, local copies, waits for them, and re-layouts: 4.46 us -> 2.78 us
    slice x2 -> x0, local copies, waits for them, and re-layouts: 1.56 us -> none  [the longest x1 0.8 us: local(): late = fields[:, :3]]
    ppermute x3 -> x1, starting transfers between devices: 3.38 us -> 1.83 us  [local(): lax.ppermute(north, 'lat', [((i + 1) % n_lat, i) for i in range(n_lat)])]
    ppermute x3 -> x1, waiting for transfers between devices: 3.54 us -> 2.02 us  [local(): lax.ppermute(north, 'lat', [((i + 1) % n_lat, i) for i in range(n_lat)])]
    concatenate x1 -> x0, other arithmetic: 0.74 us -> none  [local(): jnp.concatenate([courant, kappa[:STEPS], coupling[None], mask[None].astyp...]
    convert_element_type x1 -> x0, other arithmetic: 0.7 us -> none  [local(): mask[None].astype(F32)]
  transfers between devices with their start and end apart: 10 -> 8, of which waited for: 4 -> 6; matrix products, arithmetic and copies ran while one was open for 4% -> 0% of each run, Pallas kernels for 15% -> 19%
where the time goes in v7:
time: 65.8 us; the launch traced here: 65.1 us
  starting transfers between devices  21.8 us (33%)
  waiting for transfers between devices  20.3 us (31%)
  Pallas kernels  19.4 us (29%)
  local copies, waits for them, and re-layouts  2.78 us (4%)
  other arithmetic  0.72 us (1%)
    pallas_call x9, Pallas kernels, call(): pl.pallas_call(kernel, grid=grid, in_specs=specs, out_shape=out_shape, ou...  19.4 us
    all_to_all x4, waiting for transfers between devices, exchanged(): lax.all_to_all(send, ('mp', 'lat', 'lon'), split_axis=0, concat_axis=0, t...  16.2 us
    all_to_all x4, starting transfers between devices, exchanged(): lax.all_to_all(send, ('mp', 'lat', 'lon'), split_axis=0, concat_axis=0, t...  13.5 us
    ppermute x1, starting transfers between devices, local(): lax.ppermute(east, 'lon', [((i + 1) % n_lon, i) for i in range(n_lon)])  3.43 us
    ppermute x1, starting transfers between devices, local(): lax.ppermute(share, 'lat', [(i, (i + 1) % n_lat) for i in range(n_lat)])  2.97 us
    unnamed x14, local copies, waits for them, and re-layouts  2.78 us
    ppermute x1, waiting for transfers between devices, local(): lax.ppermute(east, 'lon', [((i + 1) % n_lon, i) for i in range(n_lon)])  2.14 us
    ppermute x1, waiting for transfers between devices, local(): lax.ppermute(north, 'lat', [((i + 1) % n_lat, i) for i in range(n_lat)])  2.02 us
  transfers between devices with their start and end apart: 8, of which 6 were waited for; matrix products, arithmetic and copies ran while one was open for 0% of the time, Pallas kernels for 19%

profile of v7, /device:TPU:0, one launch (start us, length us, event | category | flops | bytes accessed | tf_op | source)
XLA Modules:
  0.0 65.1 jit_solution(4611365420382904774)
XLA Ops:
  0.0 0.7 %fusion = (f32[1,16,128]{2,1,0:T(8,128)S(1)}, f32[1,16,128]{2,1,0:T(8,128)S(1)}) fusion(f32[1,16,128]{2,1,0:T(8,128)} %param.9, f32[1,71,16,128]{3,2,1,0:T(8,128)} %param.8), kind=kLoop, calls=%fused_computation.3 | loop fusion | flops 6144 | bytes 32768 | tf_op jit(solution)/shard_map/mul | solution.py:591
  0.7 3.0 %collective-permute-start.1 = (f32[2,16,128]{2,1,0:T(8,128)S(1)}, f32[2,16,128]{2,1,0:T(8,128)S(1)}, u32[]{:S(2)}, u32[]{:S(2)}) collective-permute-start(f32[2,16,128]{2,1,0:T(8,128)S(1)} %pad_maximum_fusion), channel_id=1, source_target_pairs={{0,8},{8,0},{1,9},{9,1},{2,10},{10,2},{3,11},{11,3},{4,12},{12,4},... | collective-permute-start | bytes 49160 | tf_op jit(solution)/shard_map/ppermute | solution.py:593
  3.7 0.7 %copy-done.2 = f32[1,2,16,128]{3,2,1,0:T(8,128)S(1)} copy-done((f32[1,2,16,128]{3,2,1,0:T(8,128)S(1)}, f32[1,2,16,128]{3,2,1,0:T(8,128)}, u32[]{:S(2)}) %copy-start.2) | copy-done | bytes 16408
  6.5 2.9 %prepare.1 = (bf16[896,128]{1,0:T(8,128)(2,1)S(1)}, f32[44,16,128]{2,1,0:T(8,128)S(1)}, f32[120,8,128]{2,1,0:T(8,128)}, f32[16,1408]{1,0:T(8,128)S(1)}) custom-call(f32[2,72,16,128]{3,2,1,0:T(8,128)} %bitcast.11, f32[71,16,128]{2,1,0:T(8,128)} %bitcast.15, f32[2,16,128]{2,1,0:T(8,128)S(1)} %bitcast.19, f32[16,128]{1,0:T(8,128)S(1)} %bitcast.23, ...), custom_call_target="tpu_custom_call" | custom-call | bytes 6000000 | tf_op jit(solution)/shard_map/prepare/pallas_call | solution.py:478
  9.4 1.3 %first_send.1 = (f32[32,8,128]{2,1,0:T(8,128)}, f32[44,16,128]{2,1,0:T(8,128)S(1)}) custom-call(f32[2,16,128]{2,1,0:T(8,128)S(1)} %collective-permute-done.west_ref, f32[2,16,128]{2,1,0:T(8,128)S(1)} %collective-permute-done.1.south_ref, bf16[896,128]{1,0:T(8,128)(2,1)S(1)} %get-tuple-element.21.table_ref, ...), custom_call_target="tpu_custom_call", output_to_operand_aliasing={{1}: (3, {})} | custom-call | bytes 3000000 | tf_op jit(solution)/shard_map/first_send/pallas_call | solution.py:478
  10.7 5.2 %all-to-all-start = ((f32[32,8,128]{2,1,0:T(8,128)}), f32[32,8,128]{2,1,0:T(8,128)S(1)}, u32[]{:S(2)}, u32[]{:S(2)}) async-start(f32[32,8,128]{2,1,0:T(8,128)} %get-tuple-element.24), calls=%async_computation | async-start | bytes 262144 | tf_op jit(solution)/shard_map/all_to_all | solution.py:596
  15.9 3.4 %collective-permute-start.2 = (f32[16,1408]{1,0:T(8,128)S(1)}, f32[16,1408]{1,0:T(8,128)S(1)}, u32[]{:S(2)}, u32[]{:S(2)}) collective-permute-start(f32[16,1408]{1,0:T(8,128)S(1)} %get-tuple-element.25), channel_id=1, source_target_pairs={{1,0},{2,1},{3,2},{4,3},{5,4},{6,5},{7,6},{0,7},{9,8},{10,9},{11,1... | collective-permute-start | bytes 270344 | tf_op jit(solution)/shard_map/ppermute | solution.py:628
  19.3 2.1 %collective-permute-done.2.refs_0_.columns_ref.refs_3_.refs_4_ = f32[16,1408]{1,0:T(8,128)S(1)} collective-permute-done((f32[16,1408]{1,0:T(8,128)S(1)}, f32[16,1408]{1,0:T(8,128)S(1)}, u32[]{:S(2)}, u32[]{:S(2)}) %collective-permute-start.2) | collective-permute-done | bytes 90144 | tf_op jit(solution)/shard_map/ppermute | solution.py:628
  21.4 2.6 %all-to-all-done.recv_ref = f32[32,8,128]{2,1,0:T(8,128)S(1)} async-done(((f32[32,8,128]{2,1,0:T(8,128)}), f32[32,8,128]{2,1,0:T(8,128)S(1)}, u32[]{:S(2)}, u32[]{:S(2)}) %all-to-all-start) | async-done | bytes 131104 | tf_op jit(solution)/shard_map/all_to_all | solution.py:596
  24.1 2.5 %exchange.3 = (f32[44,16,128]{2,1,0:T(8,128)S(1)}, f32[32,8,128]{2,1,0:T(8,128)}, f32[120,8,128]{2,1,0:T(8,128)}) custom-call(f32[44,16,128]{2,1,0:T(8,128)S(1)} %get-tuple-element.23.static_in, f32[32,8,128]{2,1,0:T(8,128)S(1)} %all-to-all-done.recv_ref, ...), custom_call_target="tpu_custom_call", output_to_operand_aliasing={{0}: (0, {}), {2}: (4, {})} | custom-call | bytes 3000000 | tf_op jit(solution)/shard_map/exchange/pallas_call | solution.py:478
  26.6 3.2 %all-to-all-start.1 = ((f32[32,8,128]{2,1,0:T(8,128)}), f32[32,8,128]{2,1,0:T(8,128)S(1)}, u32[]{:S(2)}, u32[]{:S(2)}) async-start(f32[32,8,128]{2,1,0:T(8,128)} %get-tuple-element.28), calls=%async_computation.1 | async-start | bytes 262144 | tf_op jit(solution)/shard_map/all_to_all | solution.py:596
  29.8 1.8 %collective-permute-start.3 = (f32[120,8,128]{2,1,0:T(8,128)}, f32[120,8,128]{2,1,0:T(8,128)S(1)}, u32[]{:S(2)}, u32[]{:S(2)}) collective-permute-start(f32[120,8,128]{2,1,0:T(8,128)} %get-tuple-element.31), channel_id=1, source_target_pairs={{8,0},{0,8},{9,1},{1,9},{10,2},{2,10},{11,3},{3,11},{12,4},{4,12},... | collective-permute-start | bytes 1474568 | tf_op jit(solution)/shard_map/ppermute | solution.py:666
  31.7 6.3 %all-to-all-done.1.recv_ref = f32[32,8,128]{2,1,0:T(8,128)S(1)} async-done(((f32[32,8,128]{2,1,0:T(8,128)}), f32[32,8,128]{2,1,0:T(8,128)S(1)}, u32[]{:S(2)}, u32[]{:S(2)}) %all-to-all-start.1) | async-done | bytes 131104 | tf_op jit(solution)/shard_map/all_to_all | solution.py:596
  38.0 2.2 %exchange.4 = (f32[44,16,128]{2,1,0:T(8,128)S(1)}, f32[32,8,128]{2,1,0:T(8,128)}) custom-call(f32[44,16,128]{2,1,0:T(8,128)S(1)} %get-tuple-element.27.static_in, f32[32,8,128]{2,1,0:T(8,128)S(1)} %all-to-all-done.1.recv_ref, bf16[896,128]{1,0:T(8,128)(2,1)S(1)} %get-tuple-element.21.table_ref), custom_call_target="tpu_custom_call", output_to_operand_aliasing={{0}: (0, {})} | custom-call | bytes 3000000 | tf_op jit(solution)/shard_map/exchange/pallas_call | solution.py:478
  40.2 2.6 %all-to-all-start.2 = ((f32[32,8,128]{2,1,0:T(8,128)}), f32[32,8,128]{2,1,0:T(8,128)S(1)}, u32[]{:S(2)}, u32[]{:S(2)}) async-start(f32[32,8,128]{2,1,0:T(8,128)} %get-tuple-element.30.after_ref), calls=%async_computation.2 | async-start | bytes 262144 | tf_op jit(solution)/shard_map/all_to_all | solution.py:596
  42.8 2.0 %collective-permute-done.3.rows_ref.refs_2_.refs_3_ = f32[120,8,128]{2,1,0:T(8,128)S(1)} collective-permute-done((f32[120,8,128]{2,1,0:T(8,128)}, f32[120,8,128]{2,1,0:T(8,128)S(1)}, u32[]{:S(2)}, u32[]{:S(2)}) %collective-permute-start.3) | collective-permute-done | bytes 491552 | tf_op jit(solution)/shard_map/ppermute | solution.py:666
  44.8 0.8 %early_levels.1.refs_0_ = f32[17,16,128]{2,1,0:T(8,128)S(1)} custom-call(f32[2,72,16,128]{3,2,1,0:T(8,128)S(1)} %bitcast.12, f32[71,16,128]{2,1,0:T(8,128)S(1)} %bitcast.16, f32[2,16,128]{2,1,0:T(8,128)S(1)} %bitcast.20, f32[120,8,128]{2,1,0:T(8,128)S(1)} %collective-permute-done.3.rows_ref.refs_2_.refs_3_, ...), custom_call_target="tpu_custom_call" | custom-call | bytes 6000000 | tf_op jit(solution)/shard_map/early_levels/pallas_call | solution.py:478
  45.6 3.2 %deep_levels.2 = (f32[2,72,16,128]{3,2,1,0:T(8,128)}, f32[8,128]{1,0:T(8,128)S(1)}) custom-call(f32[32,8,128]{2,1,0:T(8,128)} %get-tuple-element.30.after_ref, f32[2,72,16,128]{3,2,1,0:T(8,128)S(1)} %bitcast.13, f32[71,16,128]{2,1,0:T(8,128)S(1)} %bitcast.17, f32[2,16,128]{2,1,0:T(8,128)S(1)} %bitcast.21, ...), custom_call_target="tpu_custom_call" | custom-call | bytes 12000000 | tf_op jit(solution)/shard_map/deep_levels/pallas_call | solution.py:478
  48.7 2.2 %all-to-all-done.2.recv_ref = f32[32,8,128]{2,1,0:T(8,128)S(1)} async-done(((f32[32,8,128]{2,1,0:T(8,128)}), f32[32,8,128]{2,1,0:T(8,128)S(1)}, u32[]{:S(2)}, u32[]{:S(2)}) %all-to-all-start.2) | async-done | bytes 131104 | tf_op jit(solution)/shard_map/all_to_all | solution.py:596
  50.9 2.2 %exchange.5 = (f32[44,16,128]{2,1,0:T(8,128)S(1)}, f32[32,8,128]{2,1,0:T(8,128)}) custom-call(f32[44,16,128]{2,1,0:T(8,128)S(1)} %get-tuple-element.29.static_in, f32[32,8,128]{2,1,0:T(8,128)S(1)} %all-to-all-done.2.recv_ref, bf16[896,128]{1,0:T(8,128)(2,1)S(1)} %get-tuple-element.21.table_ref, ...), custom_call_target="tpu_custom_call", output_to_operand_aliasing={{0}: (0, {})} | custom-call | bytes 3000000 | tf_op jit(solution)/shard_map/exchange/pallas_call | solution.py:478
  53.1 2.6 %all-to-all-start.3 = ((f32[32,8,128]{2,1,0:T(8,128)}), f32[32,8,128]{2,1,0:T(8,128)S(1)}, u32[]{:S(2)}, u32[]{:S(2)}) async-start(f32[32,8,128]{2,1,0:T(8,128)} %get-tuple-element.34.after_ref), calls=%async_computation.3 | async-start | bytes 262144 | tf_op jit(solution)/shard_map/all_to_all | solution.py:596
  55.7 3.2 %deep_levels.3 = (f32[2,72,16,128]{3,2,1,0:T(8,128)}, f32[8,128]{1,0:T(8,128)}) custom-call(f32[32,8,128]{2,1,0:T(8,128)} %get-tuple-element.34.after_ref, f32[2,72,16,128]{3,2,1,0:T(8,128)S(1)} %bitcast.14, f32[2,72,16,128]{3,2,1,0:T(8,128)} %get-tuple-element.35.refs_0_, f32[71,16,128]{2,1,0:T(8,128)S(1)} %bitcast.18, ...), custom_call_target="tpu_custom_call", output_to_operand_aliasing={{0}: (2, {})} | custom-call | bytes 12000000 | tf_op jit(solution)/shard_map/deep_levels/pallas_call | solution.py:478
  58.9 5.0 %all-to-all-done.3.recv_ref = f32[32,8,128]{2,1,0:T(8,128)S(1)} async-done(((f32[32,8,128]{2,1,0:T(8,128)}), f32[32,8,128]{2,1,0:T(8,128)S(1)}, u32[]{:S(2)}, u32[]{:S(2)}) %all-to-all-start.3) | async-done | bytes 131104 | tf_op jit(solution)/shard_map/all_to_all | solution.py:596
  63.9 1.2 %last_exchange.1 = f32[2,72,16,128]{3,2,1,0:T(8,128)} custom-call(f32[44,16,128]{2,1,0:T(8,128)S(1)} %get-tuple-element.33.static_in, f32[32,8,128]{2,1,0:T(8,128)S(1)} %all-to-all-done.3.recv_ref, bf16[896,128]{1,0:T(8,128)(2,1)S(1)} %get-tuple-element.21.table_ref, f32[17,16,128]{2,1,0:T(8,128)S(1)} %early_levels.1.refs_0_, ...), custom_call_target="tpu_custom_call", output_to_operand_aliasing={{}: (4, {})} | custom-call | bytes 3000000 | tf_op jit(solution)/shard_map/last_exchange/pallas_call | solution.py:478
  (17 shorter events, 2.1 us)
Async XLA Ops:
  0.7 8.6 %collective-permute-start.1 = (f32[2,16,128]{2,1,0:T(8,128)S(1)}, f32[2,16,128]{2,1,0:T(8,128)S(1)}, u32[]{:S(2)}, u32[]{:S(2)}) collective-permute-start(f32[2,16,128]{2,1,0:T(8,128)S(1)} %pad_maximum_fusion), channel_id=1, source_target_pairs={{0,8},{8,0},{1,9},{9,1},{2,10},{10,2},{3,11},{11,3},{4,12},{12,4},... | collective-permute-start | bytes 49160 | tf_op jit(solution)/shard_map/ppermute | solution.py:593
  3.7 5.7 %collective-permute-start = (f32[2,16,128]{2,1,0:T(8,128)S(1)}, f32[2,16,128]{2,1,0:T(8,128)S(1)}, u32[]{:S(2)}, u32[]{:S(2)}) collective-permute-start(f32[2,16,128]{2,1,0:T(8,128)S(1)} %pad_maximum_fusion), channel_id=1, source_target_pairs={{0,1},{1,2},{2,3},{3,4},{4,5},{5,6},{6,7},{7,0},{8,9},{9,10},{10,1... | collective-permute-start | bytes 49160 | tf_op jit(solution)/shard_map/ppermute | solution.py:592
  3.7 0.7 %copy-start.2 = (f32[1,2,16,128]{3,2,1,0:T(8,128)S(1)}, f32[1,2,16,128]{3,2,1,0:T(8,128)}, u32[]{:S(2)}) copy-start(f32[1,2,16,128]{3,2,1,0:T(8,128)} %param.7) | copy-start | bytes 49156
  4.4 0.7 %copy-start.4 = (f32[1,16,128]{2,1,0:T(8,128)S(1)}, f32[1,16,128]{2,1,0:T(8,128)}, u32[]{:S(2)}) copy-start(f32[1,16,128]{2,1,0:T(8,128)} %param.9) | copy-start | bytes 24580
  5.1 0.7 %copy-start.5 = (s32[1,16,128]{2,1,0:T(8,128)S(1)}, s32[1,16,128]{2,1,0:T(8,128)}, u32[]{:S(2)}) copy-start(s32[1,16,128]{2,1,0:T(8,128)} %param.11) | copy-start | bytes 24580
  5.8 0.7 %copy-start.6 = (s32[1,128]{1,0:T(1,128)S(1)}, s32[1,128]{1,0:T(1,128)}, u32[]{:S(2)}) copy-start(s32[1,128]{1,0:T(1,128)} %refs_5_.1) | copy-start | bytes 1540
  10.7 13.4 %all-to-all-start = ((f32[32,8,128]{2,1,0:T(8,128)}), f32[32,8,128]{2,1,0:T(8,128)S(1)}, u32[]{:S(2)}, u32[]{:S(2)}) async-start(f32[32,8,128]{2,1,0:T(8,128)} %get-tuple-element.24), calls=%async_computation | async-start | bytes 262144 | tf_op jit(solution)/shard_map/all_to_all | solution.py:596
  15.9 5.6 %collective-permute-start.2 = (f32[16,1408]{1,0:T(8,128)S(1)}, f32[16,1408]{1,0:T(8,128)S(1)}, u32[]{:S(2)}, u32[]{:S(2)}) collective-permute-start(f32[16,1408]{1,0:T(8,128)S(1)} %get-tuple-element.25), channel_id=1, source_target_pairs={{1,0},{2,1},{3,2},{4,3},{5,4},{6,5},{7,6},{0,7},{9,8},{10,9},{11,1... | collective-permute-start | bytes 270344 | tf_op jit(solution)/shard_map/ppermute | solution.py:628
  24.0 20.7 %copy-start = (f32[1,2,72,16,128]{4,3,2,1,0:T(8,128)S(1)}, f32[1,2,72,16,128]{4,3,2,1,0:T(8,128)}, u32[]{:S(2)}) copy-start(f32[1,2,72,16,128]{4,3,2,1,0:T(8,128)} %param.6) | copy-start | bytes 3538948
  24.1 20.7 %copy-start.1 = (f32[1,71,16,128]{3,2,1,0:T(8,128)S(1)}, f32[1,71,16,128]{3,2,1,0:T(8,128)}, u32[]{:S(2)}) copy-start(f32[1,71,16,128]{3,2,1,0:T(8,128)} %param.8) | copy-start | bytes 1744900
  24.1 20.7 %copy-start.3 = (f32[1,2,16,128]{3,2,1,0:T(8,128)S(1)}, f32[1,2,16,128]{3,2,1,0:T(8,128)}, u32[]{:S(2)}) copy-start(f32[1,2,16,128]{3,2,1,0:T(8,128)} %param.7) | copy-start | bytes 49156
  26.6 11.4 %all-to-all-start.1 = ((f32[32,8,128]{2,1,0:T(8,128)}), f32[32,8,128]{2,1,0:T(8,128)S(1)}, u32[]{:S(2)}, u32[]{:S(2)}) async-start(f32[32,8,128]{2,1,0:T(8,128)} %get-tuple-element.28), calls=%async_computation.1 | async-start | bytes 262144 | tf_op jit(solution)/shard_map/all_to_all | solution.py:596
  29.8 15.0 %collective-permute-start.3 = (f32[120,8,128]{2,1,0:T(8,128)}, f32[120,8,128]{2,1,0:T(8,128)S(1)}, u32[]{:S(2)}, u32[]{:S(2)}) collective-permute-start(f32[120,8,128]{2,1,0:T(8,128)} %get-tuple-element.31), channel_id=1, source_target_pairs={{8,0},{0,8},{9,1},{1,9},{10,2},{2,10},{11,3},{3,11},{12,4},{4,12},... | collective-permute-start | bytes 1474568 | tf_op jit(solution)/shard_map/ppermute | solution.py:666
  40.2 10.8 %all-to-all-start.2 = ((f32[32,8,128]{2,1,0:T(8,128)}), f32[32,8,128]{2,1,0:T(8,128)S(1)}, u32[]{:S(2)}, u32[]{:S(2)}) async-start(f32[32,8,128]{2,1,0:T(8,128)} %get-tuple-element.30.after_ref), calls=%async_computation.2 | async-start | bytes 262144 | tf_op jit(solution)/shard_map/all_to_all | solution.py:596
  53.1 10.8 %all-to-all-start.3 = ((f32[32,8,128]{2,1,0:T(8,128)}), f32[32,8,128]{2,1,0:T(8,128)S(1)}, u32[]{:S(2)}, u32[]{:S(2)}) async-start(f32[32,8,128]{2,1,0:T(8,128)} %get-tuple-element.34.after_ref), calls=%async_computation.3 | async-start | bytes 262144 | tf_op jit(solution)/shard_map/all_to_all | solution.py:596

commit v8 on v7

--- a/solution.py
+++ b/solution.py
@@ -17,8 +17,7 @@
 ZONAL, MERIDIONAL, KAPPA = 0, 1, 2
 COUPLING = KAPPA + STEPS
 WET = COUPLING + 1
-WEST = WET + 1
-SOUTH = WEST + 2
+SOUTH = WET + 1
 LATE = SOUTH + 2
 
 
@@ -44,6 +43,14 @@
 def lane_roll(value, shift):
     shift = shift % value.shape[-1]
     return value if shift == 0 else pltpu.roll(value, shift, 1)
+
+
+def picked_by(value, one_hot):
+    total = None
+    for part in three_parts(value):
+        term = jnp.dot(part, one_hot, preferred_element_type=F32)
+        total = term if total is None else total + term
+    return total
 
 
 def next_row(value):
@@ -259,10 +266,9 @@
     kappa = static_ref[KAPPA]
     coupling = static_ref[COUPLING]
     group = lane // TILE
-    tiles, edge_north, edge_east = [], [], []
-    place = lane == (row % groups) * TILE + (TILE - 1) - row // groups
-    west_a = lane_roll(static_ref[WEST], 1)
-    west_b = lane_roll(static_ref[WEST + 1], 1)
+    tiles, edge_north = [], []
+    share = (coupling * (1.0 - kappa), coupling * kappa)
+    raw_east, factors = jnp.zeros((rows, cols), F32), jnp.zeros((rows, cols), F32)
     south_a, south_b = static_ref[SOUTH], static_ref[SOUTH + 1]
     own_north, own_east = [], jnp.zeros((rows, cols), F32)
     for tracer in range(tracers):
@@ -276,9 +282,11 @@
         mixed = over + kappa * (under - over)
         scaled = coupling * mixed
         edge_north.append(south_a[rows - 1 : rows] * north0[0:1] + south_b[rows - 1 : rows] * north1[0:1])
-        column = west_a * east0 + west_b * east1
-        column = jnp.broadcast_to(column[:, 0:1], (rows, cols))
-        edge_east.append(jnp.sum(jnp.where(place, column, 0.0), axis=0, keepdims=True))
+        for level, edge in enumerate((east0, east1)):
+            place = lane == (tracer * 2 + level) * rows + row
+            raw_east = jnp.where(place, jnp.broadcast_to(edge[:, 0:1], (rows, cols)), raw_east)
+            factor = jnp.broadcast_to(share[level][:, cols - 1 : cols], (rows, cols))
+            factors = jnp.where(place, factor, factors)
         for k, field in enumerate(late[tracer]):
             own_north.append(meridional[0:1] * field[0:1])
             column = jnp.broadcast_to((zonal * field)[:, 0:1], (rows, cols))
@@ -303,6 +311,7 @@
     first, second = packed[:, :cols], packed[:, cols:]
     upper = row_iota((2 * SLAB, cols)) < SLAB
     empty = jnp.zeros((SLAB - 2, cols), F32)
+    edge_east = [jnp.sum(edge, axis=0, keepdims=True) for edge in (raw_east, factors)]
     edges = jnp.concatenate(
         [empty, edge_north[0], edge_east[0], empty, edge_north[1], edge_east[1]], axis=0
     )
@@ -332,29 +341,34 @@
         one, two = recv_ref[other + 2 * pair], recv_ref[other + 2 * pair + 1]
         first.append(jnp.where(upper, one, pltpu.roll(two, SLAB, 0)))
         second.append(jnp.where(upper, pltpu.roll(one, SLAB, 0), two))
-    halves = [jnp.concatenate(half, axis=0) for half in (first, second)]
-    slab = jnp.concatenate(halves, axis=1)
-    shifted = jnp.concatenate([lane_roll(half, 1) for half in halves], axis=1)
-    found = picked(table_ref[0 : 3 * count], jnp.concatenate([slab, shifted], axis=0))
+    slab = jnp.concatenate([jnp.concatenate(half, axis=0) for half in (first, second)], axis=1)
+    found = picked(table_ref[0 : 4 * count, 0 : slab.shape[0]], slab)
+
+    def place(kind):
+        start = LATE + tracers * STEPS + kind * groups
+        return static_ref[start : start + groups].reshape(count, cols) > 0
+
+    edge = found[2 * count : 3 * count, :cols] * found[3 * count :, cols:]
+    edge = jnp.where(place(2), edge, 0.0)
+    shape = (cols, tracers * cols)
+    source, lane = row_iota(shape), lane_iota(shape)
+    spread = (source // (2 * rows) == lane // cols) & (lane % TILE == TILE - 1)
+    edge = picked_by(edge, spread.astype(F32).astype(BF16))
+    main, north = place(0), place(1)
     group = lane_iota((rows, cols)) // TILE
     wet, coupling = static_ref[WET], static_ref[COUPLING]
     updated = []
     for tracer in range(tracers):
+        spot = slice(tracer * cols, (tracer + 1) * cols)
+        total = jnp.where(main, found[:count, spot], 0.0) + jnp.where(north, found[count : 2 * count, spot], 0.0)
+        shift = TILE
+        while shift < cols:
+            total = total + lane_roll(total, shift)
+            shift *= 2
+        total = total + edge[:, spot]
         received = jnp.zeros((rows, cols), F32)
         for c in range(groups):
-            total = None
-            for kind in range(3):
-                start = kind * count + c * rows
-                place = static_ref[LATE + tracers * STEPS + kind * groups + c]
-                term = jnp.where(
-                    place > 0, found[start : start + rows, tracer * cols : (tracer + 1) * cols], 0.0
-                )
-                total = term if total is None else total + term
-            shift = TILE
-            while shift < cols:
-                total = total + lane_roll(total, shift)
-                shift *= 2
-            received = jnp.where(group == c, total, received)
+            received = jnp.where(group == c, total[c * rows : (c + 1) * rows], received)
         own = surface[tracer]
         updated.append(own + wet * (received - coupling * own))
     return updated
@@ -411,31 +425,35 @@
     return found
 
 
-def first_send_kernel(west_ref, south_ref, table_ref, static_in, send_ref, static_ref, *, tracers, deep_rows):
+def first_pack_kernel(table_ref, planes_ref, send_ref, *, tracers, deep_rows):
+    late = [[planes_ref[LATE + tracer * STEPS + k] for k in range(STEPS)] for tracer in range(tracers)]
+    send_surface(late, [values[1] for values in late], planes_ref, table_ref, send_ref, deep_rows)
+
+
+def first_send_kernel(pack_ref, south_ref, static_in, send_ref, static_ref, *, tracers):
     for k in range(2):
-        static_ref[WEST + k] = west_ref[k]
         static_ref[SOUTH + k] = south_ref[k]
-    late = [[static_in[LATE + tracer * STEPS + k] for k in range(STEPS)] for tracer in range(tracers)]
-    send_surface(late, [values[1] for values in late], static_ref, table_ref, send_ref, deep_rows)
+    devices = send_ref.shape[0] // 2
+    rows, cols = static_in.shape[1:]
+    factor = static_in[MERIDIONAL, 0:1, :]
+    lines = []
+    for tracer in range(tracers):
+        north = [factor * static_in[LATE + tracer * STEPS + k, 0:1, :] for k in range(2)]
+        lines.append(south_ref[0, rows - 1 : rows] * north[0] + south_ref[1, rows - 1 : rows] * north[1])
+    row = row_iota((2 * SLAB, cols))
+    edge = jnp.where(row == SLAB - 2, lines[0], jnp.where(row == 2 * SLAB - 2, lines[1], 0.0))
+    model = Place().model
+    for device in range(devices):
+        there = (1 - model) * devices + device
+        send_ref[there] = pack_ref[there] + edge
+        here = model * devices + device
+        send_ref[here] = pack_ref[here]
 
 
 def exchange_kernel(static_in, recv_ref, table_ref, *refs, step, tracers, count, deep_rows, unread=0):
     early_ref, refs = (refs[0], refs[1:]) if step >= 2 else (None, refs)
-    if step == 0:
-        east_ref, _, *refs, rows_ref, sems = refs
-        cols = rows_ref.shape[2]
-        tiles = east_ref.shape[1] // cols
-        corner = [
-            pltpu.make_async_copy(
-                east_ref.at[0 : 2 * STEPS, tile * cols : (tile + 1) * cols],
-                rows_ref.at[rows_ref.shape[0] - tiles + tile],
-                sems.at[tile],
-            )
-            for tile in range(tiles)
-        ]
-        for copy in corner:
-            copy.start()
     refs = refs[unread:]
+    static_in = static_in if step == STEPS - 1 else refs[0]
     late = [[static_in[LATE + tracer * STEPS + k] for k in range(count)] for tracer in range(tracers)]
     early = [early_levels(step, early_ref, tracer, tracers) for tracer in range(tracers)]
     stepped = upper_levels(recv_ref, late, early, static_in)
@@ -454,9 +472,6 @@
         for k, value in enumerate(stepped[tracer]):
             static_ref[LATE + tracer * STEPS + k] = value
     send_surface(stepped, [values[1] for values in stepped], static_in, table_ref, send_ref, deep_rows)
-    if step == 0:
-        for copy in corner:
-            copy.wait()
 
 
 def whole(array):
@@ -522,11 +537,11 @@
     north_ok = (row == rows - 1) & (lat < n_lat - 1)
     east_ok = group == groups - 1
     east_device = lat * n_lon + (lon + 1) % n_lon
-    east_row = (east_device + (row // groups) * devices) * SLAB + SLAB - 1
     picks = (
         target * SLAB + came // groups,
         jnp.where(north_ok, (target + n_lon) * SLAB + SLAB - 2, -1),
-        jnp.where(east_ok, east_row, -1),
+        jnp.where(east_ok, east_device * SLAB + SLAB - 1, -1),
+        jnp.where(east_ok, target * SLAB + SLAB - 1, -1),
     )
     index = lax.broadcasted_iota(jnp.int32, (count, table_ref.shape[1]), 1)
     for kind, pick in enumerate(picks):
@@ -534,15 +549,15 @@
     height = devices * SLAB
     packing = (sent % groups) * height + line_target * SLAB + sent // groups
     slots = lax.broadcasted_iota(jnp.int32, (groups * height, count), 0)
-    table_ref[3 * count :, 0:count] = (slots == packing).astype(F32).astype(BF16)
+    table_ref[4 * count :, 0:count] = (slots == packing).astype(F32).astype(BF16)
     if table_ref.shape[1] > count:
-        table_ref[3 * count :, count:] = jnp.zeros((groups * height, table_ref.shape[1] - count), BF16)
+        table_ref[4 * count :, count:] = jnp.zeros((groups * height, table_ref.shape[1] - count), BF16)
 
     lane = lax.broadcasted_iota(jnp.int32, (count, groups * TILE), 1)
     places = (
         lane // TILE == came % groups,
         lane // TILE == group,
-        lane == (row % groups) * TILE + TILE - 1,
+        (lane % rows == row) & (lane < 2 * 2 * rows),
     )
     for kind, place in enumerate(places):
         place = place.astype(F32)
@@ -551,32 +566,45 @@
 
 
 def prepare_kernel(*refs, n_lat, n_lon):
-    sources, refs = refs[:6], refs[6:]
-    (table_ref, planes_ref, rows_ref, columns_ref), refs = refs[:4], refs[4:]
-    buffers, sems = refs[:6], refs[6]
+    fields, kappa, courant, coupling, mask, partner, table_ref, planes_ref, small, flags, line, sems = refs
+    tracers, _, rows, cols = fields.shape
+    copies = [pltpu.make_async_copy(partner, line, sems.at[0]), pltpu.make_async_copy(mask, flags, sems.at[1])]
+    sources = [(courant, ZONAL, 2), (kappa.at[0:STEPS], KAPPA, STEPS)]
+    sources += [(fields.at[tracer, 0:STEPS], LATE + tracer * STEPS, STEPS) for tracer in range(tracers)]
+    for i, (source, plane, planes) in enumerate(sources):
+        copies.append(pltpu.make_async_copy(source, planes_ref.at[plane : plane + planes], sems.at[2 + i]))
+    copies.append(pltpu.make_async_copy(coupling, small, sems.at[2 + len(sources)]))
+    for copy in copies:
+        copy.start()
+    copies[0].wait()
+    write_tables(line[...], table_ref, planes_ref, LATE + tracers * STEPS, rows, cols // TILE, n_lat, n_lon)
+    for k in range(2):
+        planes_ref[SOUTH + k] = jnp.zeros((rows, cols), F32)
+    for copy in copies[1:]:
+        copy.wait()
+    planes_ref[COUPLING] = small[...]
+    planes_ref[WET] = flags[...].astype(F32)
+
+
+def corner_kernel(after_ref, east_ref, rows_in, rows_ref, sems):
+    cols = rows_ref.shape[2]
+    tiles = east_ref.shape[1] // cols
     copies = [
-        pltpu.make_async_copy(source, buffer, sems.at[i])
-        for i, (source, buffer) in enumerate(zip(sources, buffers))
+        pltpu.make_async_copy(
+            east_ref.at[0 : 2 * STEPS, tile * cols : (tile + 1) * cols],
+            rows_ref.at[rows_ref.shape[0] - tiles + tile],
+            sems.at[tile],
+        )
+        for tile in range(tiles)
     ]
     for copy in copies:
         copy.start()
-    fields, kappa, courant, coupling, mask, partner = buffers
-    tracers, _, rows, cols = fields.shape
-    copies[5].wait()
-    write_tables(partner[...], table_ref, planes_ref, LATE + tracers * STEPS, rows, cols // TILE, n_lat, n_lon)
-    for copy in copies[1:5]:
+    for copy in copies:
         copy.wait()
-    planes_ref[ZONAL] = courant[0]
-    planes_ref[MERIDIONAL] = courant[1]
-    for k in range(STEPS):
-        planes_ref[KAPPA + k] = kappa[k]
-    planes_ref[COUPLING] = coupling[...]
-    planes_ref[WET] = mask[...].astype(F32)
-    copies[0].wait()
-    for tracer in range(tracers):
-        for k in range(STEPS):
-            planes_ref[LATE + tracer * STEPS + k] = fields[tracer, k]
-    pack_halo(fields, kappa, courant, rows_ref, columns_ref)
+
+
+def halo_kernel(after_ref, fields_ref, kappa_ref, courant_ref, rows_ref, columns_ref):
+    pack_halo(fields_ref, kappa_ref, courant_ref, rows_ref, columns_ref)
 
 
 def local(adjoint, courant, diffusivity, coupling, partner, mask):
@@ -589,42 +617,66 @@
     devices = n_lat * n_lon
 
     share = jnp.stack([coupling * (1.0 - kappa[0]), coupling * kappa[0]])
-    from_west = lax.ppermute(share, "lon", [(i, (i + 1) % n_lon) for i in range(n_lon)])
     from_south = lax.ppermute(share, "lat", [(i, (i + 1) % n_lat) for i in range(n_lat)])
 
     def exchanged(send):
         return lax.all_to_all(send, ("mp", "lat", "lon"), split_axis=0, concat_axis=0, tiled=True)
 
-    deep_rows = 3 * count
+    deep_rows = 4 * count
     width = ((tracers + 1) * -(-levels // PACKED) + 2) * cols
     sources = (fields, kappa, courant, coupling, mask, partner)
     table_shape = jax.ShapeDtypeStruct(
-        (deep_rows + groups * devices * SLAB, max(count, 2 * devices * SLAB)), BF16
+        (deep_rows + groups * devices * SLAB, max(count, devices * SLAB)), BF16
     )
     planes_shape = shaped(LATE + tracers * STEPS + 3 * groups, rows, cols)
     north_shape = shaped((tracers + 1) * (levels // 2) + 1 + width // cols, 2 * STEPS, cols)
-    table, planes, north, east = call(
+    table, planes = call(
         functools.partial(prepare_kernel, n_lat=n_lat, n_lon=n_lon),
         sources,
         [FAR for _ in sources],
-        (table_shape, planes_shape, north_shape, shaped(rows, width)),
-        (NEAR, NEAR, NEAR, NEAR),
+        (table_shape, planes_shape),
+        (NEAR, NEAR),
         "prepare",
-        scratch=[*(pltpu.VMEM(a.shape, a.dtype) for a in sources), pltpu.SemaphoreType.DMA((len(sources),))],
+        scratch=[
+            pltpu.VMEM((rows, cols), F32),
+            pltpu.VMEM((rows, cols), jnp.int32),
+            pltpu.VMEM(partner.shape, jnp.int32),
+            pltpu.SemaphoreType.DMA((5 + tracers,)),
+        ],
         us=2,
         mib=53,
     )
     send_shape = shaped(2 * devices, 2 * SLAB, cols)
+    pack = call(
+        functools.partial(first_pack_kernel, tracers=tracers, deep_rows=deep_rows),
+        (table, planes),
+        [NEAR, NEAR],
+        send_shape,
+        NEAR,
+        "first_pack",
+    )
     send, planes = call(
-        functools.partial(first_send_kernel, tracers=tracers, deep_rows=deep_rows),
-        (from_west, from_south, table, planes),
-        [NEAR, NEAR, NEAR, NEAR],
+        functools.partial(first_send_kernel, tracers=tracers),
+        (pack, from_south, planes),
+        [NEAR, NEAR, NEAR],
         (send_shape, planes_shape),
         (NEAR, NEAR),
         "first_send",
-        aliases={3: 1},
+        aliases={2: 1},
     )
     recv = exchanged(send)
+    halo_shapes = (north_shape, shaped(rows, width))
+    north, east = call(
+        halo_kernel,
+        (send, fields, kappa, courant),
+        [UNREAD, *(whole(a) for a in (fields, kappa, courant))],
+        halo_shapes,
+        tuple(whole(a) for a in halo_shapes),
+        "halo",
+        grid=(1,),
+        us=2,
+        mib=53,
+    )
     east = lax.ppermute(east, "lon", [((i + 1) % n_lon, i) for i in range(n_lon)])
     tall = rows + 2 * STEPS
 
@@ -653,14 +705,17 @@
         )
         operands = (planes, recv, table)
         if step == 0:
-            planes, send, north = call(
-                kernel,
-                (*operands, east, north),
-                [*[NEAR] * 4, UNREAD],
-                (planes_shape, send_shape, north_shape),
-                (NEAR, NEAR, UNREAD),
-                "exchange",
-                aliases={0: 0, 4: 2},
+            planes, send = call(
+                kernel, operands, [NEAR] * 3, (planes_shape, send_shape), (NEAR, NEAR), "exchange", aliases={0: 0}
+            )
+            north = call(
+                corner_kernel,
+                (send, east, north),
+                [UNREAD, NEAR, UNREAD],
+                north_shape,
+                UNREAD,
+                "corner",
+                aliases={2: 0},
                 scratch=[pltpu.SemaphoreType.DMA((width // cols,))],
             )
             north = lax.ppermute(north, "lat", [((i + 1) % n_lat, i) for i in range(n_lat)])

time: 65.8 us -> 63.5 us (0.965)
  waiting for transfers between devices: 20.3 us -> 17.4 us
  local copies, waits for them, and re-layouts: 2.78 us -> 3.55 us
    ppermute x1, waiting for transfers between devices: 2.14 us -> 0.01 us  [local(): lax.ppermute(east, 'lon', [((i + 1) % n_lon, i) for i in range(n_lon)])]
    all_to_all x4, waiting for transfers between devices: 16.2 us -> 14.8 us  [exchanged(): lax.all_to_all(send, ('mp', 'lat', 'lon'), split_axis=0, concat_axis=0, t...]
    unnamed x14 -> x16, local copies, waits for them, and re-layouts: 2.78 us -> 3.55 us
    pallas_call x9 -> x12, Pallas kernels: 19.4 us -> 19.4 us  [call(): pl.pallas_call(kernel, grid=grid, in_specs=specs, out_shape=out_shape, ou...]
  transfers between devices with their start and end apart: 8 -> 7, of which waited for: 6 -> 5; matrix products, arithmetic and copies ran while one was open for 0% -> 0% of each run, Pallas kernels for 19% -> 24%
where the time goes in v8:
time: 63.5 us; the launch traced here: 62.9 us
  starting transfers between devices  21.7 us (34%)
  Pallas kernels  19.4 us (31%)
  waiting for transfers between devices  17.4 us (27%)
  local copies, waits for them, and re-layouts  3.55 us (6%)
  other arithmetic  0.72 us (1%)
    pallas_call x12, Pallas kernels, call(): pl.pallas_call(kernel, grid=grid, in_specs=specs, out_shape=out_shape, ou...  19.4 us
    all_to_all x4, waiting for transfers between devices, exchanged(): lax.all_to_all(send, ('mp', 'lat', 'lon'), split_axis=0, concat_axis=0, t...  14.8 us
    all_to_all x4, starting transfers between devices, exchanged(): lax.all_to_all(send, ('mp', 'lat', 'lon'), split_axis=0, concat_axis=0, t...  13.6 us
    unnamed x16, local copies, waits for them, and re-layouts  3.55 us
    ppermute x1, starting transfers between devices, local(): lax.ppermute(east, 'lon', [((i + 1) % n_lon, i) for i in range(n_lon)])  3.43 us
    ppermute x1, starting transfers between devices, local(): lax.ppermute(share, 'lat', [(i, (i + 1) % n_lat) for i in range(n_lat)])  2.97 us
    ppermute x1, waiting for transfers between devices, local(): lax.ppermute(north, 'lat', [((i + 1) % n_lat, i) for i in range(n_lat)])  2.59 us
    ppermute x1, starting transfers between devices, local(): lax.ppermute(north, 'lat', [((i + 1) % n_lat, i) for i in range(n_lat)])  1.65 us
  transfers between devices with their start and end apart: 7, of which 5 were waited for; matrix products, arithmetic and copies ran while one was open for 0% of the time, Pallas kernels for 24%

profile of v8, /device:TPU:0, one launch (start us, length us, event | category | flops | bytes accessed | tf_op | source)
XLA Modules:
  0.0 62.9 jit_solution(10663912538832172964)
XLA Ops:
  0.0 0.7 %fusion = (f32[1,16,128]{2,1,0:T(8,128)S(1)}, f32[1,16,128]{2,1,0:T(8,128)S(1)}) fusion(f32[1,16,128]{2,1,0:T(8,128)} %param.9, f32[1,71,16,128]{3,2,1,0:T(8,128)} %param.8), kind=kLoop, calls=%fused_computation.3 | loop fusion | flops 6144 | bytes 32768 | tf_op jit(solution)/shard_map/mul | solution.py:619
  0.7 3.0 %collective-permute-start = (f32[2,16,128]{2,1,0:T(8,128)S(1)}, f32[2,16,128]{2,1,0:T(8,128)S(1)}, u32[]{:S(2)}, u32[]{:S(2)}) collective-permute-start(f32[2,16,128]{2,1,0:T(8,128)S(1)} %pad_maximum_fusion), channel_id=1, source_target_pairs={{0,8},{8,0},{1,9},{9,1},{2,10},{10,2},{3,11},{11,3},{4,12},{12,4},... | collective-permute-start | bytes 49160 | tf_op jit(solution)/shard_map/ppermute | solution.py:620
  3.7 0.7 %copy-done.3 = f32[1,2,16,128]{3,2,1,0:T(8,128)S(1)} copy-done((f32[1,2,16,128]{3,2,1,0:T(8,128)S(1)}, f32[1,2,16,128]{3,2,1,0:T(8,128)}, u32[]{:S(2)}) %copy-start.3) | copy-done | bytes 16408
  6.5 0.9 %prepare.1 = (bf16[1024,128]{1,0:T(8,128)(2,1)S(1)}, f32[42,16,128]{2,1,0:T(8,128)S(1)}) custom-call(f32[2,72,16,128]{3,2,1,0:T(8,128)} %bitcast.11, f32[71,16,128]{2,1,0:T(8,128)} %bitcast.16, f32[2,16,128]{2,1,0:T(8,128)S(1)} %bitcast.21, f32[16,128]{1,0:T(8,128)S(1)} %bitcast.26, s32[16,128]{1,0:T(8,128)S(1)} %bitcast.27, s32[1,128]{1,0:T(1,128)S(1)} %copy-done.7), custom_call_target="tpu_custom_call" | custom-call | bytes 6000000 | tf_op jit(solution)/shard_map/prepare/pallas_call | solution.py:493
  8.7 4.9 %all-to-all-start = ((f32[32,8,128]{2,1,0:T(8,128)}), f32[32,8,128]{2,1,0:T(8,128)S(1)}, u32[]{:S(2)}, u32[]{:S(2)}) async-start(f32[32,8,128]{2,1,0:T(8,128)} %get-tuple-element.23.after_ref), calls=%async_computation | async-start | bytes 262144 | tf_op jit(solution)/shard_map/all_to_all | solution.py:623
  13.6 2.1 %halo.1 = (f32[120,8,128]{2,1,0:T(8,128)S(1)}, f32[16,1408]{1,0:T(8,128)S(1)}) custom-call(f32[32,8,128]{2,1,0:T(8,128)} %get-tuple-element.23.after_ref, f32[2,72,16,128]{3,2,1,0:T(8,128)} %bitcast.12, f32[71,16,128]{2,1,0:T(8,128)} %bitcast.17, f32[2,16,128]{2,1,0:T(8,128)S(1)} %bitcast.22), custom_call_target="tpu_custom_call" | custom-call | bytes 6000000 | tf_op jit(solution)/shard_map/halo/pallas_call | solution.py:493
  15.7 3.4 %collective-permute-start.1 = (f32[16,1408]{1,0:T(8,128)S(1)}, f32[16,1408]{1,0:T(8,128)S(1)}, u32[]{:S(2)}, u32[]{:S(2)}) collective-permute-start(f32[16,1408]{1,0:T(8,128)S(1)} %get-tuple-element.28), channel_id=1, source_target_pairs={{1,0},{2,1},{3,2},{4,3},{5,4},{6,5},{7,6},{0,7},{9,8},{10,9},{11,1... | collective-permute-start | bytes 270344 | tf_op jit(solution)/shard_map/ppermute | solution.py:680
  19.1 2.7 %all-to-all-done.recv_ref = f32[32,8,128]{2,1,0:T(8,128)S(1)} async-done(((f32[32,8,128]{2,1,0:T(8,128)}), f32[32,8,128]{2,1,0:T(8,128)S(1)}, u32[]{:S(2)}, u32[]{:S(2)}) %all-to-all-start) | async-done | bytes 131104 | tf_op jit(solution)/shard_map/all_to_all | solution.py:623
  21.8 2.2 %exchange.3 = (f32[42,16,128]{2,1,0:T(8,128)S(1)}, f32[32,8,128]{2,1,0:T(8,128)}) custom-call(f32[42,16,128]{2,1,0:T(8,128)S(1)} %get-tuple-element.22.static_in, f32[32,8,128]{2,1,0:T(8,128)S(1)} %all-to-all-done.recv_ref, bf16[1024,128]{1,0:T(8,128)(2,1)S(1)} %get-tuple-element.20.table_ref), custom_call_target="tpu_custom_call", output_to_operand_aliasing={{0}: (0, {})} | custom-call | bytes 3000000 | tf_op jit(solution)/shard_map/exchange/pallas_call | solution.py:493
  24.0 2.7 %all-to-all-start.1 = ((f32[32,8,128]{2,1,0:T(8,128)}), f32[32,8,128]{2,1,0:T(8,128)S(1)}, u32[]{:S(2)}, u32[]{:S(2)}) async-start(f32[32,8,128]{2,1,0:T(8,128)} %get-tuple-element.25.after_ref), calls=%async_computation.1 | async-start | bytes 262144 | tf_op jit(solution)/shard_map/all_to_all | solution.py:623
  26.9 0.8 %copy-done.2 = f32[120,8,128]{2,1,0:T(8,128)} copy-done((f32[120,8,128]{2,1,0:T(8,128)}, f32[120,8,128]{2,1,0:T(8,128)S(1)}, u32[]{:S(2)}) %copy-start.2) | copy-done | bytes 491544
  27.7 1.7 %collective-permute-start.2 = (f32[120,8,128]{2,1,0:T(8,128)}, f32[120,8,128]{2,1,0:T(8,128)S(1)}, u32[]{:S(2)}, u32[]{:S(2)}) collective-permute-start(f32[120,8,128]{2,1,0:T(8,128)} %copy-done.2), channel_id=1, source_target_pairs={{8,0},{0,8},{9,1},{1,9},{10,2},{2,10},{11,3},{3,11},{12,4},{4,12},... | collective-permute-start | bytes 1474568 | tf_op jit(solution)/shard_map/ppermute | solution.py:721
  29.3 5.5 %all-to-all-done.1.recv_ref = f32[32,8,128]{2,1,0:T(8,128)S(1)} async-done(((f32[32,8,128]{2,1,0:T(8,128)}), f32[32,8,128]{2,1,0:T(8,128)S(1)}, u32[]{:S(2)}, u32[]{:S(2)}) %all-to-all-start.1) | async-done | bytes 131104 | tf_op jit(solution)/shard_map/all_to_all | solution.py:623
  34.9 2.2 %exchange.4 = (f32[42,16,128]{2,1,0:T(8,128)S(1)}, f32[32,8,128]{2,1,0:T(8,128)}) custom-call(f32[42,16,128]{2,1,0:T(8,128)S(1)} %get-tuple-element.24.static_in, f32[32,8,128]{2,1,0:T(8,128)S(1)} %all-to-all-done.1.recv_ref, bf16[1024,128]{1,0:T(8,128)(2,1)S(1)} %get-tuple-element.20.table_ref), custom_call_target="tpu_custom_call", output_to_operand_aliasing={{0}: (0, {})} | custom-call | bytes 3000000 | tf_op jit(solution)/shard_map/exchange/pallas_call | solution.py:493
  37.0 2.6 %all-to-all-start.2 = ((f32[32,8,128]{2,1,0:T(8,128)}), f32[32,8,128]{2,1,0:T(8,128)S(1)}, u32[]{:S(2)}, u32[]{:S(2)}) async-start(f32[32,8,128]{2,1,0:T(8,128)} %get-tuple-element.27.after_ref), calls=%async_computation.2 | async-start | bytes 262144 | tf_op jit(solution)/shard_map/all_to_all | solution.py:623
  39.6 2.6 %collective-permute-done.2.rows_ref.refs_2_.refs_3_ = f32[120,8,128]{2,1,0:T(8,128)S(1)} collective-permute-done((f32[120,8,128]{2,1,0:T(8,128)}, f32[120,8,128]{2,1,0:T(8,128)S(1)}, u32[]{:S(2)}, u32[]{:S(2)}) %collective-permute-start.2) | collective-permute-done | bytes 491552 | tf_op jit(solution)/shard_map/ppermute | solution.py:721
  42.2 0.8 %early_levels.1.refs_0_ = f32[17,16,128]{2,1,0:T(8,128)S(1)} custom-call(f32[2,72,16,128]{3,2,1,0:T(8,128)S(1)} %bitcast.13, f32[71,16,128]{2,1,0:T(8,128)S(1)} %bitcast.18, f32[2,16,128]{2,1,0:T(8,128)S(1)} %bitcast.23, f32[120,8,128]{2,1,0:T(8,128)S(1)} %collective-permute-done.2.rows_ref.refs_2_.refs_3_, ...), custom_call_target="tpu_custom_call" | custom-call | bytes 6000000 | tf_op jit(solution)/shard_map/early_levels/pallas_call | solution.py:493
  43.0 3.2 %deep_levels.2 = (f32[2,72,16,128]{3,2,1,0:T(8,128)}, f32[8,128]{1,0:T(8,128)S(1)}) custom-call(f32[32,8,128]{2,1,0:T(8,128)} %get-tuple-element.27.after_ref, f32[2,72,16,128]{3,2,1,0:T(8,128)S(1)} %bitcast.14, f32[71,16,128]{2,1,0:T(8,128)S(1)} %bitcast.19, f32[2,16,128]{2,1,0:T(8,128)S(1)} %bitcast.24, ...), custom_call_target="tpu_custom_call" | custom-call | bytes 12000000 | tf_op jit(solution)/shard_map/deep_levels/pallas_call | solution.py:493
  46.2 1.6 %all-to-all-done.2.recv_ref = f32[32,8,128]{2,1,0:T(8,128)S(1)} async-done(((f32[32,8,128]{2,1,0:T(8,128)}), f32[32,8,128]{2,1,0:T(8,128)S(1)}, u32[]{:S(2)}, u32[]{:S(2)}) %all-to-all-start.2) | async-done | bytes 131104 | tf_op jit(solution)/shard_map/all_to_all | solution.py:623
  47.8 2.2 %exchange.5 = (f32[42,16,128]{2,1,0:T(8,128)S(1)}, f32[32,8,128]{2,1,0:T(8,128)}) custom-call(f32[42,16,128]{2,1,0:T(8,128)S(1)} %get-tuple-element.26.static_in, f32[32,8,128]{2,1,0:T(8,128)S(1)} %all-to-all-done.2.recv_ref, bf16[1024,128]{1,0:T(8,128)(2,1)S(1)} %get-tuple-element.20.table_ref, ...), custom_call_target="tpu_custom_call", output_to_operand_aliasing={{0}: (0, {})} | custom-call | bytes 3000000 | tf_op jit(solution)/shard_map/exchange/pallas_call | solution.py:493
  50.0 3.5 %all-to-all-start.3 = ((f32[32,8,128]{2,1,0:T(8,128)}), f32[32,8,128]{2,1,0:T(8,128)S(1)}, u32[]{:S(2)}, u32[]{:S(2)}) async-start(f32[32,8,128]{2,1,0:T(8,128)} %get-tuple-element.32.after_ref), calls=%async_computation.3 | async-start | bytes 262144 | tf_op jit(solution)/shard_map/all_to_all | solution.py:623
  53.5 3.2 %deep_levels.3 = (f32[2,72,16,128]{3,2,1,0:T(8,128)}, f32[8,128]{1,0:T(8,128)}) custom-call(f32[32,8,128]{2,1,0:T(8,128)} %get-tuple-element.32.after_ref, f32[2,72,16,128]{3,2,1,0:T(8,128)S(1)} %bitcast.15, f32[2,72,16,128]{3,2,1,0:T(8,128)} %get-tuple-element.33.refs_0_, f32[71,16,128]{2,1,0:T(8,128)S(1)} %bitcast.20, ...), custom_call_target="tpu_custom_call", output_to_operand_aliasing={{0}: (2, {})} | custom-call | bytes 12000000 | tf_op jit(solution)/shard_map/deep_levels/pallas_call | solution.py:493
  56.7 5.0 %all-to-all-done.3.recv_ref = f32[32,8,128]{2,1,0:T(8,128)S(1)} async-done(((f32[32,8,128]{2,1,0:T(8,128)}), f32[32,8,128]{2,1,0:T(8,128)S(1)}, u32[]{:S(2)}, u32[]{:S(2)}) %all-to-all-start.3) | async-done | bytes 131104 | tf_op jit(solution)/shard_map/all_to_all | solution.py:623
  61.6 1.2 %last_exchange.1 = f32[2,72,16,128]{3,2,1,0:T(8,128)} custom-call(f32[42,16,128]{2,1,0:T(8,128)S(1)} %get-tuple-element.31.static_in, f32[32,8,128]{2,1,0:T(8,128)S(1)} %all-to-all-done.3.recv_ref, bf16[1024,128]{1,0:T(8,128)(2,1)S(1)} %get-tuple-element.20.table_ref, f32[17,16,128]{2,1,0:T(8,128)S(1)} %early_levels.1.refs_0_, ...), custom_call_target="tpu_custom_call", output_to_operand_aliasing={{}: (4, {})} | custom-call | bytes 3000000 | tf_op jit(solution)/shard_map/last_exchange/pallas_call | solution.py:493
  (20 shorter events, 3.6 us)
Async XLA Ops:
  0.7 7.3 %collective-permute-start = (f32[2,16,128]{2,1,0:T(8,128)S(1)}, f32[2,16,128]{2,1,0:T(8,128)S(1)}, u32[]{:S(2)}, u32[]{:S(2)}) collective-permute-start(f32[2,16,128]{2,1,0:T(8,128)S(1)} %pad_maximum_fusion), channel_id=1, source_target_pairs={{0,8},{8,0},{1,9},{9,1},{2,10},{10,2},{3,11},{11,3},{4,12},{12,4},... | collective-permute-start | bytes 49160 | tf_op jit(solution)/shard_map/ppermute | solution.py:620
  3.7 0.7 %copy-start.3 = (f32[1,2,16,128]{3,2,1,0:T(8,128)S(1)}, f32[1,2,16,128]{3,2,1,0:T(8,128)}, u32[]{:S(2)}) copy-start(f32[1,2,16,128]{3,2,1,0:T(8,128)} %param.7) | copy-start | bytes 49156
  4.4 0.7 %copy-start.5 = (f32[1,16,128]{2,1,0:T(8,128)S(1)}, f32[1,16,128]{2,1,0:T(8,128)}, u32[]{:S(2)}) copy-start(f32[1,16,128]{2,1,0:T(8,128)} %param.9) | copy-start | bytes 24580
  5.1 0.7 %copy-start.6 = (s32[1,16,128]{2,1,0:T(8,128)S(1)}, s32[1,16,128]{2,1,0:T(8,128)}, u32[]{:S(2)}) copy-start(s32[1,16,128]{2,1,0:T(8,128)} %param.11) | copy-start | bytes 24580
  5.8 0.7 %copy-start.7 = (s32[1,128]{1,0:T(1,128)S(1)}, s32[1,128]{1,0:T(1,128)}, u32[]{:S(2)}) copy-start(s32[1,128]{1,0:T(1,128)} %refs_5_.1) | copy-start | bytes 1540
  7.3 6.3 %copy-start.4 = (f32[1,2,16,128]{3,2,1,0:T(8,128)S(1)}, f32[1,2,16,128]{3,2,1,0:T(8,128)}, u32[]{:S(2)}) copy-start(f32[1,2,16,128]{3,2,1,0:T(8,128)} %param.7) | copy-start | bytes 49156
  8.7 13.1 %all-to-all-start = ((f32[32,8,128]{2,1,0:T(8,128)}), f32[32,8,128]{2,1,0:T(8,128)S(1)}, u32[]{:S(2)}, u32[]{:S(2)}) async-start(f32[32,8,128]{2,1,0:T(8,128)} %get-tuple-element.23.after_ref), calls=%async_computation | async-start | bytes 262144 | tf_op jit(solution)/shard_map/all_to_all | solution.py:623
  15.7 11.0 %collective-permute-start.1 = (f32[16,1408]{1,0:T(8,128)S(1)}, f32[16,1408]{1,0:T(8,128)S(1)}, u32[]{:S(2)}, u32[]{:S(2)}) collective-permute-start(f32[16,1408]{1,0:T(8,128)S(1)} %get-tuple-element.28), channel_id=1, source_target_pairs={{1,0},{2,1},{3,2},{4,3},{5,4},{6,5},{7,6},{0,7},{9,8},{10,9},{11,1... | collective-permute-start | bytes 270344 | tf_op jit(solution)/shard_map/ppermute | solution.py:680
  24.0 18.2 %copy-start = (f32[1,2,72,16,128]{4,3,2,1,0:T(8,128)S(1)}, f32[1,2,72,16,128]{4,3,2,1,0:T(8,128)}, u32[]{:S(2)}) copy-start(f32[1,2,72,16,128]{4,3,2,1,0:T(8,128)} %param.6) | copy-start | bytes 3538948
  24.0 18.2 %copy-start.1 = (f32[1,71,16,128]{3,2,1,0:T(8,128)S(1)}, f32[1,71,16,128]{3,2,1,0:T(8,128)}, u32[]{:S(2)}) copy-start(f32[1,71,16,128]{3,2,1,0:T(8,128)} %param.8) | copy-start | bytes 1744900
  24.0 10.9 %all-to-all-start.1 = ((f32[32,8,128]{2,1,0:T(8,128)}), f32[32,8,128]{2,1,0:T(8,128)S(1)}, u32[]{:S(2)}, u32[]{:S(2)}) async-start(f32[32,8,128]{2,1,0:T(8,128)} %get-tuple-element.25.after_ref), calls=%async_computation.1 | async-start | bytes 262144 | tf_op jit(solution)/shard_map/all_to_all | solution.py:623
  26.9 0.8 %copy-start.2 = (f32[120,8,128]{2,1,0:T(8,128)}, f32[120,8,128]{2,1,0:T(8,128)S(1)}, u32[]{:S(2)}) copy-start(f32[120,8,128]{2,1,0:T(8,128)S(1)} %corner.1) | copy-start | bytes 1474564
  27.7 14.5 %collective-permute-start.2 = (f32[120,8,128]{2,1,0:T(8,128)}, f32[120,8,128]{2,1,0:T(8,128)S(1)}, u32[]{:S(2)}, u32[]{:S(2)}) collective-permute-start(f32[120,8,128]{2,1,0:T(8,128)} %copy-done.2), channel_id=1, source_target_pairs={{8,0},{0,8},{9,1},{1,9},{10,2},{2,10},{11,3},{3,11},{12,4},{4,12},... | collective-permute-start | bytes 1474568 | tf_op jit(solution)/shard_map/ppermute | solution.py:721
  37.0 10.7 %all-to-all-start.2 = ((f32[32,8,128]{2,1,0:T(8,128)}), f32[32,8,128]{2,1,0:T(8,128)S(1)}, u32[]{:S(2)}, u32[]{:S(2)}) async-start(f32[32,8,128]{2,1,0:T(8,128)} %get-tuple-element.27.after_ref), calls=%async_computation.2 | async-start | bytes 262144 | tf_op jit(solution)/shard_map/all_to_all | solution.py:623
  50.0 11.7 %all-to-all-start.3 = ((f32[32,8,128]{2,1,0:T(8,128)}), f32[32,8,128]{2,1,0:T(8,128)S(1)}, u32[]{:S(2)}, u32[]{:S(2)}) async-start(f32[32,8,128]{2,1,0:T(8,128)} %get-tuple-element.32.after_ref), calls=%async_computation.3 | async-start | bytes 262144 | tf_op jit(solution)/shard_map/all_to_all | solution.py:623

commit v9 on v8

--- a/solution.py
+++ b/solution.py
@@ -566,24 +566,25 @@
 
 
 def prepare_kernel(*refs, n_lat, n_lon):
-    fields, kappa, courant, coupling, mask, partner, table_ref, planes_ref, small, flags, line, sems = refs
+    fields, kappa, courant, share_ref, wet_share_ref, partner, table_ref, planes_ref, sems = refs
     tracers, _, rows, cols = fields.shape
-    copies = [pltpu.make_async_copy(partner, line, sems.at[0]), pltpu.make_async_copy(mask, flags, sems.at[1])]
-    sources = [(courant, ZONAL, 2), (kappa.at[0:STEPS], KAPPA, STEPS)]
+    sources = [(kappa.at[0:STEPS], KAPPA, STEPS)]
     sources += [(fields.at[tracer, 0:STEPS], LATE + tracer * STEPS, STEPS) for tracer in range(tracers)]
-    for i, (source, plane, planes) in enumerate(sources):
-        copies.append(pltpu.make_async_copy(source, planes_ref.at[plane : plane + planes], sems.at[2 + i]))
-    copies.append(pltpu.make_async_copy(coupling, small, sems.at[2 + len(sources)]))
+    copies = [
+        pltpu.make_async_copy(source, planes_ref.at[plane : plane + planes], sems.at[i])
+        for i, (source, plane, planes) in enumerate(sources)
+    ]
     for copy in copies:
         copy.start()
-    copies[0].wait()
-    write_tables(line[...], table_ref, planes_ref, LATE + tracers * STEPS, rows, cols // TILE, n_lat, n_lon)
-    for k in range(2):
-        planes_ref[SOUTH + k] = jnp.zeros((rows, cols), F32)
-    for copy in copies[1:]:
+    write_tables(partner[...], table_ref, planes_ref, LATE + tracers * STEPS, rows, cols // TILE, n_lat, n_lon)
+    planes_ref[ZONAL] = courant[0]
+    planes_ref[MERIDIONAL] = courant[1]
+    planes_ref[COUPLING] = share_ref[0] + share_ref[1]
+    planes_ref[WET] = (wet_share_ref[...] > 0).astype(F32)
+    for k in (SOUTH, SOUTH + 1):
+        planes_ref[k] = jnp.zeros((rows, cols), F32)
+    for copy in copies:
         copy.wait()
-    planes_ref[COUPLING] = small[...]
-    planes_ref[WET] = flags[...].astype(F32)
 
 
 def corner_kernel(after_ref, east_ref, rows_in, rows_ref, sems):
@@ -617,6 +618,7 @@
     devices = n_lat * n_lon
 
     share = jnp.stack([coupling * (1.0 - kappa[0]), coupling * kappa[0]])
+    wet_share = mask.astype(F32) * coupling
     from_south = lax.ppermute(share, "lat", [(i, (i + 1) % n_lat) for i in range(n_lat)])
 
     def exchanged(send):
@@ -624,7 +626,6 @@
 
     deep_rows = 4 * count
     width = ((tracers + 1) * -(-levels // PACKED) + 2) * cols
-    sources = (fields, kappa, courant, coupling, mask, partner)
     table_shape = jax.ShapeDtypeStruct(
         (deep_rows + groups * devices * SLAB, max(count, devices * SLAB)), BF16
     )
@@ -632,17 +633,12 @@
     north_shape = shaped((tracers + 1) * (levels // 2) + 1 + width // cols, 2 * STEPS, cols)
     table, planes = call(
         functools.partial(prepare_kernel, n_lat=n_lat, n_lon=n_lon),
-        sources,
-        [FAR for _ in sources],
+        (fields, kappa, courant, share, wet_share, partner),
+        [FAR, FAR, NEAR, NEAR, NEAR, NEAR],
         (table_shape, planes_shape),
         (NEAR, NEAR),
         "prepare",
-        scratch=[
-            pltpu.VMEM((rows, cols), F32),
-            pltpu.VMEM((rows, cols), jnp.int32),
-            pltpu.VMEM(partner.shape, jnp.int32),
-            pltpu.SemaphoreType.DMA((5 + tracers,)),
-        ],
+        scratch=[pltpu.SemaphoreType.DMA((1 + tracers,))],
         us=2,
         mib=53,
     )

time: 63.5 us -> 62.3 us (0.981)
  local copies, waits for them, and re-layouts: 3.55 us -> 2.16 us
    unnamed x16 -> x12, local copies, waits for them, and re-layouts: 3.55 us -> 2.16 us
  transfers between devices with their start and end apart: 7 -> 7, of which waited for: 5 -> 5; matrix products, arithmetic and copies ran while one was open for 0% -> 0% of each run, Pallas kernels for 24% -> 25%
where the time goes in v9:
time: 62.3 us; the launch traced here: 61.8 us
  starting transfers between devices  22 us (35%)
  Pallas kernels  19.3 us (31%)
  waiting for transfers between devices  17.4 us (28%)
  local copies, waits for them, and re-layouts  2.16 us (3%)
  other arithmetic  0.74 us (1%)
    pallas_call x12, Pallas kernels, call(): pl.pallas_call(kernel, grid=grid, in_specs=specs, out_shape=out_shape, ou...  19.3 us
    all_to_all x4, waiting for transfers between devices, exchanged(): lax.all_to_all(send, ('mp', 'lat', 'lon'), split_axis=0, concat_axis=0, t...  14.8 us
    all_to_all x4, starting transfers between devices, exchanged(): lax.all_to_all(send, ('mp', 'lat', 'lon'), split_axis=0, concat_axis=0, t...  13.9 us
    ppermute x1, starting transfers between devices, local(): lax.ppermute(east, 'lon', [((i + 1) % n_lon, i) for i in range(n_lon)])  3.43 us
    ppermute x1, starting transfers between devices, local(): lax.ppermute(share, 'lat', [(i, (i + 1) % n_lat) for i in range(n_lat)])  3.02 us
    ppermute x1, waiting for transfers between devices, local(): lax.ppermute(north, 'lat', [((i + 1) % n_lat, i) for i in range(n_lat)])  2.59 us
    unnamed x12, local copies, waits for them, and re-layouts  2.16 us
    ppermute x1, starting transfers between devices, local(): lax.ppermute(north, 'lat', [((i + 1) % n_lat, i) for i in range(n_lat)])  1.65 us
  transfers between devices with their start and end apart: 7, of which 5 were waited for; matrix products, arithmetic and copies ran while one was open for 0% of the time, Pallas kernels for 25%

profile of v9, /device:TPU:0, one launch (start us, length us, event | category | flops | bytes accessed | tf_op | source)
XLA Modules:
  0.0 61.8 jit_solution(492233265916914897)
XLA Ops:
  0.0 0.7 %fusion = (f32[1,16,128]{2,1,0:T(8,128)S(1)}, f32[1,16,128]{2,1,0:T(8,128)S(1)}, f32[16,128]{1,0:T(8,128)S(1)}) fusion(f32[1,16,128]{2,1,0:T(8,128)} %param.9, f32[1,71,16,128]{3,2,1,0:T(8,128)} %param.8, s32[1,16,128]{2,1,0:T(8,128)} %param.11), kind=kLoop, calls=%fused_computation.3 | loop fusion | flops 10240 | bytes 49152 | tf_op jit(solution)/shard_map/mul | solution.py:620
  0.7 3.0 %collective-permute-start = (f32[2,16,128]{2,1,0:T(8,128)S(1)}, f32[2,16,128]{2,1,0:T(8,128)S(1)}, u32[]{:S(2)}, u32[]{:S(2)}) collective-permute-start(f32[2,16,128]{2,1,0:T(8,128)S(1)} %pad_maximum_fusion.refs_3_), channel_id=1, source_target_pairs={{0,8},{8,0},{1,9},{9,1},{2,10},{10,2},{3,11},{11,3},{4,12},{12,4},... | collective-permute-start | bytes 49160 | tf_op jit(solution)/shard_map/ppermute | solution.py:622
  3.8 0.7 %copy-done.3 = f32[1,2,16,128]{3,2,1,0:T(8,128)S(1)} copy-done((f32[1,2,16,128]{3,2,1,0:T(8,128)S(1)}, f32[1,2,16,128]{3,2,1,0:T(8,128)}, u32[]{:S(2)}) %copy-start.3) | copy-done | bytes 16408
  5.1 0.8 %prepare.1 = (bf16[1024,128]{1,0:T(8,128)(2,1)S(1)}, f32[42,16,128]{2,1,0:T(8,128)S(1)}) custom-call(f32[2,72,16,128]{3,2,1,0:T(8,128)} %bitcast.11, f32[71,16,128]{2,1,0:T(8,128)} %bitcast.16, f32[2,16,128]{2,1,0:T(8,128)S(1)} %bitcast.21, f32[2,16,128]{2,1,0:T(8,128)S(1)} %pad_maximum_fusion.refs_3_, f32[16,128]{1,0:T(8,128)S(1)} %get-tuple-element.37.refs_4_, ...), custom_call_target="tpu_custom_call" | custom-call | bytes 6000000 | tf_op jit(solution)/shard_map/prepare/pallas_call | solution.py:493
  7.3 5.2 %all-to-all-start = ((f32[32,8,128]{2,1,0:T(8,128)}), f32[32,8,128]{2,1,0:T(8,128)S(1)}, u32[]{:S(2)}, u32[]{:S(2)}) async-start(f32[32,8,128]{2,1,0:T(8,128)} %get-tuple-element.23.after_ref), calls=%async_computation | async-start | bytes 262144 | tf_op jit(solution)/shard_map/all_to_all | solution.py:625
  12.5 2.1 %halo.1 = (f32[120,8,128]{2,1,0:T(8,128)S(1)}, f32[16,1408]{1,0:T(8,128)S(1)}) custom-call(f32[32,8,128]{2,1,0:T(8,128)} %get-tuple-element.23.after_ref, f32[2,72,16,128]{3,2,1,0:T(8,128)} %bitcast.12, f32[71,16,128]{2,1,0:T(8,128)} %bitcast.17, f32[2,16,128]{2,1,0:T(8,128)S(1)} %bitcast.22), custom_call_target="tpu_custom_call" | custom-call | bytes 6000000 | tf_op jit(solution)/shard_map/halo/pallas_call | solution.py:493
  14.6 3.4 %collective-permute-start.1 = (f32[16,1408]{1,0:T(8,128)S(1)}, f32[16,1408]{1,0:T(8,128)S(1)}, u32[]{:S(2)}, u32[]{:S(2)}) collective-permute-start(f32[16,1408]{1,0:T(8,128)S(1)} %get-tuple-element.28), channel_id=1, source_target_pairs={{1,0},{2,1},{3,2},{4,3},{5,4},{6,5},{7,6},{0,7},{9,8},{10,9},{11,1... | collective-permute-start | bytes 270344 | tf_op jit(solution)/shard_map/ppermute | solution.py:676
  18.0 2.7 %all-to-all-done.recv_ref = f32[32,8,128]{2,1,0:T(8,128)S(1)} async-done(((f32[32,8,128]{2,1,0:T(8,128)}), f32[32,8,128]{2,1,0:T(8,128)S(1)}, u32[]{:S(2)}, u32[]{:S(2)}) %all-to-all-start) | async-done | bytes 131104 | tf_op jit(solution)/shard_map/all_to_all | solution.py:625
  20.7 2.2 %exchange.3 = (f32[42,16,128]{2,1,0:T(8,128)S(1)}, f32[32,8,128]{2,1,0:T(8,128)}) custom-call(f32[42,16,128]{2,1,0:T(8,128)S(1)} %get-tuple-element.22.static_in, f32[32,8,128]{2,1,0:T(8,128)S(1)} %all-to-all-done.recv_ref, bf16[1024,128]{1,0:T(8,128)(2,1)S(1)} %get-tuple-element.20.table_ref), custom_call_target="tpu_custom_call", output_to_operand_aliasing={{0}: (0, {})} | custom-call | bytes 3000000 | tf_op jit(solution)/shard_map/exchange/pallas_call | solution.py:493
  22.9 2.7 %all-to-all-start.1 = ((f32[32,8,128]{2,1,0:T(8,128)}), f32[32,8,128]{2,1,0:T(8,128)S(1)}, u32[]{:S(2)}, u32[]{:S(2)}) async-start(f32[32,8,128]{2,1,0:T(8,128)} %get-tuple-element.25.after_ref), calls=%async_computation.1 | async-start | bytes 262144 | tf_op jit(solution)/shard_map/all_to_all | solution.py:625
  25.8 0.8 %copy-done.2 = f32[120,8,128]{2,1,0:T(8,128)} copy-done((f32[120,8,128]{2,1,0:T(8,128)}, f32[120,8,128]{2,1,0:T(8,128)S(1)}, u32[]{:S(2)}) %copy-start.2) | copy-done | bytes 491544
  26.6 1.7 %collective-permute-start.2 = (f32[120,8,128]{2,1,0:T(8,128)}, f32[120,8,128]{2,1,0:T(8,128)S(1)}, u32[]{:S(2)}, u32[]{:S(2)}) collective-permute-start(f32[120,8,128]{2,1,0:T(8,128)} %copy-done.2), channel_id=1, source_target_pairs={{8,0},{0,8},{9,1},{1,9},{10,2},{2,10},{11,3},{3,11},{12,4},{4,12},... | collective-permute-start | bytes 1474568 | tf_op jit(solution)/shard_map/ppermute | solution.py:717
  28.2 5.5 %all-to-all-done.1.recv_ref = f32[32,8,128]{2,1,0:T(8,128)S(1)} async-done(((f32[32,8,128]{2,1,0:T(8,128)}), f32[32,8,128]{2,1,0:T(8,128)S(1)}, u32[]{:S(2)}, u32[]{:S(2)}) %all-to-all-start.1) | async-done | bytes 131104 | tf_op jit(solution)/shard_map/all_to_all | solution.py:625
  33.8 2.2 %exchange.4 = (f32[42,16,128]{2,1,0:T(8,128)S(1)}, f32[32,8,128]{2,1,0:T(8,128)}) custom-call(f32[42,16,128]{2,1,0:T(8,128)S(1)} %get-tuple-element.24.static_in, f32[32,8,128]{2,1,0:T(8,128)S(1)} %all-to-all-done.1.recv_ref, bf16[1024,128]{1,0:T(8,128)(2,1)S(1)} %get-tuple-element.20.table_ref), custom_call_target="tpu_custom_call", output_to_operand_aliasing={{0}: (0, {})} | custom-call | bytes 3000000 | tf_op jit(solution)/shard_map/exchange/pallas_call | solution.py:493
  35.9 2.6 %all-to-all-start.2 = ((f32[32,8,128]{2,1,0:T(8,128)}), f32[32,8,128]{2,1,0:T(8,128)S(1)}, u32[]{:S(2)}, u32[]{:S(2)}) async-start(f32[32,8,128]{2,1,0:T(8,128)} %get-tuple-element.27.after_ref), calls=%async_computation.2 | async-start | bytes 262144 | tf_op jit(solution)/shard_map/all_to_all | solution.py:625
  38.5 2.6 %collective-permute-done.2.rows_ref.refs_2_.refs_3_ = f32[120,8,128]{2,1,0:T(8,128)S(1)} collective-permute-done((f32[120,8,128]{2,1,0:T(8,128)}, f32[120,8,128]{2,1,0:T(8,128)S(1)}, u32[]{:S(2)}, u32[]{:S(2)}) %collective-permute-start.2) | collective-permute-done | bytes 491552 | tf_op jit(solution)/shard_map/ppermute | solution.py:717
  41.1 0.8 %early_levels.1.refs_0_ = f32[17,16,128]{2,1,0:T(8,128)S(1)} custom-call(f32[2,72,16,128]{3,2,1,0:T(8,128)S(1)} %bitcast.13, f32[71,16,128]{2,1,0:T(8,128)S(1)} %bitcast.18, f32[2,16,128]{2,1,0:T(8,128)S(1)} %bitcast.23, f32[120,8,128]{2,1,0:T(8,128)S(1)} %collective-permute-done.2.rows_ref.refs_2_.refs_3_, ...), custom_call_target="tpu_custom_call" | custom-call | bytes 6000000 | tf_op jit(solution)/shard_map/early_levels/pallas_call | solution.py:493
  41.9 3.2 %deep_levels.2 = (f32[2,72,16,128]{3,2,1,0:T(8,128)}, f32[8,128]{1,0:T(8,128)S(1)}) custom-call(f32[32,8,128]{2,1,0:T(8,128)} %get-tuple-element.27.after_ref, f32[2,72,16,128]{3,2,1,0:T(8,128)S(1)} %bitcast.14, f32[71,16,128]{2,1,0:T(8,128)S(1)} %bitcast.19, f32[2,16,128]{2,1,0:T(8,128)S(1)} %bitcast.24, ...), custom_call_target="tpu_custom_call" | custom-call | bytes 12000000 | tf_op jit(solution)/shard_map/deep_levels/pallas_call | solution.py:493
  45.1 1.6 %all-to-all-done.2.recv_ref = f32[32,8,128]{2,1,0:T(8,128)S(1)} async-done(((f32[32,8,128]{2,1,0:T(8,128)}), f32[32,8,128]{2,1,0:T(8,128)S(1)}, u32[]{:S(2)}, u32[]{:S(2)}) %all-to-all-start.2) | async-done | bytes 131104 | tf_op jit(solution)/shard_map/all_to_all | solution.py:625
  46.7 2.2 %exchange.5 = (f32[42,16,128]{2,1,0:T(8,128)S(1)}, f32[32,8,128]{2,1,0:T(8,128)}) custom-call(f32[42,16,128]{2,1,0:T(8,128)S(1)} %get-tuple-element.26.static_in, f32[32,8,128]{2,1,0:T(8,128)S(1)} %all-to-all-done.2.recv_ref, bf16[1024,128]{1,0:T(8,128)(2,1)S(1)} %get-tuple-element.20.table_ref, ...), custom_call_target="tpu_custom_call", output_to_operand_aliasing={{0}: (0, {})} | custom-call | bytes 3000000 | tf_op jit(solution)/shard_map/exchange/pallas_call | solution.py:493
  48.9 3.5 %all-to-all-start.3 = ((f32[32,8,128]{2,1,0:T(8,128)}), f32[32,8,128]{2,1,0:T(8,128)S(1)}, u32[]{:S(2)}, u32[]{:S(2)}) async-start(f32[32,8,128]{2,1,0:T(8,128)} %get-tuple-element.32.after_ref), calls=%async_computation.3 | async-start | bytes 262144 | tf_op jit(solution)/shard_map/all_to_all | solution.py:625
  52.4 3.2 %deep_levels.3 = (f32[2,72,16,128]{3,2,1,0:T(8,128)}, f32[8,128]{1,0:T(8,128)}) custom-call(f32[32,8,128]{2,1,0:T(8,128)} %get-tuple-element.32.after_ref, f32[2,72,16,128]{3,2,1,0:T(8,128)S(1)} %bitcast.15, f32[2,72,16,128]{3,2,1,0:T(8,128)} %get-tuple-element.33.refs_0_, f32[71,16,128]{2,1,0:T(8,128)S(1)} %bitcast.20, ...), custom_call_target="tpu_custom_call", output_to_operand_aliasing={{0}: (2, {})} | custom-call | bytes 12000000 | tf_op jit(solution)/shard_map/deep_levels/pallas_call | solution.py:493
  55.6 5.0 %all-to-all-done.3.recv_ref = f32[32,8,128]{2,1,0:T(8,128)S(1)} async-done(((f32[32,8,128]{2,1,0:T(8,128)}), f32[32,8,128]{2,1,0:T(8,128)S(1)}, u32[]{:S(2)}, u32[]{:S(2)}) %all-to-all-start.3) | async-done | bytes 131104 | tf_op jit(solution)/shard_map/all_to_all | solution.py:625
  60.5 1.2 %last_exchange.1 = f32[2,72,16,128]{3,2,1,0:T(8,128)} custom-call(f32[42,16,128]{2,1,0:T(8,128)S(1)} %get-tuple-element.31.static_in, f32[32,8,128]{2,1,0:T(8,128)S(1)} %all-to-all-done.3.recv_ref, bf16[1024,128]{1,0:T(8,128)(2,1)S(1)} %get-tuple-element.20.table_ref, f32[17,16,128]{2,1,0:T(8,128)S(1)} %early_levels.1.refs_0_, ...), custom_call_target="tpu_custom_call", output_to_operand_aliasing={{}: (4, {})} | custom-call | bytes 3000000 | tf_op jit(solution)/shard_map/last_exchange/pallas_call | solution.py:493
  (16 shorter events, 2.2 us)
Async XLA Ops:
  0.7 5.9 %collective-permute-start = (f32[2,16,128]{2,1,0:T(8,128)S(1)}, f32[2,16,128]{2,1,0:T(8,128)S(1)}, u32[]{:S(2)}, u32[]{:S(2)}) collective-permute-start(f32[2,16,128]{2,1,0:T(8,128)S(1)} %pad_maximum_fusion.refs_3_), channel_id=1, source_target_pairs={{0,8},{8,0},{1,9},{9,1},{2,10},{10,2},{3,11},{11,3},{4,12},{12,4},... | collective-permute-start | bytes 49160 | tf_op jit(solution)/shard_map/ppermute | solution.py:622
  3.8 0.7 %copy-start.3 = (f32[1,2,16,128]{3,2,1,0:T(8,128)S(1)}, f32[1,2,16,128]{3,2,1,0:T(8,128)}, u32[]{:S(2)}) copy-start(f32[1,2,16,128]{3,2,1,0:T(8,128)} %param.7) | copy-start | bytes 49156
  4.5 0.7 %copy-start.5 = (s32[1,128]{1,0:T(1,128)S(1)}, s32[1,128]{1,0:T(1,128)}, u32[]{:S(2)}) copy-start(s32[1,128]{1,0:T(1,128)} %refs_5_.1) | copy-start | bytes 1540
  6.0 6.6 %copy-start.4 = (f32[1,2,16,128]{3,2,1,0:T(8,128)S(1)}, f32[1,2,16,128]{3,2,1,0:T(8,128)}, u32[]{:S(2)}) copy-start(f32[1,2,16,128]{3,2,1,0:T(8,128)} %param.7) | copy-start | bytes 49156
  7.3 13.4 %all-to-all-start = ((f32[32,8,128]{2,1,0:T(8,128)}), f32[32,8,128]{2,1,0:T(8,128)S(1)}, u32[]{:S(2)}, u32[]{:S(2)}) async-start(f32[32,8,128]{2,1,0:T(8,128)} %get-tuple-element.23.after_ref), calls=%async_computation | async-start | bytes 262144 | tf_op jit(solution)/shard_map/all_to_all | solution.py:625
  14.6 11.0 %collective-permute-start.1 = (f32[16,1408]{1,0:T(8,128)S(1)}, f32[16,1408]{1,0:T(8,128)S(1)}, u32[]{:S(2)}, u32[]{:S(2)}) collective-permute-start(f32[16,1408]{1,0:T(8,128)S(1)} %get-tuple-element.28), channel_id=1, source_target_pairs={{1,0},{2,1},{3,2},{4,3},{5,4},{6,5},{7,6},{0,7},{9,8},{10,9},{11,1... | collective-permute-start | bytes 270344 | tf_op jit(solution)/shard_map/ppermute | solution.py:676
  22.9 18.2 %copy-start = (f32[1,2,72,16,128]{4,3,2,1,0:T(8,128)S(1)}, f32[1,2,72,16,128]{4,3,2,1,0:T(8,128)}, u32[]{:S(2)}) copy-start(f32[1,2,72,16,128]{4,3,2,1,0:T(8,128)} %param.6) | copy-start | bytes 3538948
  22.9 18.2 %copy-start.1 = (f32[1,71,16,128]{3,2,1,0:T(8,128)S(1)}, f32[1,71,16,128]{3,2,1,0:T(8,128)}, u32[]{:S(2)}) copy-start(f32[1,71,16,128]{3,2,1,0:T(8,128)} %param.8) | copy-start | bytes 1744900
  22.9 10.9 %all-to-all-start.1 = ((f32[32,8,128]{2,1,0:T(8,128)}), f32[32,8,128]{2,1,0:T(8,128)S(1)}, u32[]{:S(2)}, u32[]{:S(2)}) async-start(f32[32,8,128]{2,1,0:T(8,128)} %get-tuple-element.25.after_ref), calls=%async_computation.1 | async-start | bytes 262144 | tf_op jit(solution)/shard_map/all_to_all | solution.py:625
  25.8 0.8 %copy-start.2 = (f32[120,8,128]{2,1,0:T(8,128)}, f32[120,8,128]{2,1,0:T(8,128)S(1)}, u32[]{:S(2)}) copy-start(f32[120,8,128]{2,1,0:T(8,128)S(1)} %corner.1) | copy-start | bytes 1474564
  26.6 14.5 %collective-permute-start.2 = (f32[120,8,128]{2,1,0:T(8,128)}, f32[120,8,128]{2,1,0:T(8,128)S(1)}, u32[]{:S(2)}, u32[]{:S(2)}) collective-permute-start(f32[120,8,128]{2,1,0:T(8,128)} %copy-done.2), channel_id=1, source_target_pairs={{8,0},{0,8},{9,1},{1,9},{10,2},{2,10},{11,3},{3,11},{12,4},{4,12},... | collective-permute-start | bytes 1474568 | tf_op jit(solution)/shard_map/ppermute | solution.py:717
  35.9 10.7 %all-to-all-start.2 = ((f32[32,8,128]{2,1,0:T(8,128)}), f32[32,8,128]{2,1,0:T(8,128)S(1)}, u32[]{:S(2)}, u32[]{:S(2)}) async-start(f32[32,8,128]{2,1,0:T(8,128)} %get-tuple-element.27.after_ref), calls=%async_computation.2 | async-start | bytes 262144 | tf_op jit(solution)/shard_map/all_to_all | solution.py:625
  48.9 11.7 %all-to-all-start.3 = ((f32[32,8,128]{2,1,0:T(8,128)}), f32[32,8,128]{2,1,0:T(8,128)S(1)}, u32[]{:S(2)}, u32[]{:S(2)}) async-start(f32[32,8,128]{2,1,0:T(8,128)} %get-tuple-element.32.after_ref), calls=%async_computation.3 | async-start | bytes 262144 | tf_op jit(solution)/shard_map/all_to_all | solution.py:625

commit v10 on v9

--- a/solution.py
+++ b/solution.py
@@ -12,6 +12,7 @@
 F32 = jnp.float32
 BF16 = jnp.bfloat16
 UPPER = 8
+PARTS = 2
 PACKED = 32
 SLAB = 4
 ZONAL, MERIDIONAL, KAPPA = 0, 1, 2
@@ -45,14 +46,6 @@
     return value if shift == 0 else pltpu.roll(value, shift, 1)
 
 
-def picked_by(value, one_hot):
-    total = None
-    for part in three_parts(value):
-        term = jnp.dot(part, one_hot, preferred_element_type=F32)
-        total = term if total is None else total + term
-    return total
-
-
 def next_row(value):
     return pltpu.roll(value, value.shape[0] - 1, 0)
 
@@ -66,11 +59,12 @@
 
 
 def picked(one_hot, value):
-    total = None
-    for part in three_parts(value):
-        term = jnp.dot(one_hot, part, preferred_element_type=F32)
-        total = term if total is None else total + term
-    return total
+    return jnp.dot(one_hot, jnp.concatenate(three_parts(value), axis=0), preferred_element_type=F32)
+
+
+def spread_by(value, one_hot):
+    one_hot = jnp.concatenate([one_hot] * 3, axis=0)
+    return jnp.dot(jnp.concatenate(three_parts(value), axis=1), one_hot, preferred_element_type=F32)
 
 
 def pack_halo(fields_ref, kappa_ref, courant_ref, rows_ref, columns_ref):
@@ -237,7 +231,7 @@
 
 
 def deep_kernel(after_ref, fields_ref, *refs, tracer, tracers):
-    kappa_ref, courant_ref, rows_ref, columns_ref, out_ref, token_ref, state = refs[-7:]
+    kappa_ref, courant_ref, rows_ref, columns_ref, out_ref, state = refs[-6:]
     levels = fields_ref.shape[1]
 
     def store(k, value):
@@ -250,10 +244,9 @@
         (kappa_ref, courant_ref, rows_ref, columns_ref, state),
         tracer, levels, tracers, levels, lambda k: fields_ref[0, k], store, None,
     )
-    token_ref[...] = jnp.zeros(token_ref.shape, F32)
-
-
-def send_surface(late, below, static_ref, table_ref, send_ref, deep_rows):
+
+
+def send_surface(late, below, static_ref, pack_ref, send_ref, ready):
     here = Place()
     model = here.model
     tracers = len(late)
@@ -266,7 +259,7 @@
     kappa = static_ref[KAPPA]
     coupling = static_ref[COUPLING]
     group = lane // TILE
-    tiles, edge_north = [], []
+    tiles, edge_north, all_scaled = [], [], []
     share = (coupling * (1.0 - kappa), coupling * kappa)
     raw_east, factors = jnp.zeros((rows, cols), F32), jnp.zeros((rows, cols), F32)
     south_a, south_b = static_ref[SOUTH], static_ref[SOUTH + 1]
@@ -280,7 +273,7 @@
             parts.append((eastward, northward, (weight * field + east) + north))
         (east0, north0, over), (east1, north1, under) = parts
         mixed = over + kappa * (under - over)
-        scaled = coupling * mixed
+        all_scaled.append(coupling * mixed)
         edge_north.append(south_a[rows - 1 : rows] * north0[0:1] + south_b[rows - 1 : rows] * north1[0:1])
         for level, edge in enumerate((east0, east1)):
             place = lane == (tracer * 2 + level) * rows + row
@@ -292,6 +285,15 @@
             column = jnp.broadcast_to((zonal * field)[:, 0:1], (rows, cols))
             spot = (tracer * len(late[tracer]) + k) * rows + row
             own_east = jnp.where(lane == spot, column, own_east)
+    devices = send_ref.shape[0] // 2
+    empty = [jnp.zeros((1, cols), F32)] * (2 * SLAB - 1)
+    own_north = jnp.concatenate((own_north + empty)[: 2 * SLAB], axis=0)
+    own_east = jnp.concatenate(empty + [jnp.sum(own_east, axis=0, keepdims=True)], axis=0)
+    for device in range(devices):
+        send_ref[model * devices + device] = own_north
+    send_ref[model * devices + here.west] = own_east
+    ready(0, model * devices)
+    for scaled in all_scaled:
         blocks = []
         for c in range(groups):
             block = jnp.where(group == c, scaled, 0.0)
@@ -301,34 +303,39 @@
                 shift *= 2
             blocks.append(block)
         tiles.append(jnp.concatenate(blocks, axis=0))
-    devices = send_ref.shape[0] // 2
-    height = devices * SLAB
-    slots = picked(table_ref[deep_rows : deep_rows + groups * height, 0 : rows * groups], jnp.concatenate(tiles, axis=1))
-    slot_group = (lane_iota((height, tracers * cols)) % cols) // TILE
-    packed = jnp.zeros((height, tracers * cols), F32)
-    for g in range(groups):
-        packed = jnp.where(slot_group == g, slots[g * height : (g + 1) * height], packed)
-    first, second = packed[:, :cols], packed[:, cols:]
-    upper = row_iota((2 * SLAB, cols)) < SLAB
+    edge_east = [jnp.sum(edge, axis=0, keepdims=True) for edge in (raw_east, factors)]
     empty = jnp.zeros((SLAB - 2, cols), F32)
-    edge_east = [jnp.sum(edge, axis=0, keepdims=True) for edge in (raw_east, factors)]
     edges = jnp.concatenate(
         [empty, edge_north[0], edge_east[0], empty, edge_north[1], edge_east[1]], axis=0
     )
-    empty = [jnp.zeros((1, cols), F32)] * (2 * SLAB - 1)
-    own_north = jnp.concatenate((own_north + empty)[: 2 * SLAB], axis=0)
-    own_east = jnp.concatenate(empty + [jnp.sum(own_east, axis=0, keepdims=True)], axis=0)
-    for pair in range(devices // 2):
-        one, two = (half[pair * 2 * SLAB : (pair + 1) * 2 * SLAB] for half in (first, second))
-        there = (1 - model) * devices + 2 * pair
-        send_ref[there] = jnp.where(upper, one, pltpu.roll(two, SLAB, 0)) + edges
-        send_ref[there + 1] = jnp.where(upper, pltpu.roll(one, SLAB, 0), two) + edges
-        send_ref[model * devices + 2 * pair] = own_north
-        send_ref[model * devices + 2 * pair + 1] = own_north
-    send_ref[model * devices + here.west] = own_east
-
-
-def receive_surface(recv_ref, table_ref, static_ref, surface):
+    table = jnp.concatenate(three_parts(jnp.concatenate(tiles, axis=1)), axis=0)
+    height = pack_ref.shape[0] // (groups * PARTS)
+    main_rows = height * PARTS // devices
+    slot_group = (lane_iota((height, tracers * cols)) % cols) // TILE
+    line = row_iota((2 * SLAB, cols))
+    for part in range(PARTS):
+        start = part * groups * height
+        slots = jnp.dot(
+            pack_ref[start : start + groups * height, :], table, preferred_element_type=F32
+        )
+        packed = jnp.zeros((height, tracers * cols), F32)
+        for g in range(groups):
+            packed = jnp.where(slot_group == g, slots[g * height : (g + 1) * height], packed)
+        there = (1 - model) * devices + part * (devices // PARTS)
+        for device in range(devices // PARTS):
+            block = edges
+            first, offset = (device * main_rows) // 8 * 8, (device * main_rows) % 8
+            for tracer in range(tracers):
+                rows8 = packed[first : first + 8, tracer * cols : (tracer + 1) * cols]
+                shift = (tracer * SLAB - offset) % 8
+                rows8 = pltpu.roll(rows8, shift, 0) if shift else rows8
+                here_rows = (line >= tracer * SLAB) & (line < tracer * SLAB + main_rows)
+                block = jnp.where(here_rows, rows8, block)
+            send_ref[there + device] = block
+        ready(1 + part, there)
+
+
+def receive_surface(recv_ref, pick_ref, static_ref, surface):
     devices = recv_ref.shape[0] // 2
     rows, cols = surface[0].shape
     groups = cols // TILE
@@ -342,7 +349,7 @@
         first.append(jnp.where(upper, one, pltpu.roll(two, SLAB, 0)))
         second.append(jnp.where(upper, pltpu.roll(one, SLAB, 0), two))
     slab = jnp.concatenate([jnp.concatenate(half, axis=0) for half in (first, second)], axis=1)
-    found = picked(table_ref[0 : 4 * count, 0 : slab.shape[0]], slab)
+    found = picked(pick_ref[...], slab)
 
     def place(kind):
         start = LATE + tracers * STEPS + kind * groups
@@ -353,7 +360,7 @@
     shape = (cols, tracers * cols)
     source, lane = row_iota(shape), lane_iota(shape)
     spread = (source // (2 * rows) == lane // cols) & (lane % TILE == TILE - 1)
-    edge = picked_by(edge, spread.astype(F32).astype(BF16))
+    edge = spread_by(edge, spread.astype(F32).astype(BF16))
     main, north = place(0), place(1)
     group = lane_iota((rows, cols)) // TILE
     wet, coupling = static_ref[WET], static_ref[COUPLING]
@@ -425,9 +432,9 @@
     return found
 
 
-def first_pack_kernel(table_ref, planes_ref, send_ref, *, tracers, deep_rows):
+def first_pack_kernel(pack_ref, planes_ref, send_ref, *, tracers):
     late = [[planes_ref[LATE + tracer * STEPS + k] for k in range(STEPS)] for tracer in range(tracers)]
-    send_surface(late, [values[1] for values in late], planes_ref, table_ref, send_ref, deep_rows)
+    send_surface(late, [values[1] for values in late], planes_ref, pack_ref, send_ref, lambda part, first: None)
 
 
 def first_send_kernel(pack_ref, south_ref, static_in, send_ref, static_ref, *, tracers):
@@ -450,28 +457,45 @@
         send_ref[here] = pack_ref[here]
 
 
-def exchange_kernel(static_in, recv_ref, table_ref, *refs, step, tracers, count, deep_rows, unread=0):
+def exchange_kernel(
+    static_in, recv_ref, pick_ref, pack_ref, *refs, step, tracers, count, unread=0
+):
     early_ref, refs = (refs[0], refs[1:]) if step >= 2 else (None, refs)
     refs = refs[unread:]
-    static_in = static_in if step == STEPS - 1 else refs[0]
-    late = [[static_in[LATE + tracer * STEPS + k] for k in range(count)] for tracer in range(tracers)]
+    last = step == STEPS - 1
+    refs = refs if last else refs[1:]
+    static_ref = static_in if last else refs[0]
+    late = [[static_ref[LATE + tracer * STEPS + k] for k in range(count)] for tracer in range(tracers)]
     early = [early_levels(step, early_ref, tracer, tracers) for tracer in range(tracers)]
-    stepped = upper_levels(recv_ref, late, early, static_in)
+    stepped = upper_levels(recv_ref, late, early, static_ref)
     surface = [values[0] for values in stepped]
-    surface = receive_surface(recv_ref, table_ref, static_in, surface)
+    surface = receive_surface(recv_ref, pick_ref, static_ref, surface)
     for tracer in range(tracers):
         stepped[tracer][0] = surface[tracer]
-    if step == STEPS - 1:
+    if last:
         (out_ref,) = refs
         for tracer in range(tracers):
             for k in range(STEPS):
                 out_ref[tracer, k] = stepped[tracer][k]
         return
-    static_ref, send_ref = refs
+    _, send_ref, blocks_ref, sems = refs
     for tracer in range(tracers):
         for k, value in enumerate(stepped[tracer]):
             static_ref[LATE + tracer * STEPS + k] = value
-    send_surface(stepped, [values[1] for values in stepped], static_in, table_ref, send_ref, deep_rows)
+    copies = []
+
+    def ready(part, first):
+        size = blocks_ref.shape[0] // (2 if part == 0 else 2 * PARTS)
+        copies.append(
+            pltpu.make_async_copy(
+                blocks_ref.at[pl.ds(first, size)], send_ref.at[pl.ds(first, size)], sems.at[part]
+            )
+        )
+        copies[-1].start()
+
+    send_surface(stepped, [values[1] for values in stepped], static_ref, pack_ref, blocks_ref, ready)
+    for copy in copies:
+        copy.wait()
 
 
 def whole(array):
@@ -500,7 +524,7 @@
         input_output_aliases=aliases or {},
         name=name,
         cost_estimate=pl.CostEstimate(flops=0, bytes_accessed=us * 3_000_000, transcendentals=0),
-        compiler_params=pltpu.CompilerParams(vmem_limit_bytes=mib * 1024 * 1024),
+        compiler_params=pltpu.CompilerParams(vmem_limit_bytes=int(mib * 1024 * 1024)),
     )(*operands)
 
 
@@ -521,7 +545,7 @@
     return lines[0:1], lines[1:2], columns[:, 0:1], columns[:, 1:2]
 
 
-def write_tables(partner, table_ref, planes_ref, start, rows, groups, n_lat, n_lon):
+def write_tables(partner, pick_ref, pack_ref, planes_ref, start, rows, groups, n_lat, n_lon):
     count = rows * groups
     devices = n_lat * n_lon
     line_target, line_slot, target, slot = tile_order(partner, rows, groups)
@@ -543,15 +567,18 @@
         jnp.where(east_ok, east_device * SLAB + SLAB - 1, -1),
         jnp.where(east_ok, target * SLAB + SLAB - 1, -1),
     )
-    index = lax.broadcasted_iota(jnp.int32, (count, table_ref.shape[1]), 1)
+    index = lax.broadcasted_iota(jnp.int32, (count, pick_ref.shape[1]), 1) % (devices * SLAB)
     for kind, pick in enumerate(picks):
-        table_ref[kind * count : (kind + 1) * count, :] = (pick == index).astype(F32).astype(BF16)
-    height = devices * SLAB
-    packing = (sent % groups) * height + line_target * SLAB + sent // groups
-    slots = lax.broadcasted_iota(jnp.int32, (groups * height, count), 0)
-    table_ref[4 * count :, 0:count] = (slots == packing).astype(F32).astype(BF16)
-    if table_ref.shape[1] > count:
-        table_ref[4 * count :, count:] = jnp.zeros((groups * height, table_ref.shape[1] - count), BF16)
+        pick_ref[kind * count : (kind + 1) * count, :] = (pick == index).astype(F32).astype(BF16)
+    height = pack_ref.shape[0] // (groups * PARTS)
+    main_rows = height * PARTS // devices
+    per_part = devices // PARTS
+    packing = (line_target // per_part) * (groups * height) + (sent % groups) * height
+    packing = packing + (line_target % per_part) * main_rows + sent // groups
+    slots = lax.broadcasted_iota(jnp.int32, (pack_ref.shape[0], count), 0)
+    packing = (slots == packing).astype(F32).astype(BF16)
+    for i in range(3):
+        pack_ref[:, i * count : (i + 1) * count] = packing
 
     lane = lax.broadcasted_iota(jnp.int32, (count, groups * TILE), 1)
     places = (
@@ -566,7 +593,7 @@
 
 
 def prepare_kernel(*refs, n_lat, n_lon):
-    fields, kappa, courant, share_ref, wet_share_ref, partner, table_ref, planes_ref, sems = refs
+    fields, kappa, courant, share_ref, wet_share_ref, partner, *tables, planes_ref, sems = refs
     tracers, _, rows, cols = fields.shape
     sources = [(kappa.at[0:STEPS], KAPPA, STEPS)]
     sources += [(fields.at[tracer, 0:STEPS], LATE + tracer * STEPS, STEPS) for tracer in range(tracers)]
@@ -576,7 +603,7 @@
     ]
     for copy in copies:
         copy.start()
-    write_tables(partner[...], table_ref, planes_ref, LATE + tracers * STEPS, rows, cols // TILE, n_lat, n_lon)
+    write_tables(partner[...], *tables, planes_ref, LATE + tracers * STEPS, rows, cols // TILE, n_lat, n_lon)
     planes_ref[ZONAL] = courant[0]
     planes_ref[MERIDIONAL] = courant[1]
     planes_ref[COUPLING] = share_ref[0] + share_ref[1]
@@ -624,19 +651,20 @@
     def exchanged(send):
         return lax.all_to_all(send, ("mp", "lat", "lon"), split_axis=0, concat_axis=0, tiled=True)
 
-    deep_rows = 4 * count
+    main_rows = -(-max(2, 2 * count // devices) // groups)
     width = ((tracers + 1) * -(-levels // PACKED) + 2) * cols
-    table_shape = jax.ShapeDtypeStruct(
-        (deep_rows + groups * devices * SLAB, max(count, devices * SLAB)), BF16
+    table_shapes = (
+        jax.ShapeDtypeStruct((4 * count, 3 * devices * SLAB), BF16),
+        jax.ShapeDtypeStruct((groups * devices * main_rows, 3 * count), BF16),
     )
     planes_shape = shaped(LATE + tracers * STEPS + 3 * groups, rows, cols)
     north_shape = shaped((tracers + 1) * (levels // 2) + 1 + width // cols, 2 * STEPS, cols)
-    table, planes = call(
+    *tables, planes = call(
         functools.partial(prepare_kernel, n_lat=n_lat, n_lon=n_lon),
         (fields, kappa, courant, share, wet_share, partner),
         [FAR, FAR, NEAR, NEAR, NEAR, NEAR],
-        (table_shape, planes_shape),
-        (NEAR, NEAR),
+        (*table_shapes, planes_shape),
+        (NEAR, NEAR, NEAR),
         "prepare",
         scratch=[pltpu.SemaphoreType.DMA((1 + tracers,))],
         us=2,
@@ -644,8 +672,8 @@
     )
     send_shape = shaped(2 * devices, 2 * SLAB, cols)
     pack = call(
-        functools.partial(first_pack_kernel, tracers=tracers, deep_rows=deep_rows),
-        (table, planes),
+        functools.partial(first_pack_kernel, tracers=tracers),
+        (tables[1], planes),
         [NEAR, NEAR],
         send_shape,
         NEAR,
@@ -678,13 +706,12 @@
 
     def deep_levels(tracer, before, halo):
         block = pl.BlockSpec((1, levels, rows, cols), lambda i: (tracer, 0, 0, 0))
-        token = shaped(8, cols)
         return call(
             functools.partial(deep_kernel, tracer=tracer, tracers=tracers),
             (send, fields, *before, *halo),
             [UNREAD, block, *(UNREAD for _ in before), *(whole(a) for a in halo)],
-            (shaped(*fields.shape), token),
-            (block, whole(token)),
+            shaped(*fields.shape),
+            block,
             "deep_levels",
             grid=(1,),
             aliases={2: 0} if before else None,
@@ -692,17 +719,25 @@
             us=4,
         )
 
+    scratch = [pltpu.VMEM(send_shape.shape, F32), pltpu.SemaphoreType.DMA((1 + PARTS,))]
     reached = (STEPS, STEPS - 1, 2, 3)
     for step in range(STEPS):
         if step > 0:
             recv = exchanged(send)
         kernel = functools.partial(
-            exchange_kernel, step=step, tracers=tracers, count=reached[step], deep_rows=deep_rows
+            exchange_kernel, step=step, tracers=tracers, count=reached[step]
         )
-        operands = (planes, recv, table)
+        operands = (planes, recv, *tables)
         if step == 0:
             planes, send = call(
-                kernel, operands, [NEAR] * 3, (planes_shape, send_shape), (NEAR, NEAR), "exchange", aliases={0: 0}
+                kernel,
+                (*operands, send),
+                [*[NEAR] * 4, UNREAD],
+                (planes_shape, send_shape),
+                (NEAR, UNREAD),
+                "exchange",
+                aliases={0: 0, 4: 1},
+                scratch=scratch,
             )
             north = call(
                 corner_kernel,
@@ -718,7 +753,14 @@
             halo = (kappa, courant, north, east)
         if step == 1:
             planes, send = call(
-                kernel, operands, [NEAR] * 3, (planes_shape, send_shape), (NEAR, NEAR), "exchange", aliases={0: 0}
+                kernel,
+                (*operands, send),
+                [*[NEAR] * 4, UNREAD],
+                (planes_shape, send_shape),
+                (NEAR, UNREAD),
+                "exchange",
+                aliases={0: 0, 4: 1},
+                scratch=scratch,
             )
         if step == 2:
             early_shape = shaped((STEPS - 2) * tracers * 4 + 1, rows, cols)
@@ -737,19 +779,21 @@
                 scratch=[pltpu.VMEM((UPPER, tall, cols), F32)],
                 us=2,
             )
-            out, token = deep_levels(0, (), halo)
             planes, send = call(
-                functools.partial(kernel, unread=1),
-                (*operands, early, token),
-                [*[NEAR] * 4, UNREAD],
+                kernel,
+                (*operands, early, send),
+                [*[NEAR] * 5, UNREAD],
                 (planes_shape, send_shape),
-                (NEAR, NEAR),
+                (NEAR, UNREAD),
                 "exchange",
-                aliases={0: 0},
+                aliases={0: 0, 5: 1},
+                scratch=scratch,
             )
         if step == 3:
-            for tracer in range(1, tracers):
-                out, token = deep_levels(tracer, (out,), halo)
+            before = ()
+            for tracer in range(tracers):
+                before = (deep_levels(tracer, before, halo),)
+            (out,) = before
             operands = (*operands, early)
             return call(
                 functools.partial(kernel, unread=1),

time: 62.3 us -> 59.5 us (0.955)
  Pallas kernels: 19.3 us -> 17.4 us
  starting transfers between devices: 22 us -> 21.1 us
    pallas_call x12, Pallas kernels: 19.3 us -> 17.4 us  [call(): pl.pallas_call(kernel, grid=grid, in_specs=specs, out_shape=out_shape, ou...]
    all_to_all x4, starting transfers between devices: 13.9 us -> 13 us  [exchanged(): lax.all_to_all(send, ('mp', 'lat', 'lon'), split_axis=0, concat_axis=0, t...]
    all_to_all x4, waiting for transfers between devices: 14.8 us -> 14.1 us  [exchanged(): lax.all_to_all(send, ('mp', 'lat', 'lon'), split_axis=0, concat_axis=0, t...]
    ppermute x1, waiting for transfers between devices: 2.59 us -> 3.25 us  [local(): lax.ppermute(north, 'lat', [((i + 1) % n_lat, i) for i in range(n_lat)])]
  transfers between devices with their start and end apart: 7 -> 7, of which waited for: 5 -> 5; matrix products, arithmetic and copies ran while one was open for 0% -> 0% of each run, Pallas kernels for 25% -> 24%
where the time goes in v10:
time: 59.5 us; the launch traced here: 59 us
  starting transfers between devices  21.1 us (35%)
  Pallas kernels  17.4 us (29%)
  waiting for transfers between devices  17.4 us (29%)
  local copies, waits for them, and re-layouts  2.16 us (4%)
  other arithmetic  0.74 us (1%)
    pallas_call x12, Pallas kernels, call(): pl.pallas_call(kernel, grid=grid, in_specs=specs, out_shape=out_shape, ou...  17.4 us
    all_to_all x4, waiting for transfers between devices, exchanged(): lax.all_to_all(send, ('mp', 'lat', 'lon'), split_axis=0, concat_axis=0, t...  14.1 us
    all_to_all x4, starting transfers between devices, exchanged(): lax.all_to_all(send, ('mp', 'lat', 'lon'), split_axis=0, concat_axis=0, t...  13 us
    ppermute x1, starting transfers between devices, local(): lax.ppermute(east, 'lon', [((i + 1) % n_lon, i) for i in range(n_lon)])  3.43 us
    ppermute x1, waiting for transfers between devices, local(): lax.ppermute(north, 'lat', [((i + 1) % n_lat, i) for i in range(n_lat)])  3.25 us
    ppermute x1, starting transfers between devices, local(): lax.ppermute(share, 'lat', [(i, (i + 1) % n_lat) for i in range(n_lat)])  3.02 us
    unnamed x12, local copies, waits for them, and re-layouts  2.16 us
    ppermute x1, starting transfers between devices, local(): lax.ppermute(north, 'lat', [((i + 1) % n_lat, i) for i in range(n_lat)])  1.65 us
  transfers between devices with their start and end apart: 7, of which 5 were waited for; matrix products, arithmetic and copies ran while one was open for 0% of the time, Pallas kernels for 24%

profile of v10, /device:TPU:0, one launch (start us, length us, event | category | flops | bytes accessed | tf_op | source)
XLA Modules:
  0.0 59.0 jit_solution(623391104863021585)
XLA Ops:
  0.0 0.7 %fusion = (f32[1,16,128]{2,1,0:T(8,128)S(1)}, f32[1,16,128]{2,1,0:T(8,128)S(1)}, f32[16,128]{1,0:T(8,128)S(1)}) fusion(f32[1,16,128]{2,1,0:T(8,128)} %param.9, f32[1,71,16,128]{3,2,1,0:T(8,128)} %param.8, s32[1,16,128]{2,1,0:T(8,128)} %param.11), kind=kLoop, calls=%fused_computation.3 | loop fusion | flops 10240 | bytes 49152 | tf_op jit(solution)/shard_map/mul | solution.py:647
  0.7 3.0 %collective-permute-start = (f32[2,16,128]{2,1,0:T(8,128)S(1)}, f32[2,16,128]{2,1,0:T(8,128)S(1)}, u32[]{:S(2)}, u32[]{:S(2)}) collective-permute-start(f32[2,16,128]{2,1,0:T(8,128)S(1)} %pad_maximum_fusion.refs_3_), channel_id=1, source_target_pairs={{0,8},{8,0},{1,9},{9,1},{2,10},{10,2},{3,11},{11,3},{4,12},{12,4},... | collective-permute-start | bytes 49160 | tf_op jit(solution)/shard_map/ppermute | solution.py:649
  3.8 0.7 %copy-done.3 = f32[1,2,16,128]{3,2,1,0:T(8,128)S(1)} copy-done((f32[1,2,16,128]{3,2,1,0:T(8,128)S(1)}, f32[1,2,16,128]{3,2,1,0:T(8,128)}, u32[]{:S(2)}) %copy-start.3) | copy-done | bytes 16408
  5.1 0.8 %prepare.1 = (bf16[512,192]{1,0:T(8,128)(2,1)S(1)}, bf16[256,384]{1,0:T(8,128)(2,1)S(1)}, f32[42,16,128]{2,1,0:T(8,128)S(1)}) custom-call(f32[2,72,16,128]{3,2,1,0:T(8,128)} %bitcast.11, f32[71,16,128]{2,1,0:T(8,128)} %bitcast.16, f32[2,16,128]{2,1,0:T(8,128)S(1)} %bitcast.21, f32[2,16,128]{2,1,0:T(8,128)S(1)} %pad_maximum_fusion.refs_3_, ...), custom_call_target="tpu_custom_call" | custom-call | bytes 6000000 | tf_op jit(solution)/shard_map/prepare/pallas_call | solution.py:517
  7.2 5.3 %all-to-all-start = ((f32[32,8,128]{2,1,0:T(8,128)}), f32[32,8,128]{2,1,0:T(8,128)S(1)}, u32[]{:S(2)}, u32[]{:S(2)}) async-start(f32[32,8,128]{2,1,0:T(8,128)} %get-tuple-element.21.refs_0_.after_ref), calls=%async_computation | async-start | bytes 262144 | tf_op jit(solution)/shard_map/all_to_all | solution.py:652
  12.5 2.1 %halo.1 = (f32[120,8,128]{2,1,0:T(8,128)S(1)}, f32[16,1408]{1,0:T(8,128)S(1)}) custom-call(f32[32,8,128]{2,1,0:T(8,128)} %get-tuple-element.21.refs_0_.after_ref, f32[2,72,16,128]{3,2,1,0:T(8,128)} %bitcast.12, f32[71,16,128]{2,1,0:T(8,128)} %bitcast.17, f32[2,16,128]{2,1,0:T(8,128)S(1)} %bitcast.22), custom_call_target="tpu_custom_call" | custom-call | bytes 6000000 | tf_op jit(solution)/shard_map/halo/pallas_call | solution.py:517
  14.6 3.4 %collective-permute-start.1 = (f32[16,1408]{1,0:T(8,128)S(1)}, f32[16,1408]{1,0:T(8,128)S(1)}, u32[]{:S(2)}, u32[]{:S(2)}) collective-permute-start(f32[16,1408]{1,0:T(8,128)S(1)} %get-tuple-element.27), channel_id=1, source_target_pairs={{1,0},{2,1},{3,2},{4,3},{5,4},{6,5},{7,6},{0,7},{9,8},{10,9},{11,1... | collective-permute-start | bytes 270344 | tf_op jit(solution)/shard_map/ppermute | solution.py:704
  18.0 2.7 %all-to-all-done.recv_ref = f32[32,8,128]{2,1,0:T(8,128)S(1)} async-done(((f32[32,8,128]{2,1,0:T(8,128)}), f32[32,8,128]{2,1,0:T(8,128)S(1)}, u32[]{:S(2)}, u32[]{:S(2)}) %all-to-all-start) | async-done | bytes 131104 | tf_op jit(solution)/shard_map/all_to_all | solution.py:652
  20.7 1.6 %exchange.3 = (f32[42,16,128]{2,1,0:T(8,128)S(1)}, f32[32,8,128]{2,1,0:T(8,128)}) custom-call(f32[42,16,128]{2,1,0:T(8,128)S(1)} %get-tuple-element.20.static_in, f32[32,8,128]{2,1,0:T(8,128)S(1)} %all-to-all-done.recv_ref, bf16[512,192]{1,0:T(8,128)(2,1)S(1)} %get-tuple-element.22.pick_ref, ...), custom_call_target="tpu_custom_call", output_to_operand_aliasing={{0}: (0, {}), {1}: (4, {})} | custom-call | bytes 3000000 | tf_op jit(solution)/shard_map/exchange/pallas_call | solution.py:517
  22.3 2.6 %all-to-all-start.1 = ((f32[32,8,128]{2,1,0:T(8,128)}), f32[32,8,128]{2,1,0:T(8,128)S(1)}, u32[]{:S(2)}, u32[]{:S(2)}) async-start(f32[32,8,128]{2,1,0:T(8,128)} %get-tuple-element.24.refs_0_.after_ref), calls=%async_computation.1 | async-start | bytes 262144 | tf_op jit(solution)/shard_map/all_to_all | solution.py:652
  25.1 0.8 %copy-done.2 = f32[120,8,128]{2,1,0:T(8,128)} copy-done((f32[120,8,128]{2,1,0:T(8,128)}, f32[120,8,128]{2,1,0:T(8,128)S(1)}, u32[]{:S(2)}) %copy-start.2) | copy-done | bytes 491544
  25.9 1.7 %collective-permute-start.2 = (f32[120,8,128]{2,1,0:T(8,128)}, f32[120,8,128]{2,1,0:T(8,128)S(1)}, u32[]{:S(2)}, u32[]{:S(2)}) collective-permute-start(f32[120,8,128]{2,1,0:T(8,128)} %copy-done.2), channel_id=1, source_target_pairs={{8,0},{0,8},{9,1},{1,9},{10,2},{2,10},{11,3},{3,11},{12,4},{4,12},... | collective-permute-start | bytes 1474568 | tf_op jit(solution)/shard_map/ppermute | solution.py:752
  27.6 5.5 %all-to-all-done.1.recv_ref = f32[32,8,128]{2,1,0:T(8,128)S(1)} async-done(((f32[32,8,128]{2,1,0:T(8,128)}), f32[32,8,128]{2,1,0:T(8,128)S(1)}, u32[]{:S(2)}, u32[]{:S(2)}) %all-to-all-start.1) | async-done | bytes 131104 | tf_op jit(solution)/shard_map/all_to_all | solution.py:652
  33.1 1.6 %exchange.4 = (f32[42,16,128]{2,1,0:T(8,128)S(1)}, f32[32,8,128]{2,1,0:T(8,128)}) custom-call(f32[42,16,128]{2,1,0:T(8,128)S(1)} %get-tuple-element.23.static_in, f32[32,8,128]{2,1,0:T(8,128)S(1)} %all-to-all-done.1.recv_ref, bf16[512,192]{1,0:T(8,128)(2,1)S(1)} %get-tuple-element.22.pick_ref, ...), custom_call_target="tpu_custom_call", output_to_operand_aliasing={{0}: (0, {}), {1}: (4, {})} | custom-call | bytes 3000000 | tf_op jit(solution)/shard_map/exchange/pallas_call | solution.py:517
  34.7 2.6 %all-to-all-start.2 = ((f32[32,8,128]{2,1,0:T(8,128)}), f32[32,8,128]{2,1,0:T(8,128)S(1)}, u32[]{:S(2)}, u32[]{:S(2)}) async-start(f32[32,8,128]{2,1,0:T(8,128)} %get-tuple-element.26.refs_1_), calls=%async_computation.2 | async-start | bytes 262144 | tf_op jit(solution)/shard_map/all_to_all | solution.py:652
  37.3 3.2 %collective-permute-done.2.rows_ref.refs_2_.refs_3_ = f32[120,8,128]{2,1,0:T(8,128)S(1)} collective-permute-done((f32[120,8,128]{2,1,0:T(8,128)}, f32[120,8,128]{2,1,0:T(8,128)S(1)}, u32[]{:S(2)}, u32[]{:S(2)}) %collective-permute-start.2) | collective-permute-done | bytes 491552 | tf_op jit(solution)/shard_map/ppermute | solution.py:752
  40.6 0.8 %early_levels.1.refs_0_ = f32[17,16,128]{2,1,0:T(8,128)S(1)} custom-call(f32[2,72,16,128]{3,2,1,0:T(8,128)S(1)} %bitcast.13, f32[71,16,128]{2,1,0:T(8,128)S(1)} %bitcast.18, f32[2,16,128]{2,1,0:T(8,128)S(1)} %bitcast.23, f32[120,8,128]{2,1,0:T(8,128)S(1)} %collective-permute-done.2.rows_ref.refs_2_.refs_3_, ...), custom_call_target="tpu_custom_call" | custom-call | bytes 6000000 | tf_op jit(solution)/shard_map/early_levels/pallas_call | solution.py:517
  41.3 4.2 %all-to-all-done.2.recv_ref = f32[32,8,128]{2,1,0:T(8,128)S(1)} async-done(((f32[32,8,128]{2,1,0:T(8,128)}), f32[32,8,128]{2,1,0:T(8,128)S(1)}, u32[]{:S(2)}, u32[]{:S(2)}) %all-to-all-start.2) | async-done | bytes 131104 | tf_op jit(solution)/shard_map/all_to_all | solution.py:652
  45.5 1.6 %exchange.5 = (f32[42,16,128]{2,1,0:T(8,128)S(1)}, f32[32,8,128]{2,1,0:T(8,128)}) custom-call(f32[42,16,128]{2,1,0:T(8,128)S(1)} %get-tuple-element.25.static_in, f32[32,8,128]{2,1,0:T(8,128)S(1)} %all-to-all-done.2.recv_ref, bf16[512,192]{1,0:T(8,128)(2,1)S(1)} %get-tuple-element.22.pick_ref, ...), custom_call_target="tpu_custom_call", output_to_operand_aliasing={{0}: (0, {}), {1}: (5, {})} | custom-call | bytes 3000000 | tf_op jit(solution)/shard_map/exchange/pallas_call | solution.py:517
  47.1 2.6 %all-to-all-start.3 = ((f32[32,8,128]{2,1,0:T(8,128)}), f32[32,8,128]{2,1,0:T(8,128)S(1)}, u32[]{:S(2)}, u32[]{:S(2)}) async-start(f32[32,8,128]{2,1,0:T(8,128)} %get-tuple-element.30.after_ref), calls=%async_computation.3 | async-start | bytes 262144 | tf_op jit(solution)/shard_map/all_to_all | solution.py:652
  49.7 3.2 %deep_levels.2.refs_0_ = f32[2,72,16,128]{3,2,1,0:T(8,128)} custom-call(f32[32,8,128]{2,1,0:T(8,128)} %get-tuple-element.30.after_ref, f32[2,72,16,128]{3,2,1,0:T(8,128)S(1)} %bitcast.14, f32[71,16,128]{2,1,0:T(8,128)S(1)} %bitcast.19, f32[2,16,128]{2,1,0:T(8,128)S(1)} %bitcast.24, f32[120,8,128]{2,1,0:T(8,128)S(1)} %collective-permute-done.2.rows_ref.refs_2_.refs_3_, ...), custom_call_target="tpu_custom_call" | custom-call | bytes 12000000 | tf_op jit(solution)/shard_map/deep_levels/pallas_call | solution.py:517
  52.9 3.2 %deep_levels.3.refs_1_ = f32[2,72,16,128]{3,2,1,0:T(8,128)} custom-call(f32[32,8,128]{2,1,0:T(8,128)} %get-tuple-element.30.after_ref, f32[2,72,16,128]{3,2,1,0:T(8,128)S(1)} %bitcast.15, f32[2,72,16,128]{3,2,1,0:T(8,128)} %deep_levels.2.refs_0_, f32[71,16,128]{2,1,0:T(8,128)S(1)} %bitcast.20, ...), custom_call_target="tpu_custom_call", output_to_operand_aliasing={{}: (2, {})} | custom-call | bytes 12000000 | tf_op jit(solution)/shard_map/deep_levels/pallas_call | solution.py:517
  56.1 1.7 %all-to-all-done.3.recv_ref = f32[32,8,128]{2,1,0:T(8,128)S(1)} async-done(((f32[32,8,128]{2,1,0:T(8,128)}), f32[32,8,128]{2,1,0:T(8,128)S(1)}, u32[]{:S(2)}, u32[]{:S(2)}) %all-to-all-start.3) | async-done | bytes 131104 | tf_op jit(solution)/shard_map/all_to_all | solution.py:652
  57.9 1.1 %last_exchange.1 = f32[2,72,16,128]{3,2,1,0:T(8,128)} custom-call(f32[42,16,128]{2,1,0:T(8,128)S(1)} %get-tuple-element.29.static_in, f32[32,8,128]{2,1,0:T(8,128)S(1)} %all-to-all-done.3.recv_ref, bf16[512,192]{1,0:T(8,128)(2,1)S(1)} %get-tuple-element.22.pick_ref, bf16[256,384]{1,0:T(8,128)(2,1)S(1)} %get-tuple-element.18.pack_ref, ...), custom_call_target="tpu_custom_call", output_to_operand_aliasing={{}: (5, {})} | custom-call | bytes 3000000 | tf_op jit(solution)/shard_map/last_exchange/pallas_call | solution.py:517
  (16 shorter events, 2.1 us)
Async XLA Ops:
  0.7 5.8 %collective-permute-start = (f32[2,16,128]{2,1,0:T(8,128)S(1)}, f32[2,16,128]{2,1,0:T(8,128)S(1)}, u32[]{:S(2)}, u32[]{:S(2)}) collective-permute-start(f32[2,16,128]{2,1,0:T(8,128)S(1)} %pad_maximum_fusion.refs_3_), channel_id=1, source_target_pairs={{0,8},{8,0},{1,9},{9,1},{2,10},{10,2},{3,11},{11,3},{4,12},{12,4},... | collective-permute-start | bytes 49160 | tf_op jit(solution)/shard_map/ppermute | solution.py:649
  3.8 0.7 %copy-start.3 = (f32[1,2,16,128]{3,2,1,0:T(8,128)S(1)}, f32[1,2,16,128]{3,2,1,0:T(8,128)}, u32[]{:S(2)}) copy-start(f32[1,2,16,128]{3,2,1,0:T(8,128)} %param.7) | copy-start | bytes 49156
  4.5 0.7 %copy-start.5 = (s32[1,128]{1,0:T(1,128)S(1)}, s32[1,128]{1,0:T(1,128)}, u32[]{:S(2)}) copy-start(s32[1,128]{1,0:T(1,128)} %refs_5_.1) | copy-start | bytes 1540
  5.1 7.4 %copy-start.4 = (f32[1,2,16,128]{3,2,1,0:T(8,128)S(1)}, f32[1,2,16,128]{3,2,1,0:T(8,128)}, u32[]{:S(2)}) copy-start(f32[1,2,16,128]{3,2,1,0:T(8,128)} %param.7) | copy-start | bytes 49156
  7.2 13.5 %all-to-all-start = ((f32[32,8,128]{2,1,0:T(8,128)}), f32[32,8,128]{2,1,0:T(8,128)S(1)}, u32[]{:S(2)}, u32[]{:S(2)}) async-start(f32[32,8,128]{2,1,0:T(8,128)} %get-tuple-element.21.refs_0_.after_ref), calls=%async_computation | async-start | bytes 262144 | tf_op jit(solution)/shard_map/all_to_all | solution.py:652
  14.6 10.3 %collective-permute-start.1 = (f32[16,1408]{1,0:T(8,128)S(1)}, f32[16,1408]{1,0:T(8,128)S(1)}, u32[]{:S(2)}, u32[]{:S(2)}) collective-permute-start(f32[16,1408]{1,0:T(8,128)S(1)} %get-tuple-element.27), channel_id=1, source_target_pairs={{1,0},{2,1},{3,2},{4,3},{5,4},{6,5},{7,6},{0,7},{9,8},{10,9},{11,1... | collective-permute-start | bytes 270344 | tf_op jit(solution)/shard_map/ppermute | solution.py:704
  22.3 10.8 %all-to-all-start.1 = ((f32[32,8,128]{2,1,0:T(8,128)}), f32[32,8,128]{2,1,0:T(8,128)S(1)}, u32[]{:S(2)}, u32[]{:S(2)}) async-start(f32[32,8,128]{2,1,0:T(8,128)} %get-tuple-element.24.refs_0_.after_ref), calls=%async_computation.1 | async-start | bytes 262144 | tf_op jit(solution)/shard_map/all_to_all | solution.py:652
  24.9 15.6 %copy-start = (f32[1,2,72,16,128]{4,3,2,1,0:T(8,128)S(1)}, f32[1,2,72,16,128]{4,3,2,1,0:T(8,128)}, u32[]{:S(2)}) copy-start(f32[1,2,72,16,128]{4,3,2,1,0:T(8,128)} %param.6) | copy-start | bytes 3538948
  24.9 15.6 %copy-start.1 = (f32[1,71,16,128]{3,2,1,0:T(8,128)S(1)}, f32[1,71,16,128]{3,2,1,0:T(8,128)}, u32[]{:S(2)}) copy-start(f32[1,71,16,128]{3,2,1,0:T(8,128)} %param.8) | copy-start | bytes 1744900
  25.1 0.8 %copy-start.2 = (f32[120,8,128]{2,1,0:T(8,128)}, f32[120,8,128]{2,1,0:T(8,128)S(1)}, u32[]{:S(2)}) copy-start(f32[120,8,128]{2,1,0:T(8,128)S(1)} %corner.1) | copy-start | bytes 1474564
  25.9 14.6 %collective-permute-start.2 = (f32[120,8,128]{2,1,0:T(8,128)}, f32[120,8,128]{2,1,0:T(8,128)S(1)}, u32[]{:S(2)}, u32[]{:S(2)}) collective-permute-start(f32[120,8,128]{2,1,0:T(8,128)} %copy-done.2), channel_id=1, source_target_pairs={{8,0},{0,8},{9,1},{1,9},{10,2},{2,10},{11,3},{3,11},{12,4},{4,12},... | collective-permute-start | bytes 1474568 | tf_op jit(solution)/shard_map/ppermute | solution.py:752
  34.7 10.8 %all-to-all-start.2 = ((f32[32,8,128]{2,1,0:T(8,128)}), f32[32,8,128]{2,1,0:T(8,128)S(1)}, u32[]{:S(2)}, u32[]{:S(2)}) async-start(f32[32,8,128]{2,1,0:T(8,128)} %get-tuple-element.26.refs_1_), calls=%async_computation.2 | async-start | bytes 262144 | tf_op jit(solution)/shard_map/all_to_all | solution.py:652
  47.1 10.8 %all-to-all-start.3 = ((f32[32,8,128]{2,1,0:T(8,128)}), f32[32,8,128]{2,1,0:T(8,128)S(1)}, u32[]{:S(2)}, u32[]{:S(2)}) async-start(f32[32,8,128]{2,1,0:T(8,128)} %get-tuple-element.30.after_ref), calls=%async_computation.3 | async-start | bytes 262144 | tf_op jit(solution)/shard_map/all_to_all | solution.py:652

commit v11 on v10

--- a/solution.py
+++ b/solution.py
@@ -44,6 +44,10 @@
 def lane_roll(value, shift):
     shift = shift % value.shape[-1]
     return value if shift == 0 else pltpu.roll(value, shift, 1)
+
+
+def lanes_at(value, index):
+    return jnp.take_along_axis(value, index, axis=1)
 
 
 def next_row(value):
@@ -294,14 +298,7 @@
     send_ref[model * devices + here.west] = own_east
     ready(0, model * devices)
     for scaled in all_scaled:
-        blocks = []
-        for c in range(groups):
-            block = jnp.where(group == c, scaled, 0.0)
-            shift = TILE
-            while shift < cols:
-                block = block + lane_roll(block, shift)
-                shift *= 2
-            blocks.append(block)
+        blocks = [lanes_at(scaled, c * TILE + lane % TILE) for c in range(groups)]
         tiles.append(jnp.concatenate(blocks, axis=0))
     edge_east = [jnp.sum(edge, axis=0, keepdims=True) for edge in (raw_east, factors)]
     empty = jnp.zeros((SLAB - 2, cols), F32)
@@ -353,25 +350,21 @@
 
     def place(kind):
         start = LATE + tracers * STEPS + kind * groups
-        return static_ref[start : start + groups].reshape(count, cols) > 0
+        return static_ref[start : start + groups].reshape(count, cols)
 
     edge = found[2 * count : 3 * count, :cols] * found[3 * count :, cols:]
-    edge = jnp.where(place(2), edge, 0.0)
+    edge = jnp.where(place(2) > 0, edge, 0.0)
     shape = (cols, tracers * cols)
     source, lane = row_iota(shape), lane_iota(shape)
     spread = (source // (2 * rows) == lane // cols) & (lane % TILE == TILE - 1)
     edge = spread_by(edge, spread.astype(F32).astype(BF16))
-    main, north = place(0), place(1)
+    main, north = place(0).astype(jnp.int32), place(1).astype(jnp.int32)
     group = lane_iota((rows, cols)) // TILE
     wet, coupling = static_ref[WET], static_ref[COUPLING]
     updated = []
     for tracer in range(tracers):
         spot = slice(tracer * cols, (tracer + 1) * cols)
-        total = jnp.where(main, found[:count, spot], 0.0) + jnp.where(north, found[count : 2 * count, spot], 0.0)
-        shift = TILE
-        while shift < cols:
-            total = total + lane_roll(total, shift)
-            shift *= 2
+        total = lanes_at(found[:count, spot], main) + lanes_at(found[count : 2 * count, spot], north)
         total = total + edge[:, spot]
         received = jnp.zeros((rows, cols), F32)
         for c in range(groups):
@@ -582,8 +575,8 @@
 
     lane = lax.broadcasted_iota(jnp.int32, (count, groups * TILE), 1)
     places = (
-        lane // TILE == came % groups,
-        lane // TILE == group,
+        (came % groups) * TILE + lane % TILE,
+        group * TILE + lane % TILE,
         (lane % rows == row) & (lane < 2 * 2 * rows),
     )
     for kind, place in enumerate(places):

time: 59.5 us -> 59.1 us (level)
  transfers between devices with their start and end apart: 7 -> 7, of which waited for: 5 -> 5; matrix products, arithmetic and copies ran while one was open for 0% -> 0% of each run, Pallas kernels for 24% -> 23%
where the time goes in v11:
time: 59.1 us; the launch traced here: 58.6 us
  starting transfers between devices  21.2 us (36%)
  waiting for transfers between devices  17.4 us (29%)
  Pallas kernels  17 us (29%)
  local copies, waits for them, and re-layouts  2.16 us (4%)
  other arithmetic  0.74 us (1%)
    pallas_call x12, Pallas kernels, call(): pl.pallas_call(kernel, grid=grid, in_specs=specs, out_shape=out_shape, ou...  17 us
    all_to_all x4, waiting for transfers between devices, exchanged(): lax.all_to_all(send, ('mp', 'lat', 'lon'), split_axis=0, concat_axis=0, t...  14 us
    all_to_all x4, starting transfers between devices, exchanged(): lax.all_to_all(send, ('mp', 'lat', 'lon'), split_axis=0, concat_axis=0, t...  13.1 us
    ppermute x1, starting transfers between devices, local(): lax.ppermute(east, 'lon', [((i + 1) % n_lon, i) for i in range(n_lon)])  3.43 us
    ppermute x1, waiting for transfers between devices, local(): lax.ppermute(north, 'lat', [((i + 1) % n_lat, i) for i in range(n_lat)])  3.36 us
    ppermute x1, starting transfers between devices, local(): lax.ppermute(share, 'lat', [(i, (i + 1) % n_lat) for i in range(n_lat)])  3.02 us
    unnamed x12, local copies, waits for them, and re-layouts  2.16 us
    ppermute x1, starting transfers between devices, local(): lax.ppermute(north, 'lat', [((i + 1) % n_lat, i) for i in range(n_lat)])  1.65 us
  transfers between devices with their start and end apart: 7, of which 5 were waited for; matrix products, arithmetic and copies ran while one was open for 0% of the time, Pallas kernels for 23%

profile of v11, /device:TPU:0, one launch (start us, length us, event | category | flops | bytes accessed | tf_op | source)
XLA Modules:
  0.0 58.6 jit_solution(9817617784687331550)
XLA Ops:
  0.0 0.7 %fusion = (f32[1,16,128]{2,1,0:T(8,128)S(1)}, f32[1,16,128]{2,1,0:T(8,128)S(1)}, f32[16,128]{1,0:T(8,128)S(1)}) fusion(f32[1,16,128]{2,1,0:T(8,128)} %param.9, f32[1,71,16,128]{3,2,1,0:T(8,128)} %param.8, s32[1,16,128]{2,1,0:T(8,128)} %param.11), kind=kLoop, calls=%fused_computation.3 | loop fusion | flops 10240 | bytes 49152 | tf_op jit(solution)/shard_map/mul | solution.py:640
  0.7 3.0 %collective-permute-start = (f32[2,16,128]{2,1,0:T(8,128)S(1)}, f32[2,16,128]{2,1,0:T(8,128)S(1)}, u32[]{:S(2)}, u32[]{:S(2)}) collective-permute-start(f32[2,16,128]{2,1,0:T(8,128)S(1)} %pad_maximum_fusion.refs_3_), channel_id=1, source_target_pairs={{0,8},{8,0},{1,9},{9,1},{2,10},{10,2},{3,11},{11,3},{4,12},{12,4},... | collective-permute-start | bytes 49160 | tf_op jit(solution)/shard_map/ppermute | solution.py:642
  3.8 0.7 %copy-done.3 = f32[1,2,16,128]{3,2,1,0:T(8,128)S(1)} copy-done((f32[1,2,16,128]{3,2,1,0:T(8,128)S(1)}, f32[1,2,16,128]{3,2,1,0:T(8,128)}, u32[]{:S(2)}) %copy-start.3) | copy-done | bytes 16408
  5.1 0.8 %prepare.1 = (bf16[512,192]{1,0:T(8,128)(2,1)S(1)}, bf16[256,384]{1,0:T(8,128)(2,1)S(1)}, f32[42,16,128]{2,1,0:T(8,128)S(1)}) custom-call(f32[2,72,16,128]{3,2,1,0:T(8,128)} %bitcast.11, f32[71,16,128]{2,1,0:T(8,128)} %bitcast.16, f32[2,16,128]{2,1,0:T(8,128)S(1)} %bitcast.21, f32[2,16,128]{2,1,0:T(8,128)S(1)} %pad_maximum_fusion.refs_3_, ...), custom_call_target="tpu_custom_call" | custom-call | bytes 6000000 | tf_op jit(solution)/shard_map/prepare/pallas_call | solution.py:510
  7.1 5.4 %all-to-all-start = ((f32[32,8,128]{2,1,0:T(8,128)}), f32[32,8,128]{2,1,0:T(8,128)S(1)}, u32[]{:S(2)}, u32[]{:S(2)}) async-start(f32[32,8,128]{2,1,0:T(8,128)} %get-tuple-element.21.refs_0_.after_ref), calls=%async_computation | async-start | bytes 262144 | tf_op jit(solution)/shard_map/all_to_all | solution.py:645
  12.5 2.1 %halo.1 = (f32[120,8,128]{2,1,0:T(8,128)S(1)}, f32[16,1408]{1,0:T(8,128)S(1)}) custom-call(f32[32,8,128]{2,1,0:T(8,128)} %get-tuple-element.21.refs_0_.after_ref, f32[2,72,16,128]{3,2,1,0:T(8,128)} %bitcast.12, f32[71,16,128]{2,1,0:T(8,128)} %bitcast.17, f32[2,16,128]{2,1,0:T(8,128)S(1)} %bitcast.22), custom_call_target="tpu_custom_call" | custom-call | bytes 6000000 | tf_op jit(solution)/shard_map/halo/pallas_call | solution.py:510
  14.6 3.4 %collective-permute-start.1 = (f32[16,1408]{1,0:T(8,128)S(1)}, f32[16,1408]{1,0:T(8,128)S(1)}, u32[]{:S(2)}, u32[]{:S(2)}) collective-permute-start(f32[16,1408]{1,0:T(8,128)S(1)} %get-tuple-element.27), channel_id=1, source_target_pairs={{1,0},{2,1},{3,2},{4,3},{5,4},{6,5},{7,6},{0,7},{9,8},{10,9},{11,1... | collective-permute-start | bytes 270344 | tf_op jit(solution)/shard_map/ppermute | solution.py:697
  18.0 2.7 %all-to-all-done.recv_ref = f32[32,8,128]{2,1,0:T(8,128)S(1)} async-done(((f32[32,8,128]{2,1,0:T(8,128)}), f32[32,8,128]{2,1,0:T(8,128)S(1)}, u32[]{:S(2)}, u32[]{:S(2)}) %all-to-all-start) | async-done | bytes 131104 | tf_op jit(solution)/shard_map/all_to_all | solution.py:645
  20.7 1.5 %exchange.3 = (f32[42,16,128]{2,1,0:T(8,128)S(1)}, f32[32,8,128]{2,1,0:T(8,128)}) custom-call(f32[42,16,128]{2,1,0:T(8,128)S(1)} %get-tuple-element.20.static_in, f32[32,8,128]{2,1,0:T(8,128)S(1)} %all-to-all-done.recv_ref, bf16[512,192]{1,0:T(8,128)(2,1)S(1)} %get-tuple-element.22.pick_ref, ...), custom_call_target="tpu_custom_call", output_to_operand_aliasing={{0}: (0, {}), {1}: (4, {})} | custom-call | bytes 3000000 | tf_op jit(solution)/shard_map/exchange/pallas_call | solution.py:510
  22.2 2.6 %all-to-all-start.1 = ((f32[32,8,128]{2,1,0:T(8,128)}), f32[32,8,128]{2,1,0:T(8,128)S(1)}, u32[]{:S(2)}, u32[]{:S(2)}) async-start(f32[32,8,128]{2,1,0:T(8,128)} %get-tuple-element.24.refs_0_.after_ref), calls=%async_computation.1 | async-start | bytes 262144 | tf_op jit(solution)/shard_map/all_to_all | solution.py:645
  25.1 0.8 %copy-done.2 = f32[120,8,128]{2,1,0:T(8,128)} copy-done((f32[120,8,128]{2,1,0:T(8,128)}, f32[120,8,128]{2,1,0:T(8,128)S(1)}, u32[]{:S(2)}) %copy-start.2) | copy-done | bytes 491544
  25.8 1.7 %collective-permute-start.2 = (f32[120,8,128]{2,1,0:T(8,128)}, f32[120,8,128]{2,1,0:T(8,128)S(1)}, u32[]{:S(2)}, u32[]{:S(2)}) collective-permute-start(f32[120,8,128]{2,1,0:T(8,128)} %copy-done.2), channel_id=1, source_target_pairs={{8,0},{0,8},{9,1},{1,9},{10,2},{2,10},{11,3},{3,11},{12,4},{4,12},... | collective-permute-start | bytes 1474568 | tf_op jit(solution)/shard_map/ppermute | solution.py:745
  27.5 5.5 %all-to-all-done.1.recv_ref = f32[32,8,128]{2,1,0:T(8,128)S(1)} async-done(((f32[32,8,128]{2,1,0:T(8,128)}), f32[32,8,128]{2,1,0:T(8,128)S(1)}, u32[]{:S(2)}, u32[]{:S(2)}) %all-to-all-start.1) | async-done | bytes 131104 | tf_op jit(solution)/shard_map/all_to_all | solution.py:645
  33.0 1.5 %exchange.4 = (f32[42,16,128]{2,1,0:T(8,128)S(1)}, f32[32,8,128]{2,1,0:T(8,128)}) custom-call(f32[42,16,128]{2,1,0:T(8,128)S(1)} %get-tuple-element.23.static_in, f32[32,8,128]{2,1,0:T(8,128)S(1)} %all-to-all-done.1.recv_ref, bf16[512,192]{1,0:T(8,128)(2,1)S(1)} %get-tuple-element.22.pick_ref, ...), custom_call_target="tpu_custom_call", output_to_operand_aliasing={{0}: (0, {}), {1}: (4, {})} | custom-call | bytes 3000000 | tf_op jit(solution)/shard_map/exchange/pallas_call | solution.py:510
  34.5 2.6 %all-to-all-start.2 = ((f32[32,8,128]{2,1,0:T(8,128)}), f32[32,8,128]{2,1,0:T(8,128)S(1)}, u32[]{:S(2)}, u32[]{:S(2)}) async-start(f32[32,8,128]{2,1,0:T(8,128)} %get-tuple-element.26.refs_1_), calls=%async_computation.2 | async-start | bytes 262144 | tf_op jit(solution)/shard_map/all_to_all | solution.py:645
  37.1 3.4 %collective-permute-done.2.rows_ref.refs_2_.refs_3_ = f32[120,8,128]{2,1,0:T(8,128)S(1)} collective-permute-done((f32[120,8,128]{2,1,0:T(8,128)}, f32[120,8,128]{2,1,0:T(8,128)S(1)}, u32[]{:S(2)}, u32[]{:S(2)}) %collective-permute-start.2) | collective-permute-done | bytes 491552 | tf_op jit(solution)/shard_map/ppermute | solution.py:745
  40.5 0.8 %early_levels.1.refs_0_ = f32[17,16,128]{2,1,0:T(8,128)S(1)} custom-call(f32[2,72,16,128]{3,2,1,0:T(8,128)S(1)} %bitcast.13, f32[71,16,128]{2,1,0:T(8,128)S(1)} %bitcast.18, f32[2,16,128]{2,1,0:T(8,128)S(1)} %bitcast.23, f32[120,8,128]{2,1,0:T(8,128)S(1)} %collective-permute-done.2.rows_ref.refs_2_.refs_3_, ...), custom_call_target="tpu_custom_call" | custom-call | bytes 6000000 | tf_op jit(solution)/shard_map/early_levels/pallas_call | solution.py:510
  41.2 4.0 %all-to-all-done.2.recv_ref = f32[32,8,128]{2,1,0:T(8,128)S(1)} async-done(((f32[32,8,128]{2,1,0:T(8,128)}), f32[32,8,128]{2,1,0:T(8,128)S(1)}, u32[]{:S(2)}, u32[]{:S(2)}) %all-to-all-start.2) | async-done | bytes 131104 | tf_op jit(solution)/shard_map/all_to_all | solution.py:645
  45.3 1.5 %exchange.5 = (f32[42,16,128]{2,1,0:T(8,128)S(1)}, f32[32,8,128]{2,1,0:T(8,128)}) custom-call(f32[42,16,128]{2,1,0:T(8,128)S(1)} %get-tuple-element.25.static_in, f32[32,8,128]{2,1,0:T(8,128)S(1)} %all-to-all-done.2.recv_ref, bf16[512,192]{1,0:T(8,128)(2,1)S(1)} %get-tuple-element.22.pick_ref, ...), custom_call_target="tpu_custom_call", output_to_operand_aliasing={{0}: (0, {}), {1}: (5, {})} | custom-call | bytes 3000000 | tf_op jit(solution)/shard_map/exchange/pallas_call | solution.py:510
  46.8 2.6 %all-to-all-start.3 = ((f32[32,8,128]{2,1,0:T(8,128)}), f32[32,8,128]{2,1,0:T(8,128)S(1)}, u32[]{:S(2)}, u32[]{:S(2)}) async-start(f32[32,8,128]{2,1,0:T(8,128)} %get-tuple-element.30.after_ref), calls=%async_computation.3 | async-start | bytes 262144 | tf_op jit(solution)/shard_map/all_to_all | solution.py:645
  49.4 3.2 %deep_levels.2.refs_0_ = f32[2,72,16,128]{3,2,1,0:T(8,128)} custom-call(f32[32,8,128]{2,1,0:T(8,128)} %get-tuple-element.30.after_ref, f32[2,72,16,128]{3,2,1,0:T(8,128)S(1)} %bitcast.14, f32[71,16,128]{2,1,0:T(8,128)S(1)} %bitcast.19, f32[2,16,128]{2,1,0:T(8,128)S(1)} %bitcast.24, f32[120,8,128]{2,1,0:T(8,128)S(1)} %collective-permute-done.2.rows_ref.refs_2_.refs_3_, ...), custom_call_target="tpu_custom_call" | custom-call | bytes 12000000 | tf_op jit(solution)/shard_map/deep_levels/pallas_call | solution.py:510
  52.6 3.2 %deep_levels.3.refs_1_ = f32[2,72,16,128]{3,2,1,0:T(8,128)} custom-call(f32[32,8,128]{2,1,0:T(8,128)} %get-tuple-element.30.after_ref, f32[2,72,16,128]{3,2,1,0:T(8,128)S(1)} %bitcast.15, f32[2,72,16,128]{3,2,1,0:T(8,128)} %deep_levels.2.refs_0_, f32[71,16,128]{2,1,0:T(8,128)S(1)} %bitcast.20, ...), custom_call_target="tpu_custom_call", output_to_operand_aliasing={{}: (2, {})} | custom-call | bytes 12000000 | tf_op jit(solution)/shard_map/deep_levels/pallas_call | solution.py:510
  55.8 1.7 %all-to-all-done.3.recv_ref = f32[32,8,128]{2,1,0:T(8,128)S(1)} async-done(((f32[32,8,128]{2,1,0:T(8,128)}), f32[32,8,128]{2,1,0:T(8,128)S(1)}, u32[]{:S(2)}, u32[]{:S(2)}) %all-to-all-start.3) | async-done | bytes 131104 | tf_op jit(solution)/shard_map/all_to_all | solution.py:645
  57.6 1.1 %last_exchange.1 = f32[2,72,16,128]{3,2,1,0:T(8,128)} custom-call(f32[42,16,128]{2,1,0:T(8,128)S(1)} %get-tuple-element.29.static_in, f32[32,8,128]{2,1,0:T(8,128)S(1)} %all-to-all-done.3.recv_ref, bf16[512,192]{1,0:T(8,128)(2,1)S(1)} %get-tuple-element.22.pick_ref, bf16[256,384]{1,0:T(8,128)(2,1)S(1)} %get-tuple-element.18.pack_ref, ...), custom_call_target="tpu_custom_call", output_to_operand_aliasing={{}: (5, {})} | custom-call | bytes 3000000 | tf_op jit(solution)/shard_map/last_exchange/pallas_call | solution.py:510
  (16 shorter events, 2.0 us)
Async XLA Ops:
  0.7 5.7 %collective-permute-start = (f32[2,16,128]{2,1,0:T(8,128)S(1)}, f32[2,16,128]{2,1,0:T(8,128)S(1)}, u32[]{:S(2)}, u32[]{:S(2)}) collective-permute-start(f32[2,16,128]{2,1,0:T(8,128)S(1)} %pad_maximum_fusion.refs_3_), channel_id=1, source_target_pairs={{0,8},{8,0},{1,9},{9,1},{2,10},{10,2},{3,11},{11,3},{4,12},{12,4},... | collective-permute-start | bytes 49160 | tf_op jit(solution)/shard_map/ppermute | solution.py:642
  3.8 0.7 %copy-start.3 = (f32[1,2,16,128]{3,2,1,0:T(8,128)S(1)}, f32[1,2,16,128]{3,2,1,0:T(8,128)}, u32[]{:S(2)}) copy-start(f32[1,2,16,128]{3,2,1,0:T(8,128)} %param.7) | copy-start | bytes 49156
  4.5 0.7 %copy-start.5 = (s32[1,128]{1,0:T(1,128)S(1)}, s32[1,128]{1,0:T(1,128)}, u32[]{:S(2)}) copy-start(s32[1,128]{1,0:T(1,128)} %refs_5_.1) | copy-start | bytes 1540
  5.1 7.4 %copy-start.4 = (f32[1,2,16,128]{3,2,1,0:T(8,128)S(1)}, f32[1,2,16,128]{3,2,1,0:T(8,128)}, u32[]{:S(2)}) copy-start(f32[1,2,16,128]{3,2,1,0:T(8,128)} %param.7) | copy-start | bytes 49156
  7.1 13.6 %all-to-all-start = ((f32[32,8,128]{2,1,0:T(8,128)}), f32[32,8,128]{2,1,0:T(8,128)S(1)}, u32[]{:S(2)}, u32[]{:S(2)}) async-start(f32[32,8,128]{2,1,0:T(8,128)} %get-tuple-element.21.refs_0_.after_ref), calls=%async_computation | async-start | bytes 262144 | tf_op jit(solution)/shard_map/all_to_all | solution.py:645
  14.6 10.2 %collective-permute-start.1 = (f32[16,1408]{1,0:T(8,128)S(1)}, f32[16,1408]{1,0:T(8,128)S(1)}, u32[]{:S(2)}, u32[]{:S(2)}) collective-permute-start(f32[16,1408]{1,0:T(8,128)S(1)} %get-tuple-element.27), channel_id=1, source_target_pairs={{1,0},{2,1},{3,2},{4,3},{5,4},{6,5},{7,6},{0,7},{9,8},{10,9},{11,1... | collective-permute-start | bytes 270344 | tf_op jit(solution)/shard_map/ppermute | solution.py:697
  22.2 10.8 %all-to-all-start.1 = ((f32[32,8,128]{2,1,0:T(8,128)}), f32[32,8,128]{2,1,0:T(8,128)S(1)}, u32[]{:S(2)}, u32[]{:S(2)}) async-start(f32[32,8,128]{2,1,0:T(8,128)} %get-tuple-element.24.refs_0_.after_ref), calls=%async_computation.1 | async-start | bytes 262144 | tf_op jit(solution)/shard_map/all_to_all | solution.py:645
  24.8 15.6 %copy-start = (f32[1,2,72,16,128]{4,3,2,1,0:T(8,128)S(1)}, f32[1,2,72,16,128]{4,3,2,1,0:T(8,128)}, u32[]{:S(2)}) copy-start(f32[1,2,72,16,128]{4,3,2,1,0:T(8,128)} %param.6) | copy-start | bytes 3538948
  24.8 15.6 %copy-start.1 = (f32[1,71,16,128]{3,2,1,0:T(8,128)S(1)}, f32[1,71,16,128]{3,2,1,0:T(8,128)}, u32[]{:S(2)}) copy-start(f32[1,71,16,128]{3,2,1,0:T(8,128)} %param.8) | copy-start | bytes 1744900
  25.0 0.8 %copy-start.2 = (f32[120,8,128]{2,1,0:T(8,128)}, f32[120,8,128]{2,1,0:T(8,128)S(1)}, u32[]{:S(2)}) copy-start(f32[120,8,128]{2,1,0:T(8,128)S(1)} %corner.1) | copy-start | bytes 1474564
  25.8 14.6 %collective-permute-start.2 = (f32[120,8,128]{2,1,0:T(8,128)}, f32[120,8,128]{2,1,0:T(8,128)S(1)}, u32[]{:S(2)}, u32[]{:S(2)}) collective-permute-start(f32[120,8,128]{2,1,0:T(8,128)} %copy-done.2), channel_id=1, source_target_pairs={{8,0},{0,8},{9,1},{1,9},{10,2},{2,10},{11,3},{3,11},{12,4},{4,12},... | collective-permute-start | bytes 1474568 | tf_op jit(solution)/shard_map/ppermute | solution.py:745
  34.5 10.8 %all-to-all-start.2 = ((f32[32,8,128]{2,1,0:T(8,128)}), f32[32,8,128]{2,1,0:T(8,128)S(1)}, u32[]{:S(2)}, u32[]{:S(2)}) async-start(f32[32,8,128]{2,1,0:T(8,128)} %get-tuple-element.26.refs_1_), calls=%async_computation.2 | async-start | bytes 262144 | tf_op jit(solution)/shard_map/all_to_all | solution.py:645
  46.8 10.8 %all-to-all-start.3 = ((f32[32,8,128]{2,1,0:T(8,128)}), f32[32,8,128]{2,1,0:T(8,128)S(1)}, u32[]{:S(2)}, u32[]{:S(2)}) async-start(f32[32,8,128]{2,1,0:T(8,128)} %get-tuple-element.30.after_ref), calls=%async_computation.3 | async-start | bytes 262144 | tf_op jit(solution)/shard_map/all_to_all | solution.py:645

commit v12 on v11

--- a/solution.py
+++ b/solution.py
@@ -692,7 +692,7 @@
         "halo",
         grid=(1,),
         us=2,
-        mib=53,
+        mib=16,
     )
     east = lax.ppermute(east, "lon", [((i + 1) % n_lon, i) for i in range(n_lon)])
     tall = rows + 2 * STEPS

time: 59.1 us -> 59.2 us (level)
  waiting for transfers between devices: 17.4 us -> 18.4 us
  local copies, waits for them, and re-layouts: 2.16 us -> 1.38 us
    all_to_all x4, waiting for transfers between devices: 14 us -> 15.1 us  [exchanged(): lax.all_to_all(send, ('mp', 'lat', 'lon'), split_axis=0, concat_axis=0, t...]
    unnamed x12 -> x10, local copies, waits for them, and re-layouts: 2.16 us -> 1.38 us
where the time goes in v12:
time: 59.2 us; the launch traced here: 58.7 us
  starting transfers between devices  21.1 us (36%)
  waiting for transfers between devices  18.4 us (31%)
  Pallas kernels  16.9 us (29%)
  local copies, waits for them, and re-layouts  1.38 us (2%)
  other arithmetic  0.74 us (1%)
    pallas_call x12, Pallas kernels, call(): pl.pallas_call(kernel, grid=grid, in_specs=specs, out_shape=out_shape, ou...  16.9 us
    all_to_all x4, waiting for transfers between devices, exchanged(): lax.all_to_all(send, ('mp', 'lat', 'lon'), split_axis=0, concat_axis=0, t...  15.1 us
    all_to_all x4, starting transfers between devices, exchanged(): lax.all_to_all(send, ('mp', 'lat', 'lon'), split_axis=0, concat_axis=0, t...  13 us
    ppermute x1, starting transfers between devices, local(): lax.ppermute(east, 'lon', [((i + 1) % n_lon, i) for i in range(n_lon)])  3.37 us
    ppermute x1, waiting for transfers between devices, local(): lax.ppermute(north, 'lat', [((i + 1) % n_lat, i) for i in range(n_lat)])  3.25 us
    ppermute x1, starting transfers between devices, local(): lax.ppermute(share, 'lat', [(i, (i + 1) % n_lat) for i in range(n_lat)])  3.02 us
    ppermute x1, starting transfers between devices, local(): lax.ppermute(north, 'lat', [((i + 1) % n_lat, i) for i in range(n_lat)])  1.72 us
    unnamed x10, local copies, waits for them, and re-layouts  1.38 us
  transfers between devices with their start and end apart: 7, of which 5 were waited for; matrix products, arithmetic and copies ran while one was open for 0% of the time, Pallas kernels for 23%

profile of v12, /device:TPU:0, one launch (start us, length us, event | category | flops | bytes accessed | tf_op | source)
XLA Modules:
  0.0 58.7 jit_solution(8970053956595958541)
XLA Ops:
  0.0 0.7 %fusion = (f32[1,16,128]{2,1,0:T(8,128)S(1)}, f32[1,16,128]{2,1,0:T(8,128)S(1)}, f32[16,128]{1,0:T(8,128)S(1)}) fusion(f32[1,16,128]{2,1,0:T(8,128)} %param.9, f32[1,71,16,128]{3,2,1,0:T(8,128)} %param.8, s32[1,16,128]{2,1,0:T(8,128)} %param.11), kind=kLoop, calls=%fused_computation.3 | loop fusion | flops 10240 | bytes 49152 | tf_op jit(solution)/shard_map/mul | solution.py:640
  0.7 3.0 %collective-permute-start = (f32[2,16,128]{2,1,0:T(8,128)S(1)}, f32[2,16,128]{2,1,0:T(8,128)S(1)}, u32[]{:S(2)}, u32[]{:S(2)}) collective-permute-start(f32[2,16,128]{2,1,0:T(8,128)S(1)} %pad_maximum_fusion.refs_3_), channel_id=1, source_target_pairs={{0,8},{8,0},{1,9},{9,1},{2,10},{10,2},{3,11},{11,3},{4,12},{12,4},... | collective-permute-start | bytes 49160 | tf_op jit(solution)/shard_map/ppermute | solution.py:642
  3.8 0.7 %copy-done.2 = f32[1,2,16,128]{3,2,1,0:T(8,128)S(1)} copy-done((f32[1,2,16,128]{3,2,1,0:T(8,128)S(1)}, f32[1,2,16,128]{3,2,1,0:T(8,128)}, u32[]{:S(2)}) %copy-start.2) | copy-done | bytes 16408
  5.1 0.9 %prepare.1 = (bf16[512,192]{1,0:T(8,128)(2,1)S(1)}, bf16[256,384]{1,0:T(8,128)(2,1)S(1)}, f32[42,16,128]{2,1,0:T(8,128)S(1)}) custom-call(f32[2,72,16,128]{3,2,1,0:T(8,128)} %bitcast.11, f32[71,16,128]{2,1,0:T(8,128)} %bitcast.16, f32[2,16,128]{2,1,0:T(8,128)S(1)} %bitcast.21, f32[2,16,128]{2,1,0:T(8,128)S(1)} %pad_maximum_fusion.refs_3_, ...), custom_call_target="tpu_custom_call" | custom-call | bytes 6000000 | tf_op jit(solution)/shard_map/prepare/pallas_call | solution.py:510
  7.2 5.3 %all-to-all-start = ((f32[32,8,128]{2,1,0:T(8,128)}), f32[32,8,128]{2,1,0:T(8,128)S(1)}, u32[]{:S(2)}, u32[]{:S(2)}) async-start(f32[32,8,128]{2,1,0:T(8,128)} %get-tuple-element.21.refs_0_.after_ref), calls=%async_computation | async-start | bytes 262144 | tf_op jit(solution)/shard_map/all_to_all | solution.py:645
  12.5 1.4 %halo.1 = (f32[120,8,128]{2,1,0:T(8,128)}, f32[16,1408]{1,0:T(8,128)S(1)}) custom-call(f32[32,8,128]{2,1,0:T(8,128)} %get-tuple-element.21.refs_0_.after_ref, f32[2,72,16,128]{3,2,1,0:T(8,128)S(1)} %bitcast.12, f32[71,16,128]{2,1,0:T(8,128)S(1)} %bitcast.17, f32[2,16,128]{2,1,0:T(8,128)S(1)} %bitcast.22), custom_call_target="tpu_custom_call" | custom-call | bytes 6000000 | tf_op jit(solution)/shard_map/halo/pallas_call | solution.py:510
  13.9 3.4 %collective-permute-start.1 = (f32[16,1408]{1,0:T(8,128)S(1)}, f32[16,1408]{1,0:T(8,128)S(1)}, u32[]{:S(2)}, u32[]{:S(2)}) collective-permute-start(f32[16,1408]{1,0:T(8,128)S(1)} %get-tuple-element.27), channel_id=1, source_target_pairs={{1,0},{2,1},{3,2},{4,3},{5,4},{6,5},{7,6},{0,7},{9,8},{10,9},{11,1... | collective-permute-start | bytes 270344 | tf_op jit(solution)/shard_map/ppermute | solution.py:697
  17.3 3.4 %all-to-all-done.recv_ref = f32[32,8,128]{2,1,0:T(8,128)S(1)} async-done(((f32[32,8,128]{2,1,0:T(8,128)}), f32[32,8,128]{2,1,0:T(8,128)S(1)}, u32[]{:S(2)}, u32[]{:S(2)}) %all-to-all-start) | async-done | bytes 131104 | tf_op jit(solution)/shard_map/all_to_all | solution.py:645
  20.7 1.6 %exchange.3 = (f32[42,16,128]{2,1,0:T(8,128)S(1)}, f32[32,8,128]{2,1,0:T(8,128)}) custom-call(f32[42,16,128]{2,1,0:T(8,128)S(1)} %get-tuple-element.20.static_in, f32[32,8,128]{2,1,0:T(8,128)S(1)} %all-to-all-done.recv_ref, bf16[512,192]{1,0:T(8,128)(2,1)S(1)} %get-tuple-element.22.pick_ref, ...), custom_call_target="tpu_custom_call", output_to_operand_aliasing={{0}: (0, {}), {1}: (4, {})} | custom-call | bytes 3000000 | tf_op jit(solution)/shard_map/exchange/pallas_call | solution.py:510
  22.3 2.6 %all-to-all-start.1 = ((f32[32,8,128]{2,1,0:T(8,128)}), f32[32,8,128]{2,1,0:T(8,128)S(1)}, u32[]{:S(2)}, u32[]{:S(2)}) async-start(f32[32,8,128]{2,1,0:T(8,128)} %get-tuple-element.24.refs_0_.after_ref), calls=%async_computation.1 | async-start | bytes 262144 | tf_op jit(solution)/shard_map/all_to_all | solution.py:645
  24.9 0.7 %corner.1 = f32[120,8,128]{2,1,0:T(8,128)} custom-call(f32[32,8,128]{2,1,0:T(8,128)} %get-tuple-element.24.refs_0_.after_ref, f32[16,1408]{1,0:T(8,128)S(1)} %collective-permute-done.1.east_ref.columns_ref.refs_3_.refs_4_, f32[120,8,128]{2,1,0:T(8,128)} %get-tuple-element.28.rows_in), custom_call_target="tpu_custom_call", output_to_operand_aliasing={{}: (2, {})} | custom-call | bytes 3000000 | tf_op jit(solution)/shard_map/corner/pallas_call | solution.py:510
  25.6 1.7 %collective-permute-start.2 = (f32[120,8,128]{2,1,0:T(8,128)}, f32[120,8,128]{2,1,0:T(8,128)S(1)}, u32[]{:S(2)}, u32[]{:S(2)}) collective-permute-start(f32[120,8,128]{2,1,0:T(8,128)} %corner.1), channel_id=1, source_target_pairs={{8,0},{0,8},{9,1},{1,9},{10,2},{2,10},{11,3},{3,11},{12,4},{4,12},... | collective-permute-start | bytes 1474568 | tf_op jit(solution)/shard_map/ppermute | solution.py:745
  27.3 5.7 %all-to-all-done.1.recv_ref = f32[32,8,128]{2,1,0:T(8,128)S(1)} async-done(((f32[32,8,128]{2,1,0:T(8,128)}), f32[32,8,128]{2,1,0:T(8,128)S(1)}, u32[]{:S(2)}, u32[]{:S(2)}) %all-to-all-start.1) | async-done | bytes 131104 | tf_op jit(solution)/shard_map/all_to_all | solution.py:645
  33.0 1.5 %exchange.4 = (f32[42,16,128]{2,1,0:T(8,128)S(1)}, f32[32,8,128]{2,1,0:T(8,128)}) custom-call(f32[42,16,128]{2,1,0:T(8,128)S(1)} %get-tuple-element.23.static_in, f32[32,8,128]{2,1,0:T(8,128)S(1)} %all-to-all-done.1.recv_ref, bf16[512,192]{1,0:T(8,128)(2,1)S(1)} %get-tuple-element.22.pick_ref, ...), custom_call_target="tpu_custom_call", output_to_operand_aliasing={{0}: (0, {}), {1}: (4, {})} | custom-call | bytes 3000000 | tf_op jit(solution)/shard_map/exchange/pallas_call | solution.py:510
  34.5 2.6 %all-to-all-start.2 = ((f32[32,8,128]{2,1,0:T(8,128)}), f32[32,8,128]{2,1,0:T(8,128)S(1)}, u32[]{:S(2)}, u32[]{:S(2)}) async-start(f32[32,8,128]{2,1,0:T(8,128)} %get-tuple-element.26.refs_1_), calls=%async_computation.2 | async-start | bytes 262144 | tf_op jit(solution)/shard_map/all_to_all | solution.py:645
  37.1 3.2 %collective-permute-done.2.rows_ref.refs_2_.refs_3_ = f32[120,8,128]{2,1,0:T(8,128)S(1)} collective-permute-done((f32[120,8,128]{2,1,0:T(8,128)}, f32[120,8,128]{2,1,0:T(8,128)S(1)}, u32[]{:S(2)}, u32[]{:S(2)}) %collective-permute-start.2) | collective-permute-done | bytes 491552 | tf_op jit(solution)/shard_map/ppermute | solution.py:745
  40.4 0.8 %early_levels.1.refs_0_ = f32[17,16,128]{2,1,0:T(8,128)S(1)} custom-call(f32[2,72,16,128]{3,2,1,0:T(8,128)S(1)} %bitcast.13, f32[71,16,128]{2,1,0:T(8,128)S(1)} %bitcast.18, f32[2,16,128]{2,1,0:T(8,128)S(1)} %bitcast.23, f32[120,8,128]{2,1,0:T(8,128)S(1)} %collective-permute-done.2.rows_ref.refs_2_.refs_3_, ...), custom_call_target="tpu_custom_call" | custom-call | bytes 6000000 | tf_op jit(solution)/shard_map/early_levels/pallas_call | solution.py:510
  41.1 4.2 %all-to-all-done.2.recv_ref = f32[32,8,128]{2,1,0:T(8,128)S(1)} async-done(((f32[32,8,128]{2,1,0:T(8,128)}), f32[32,8,128]{2,1,0:T(8,128)S(1)}, u32[]{:S(2)}, u32[]{:S(2)}) %all-to-all-start.2) | async-done | bytes 131104 | tf_op jit(solution)/shard_map/all_to_all | solution.py:645
  45.3 1.5 %exchange.5 = (f32[42,16,128]{2,1,0:T(8,128)S(1)}, f32[32,8,128]{2,1,0:T(8,128)}) custom-call(f32[42,16,128]{2,1,0:T(8,128)S(1)} %get-tuple-element.25.static_in, f32[32,8,128]{2,1,0:T(8,128)S(1)} %all-to-all-done.2.recv_ref, bf16[512,192]{1,0:T(8,128)(2,1)S(1)} %get-tuple-element.22.pick_ref, ...), custom_call_target="tpu_custom_call", output_to_operand_aliasing={{0}: (0, {}), {1}: (5, {})} | custom-call | bytes 3000000 | tf_op jit(solution)/shard_map/exchange/pallas_call | solution.py:510
  46.8 2.6 %all-to-all-start.3 = ((f32[32,8,128]{2,1,0:T(8,128)}), f32[32,8,128]{2,1,0:T(8,128)S(1)}, u32[]{:S(2)}, u32[]{:S(2)}) async-start(f32[32,8,128]{2,1,0:T(8,128)} %get-tuple-element.30.after_ref), calls=%async_computation.3 | async-start | bytes 262144 | tf_op jit(solution)/shard_map/all_to_all | solution.py:645
  49.4 3.2 %deep_levels.2.refs_0_ = f32[2,72,16,128]{3,2,1,0:T(8,128)} custom-call(f32[32,8,128]{2,1,0:T(8,128)} %get-tuple-element.30.after_ref, f32[2,72,16,128]{3,2,1,0:T(8,128)S(1)} %bitcast.14, f32[71,16,128]{2,1,0:T(8,128)S(1)} %bitcast.19, f32[2,16,128]{2,1,0:T(8,128)S(1)} %bitcast.24, f32[120,8,128]{2,1,0:T(8,128)S(1)} %collective-permute-done.2.rows_ref.refs_2_.refs_3_, ...), custom_call_target="tpu_custom_call" | custom-call | bytes 12000000 | tf_op jit(solution)/shard_map/deep_levels/pallas_call | solution.py:510
  52.6 3.1 %deep_levels.3.refs_1_ = f32[2,72,16,128]{3,2,1,0:T(8,128)} custom-call(f32[32,8,128]{2,1,0:T(8,128)} %get-tuple-element.30.after_ref, f32[2,72,16,128]{3,2,1,0:T(8,128)S(1)} %bitcast.15, f32[2,72,16,128]{3,2,1,0:T(8,128)} %deep_levels.2.refs_0_, f32[71,16,128]{2,1,0:T(8,128)S(1)} %bitcast.20, ...), custom_call_target="tpu_custom_call", output_to_operand_aliasing={{}: (2, {})} | custom-call | bytes 12000000 | tf_op jit(solution)/shard_map/deep_levels/pallas_call | solution.py:510
  55.7 1.9 %all-to-all-done.3.recv_ref = f32[32,8,128]{2,1,0:T(8,128)S(1)} async-done(((f32[32,8,128]{2,1,0:T(8,128)}), f32[32,8,128]{2,1,0:T(8,128)S(1)}, u32[]{:S(2)}, u32[]{:S(2)}) %all-to-all-start.3) | async-done | bytes 131104 | tf_op jit(solution)/shard_map/all_to_all | solution.py:645
  57.6 1.1 %last_exchange.1 = f32[2,72,16,128]{3,2,1,0:T(8,128)} custom-call(f32[42,16,128]{2,1,0:T(8,128)S(1)} %get-tuple-element.29.static_in, f32[32,8,128]{2,1,0:T(8,128)S(1)} %all-to-all-done.3.recv_ref, bf16[512,192]{1,0:T(8,128)(2,1)S(1)} %get-tuple-element.22.pick_ref, bf16[256,384]{1,0:T(8,128)(2,1)S(1)} %get-tuple-element.18.pack_ref, ...), custom_call_target="tpu_custom_call", output_to_operand_aliasing={{}: (5, {})} | custom-call | bytes 3000000 | tf_op jit(solution)/shard_map/last_exchange/pallas_call | solution.py:510
  (14 shorter events, 1.8 us)
Async XLA Ops:
  0.7 5.8 %collective-permute-start = (f32[2,16,128]{2,1,0:T(8,128)S(1)}, f32[2,16,128]{2,1,0:T(8,128)S(1)}, u32[]{:S(2)}, u32[]{:S(2)}) collective-permute-start(f32[2,16,128]{2,1,0:T(8,128)S(1)} %pad_maximum_fusion.refs_3_), channel_id=1, source_target_pairs={{0,8},{8,0},{1,9},{9,1},{2,10},{10,2},{3,11},{11,3},{4,12},{12,4},... | collective-permute-start | bytes 49160 | tf_op jit(solution)/shard_map/ppermute | solution.py:642
  3.8 0.7 %copy-start.2 = (f32[1,2,16,128]{3,2,1,0:T(8,128)S(1)}, f32[1,2,16,128]{3,2,1,0:T(8,128)}, u32[]{:S(2)}) copy-start(f32[1,2,16,128]{3,2,1,0:T(8,128)} %param.7) | copy-start | bytes 49156
  4.5 0.7 %copy-start.4 = (s32[1,128]{1,0:T(1,128)S(1)}, s32[1,128]{1,0:T(1,128)}, u32[]{:S(2)}) copy-start(s32[1,128]{1,0:T(1,128)} %refs_5_.1) | copy-start | bytes 1540
  5.1 7.4 %copy-start = (f32[1,2,72,16,128]{4,3,2,1,0:T(8,128)S(1)}, f32[1,2,72,16,128]{4,3,2,1,0:T(8,128)}, u32[]{:S(2)}) copy-start(f32[1,2,72,16,128]{4,3,2,1,0:T(8,128)} %param.6) | copy-start | bytes 3538948
  5.1 7.4 %copy-start.1 = (f32[1,71,16,128]{3,2,1,0:T(8,128)S(1)}, f32[1,71,16,128]{3,2,1,0:T(8,128)}, u32[]{:S(2)}) copy-start(f32[1,71,16,128]{3,2,1,0:T(8,128)} %param.8) | copy-start | bytes 1744900
  5.1 7.4 %copy-start.3 = (f32[1,2,16,128]{3,2,1,0:T(8,128)S(1)}, f32[1,2,16,128]{3,2,1,0:T(8,128)}, u32[]{:S(2)}) copy-start(f32[1,2,16,128]{3,2,1,0:T(8,128)} %param.7) | copy-start | bytes 49156
  7.2 13.5 %all-to-all-start = ((f32[32,8,128]{2,1,0:T(8,128)}), f32[32,8,128]{2,1,0:T(8,128)S(1)}, u32[]{:S(2)}, u32[]{:S(2)}) async-start(f32[32,8,128]{2,1,0:T(8,128)} %get-tuple-element.21.refs_0_.after_ref), calls=%async_computation | async-start | bytes 262144 | tf_op jit(solution)/shard_map/all_to_all | solution.py:645
  13.9 10.9 %collective-permute-start.1 = (f32[16,1408]{1,0:T(8,128)S(1)}, f32[16,1408]{1,0:T(8,128)S(1)}, u32[]{:S(2)}, u32[]{:S(2)}) collective-permute-start(f32[16,1408]{1,0:T(8,128)S(1)} %get-tuple-element.27), channel_id=1, source_target_pairs={{1,0},{2,1},{3,2},{4,3},{5,4},{6,5},{7,6},{0,7},{9,8},{10,9},{11,1... | collective-permute-start | bytes 270344 | tf_op jit(solution)/shard_map/ppermute | solution.py:697
  22.3 10.8 %all-to-all-start.1 = ((f32[32,8,128]{2,1,0:T(8,128)}), f32[32,8,128]{2,1,0:T(8,128)S(1)}, u32[]{:S(2)}, u32[]{:S(2)}) async-start(f32[32,8,128]{2,1,0:T(8,128)} %get-tuple-element.24.refs_0_.after_ref), calls=%async_computation.1 | async-start | bytes 262144 | tf_op jit(solution)/shard_map/all_to_all | solution.py:645
  25.6 14.8 %collective-permute-start.2 = (f32[120,8,128]{2,1,0:T(8,128)}, f32[120,8,128]{2,1,0:T(8,128)S(1)}, u32[]{:S(2)}, u32[]{:S(2)}) collective-permute-start(f32[120,8,128]{2,1,0:T(8,128)} %corner.1), channel_id=1, source_target_pairs={{8,0},{0,8},{9,1},{1,9},{10,2},{2,10},{11,3},{3,11},{12,4},{4,12},... | collective-permute-start | bytes 1474568 | tf_op jit(solution)/shard_map/ppermute | solution.py:745
  34.5 10.8 %all-to-all-start.2 = ((f32[32,8,128]{2,1,0:T(8,128)}), f32[32,8,128]{2,1,0:T(8,128)S(1)}, u32[]{:S(2)}, u32[]{:S(2)}) async-start(f32[32,8,128]{2,1,0:T(8,128)} %get-tuple-element.26.refs_1_), calls=%async_computation.2 | async-start | bytes 262144 | tf_op jit(solution)/shard_map/all_to_all | solution.py:645
  46.8 10.8 %all-to-all-start.3 = ((f32[32,8,128]{2,1,0:T(8,128)}), f32[32,8,128]{2,1,0:T(8,128)S(1)}, u32[]{:S(2)}, u32[]{:S(2)}) async-start(f32[32,8,128]{2,1,0:T(8,128)} %get-tuple-element.30.after_ref), calls=%async_computation.3 | async-start | bytes 262144 | tf_op jit(solution)/shard_map/all_to_all | solution.py:645

commit v13 on v12

--- a/solution.py
+++ b/solution.py
@@ -54,21 +54,18 @@
     return pltpu.roll(value, value.shape[0] - 1, 0)
 
 
-def three_parts(value):
+def two_parts(value):
     high = value.astype(BF16)
-    rest = value - high.astype(F32)
-    middle = rest.astype(BF16)
-    low = (rest - middle.astype(F32)).astype(BF16)
-    return high, middle, low
+    return high, (value - high.astype(F32)).astype(BF16)
 
 
 def picked(one_hot, value):
-    return jnp.dot(one_hot, jnp.concatenate(three_parts(value), axis=0), preferred_element_type=F32)
+    return jnp.dot(one_hot, jnp.concatenate(two_parts(value), axis=0), preferred_element_type=F32)
 
 
 def spread_by(value, one_hot):
-    one_hot = jnp.concatenate([one_hot] * 3, axis=0)
-    return jnp.dot(jnp.concatenate(three_parts(value), axis=1), one_hot, preferred_element_type=F32)
+    one_hot = jnp.concatenate([one_hot] * 2, axis=0)
+    return jnp.dot(jnp.concatenate(two_parts(value), axis=1), one_hot, preferred_element_type=F32)
 
 
 def pack_halo(fields_ref, kappa_ref, courant_ref, rows_ref, columns_ref):
@@ -305,7 +302,7 @@
     edges = jnp.concatenate(
         [empty, edge_north[0], edge_east[0], empty, edge_north[1], edge_east[1]], axis=0
     )
-    table = jnp.concatenate(three_parts(jnp.concatenate(tiles, axis=1)), axis=0)
+    table = jnp.concatenate(two_parts(jnp.concatenate(tiles, axis=1)), axis=0)
     height = pack_ref.shape[0] // (groups * PARTS)
     main_rows = height * PARTS // devices
     slot_group = (lane_iota((height, tracers * cols)) % cols) // TILE
@@ -570,7 +567,7 @@
     packing = packing + (line_target % per_part) * main_rows + sent // groups
     slots = lax.broadcasted_iota(jnp.int32, (pack_ref.shape[0], count), 0)
     packing = (slots == packing).astype(F32).astype(BF16)
-    for i in range(3):
+    for i in range(2):
         pack_ref[:, i * count : (i + 1) * count] = packing
 
     lane = lax.broadcasted_iota(jnp.int32, (count, groups * TILE), 1)
@@ -647,8 +644,8 @@
     main_rows = -(-max(2, 2 * count // devices) // groups)
     width = ((tracers + 1) * -(-levels // PACKED) + 2) * cols
     table_shapes = (
-        jax.ShapeDtypeStruct((4 * count, 3 * devices * SLAB), BF16),
-        jax.ShapeDtypeStruct((groups * devices * main_rows, 3 * count), BF16),
+        jax.ShapeDtypeStruct((4 * count, 2 * devices * SLAB), BF16),
+        jax.ShapeDtypeStruct((groups * devices * main_rows, 2 * count), BF16),
     )
     planes_shape = shaped(LATE + tracers * STEPS + 3 * groups, rows, cols)
     north_shape = shaped((tracers + 1) * (levels // 2) + 1 + width // cols, 2 * STEPS, cols)

time: 59.2 us -> 59 us (level)
  no operation moved by 1% of the time
where the time goes in v13:
time: 59 us; the launch traced here: 58.5 us
  starting transfers between devices  21.2 us (36%)
  waiting for transfers between devices  18.4 us (31%)
  Pallas kernels  16.7 us (28%)
  local copies, waits for them, and re-layouts  1.38 us (2%)
  other arithmetic  0.74 us (1%)
    pallas_call x12, Pallas kernels, call(): pl.pallas_call(kernel, grid=grid, in_specs=specs, out_shape=out_shape, ou...  16.7 us
    all_to_all x4, waiting for transfers between devices, exchanged(): lax.all_to_all(send, ('mp', 'lat', 'lon'), split_axis=0, concat_axis=0, t...  15.1 us
    all_to_all x4, starting transfers between devices, exchanged(): lax.all_to_all(send, ('mp', 'lat', 'lon'), split_axis=0, concat_axis=0, t...  13.1 us
    ppermute x1, starting transfers between devices, local(): lax.ppermute(east, 'lon', [((i + 1) % n_lon, i) for i in range(n_lon)])  3.37 us
    ppermute x1, waiting for transfers between devices, local(): lax.ppermute(north, 'lat', [((i + 1) % n_lat, i) for i in range(n_lat)])  3.3 us
    ppermute x1, starting transfers between devices, local(): lax.ppermute(share, 'lat', [(i, (i + 1) % n_lat) for i in range(n_lat)])  3.02 us
    ppermute x1, starting transfers between devices, local(): lax.ppermute(north, 'lat', [((i + 1) % n_lat, i) for i in range(n_lat)])  1.72 us
    unnamed x10, local copies, waits for them, and re-layouts  1.38 us
  transfers between devices with their start and end apart: 7, of which 5 were waited for; matrix products, arithmetic and copies ran while one was open for 0% of the time, Pallas kernels for 23%

profile of v13, /device:TPU:0, one launch (start us, length us, event | category | flops | bytes accessed | tf_op | source)
XLA Modules:
  0.0 58.5 jit_solution(10106140605702291787)
XLA Ops:
  0.0 0.7 %fusion = (f32[1,16,128]{2,1,0:T(8,128)S(1)}, f32[1,16,128]{2,1,0:T(8,128)S(1)}, f32[16,128]{1,0:T(8,128)S(1)}) fusion(f32[1,16,128]{2,1,0:T(8,128)} %param.9, f32[1,71,16,128]{3,2,1,0:T(8,128)} %param.8, s32[1,16,128]{2,1,0:T(8,128)} %param.11), kind=kLoop, calls=%fused_computation.3 | loop fusion | flops 10240 | bytes 49152 | tf_op jit(solution)/shard_map/mul | solution.py:637
  0.7 3.0 %collective-permute-start = (f32[2,16,128]{2,1,0:T(8,128)S(1)}, f32[2,16,128]{2,1,0:T(8,128)S(1)}, u32[]{:S(2)}, u32[]{:S(2)}) collective-permute-start(f32[2,16,128]{2,1,0:T(8,128)S(1)} %pad_maximum_fusion.refs_3_), channel_id=1, source_target_pairs={{0,8},{8,0},{1,9},{9,1},{2,10},{10,2},{3,11},{11,3},{4,12},{12,4},... | collective-permute-start | bytes 49160 | tf_op jit(solution)/shard_map/ppermute | solution.py:639
  3.8 0.7 %copy-done.2 = f32[1,2,16,128]{3,2,1,0:T(8,128)S(1)} copy-done((f32[1,2,16,128]{3,2,1,0:T(8,128)S(1)}, f32[1,2,16,128]{3,2,1,0:T(8,128)}, u32[]{:S(2)}) %copy-start.2) | copy-done | bytes 16408
  5.1 0.9 %prepare.1 = (bf16[512,128]{1,0:T(8,128)(2,1)S(1)}, bf16[256,256]{1,0:T(8,128)(2,1)S(1)}, f32[42,16,128]{2,1,0:T(8,128)S(1)}) custom-call(f32[2,72,16,128]{3,2,1,0:T(8,128)} %bitcast.11, f32[71,16,128]{2,1,0:T(8,128)} %bitcast.16, f32[2,16,128]{2,1,0:T(8,128)S(1)} %bitcast.21, f32[2,16,128]{2,1,0:T(8,128)S(1)} %pad_maximum_fusion.refs_3_, ...), custom_call_target="tpu_custom_call" | custom-call | bytes 6000000 | tf_op jit(solution)/shard_map/prepare/pallas_call | solution.py:507
  7.2 5.3 %all-to-all-start = ((f32[32,8,128]{2,1,0:T(8,128)}), f32[32,8,128]{2,1,0:T(8,128)S(1)}, u32[]{:S(2)}, u32[]{:S(2)}) async-start(f32[32,8,128]{2,1,0:T(8,128)} %get-tuple-element.21.refs_0_.after_ref), calls=%async_computation | async-start | bytes 262144 | tf_op jit(solution)/shard_map/all_to_all | solution.py:642
  12.5 1.4 %halo.1 = (f32[120,8,128]{2,1,0:T(8,128)}, f32[16,1408]{1,0:T(8,128)S(1)}) custom-call(f32[32,8,128]{2,1,0:T(8,128)} %get-tuple-element.21.refs_0_.after_ref, f32[2,72,16,128]{3,2,1,0:T(8,128)S(1)} %bitcast.12, f32[71,16,128]{2,1,0:T(8,128)S(1)} %bitcast.17, f32[2,16,128]{2,1,0:T(8,128)S(1)} %bitcast.22), custom_call_target="tpu_custom_call" | custom-call | bytes 6000000 | tf_op jit(solution)/shard_map/halo/pallas_call | solution.py:507
  13.9 3.4 %collective-permute-start.1 = (f32[16,1408]{1,0:T(8,128)S(1)}, f32[16,1408]{1,0:T(8,128)S(1)}, u32[]{:S(2)}, u32[]{:S(2)}) collective-permute-start(f32[16,1408]{1,0:T(8,128)S(1)} %get-tuple-element.27), channel_id=1, source_target_pairs={{1,0},{2,1},{3,2},{4,3},{5,4},{6,5},{7,6},{0,7},{9,8},{10,9},{11,1... | collective-permute-start | bytes 270344 | tf_op jit(solution)/shard_map/ppermute | solution.py:694
  17.3 3.4 %all-to-all-done.recv_ref = f32[32,8,128]{2,1,0:T(8,128)S(1)} async-done(((f32[32,8,128]{2,1,0:T(8,128)}), f32[32,8,128]{2,1,0:T(8,128)S(1)}, u32[]{:S(2)}, u32[]{:S(2)}) %all-to-all-start) | async-done | bytes 131104 | tf_op jit(solution)/shard_map/all_to_all | solution.py:642
  20.7 1.5 %exchange.3 = (f32[42,16,128]{2,1,0:T(8,128)S(1)}, f32[32,8,128]{2,1,0:T(8,128)}) custom-call(f32[42,16,128]{2,1,0:T(8,128)S(1)} %get-tuple-element.20.static_in, f32[32,8,128]{2,1,0:T(8,128)S(1)} %all-to-all-done.recv_ref, bf16[512,128]{1,0:T(8,128)(2,1)S(1)} %get-tuple-element.22.pick_ref, ...), custom_call_target="tpu_custom_call", output_to_operand_aliasing={{0}: (0, {}), {1}: (4, {})} | custom-call | bytes 3000000 | tf_op jit(solution)/shard_map/exchange/pallas_call | solution.py:507
  22.2 2.6 %all-to-all-start.1 = ((f32[32,8,128]{2,1,0:T(8,128)}), f32[32,8,128]{2,1,0:T(8,128)S(1)}, u32[]{:S(2)}, u32[]{:S(2)}) async-start(f32[32,8,128]{2,1,0:T(8,128)} %get-tuple-element.24.refs_0_.after_ref), calls=%async_computation.1 | async-start | bytes 262144 | tf_op jit(solution)/shard_map/all_to_all | solution.py:642
  24.8 0.7 %corner.1 = f32[120,8,128]{2,1,0:T(8,128)} custom-call(f32[32,8,128]{2,1,0:T(8,128)} %get-tuple-element.24.refs_0_.after_ref, f32[16,1408]{1,0:T(8,128)S(1)} %collective-permute-done.1.east_ref.columns_ref.refs_3_.refs_4_, f32[120,8,128]{2,1,0:T(8,128)} %get-tuple-element.28.rows_in), custom_call_target="tpu_custom_call", output_to_operand_aliasing={{}: (2, {})} | custom-call | bytes 3000000 | tf_op jit(solution)/shard_map/corner/pallas_call | solution.py:507
  25.5 1.7 %collective-permute-start.2 = (f32[120,8,128]{2,1,0:T(8,128)}, f32[120,8,128]{2,1,0:T(8,128)S(1)}, u32[]{:S(2)}, u32[]{:S(2)}) collective-permute-start(f32[120,8,128]{2,1,0:T(8,128)} %corner.1), channel_id=1, source_target_pairs={{8,0},{0,8},{9,1},{1,9},{10,2},{2,10},{11,3},{3,11},{12,4},{4,12},... | collective-permute-start | bytes 1474568 | tf_op jit(solution)/shard_map/ppermute | solution.py:742
  27.2 5.7 %all-to-all-done.1.recv_ref = f32[32,8,128]{2,1,0:T(8,128)S(1)} async-done(((f32[32,8,128]{2,1,0:T(8,128)}), f32[32,8,128]{2,1,0:T(8,128)S(1)}, u32[]{:S(2)}, u32[]{:S(2)}) %all-to-all-start.1) | async-done | bytes 131104 | tf_op jit(solution)/shard_map/all_to_all | solution.py:642
  33.0 1.5 %exchange.4 = (f32[42,16,128]{2,1,0:T(8,128)S(1)}, f32[32,8,128]{2,1,0:T(8,128)}) custom-call(f32[42,16,128]{2,1,0:T(8,128)S(1)} %get-tuple-element.23.static_in, f32[32,8,128]{2,1,0:T(8,128)S(1)} %all-to-all-done.1.recv_ref, bf16[512,128]{1,0:T(8,128)(2,1)S(1)} %get-tuple-element.22.pick_ref, ...), custom_call_target="tpu_custom_call", output_to_operand_aliasing={{0}: (0, {}), {1}: (4, {})} | custom-call | bytes 3000000 | tf_op jit(solution)/shard_map/exchange/pallas_call | solution.py:507
  34.4 2.6 %all-to-all-start.2 = ((f32[32,8,128]{2,1,0:T(8,128)}), f32[32,8,128]{2,1,0:T(8,128)S(1)}, u32[]{:S(2)}, u32[]{:S(2)}) async-start(f32[32,8,128]{2,1,0:T(8,128)} %get-tuple-element.26.refs_1_), calls=%async_computation.2 | async-start | bytes 262144 | tf_op jit(solution)/shard_map/all_to_all | solution.py:642
  37.0 3.3 %collective-permute-done.2.rows_ref.refs_2_.refs_3_ = f32[120,8,128]{2,1,0:T(8,128)S(1)} collective-permute-done((f32[120,8,128]{2,1,0:T(8,128)}, f32[120,8,128]{2,1,0:T(8,128)S(1)}, u32[]{:S(2)}, u32[]{:S(2)}) %collective-permute-start.2) | collective-permute-done | bytes 491552 | tf_op jit(solution)/shard_map/ppermute | solution.py:742
  40.3 0.8 %early_levels.1.refs_0_ = f32[17,16,128]{2,1,0:T(8,128)S(1)} custom-call(f32[2,72,16,128]{3,2,1,0:T(8,128)S(1)} %bitcast.13, f32[71,16,128]{2,1,0:T(8,128)S(1)} %bitcast.18, f32[2,16,128]{2,1,0:T(8,128)S(1)} %bitcast.23, f32[120,8,128]{2,1,0:T(8,128)S(1)} %collective-permute-done.2.rows_ref.refs_2_.refs_3_, ...), custom_call_target="tpu_custom_call" | custom-call | bytes 6000000 | tf_op jit(solution)/shard_map/early_levels/pallas_call | solution.py:507
  41.1 4.1 %all-to-all-done.2.recv_ref = f32[32,8,128]{2,1,0:T(8,128)S(1)} async-done(((f32[32,8,128]{2,1,0:T(8,128)}), f32[32,8,128]{2,1,0:T(8,128)S(1)}, u32[]{:S(2)}, u32[]{:S(2)}) %all-to-all-start.2) | async-done | bytes 131104 | tf_op jit(solution)/shard_map/all_to_all | solution.py:642
  45.2 1.5 %exchange.5 = (f32[42,16,128]{2,1,0:T(8,128)S(1)}, f32[32,8,128]{2,1,0:T(8,128)}) custom-call(f32[42,16,128]{2,1,0:T(8,128)S(1)} %get-tuple-element.25.static_in, f32[32,8,128]{2,1,0:T(8,128)S(1)} %all-to-all-done.2.recv_ref, bf16[512,128]{1,0:T(8,128)(2,1)S(1)} %get-tuple-element.22.pick_ref, ...), custom_call_target="tpu_custom_call", output_to_operand_aliasing={{0}: (0, {}), {1}: (5, {})} | custom-call | bytes 3000000 | tf_op jit(solution)/shard_map/exchange/pallas_call | solution.py:507
  46.7 2.6 %all-to-all-start.3 = ((f32[32,8,128]{2,1,0:T(8,128)}), f32[32,8,128]{2,1,0:T(8,128)S(1)}, u32[]{:S(2)}, u32[]{:S(2)}) async-start(f32[32,8,128]{2,1,0:T(8,128)} %get-tuple-element.30.after_ref), calls=%async_computation.3 | async-start | bytes 262144 | tf_op jit(solution)/shard_map/all_to_all | solution.py:642
  49.3 3.2 %deep_levels.2.refs_0_ = f32[2,72,16,128]{3,2,1,0:T(8,128)} custom-call(f32[32,8,128]{2,1,0:T(8,128)} %get-tuple-element.30.after_ref, f32[2,72,16,128]{3,2,1,0:T(8,128)S(1)} %bitcast.14, f32[71,16,128]{2,1,0:T(8,128)S(1)} %bitcast.19, f32[2,16,128]{2,1,0:T(8,128)S(1)} %bitcast.24, f32[120,8,128]{2,1,0:T(8,128)S(1)} %collective-permute-done.2.rows_ref.refs_2_.refs_3_, ...), custom_call_target="tpu_custom_call" | custom-call | bytes 12000000 | tf_op jit(solution)/shard_map/deep_levels/pallas_call | solution.py:507
  52.4 3.1 %deep_levels.3.refs_1_ = f32[2,72,16,128]{3,2,1,0:T(8,128)} custom-call(f32[32,8,128]{2,1,0:T(8,128)} %get-tuple-element.30.after_ref, f32[2,72,16,128]{3,2,1,0:T(8,128)S(1)} %bitcast.15, f32[2,72,16,128]{3,2,1,0:T(8,128)} %deep_levels.2.refs_0_, f32[71,16,128]{2,1,0:T(8,128)S(1)} %bitcast.20, ...), custom_call_target="tpu_custom_call", output_to_operand_aliasing={{}: (2, {})} | custom-call | bytes 12000000 | tf_op jit(solution)/shard_map/deep_levels/pallas_call | solution.py:507
  55.6 1.9 %all-to-all-done.3.recv_ref = f32[32,8,128]{2,1,0:T(8,128)S(1)} async-done(((f32[32,8,128]{2,1,0:T(8,128)}), f32[32,8,128]{2,1,0:T(8,128)S(1)}, u32[]{:S(2)}, u32[]{:S(2)}) %all-to-all-start.3) | async-done | bytes 131104 | tf_op jit(solution)/shard_map/all_to_all | solution.py:642
  57.5 1.0 %last_exchange.1 = f32[2,72,16,128]{3,2,1,0:T(8,128)} custom-call(f32[42,16,128]{2,1,0:T(8,128)S(1)} %get-tuple-element.29.static_in, f32[32,8,128]{2,1,0:T(8,128)S(1)} %all-to-all-done.3.recv_ref, bf16[512,128]{1,0:T(8,128)(2,1)S(1)} %get-tuple-element.22.pick_ref, bf16[256,256]{1,0:T(8,128)(2,1)S(1)} %get-tuple-element.18.pack_ref, ...), custom_call_target="tpu_custom_call", output_to_operand_aliasing={{}: (5, {})} | custom-call | bytes 3000000 | tf_op jit(solution)/shard_map/last_exchange/pallas_call | solution.py:507
  (14 shorter events, 1.7 us)
Async XLA Ops:
  0.7 5.8 %collective-permute-start = (f32[2,16,128]{2,1,0:T(8,128)S(1)}, f32[2,16,128]{2,1,0:T(8,128)S(1)}, u32[]{:S(2)}, u32[]{:S(2)}) collective-permute-start(f32[2,16,128]{2,1,0:T(8,128)S(1)} %pad_maximum_fusion.refs_3_), channel_id=1, source_target_pairs={{0,8},{8,0},{1,9},{9,1},{2,10},{10,2},{3,11},{11,3},{4,12},{12,4},... | collective-permute-start | bytes 49160 | tf_op jit(solution)/shard_map/ppermute | solution.py:639
  3.8 0.7 %copy-start.2 = (f32[1,2,16,128]{3,2,1,0:T(8,128)S(1)}, f32[1,2,16,128]{3,2,1,0:T(8,128)}, u32[]{:S(2)}) copy-start(f32[1,2,16,128]{3,2,1,0:T(8,128)} %param.7) | copy-start | bytes 49156
  4.5 0.7 %copy-start.4 = (s32[1,128]{1,0:T(1,128)S(1)}, s32[1,128]{1,0:T(1,128)}, u32[]{:S(2)}) copy-start(s32[1,128]{1,0:T(1,128)} %refs_5_.1) | copy-start | bytes 1540
  5.1 7.4 %copy-start = (f32[1,2,72,16,128]{4,3,2,1,0:T(8,128)S(1)}, f32[1,2,72,16,128]{4,3,2,1,0:T(8,128)}, u32[]{:S(2)}) copy-start(f32[1,2,72,16,128]{4,3,2,1,0:T(8,128)} %param.6) | copy-start | bytes 3538948
  5.1 7.4 %copy-start.1 = (f32[1,71,16,128]{3,2,1,0:T(8,128)S(1)}, f32[1,71,16,128]{3,2,1,0:T(8,128)}, u32[]{:S(2)}) copy-start(f32[1,71,16,128]{3,2,1,0:T(8,128)} %param.8) | copy-start | bytes 1744900
  5.1 7.4 %copy-start.3 = (f32[1,2,16,128]{3,2,1,0:T(8,128)S(1)}, f32[1,2,16,128]{3,2,1,0:T(8,128)}, u32[]{:S(2)}) copy-start(f32[1,2,16,128]{3,2,1,0:T(8,128)} %param.7) | copy-start | bytes 49156
  7.2 13.5 %all-to-all-start = ((f32[32,8,128]{2,1,0:T(8,128)}), f32[32,8,128]{2,1,0:T(8,128)S(1)}, u32[]{:S(2)}, u32[]{:S(2)}) async-start(f32[32,8,128]{2,1,0:T(8,128)} %get-tuple-element.21.refs_0_.after_ref), calls=%async_computation | async-start | bytes 262144 | tf_op jit(solution)/shard_map/all_to_all | solution.py:642
  13.9 10.9 %collective-permute-start.1 = (f32[16,1408]{1,0:T(8,128)S(1)}, f32[16,1408]{1,0:T(8,128)S(1)}, u32[]{:S(2)}, u32[]{:S(2)}) collective-permute-start(f32[16,1408]{1,0:T(8,128)S(1)} %get-tuple-element.27), channel_id=1, source_target_pairs={{1,0},{2,1},{3,2},{4,3},{5,4},{6,5},{7,6},{0,7},{9,8},{10,9},{11,1... | collective-permute-start | bytes 270344 | tf_op jit(solution)/shard_map/ppermute | solution.py:694
  22.2 10.8 %all-to-all-start.1 = ((f32[32,8,128]{2,1,0:T(8,128)}), f32[32,8,128]{2,1,0:T(8,128)S(1)}, u32[]{:S(2)}, u32[]{:S(2)}) async-start(f32[32,8,128]{2,1,0:T(8,128)} %get-tuple-element.24.refs_0_.after_ref), calls=%async_computation.1 | async-start | bytes 262144 | tf_op jit(solution)/shard_map/all_to_all | solution.py:642
  25.5 14.8 %collective-permute-start.2 = (f32[120,8,128]{2,1,0:T(8,128)}, f32[120,8,128]{2,1,0:T(8,128)S(1)}, u32[]{:S(2)}, u32[]{:S(2)}) collective-permute-start(f32[120,8,128]{2,1,0:T(8,128)} %corner.1), channel_id=1, source_target_pairs={{8,0},{0,8},{9,1},{1,9},{10,2},{2,10},{11,3},{3,11},{12,4},{4,12},... | collective-permute-start | bytes 1474568 | tf_op jit(solution)/shard_map/ppermute | solution.py:742
  34.4 10.8 %all-to-all-start.2 = ((f32[32,8,128]{2,1,0:T(8,128)}), f32[32,8,128]{2,1,0:T(8,128)S(1)}, u32[]{:S(2)}, u32[]{:S(2)}) async-start(f32[32,8,128]{2,1,0:T(8,128)} %get-tuple-element.26.refs_1_), calls=%async_computation.2 | async-start | bytes 262144 | tf_op jit(solution)/shard_map/all_to_all | solution.py:642
  46.7 10.8 %all-to-all-start.3 = ((f32[32,8,128]{2,1,0:T(8,128)}), f32[32,8,128]{2,1,0:T(8,128)S(1)}, u32[]{:S(2)}, u32[]{:S(2)}) async-start(f32[32,8,128]{2,1,0:T(8,128)} %get-tuple-element.30.after_ref), calls=%async_computation.3 | async-start | bytes 262144 | tf_op jit(solution)/shard_map/all_to_all | solution.py:642
